TPU v7x, 32 devices: a whole 2x2x4 slice. The times are simulated.
32 devices in a mesh: groups: 2 (over y), dp: 16 (over z, x, core), tensor: 1.
Axes of the slice: x: 2, y: 2, z: 4, core: 2. Of those that a mesh axis runs over, the one named last changes fastest.
Arguments:
- hidden: bfloat16 [8192, 8192], P(('groups', 'dp'), 'tensor'), parts along dimension 0, may hold values from -6 to 6
- norm_gain: bfloat16 [8192], replicated, may hold values from 0.099609375 to 1.8984375
- key_weight: bfloat16 [8192, 512], P('dp', 'tensor'), may hold values from -0.0625 to 0.0625
- value_weight: bfloat16 [8192, 512], P('dp', 'tensor'), may hold values from -0.0625 to 0.0625
- queries: bfloat16 [8192, 4096], P(('groups', 'dp'), 'tensor'), parts along dimension 0, may hold values from -70 to 70
- segment_ids: int32 [8192], P(('groups', 'dp')), parts along dimension 0, may hold values from 0 to 63, never falling along the last dimension, each value on 1 to 128 neighbouring positions
Outputs:
- context: bfloat16 [8192, 4096], P(('groups', 'dp'), 'tensor'), parts along dimension 0
There are 2 independent parts, one for each index of `groups`. A program takes and returns all parts, laid end to end along the dimension named above; an argument that names none is the same for every part. Nothing has to cross between parts.
Inputs may be any that keep to these rules, and one draw needn't show every extreme that they name: `segment_ids`: ids never fall along the tokens; each completion has 1 to 128 tokens and one has exactly 128.
All inputs are finite; a program needn't handle non-finite values.
Results may differ from a plain program's by a relative error of at most 0.011.
Values may be sent and summed in bfloat16 or wider, within the bound.
No kernel may reach another device: no remote copies, remote signals or barrier semaphores. Data moves between devices by JAX's collectives and lax.ppermute only.
A program may use at most 128 MiB of HBM per device.

v0:
```python
import jax
import jax.numpy as jnp
from jax import lax
from jax.sharding import PartitionSpec as P

HD = 128
GROUP = 8


def from_behind(value, axis, steps):
    count = lax.axis_size(axis)
    initial, last = (max(0, -steps), min(count, count - steps))
    return lax.ppermute(value, axis, [(source, source + steps) for source in range(initial, last)])


def rotary(block, positions):
    half = HD // 2
    freqs = 500000.0 ** (-(2.0 * jnp.arange(half, dtype=jnp.float32)) / HD)
    angles = positions[:, None] * freqs[None, :]
    cosine = jnp.cos(angles)[:, None, :]
    sine = jnp.sin(angles)[:, None, :]
    first = block[..., :half]
    second = block[..., half:]
    return jnp.concatenate(
        [first * cosine - second * sine, second * cosine + first * sine], axis=-1
    )


def on_device(hidden, norm_gain, key_weight, value_weight, queries, segment_ids):
    whole = lax.all_gather(hidden, "tensor", axis=1, tiled=True)
    states = whole.astype(jnp.float32)
    meansq = jnp.mean(states * states, axis=-1, keepdims=True)
    normed = (states * lax.rsqrt(meansq + 1e-05) * norm_gain.astype(jnp.float32)).astype(
        jnp.bfloat16
    )
    local_rows = normed.shape[0]
    head_cols = key_weight.shape[1]

    def add_rows(piece):
        return jnp.dot(normed, piece, preferred_element_type=jnp.float32)

    key_sum = add_rows(lax.all_gather(key_weight, "dp", axis=0, tiled=True))
    value_sum = add_rows(lax.all_gather(value_weight, "dp", axis=0, tiled=True))
    keys_raw = key_sum.astype(jnp.bfloat16)
    values = value_sum.astype(jnp.bfloat16)
    earlier_keys, earlier_values, earlier_segs = from_behind(
        (keys_raw, values, segment_ids), "dp", 1
    )
    earlier_count = earlier_keys.shape[0]
    has_earlier = lax.axis_index("dp") > 0
    earlier_segs = jnp.where(has_earlier, earlier_segs, -1)
    window_segs = jnp.concatenate([earlier_segs, segment_ids], axis=0)
    window_len = window_segs.shape[0]
    window_index = jnp.arange(window_len, dtype=jnp.int32)
    same_seg = window_segs[:, None] == window_segs[None, :]
    before = window_index[None, :] < window_index[:, None]
    positions = jnp.sum((same_seg & before).astype(jnp.int32), axis=1)
    heads_here = head_cols // HD
    window_raw = (
        jnp.concatenate([earlier_keys, keys_raw], axis=0)
        .astype(jnp.float32)
        .reshape(window_len, heads_here, HD)
    )
    window_keys = rotary(window_raw, positions.astype(jnp.float32)).astype(jnp.bfloat16)
    window_values = jnp.concatenate([earlier_values, values], axis=0).reshape(
        window_len, heads_here, HD
    )
    query_heads = queries.reshape(local_rows, heads_here, GROUP, HD)
    scale = 1.0 / HD**0.5
    scores = (
        jnp.einsum("tkgd,skd->kgts", query_heads, window_keys, preferred_element_type=jnp.float32)
        * scale
    )
    query_pos = jnp.arange(local_rows, dtype=jnp.int32)[:, None] + earlier_count
    allowed = (window_index[None, :] <= query_pos) & (segment_ids[:, None] == window_segs[None, :])
    masked = jnp.where(allowed, scores, -1e30)
    largest = jnp.max(masked, axis=-1, keepdims=True)
    expd = jnp.where(allowed, jnp.exp(masked - largest), 0.0)
    weights = (expd / jnp.sum(expd, axis=-1, keepdims=True)).astype(jnp.bfloat16)
    out_heads = jnp.einsum(
        "kgts,skd->tkgd", weights, window_values, preferred_element_type=jnp.float32
    )
    return out_heads.reshape(local_rows, heads_here * GROUP * HD).astype(jnp.bfloat16)


def solution(mesh):
    in_specs = (
        P(("groups", "dp"), "tensor"),
        P(),
        P("dp", "tensor"),
        P("dp", "tensor"),
        P(("groups", "dp"), "tensor"),
        P(("groups", "dp")),
    )
    out_specs = P(("groups", "dp"), "tensor")
    return jax.shard_map(
        on_device, mesh=mesh, in_specs=in_specs, out_specs=out_specs, check_vma=False
    )
```

profile of v0, /device:TPU:8, one launch (start us, length us, event | category | flops | bytes accessed | tf_op | source)
XLA Modules:
  0.0 224.4 jit_solution(6049191343507936325)
XLA Ops:
  6.5 0.7 all-gather.3.cloned.1.call-update
  7.3 0.0 all-gather.5.cloned.1.call-start
  7.3 0.7 all-gather.5.cloned.1.call-update
  8.0 1.9 collective-permute-start.1
  9.9 3.1 %fusion.2 = f32[256]{0:T(256)S(1)} fusion(bf16[256,8192]{1,0:T(8,128)(2,1)} %param.6), kind=kLoop, calls=%fused_computation.7 | loop fusion | flops 6291200 | bytes 4195328 | tf_op jit(solution)/shard_map/reduce_sum | solution.py:32
  13.1 0.7 convert_element_type.43
  13.8 2.1 copy.25
  15.9 0.0 collective-permute-done.1
  15.9 0.0 copy-done.2
  15.9 0.2 convert_reduce_fusion
  16.2 0.2 fusion.17
  16.4 1.0 multiply_cosine_fusion
  17.4 67.7 %all-gather.3.cloned.1.call-done = bf16[8192,512]{1,0:T(8,128)(2,1)} async-done(((bf16[512,512]{1,0:T(8,128)(2,1)}), bf16[8192,512]{1,0:T(8,128)(2,1)}) %all-gather.3.cloned.1.call-update) | async-done | bytes 8388624 | tf_op jit(solution)/shard_map/all_gather | solution.py:43
  85.0 7.0 %convolution_convert_fusion.1 = bf16[256,512]{1,0:T(8,128)(2,1)S(1)} fusion(bf16[8192,512]{1,0:T(8,128)(2,1)} %all-gather.3.cloned.1.call-done, bf16[256,8192]{1,0:T(8,128)(2,1)} %param.6, f32[8192]{0:T(1024)S(1)} %convert_element_type.43, f32[256]{0:T(256)S(1)} %add_rsqrt_fusion), kind=kOutput, calls=%fused_computation.18 | convolution fusion | flops 2156003328 | bytes 12878848 | tf_op jit(solution)/shard_map/dot_general | solution.py:40
  92.0 0.0 copy-start.1
  92.1 2.2 collective-permute-start
  94.2 68.8 %all-gather.5.cloned.1.call-done = bf16[8192,512]{1,0:T(8,128)(2,1)} async-done(((bf16[512,512]{1,0:T(8,128)(2,1)}), bf16[8192,512]{1,0:T(8,128)(2,1)}) %all-gather.5.cloned.1.call-update) | async-done | bytes 8388624 | tf_op jit(solution)/shard_map/all_gather | solution.py:42
  163.1 7.8 %convolution_convert_fusion = bf16[256,512]{1,0:T(8,128)(2,1)} fusion(bf16[8192,512]{1,0:T(8,128)(2,1)} %all-gather.5.cloned.1.call-done, bf16[256,8192]{1,0:T(8,128)(2,1)} %param.6, f32[8192]{0:T(1024)S(1)} %convert_element_type.43, f32[256]{0:T(256)S(1)} %add_rsqrt_fusion), kind=kOutput, calls=%fused_computation.17 | convolution fusion | flops 2156003328 | bytes 12878848 | tf_op jit(solution)/shard_map/dot_general | solution.py:40
  170.8 0.0 copy-done.1
  170.8 2.3 %collective-permute-start.2 = (bf16[256,512]{1,0:T(8,128)(2,1)}, bf16[256,512]{1,0:T(8,128)(2,1)}, u32[]{:S(2)}, u32[]{:S(2)}) collective-permute-start(bf16[256,512]{1,0:T(8,128)(2,1)} %convolution_convert_fusion), channel_id=1, source_target_pairs={{0,1},{1,2},{2,3},{3,4},{4,5},{5,6},{6,7},{7,8},{8,9},{9,10},{10,1... | collective-permute-start | bytes 786440 | tf_op jit(solution)/shard_map/ppermute | solution.py:13
  173.2 1.0 copy_bitcast_fusion
  174.2 0.0 collective-permute-done
  174.2 1.1 pad_maximum_fusion
  175.3 1.0 copy.22
  176.3 3.5 %collective-permute-done.2 = bf16[256,512]{1,0:T(8,128)(2,1)} collective-permute-done((bf16[256,512]{1,0:T(8,128)(2,1)}, bf16[256,512]{1,0:T(8,128)(2,1)}, u32[]{:S(2)}, u32[]{:S(2)}) %collective-permute-start.2) | collective-permute-done | bytes 262176 | tf_op jit(solution)/shard_map/ppermute | solution.py:13
  179.7 1.0 copy_bitcast_fusion.1
  180.7 0.1 maximum_convert_fusion
  180.8 0.4 subtract_convert_fusion
  181.3 8.2 %fusion.9 = f32[4,512,256,8]{2,1,3,0:T(8,128)} fusion(bf16[256,4,8,128]{3,2,1,0:T(8,128)(2,1)S(1)} %bitcast.40, bf16[512,4,64]{2,0,1:T(8,128)(2,1)S(1)} %get-tuple-element.6, bf16[512,4,64]{2,0,1:T(8,128)(2,1)S(1)} %get-tuple-element.5), kind=kOutput, calls=%fused_computation.14 | convolution fusion | flops 1074790400 | bytes 19398656 | tf_op jit(solution)/shard_map/tkgd,skd->kgts/dot_general | solution.py:71
  189.4 18.0 %fusion.21 = (f32[4,8,256]{2,1,0:T(8,128)S(1)}, f32[4,8,256,512]{2,3,1,0:T(8,128)}) fusion(f32[4,512,256,8]{2,1,3,0:T(8,128)} %fusion.9, pred[256,512]{0,1:T(8,128)(4,1)S(1)} %fusion.17), kind=kOutput, calls=%fused_computation.43 | output fusion | flops 29360640 | bytes 33718272 | tf_op jit(solution)/shard_map/sub | solution.py:78
  207.5 7.2 %fusion.11 = bf16[4,128,8,256]{3,1,2,0:T(8,128)(2,1)S(1)} fusion(bf16[512,4,128,1]{0,2,3,1:T(8,128)(2,1)S(1)} %bitcast.43, f32[4,8,256,512]{2,3,1,0:T(8,128)} %get-tuple-element.10, f32[4,8,256]{2,1,0:T(8,128)S(1)} %get-tuple-element.9), kind=kOutput, calls=%fused_computation.16 | convolution fusion | flops 1083179008 | bytes 19431424 | tf_op jit(solution)/shard_map/kgts,skd->tkgd/dot_general | solution.py:80
  214.7 2.9 %copy.18 = bf16[256,4096]{1,0:T(8,128)(2,1)} copy(bf16[256,4096]{0,1:T(8,128)(2,1)S(1)} %bitcast.42) | data formatting | bytes 4194304 | tf_op jit(solution)/shard_map/convert_element_type | solution.py:83
  (10 shorter events, 0.0 us)
Async XLA Ops:
  6.5 9.4 %copy-start.2 = (s32[256]{0:T(256)S(1)}, s32[256]{0:T(256)}, u32[]{:S(2)}) copy-start(s32[256]{0:T(256)} %param.11) | copy-start | bytes 3076
  6.5 78.5 %all-gather.3.cloned.1.call-start = ((), (), s32[]{:S(2)}) async-start(), calls=%async_computation | async-start | bytes 8912896 | tf_op jit(solution)/shard_map/all_gather | solution.py:43
  7.3 155.8 %all-gather.5.cloned.1.call-start = ((), (), s32[]{:S(2)}) async-start(), calls=%async_computation.1 | async-start | bytes 8912896 | tf_op jit(solution)/shard_map/all_gather | solution.py:42
  8.0 7.9 %collective-permute-start.1 = (s32[256]{0:T(256)}, s32[256]{0:T(256)S(1)}, u32[]{:S(2)}, u32[]{:S(2)}) collective-permute-start(s32[256]{0:T(256)} %param.11), channel_id=1, source_target_pairs={{0,1},{1,2},{2,3},{3,4},{4,5},{5,6},{6,7},{7,8},{8,9},{9,10},{10,1... | collective-permute-start | bytes 3080 | tf_op jit(solution)/shard_map/ppermute | solution.py:13
  92.0 78.8 %copy-start.1 = (bf16[256,512]{1,0:T(8,128)(2,1)}, bf16[256,512]{1,0:T(8,128)(2,1)S(1)}, u32[]{:S(2)}) copy-start(bf16[256,512]{1,0:T(8,128)(2,1)S(1)} %convolution_convert_fusion.1) | copy-start | bytes 786436
  92.1 82.1 %collective-permute-start = (bf16[256,512]{1,0:T(8,128)(2,1)S(1)}, bf16[256,512]{1,0:T(8,128)(2,1)}, u32[]{:S(2)}, u32[]{:S(2)}) collective-permute-start(bf16[256,512]{1,0:T(8,128)(2,1)S(1)} %convolution_convert_fusion.1), channel_id=1, source_target_pairs={{0,1},{1,2},{2,3},{3,4},{4,5},{5,6},{6,7},{7,8},{8,9},{9,10},{10,1... | collective-permute-start | bytes 786440 | tf_op jit(solution)/shard_map/ppermute | solution.py:13
  170.8 8.9 %collective-permute-start.2 = (bf16[256,512]{1,0:T(8,128)(2,1)}, bf16[256,512]{1,0:T(8,128)(2,1)}, u32[]{:S(2)}, u32[]{:S(2)}) collective-permute-start(bf16[256,512]{1,0:T(8,128)(2,1)} %convolution_convert_fusion), channel_id=1, source_target_pairs={{0,1},{1,2},{2,3},{3,4},{4,5},{5,6},{6,7},{7,8},{8,9},{9,10},{10,1... | collective-permute-start | bytes 786440 | tf_op jit(solution)/shard_map/ppermute | solution.py:13
  189.4 18.0 %copy-start = (bf16[512,512]{0,1:T(8,128)(2,1)S(1)}, bf16[512,512]{0,1:T(8,128)(2,1)}, u32[]{:S(2)}) copy-start(bf16[512,512]{0,1:T(8,128)(2,1)} %copy.22) | copy-start | bytes 1572868
Sparse Core Ops, SparseCore 0:
  9.5 75.4 all-gather.2
  87.2 75.8 all-gather.4
where the time goes:
time: 225 us; the launch traced here: 224 us
  waiting for transfers between devices  141 us (63%)
  matrix products  30.2 us (13%)
  other arithmetic  24.9 us (11%)
  between operations  13.6 us (6%)
  local copies, waits for them, and re-layouts  7.93 us (4%)
  starting transfers between devices  6.47 us (3%)
    all_gather x1, waiting for transfers between devices, on_device(): key_sum = add_rows(lax.all_gather(key_weight, 'dp', axis=0, tiled=True))  68.8 us
    all_gather x1, waiting for transfers between devices, on_device(): value_sum = add_rows(lax.all_gather(value_weight, 'dp', axis=0, tiled=True))  67.7 us
    sub x1, other arithmetic, on_device(): expd = jnp.where(allowed, jnp.exp(masked - largest), 0.0)  18 us
    dot_general x2, matrix products, add_rows(): return jnp.dot(normed, piece, preferred_element_type=jnp.float32)  14.8 us
    dot_general x1, matrix products, on_device(): jnp.einsum('tkgd,skd->kgts', query_heads, window_keys, preferred_element_...  8.16 us
    dot_general x1, matrix products, on_device(): jnp.einsum('kgts,skd->tkgd', weights, window_values, preferred_element_ty...  7.21 us
    ppermute x3, starting transfers between devices, from_behind(): lax.ppermute(value, axis, [(source, source + steps) for source in range(i...  6.43 us
  transfers between devices with their start and end apart: 5, of which 3 were waited for; matrix products, arithmetic and copies ran while one was open for 11% of the time, Pallas kernels for 0%

commit v1 on v0

--- a/solution.py
+++ b/solution.py
@@ -1,16 +1,280 @@
+import functools
+
 import jax
 import jax.numpy as jnp
 from jax import lax
+from jax.experimental import pallas as pl
+from jax.experimental.pallas import tpu as pltpu
 from jax.sharding import PartitionSpec as P
 
 HD = 128
 GROUP = 8
+REACH = 128
+EPS = 1e-05
+F32 = jnp.float32
+BF16 = jnp.bfloat16
+VMEM_LIMIT = 48 * 1024 * 1024
+
+
+def params():
+    return pltpu.CompilerParams(vmem_limit_bytes=VMEM_LIMIT)
+
+
+def cost(flops, nbytes, trans=0):
+    return pl.CostEstimate(flops=flops, bytes_accessed=nbytes, transcendentals=trans)
 
 
 def from_behind(value, axis, steps):
     count = lax.axis_size(axis)
     initial, last = (max(0, -steps), min(count, count - steps))
     return lax.ppermute(value, axis, [(source, source + steps) for source in range(initial, last)])
+
+
+def norm_kernel(core_ref, h_ref, g_ref, mine_ref, theirs_ref):
+    width = h_ref.shape[1]
+    half = width // 16
+    x = h_ref[...].astype(F32)
+    meansq = jnp.sum(x * x, axis=-1, keepdims=True) * (1.0 / width)
+    scale = lax.rsqrt(meansq + EPS)
+    first = core_ref[0] == 0
+    for b in range(8):
+        lo = slice(2 * b * half, (2 * b + 1) * half)
+        hi = slice((2 * b + 1) * half, (2 * b + 2) * half)
+        n_lo = h_ref[:, lo].astype(F32) * scale * g_ref[:, lo].astype(F32)
+        n_hi = h_ref[:, hi].astype(F32) * scale * g_ref[:, hi].astype(F32)
+        out = slice(b * half, (b + 1) * half)
+        mine_ref[:, out] = jnp.where(first, n_lo, n_hi).astype(BF16)
+        theirs_ref[:, out] = jnp.where(first, n_hi, n_lo).astype(BF16)
+
+
+def normalise(core, hidden, gain):
+    rows, width = hidden.shape
+    step = 64
+    out = jax.ShapeDtypeStruct((rows, width // 2), BF16)
+    return pl.pallas_call(
+        norm_kernel,
+        grid_spec=pltpu.PrefetchScalarGridSpec(
+            num_scalar_prefetch=1,
+            grid=(rows // step,),
+            in_specs=[
+                pl.BlockSpec((step, width), lambda i, c: (i, 0)),
+                pl.BlockSpec((1, width), lambda i, c: (0, 0)),
+            ],
+            out_specs=[pl.BlockSpec((step, width // 2), lambda i, c: (i, 0))] * 2,
+        ),
+        out_shape=[out, out],
+        compiler_params=params(),
+        cost_estimate=cost(8 * rows * width, 4 * rows * width),
+        name="norm",
+    )(core, hidden, gain.reshape(1, width))
+
+
+def project_kernel(count, carried, index_ref, xa_ref, xb_ref, *refs):
+    weights, refs = refs[:count], refs[count:]
+    before, (oa_ref, ob_ref) = refs[:-2], refs[-2:]
+    rows = xa_ref.shape[0]
+    total = None
+    for j in range(count):
+        depth = weights[j].shape[0]
+        columns = pl.ds(pl.multiple_of(index_ref[j] * depth, depth), depth)
+        x = jnp.concatenate([xa_ref[:, columns], xb_ref[:, columns]], axis=0)
+        part = jnp.dot(x, weights[j][...], preferred_element_type=F32)
+        total = part if total is None else total + part
+    if carried:
+        oa_ref[...] = before[0][...] + total[:rows]
+        ob_ref[...] = before[1][...] + total[rows:]
+    else:
+        oa_ref[...] = total[:rows]
+        ob_ref[...] = total[rows:]
+
+
+def project(index, xa, xb, weights, before=()):
+    rows = xa.shape[0]
+    depth, feats = weights[0].shape
+    out = jax.ShapeDtypeStruct((rows, feats), F32)
+    whole = pl.BlockSpec(memory_space=pltpu.VMEM)
+    return pl.pallas_call(
+        functools.partial(project_kernel, len(weights), bool(before)),
+        in_specs=[pl.BlockSpec(memory_space=pltpu.SMEM)]
+        + [whole] * (2 + len(weights) + len(before)),
+        out_specs=[whole, whole],
+        out_shape=[out, out],
+        compiler_params=params(),
+        cost_estimate=cost(
+            4 * rows * depth * feats * len(weights), 2 * depth * feats * len(weights) + 4 * rows * 4096
+        ),
+        name="project",
+    )(index, xa, xb, *weights, *before)
+
+
+def keys_kernel(a_ref, b_ref, cos_ref, sin_ref, out_ref):
+    cos, sin = cos_ref[...], sin_ref[...]
+    for h in range(a_ref.shape[1] // HD):
+        at = slice(h * HD, (h + 1) * HD)
+        raw = (a_ref[:, at] + b_ref[:, at]).astype(BF16).astype(F32)
+        out_ref[:, at] = (raw * cos + pltpu.roll(raw, HD // 2, 1) * sin).astype(BF16)
+
+
+def finish_keys(a, b, cos, sin):
+    rows, feats = a.shape
+    return pl.pallas_call(
+        keys_kernel,
+        out_shape=jax.ShapeDtypeStruct((rows, feats), BF16),
+        compiler_params=params(),
+        cost_estimate=cost(6 * rows * feats, 10 * rows * feats),
+        name="keys",
+    )(a, b, cos, sin)
+
+
+def scores_kernel(q_ref, ka_ref, kb_ref, sq_ref, sk_ref, out_ref):
+    rows, span = q_ref.shape[0], sk_ref.shape[1]
+    keys = jnp.concatenate([ka_ref[...], kb_ref[...]], axis=0)
+    q_at = lax.broadcasted_iota(jnp.int32, (rows, span), 0) + (span - rows)
+    k_at = lax.broadcasted_iota(jnp.int32, (rows, span), 1)
+    allowed = (k_at <= q_at) & (sq_ref[...] == sk_ref[...])
+    scale = 1.0 / HD**0.5
+    for j in range(GROUP):
+        q = q_ref[:, j * HD : (j + 1) * HD]
+        s = lax.dot_general(q, keys, (((1,), (1,)), ((), ())), preferred_element_type=F32)
+        s = jnp.where(allowed, s * scale, -1e30)
+        e = jnp.exp(s - jnp.max(s, axis=-1, keepdims=True))
+        w = e * (1.0 / jnp.sum(e, axis=-1, keepdims=True))
+        out_ref[0, j * rows : (j + 1) * rows, :] = w.astype(BF16)
+
+
+def softmax_weights(queries, block, keys_a, block_a, keys_b, block_b, segs_q, segs_k):
+    rows = REACH
+    heads = keys_a.shape[1] // HD
+    return pl.pallas_call(
+        scores_kernel,
+        grid=(heads,),
+        in_specs=[
+            pl.BlockSpec((rows, GROUP * HD), lambda h: (block, h)),
+            pl.BlockSpec((rows, HD), lambda h: (block_a, h)),
+            pl.BlockSpec((rows, HD), lambda h: (block_b, h)),
+            pl.BlockSpec((rows, 1), lambda h: (0, 0)),
+            pl.BlockSpec((1, 2 * rows), lambda h: (0, 0)),
+        ],
+        out_specs=pl.BlockSpec((1, GROUP * rows, 2 * rows), lambda h: (h, 0, 0)),
+        out_shape=jax.ShapeDtypeStruct((heads, GROUP * rows, 2 * rows), BF16),
+        compiler_params=params(),
+        cost_estimate=cost(
+            4 * heads * GROUP * rows * rows * HD, 6 * rows * heads * GROUP * HD, 2 * heads * GROUP * rows * rows
+        ),
+        name="scores",
+    )(queries, keys_a, keys_b, segs_q, segs_k)
+
+
+def context_kernel(p0_ref, p1_ref, prev_ref, own_ref, out_ref):
+    rows = prev_ref.shape[0]
+    first = jnp.concatenate([prev_ref[...], own_ref[:rows, :]], axis=0)
+    for block, (p_ref, values) in enumerate(((p0_ref, first), (p1_ref, own_ref[...]))):
+        c = jnp.dot(p_ref[0], values, preferred_element_type=F32).astype(BF16)
+        for j in range(GROUP):
+            out_ref[block * rows : (block + 1) * rows, j * HD : (j + 1) * HD] = c[j * rows : (j + 1) * rows]
+
+
+def contexts(p0, p1, prev, own):
+    heads, _, span = p0.shape
+    rows = prev.shape[0]
+    weights = pl.BlockSpec((1, GROUP * rows, span), lambda h: (h, 0, 0))
+    return pl.pallas_call(
+        context_kernel,
+        grid=(heads,),
+        in_specs=[
+            weights,
+            weights,
+            pl.BlockSpec((rows, HD), lambda h: (0, h)),
+            pl.BlockSpec((2 * rows, HD), lambda h: (0, h)),
+        ],
+        out_specs=pl.BlockSpec((2 * rows, GROUP * HD), lambda h: (0, h)),
+        out_shape=jax.ShapeDtypeStruct((2 * rows, heads * GROUP * HD), BF16),
+        compiler_params=params(),
+        cost_estimate=cost(4 * heads * GROUP * rows * span * HD, 12 * rows * heads * GROUP * HD),
+        name="context",
+    )(p0, p1, prev, own)
+
+
+def place(p):
+    z, x = (p, 0) if p < 4 else (7 - p, 1)
+    return z * 2 + x
+
+
+def ring(signs):
+    return [
+        (y * 16 + place(p) * 2 + c, y * 16 + place((p + sign) % 8) * 2 + c)
+        for y, sign in enumerate(signs)
+        for p in range(8)
+        for c in range(2)
+    ]
+
+
+def on_ring(hidden, norm_gain, key_weight, value_weight, queries, segment_ids):
+    both = ("groups", "dp")
+    key_way, value_way = ring((1, -1)), ring((-1, 1))
+    other_group = [(i, (i + 16) % 32) for i in range(32)]
+    other_core = [(i, i ^ 1) for i in range(16)]
+
+    def send(value, way):
+        return lax.ppermute(value, both, way)
+
+    def swap(value):
+        return lax.ppermute(value, "dp", other_core)
+
+    me = lax.axis_index("dp")
+    chip, core = me // 2, me % 2
+    z, x = chip // 2, chip % 2
+    position = jnp.where(x == 0, z, 7 - z)
+    sign = jnp.where(lax.axis_index("groups") == 0, 1, -1)
+
+    k1, v1 = send(key_weight, key_way), send(value_weight, value_way)
+    yk1 = send(k1, other_group)
+    k2, v2 = send(k1, key_way), send(v1, value_way)
+    yk2, yv2 = send(k2, other_group), send(v2, other_group)
+    k3, v3 = send(k2, key_way), send(v2, value_way)
+    yv1 = send(v1, other_group)
+    k4, k3b = send(k3, key_way), send(yk2, value_way)
+    v4, v3b = send(v3, value_way), send(yv2, key_way)
+
+    def blocks(steps):
+        p = jnp.mod(position + sign * jnp.array(steps, jnp.int32), 8)
+        return jnp.where(p < 4, 2 * p, 2 * (7 - p) + 1).astype(jnp.int32)
+
+    rows = segment_ids.shape[0]
+    behind = from_behind(segment_ids[rows - REACH :], "dp", 1)
+    behind = jnp.where(me > 0, behind, -1)
+    window = jnp.concatenate([behind, segment_ids], axis=0)
+    index = jnp.arange(window.shape[0], dtype=jnp.int32)
+    earlier = (window[None, :] == segment_ids[:, None]) & (index[None, :] < index[REACH:, None])
+    positions = jnp.sum(earlier.astype(jnp.int32), axis=1).astype(F32)
+    half = HD // 2
+    freqs = 500000.0 ** (-(2.0 * jnp.arange(half, dtype=F32)) / HD)
+    angles = positions[:, None] * freqs[None, :]
+    cos, sin = jnp.cos(angles), jnp.sin(angles)
+    cos = jnp.concatenate([cos, cos], axis=1)
+    sin = jnp.concatenate([-sin, sin], axis=1)
+
+    mine, theirs = normalise(core.reshape(1).astype(jnp.int32), hidden, norm_gain)
+    other = swap(theirs)
+
+    part = project(blocks([0, -1, 1, -2, -3, 2]), mine, other, [key_weight, k1, yk1, k2, k3, yk2])
+    own_k, other_k = project(blocks([-4, 3]), mine, other, [k4, k3b], part)
+    keys = finish_keys(own_k, swap(other_k), cos, sin)
+    prev_keys = from_behind(keys[rows - REACH :], "dp", 1)
+
+    segs_q = segment_ids.reshape(rows, 1)
+    p1 = softmax_weights(
+        queries, 1, keys, 0, keys, 1, segs_q[REACH:], segment_ids.reshape(1, rows)
+    )
+    p0 = softmax_weights(
+        queries, 0, prev_keys, 0, keys, 0, segs_q[:REACH], window[: 2 * REACH].reshape(1, 2 * REACH)
+    )
+
+    part = project(blocks([0, 1, 2, 3, -2]), mine, other, [value_weight, v1, v2, v3, yv2])
+    own_v, other_v = project(blocks([-1, 4, -3]), mine, other, [yv1, v4, v3b], part)
+    values = (own_v + swap(other_v)).astype(BF16)
+    prev_values = from_behind(values[rows - REACH :], "dp", 1)
+    return contexts(p0, p1, prev_values, values)
 
 
 def rotary(block, positions):
@@ -26,13 +290,11 @@
     )
 
 
-def on_device(hidden, norm_gain, key_weight, value_weight, queries, segment_ids):
+def on_any(hidden, norm_gain, key_weight, value_weight, queries, segment_ids):
     whole = lax.all_gather(hidden, "tensor", axis=1, tiled=True)
     states = whole.astype(jnp.float32)
     meansq = jnp.mean(states * states, axis=-1, keepdims=True)
-    normed = (states * lax.rsqrt(meansq + 1e-05) * norm_gain.astype(jnp.float32)).astype(
-        jnp.bfloat16
-    )
+    normed = (states * lax.rsqrt(meansq + EPS) * norm_gain.astype(jnp.float32)).astype(BF16)
     local_rows = normed.shape[0]
     head_cols = key_weight.shape[1]
 
@@ -41,8 +303,8 @@
 
     key_sum = add_rows(lax.all_gather(key_weight, "dp", axis=0, tiled=True))
     value_sum = add_rows(lax.all_gather(value_weight, "dp", axis=0, tiled=True))
-    keys_raw = key_sum.astype(jnp.bfloat16)
-    values = value_sum.astype(jnp.bfloat16)
+    keys_raw = key_sum.astype(BF16)
+    values = value_sum.astype(BF16)
     earlier_keys, earlier_values, earlier_segs = from_behind(
         (keys_raw, values, segment_ids), "dp", 1
     )
@@ -61,7 +323,7 @@
         .astype(jnp.float32)
         .reshape(window_len, heads_here, HD)
     )
-    window_keys = rotary(window_raw, positions.astype(jnp.float32)).astype(jnp.bfloat16)
+    window_keys = rotary(window_raw, positions.astype(jnp.float32)).astype(BF16)
     window_values = jnp.concatenate([earlier_values, values], axis=0).reshape(
         window_len, heads_here, HD
     )
@@ -76,11 +338,11 @@
     masked = jnp.where(allowed, scores, -1e30)
     largest = jnp.max(masked, axis=-1, keepdims=True)
     expd = jnp.where(allowed, jnp.exp(masked - largest), 0.0)
-    weights = (expd / jnp.sum(expd, axis=-1, keepdims=True)).astype(jnp.bfloat16)
+    weights = (expd / jnp.sum(expd, axis=-1, keepdims=True)).astype(BF16)
     out_heads = jnp.einsum(
         "kgts,skd->tkgd", weights, window_values, preferred_element_type=jnp.float32
     )
-    return out_heads.reshape(local_rows, heads_here * GROUP * HD).astype(jnp.bfloat16)
+    return out_heads.reshape(local_rows, heads_here * GROUP * HD).astype(BF16)
 
 
 def solution(mesh):
@@ -93,6 +355,11 @@
         P(("groups", "dp")),
     )
     out_specs = P(("groups", "dp"), "tensor")
+    small = (mesh.shape["groups"], mesh.shape["dp"], mesh.shape["tensor"]) == (2, 16, 1)
     return jax.shard_map(
-        on_device, mesh=mesh, in_specs=in_specs, out_specs=out_specs, check_vma=False
-    )
+        on_ring if small else on_any,
+        mesh=mesh,
+        in_specs=in_specs,
+        out_specs=out_specs,
+        check_vma=False,
+    )

time: 225 us -> 96.1 us (0.43)
  waiting for transfers between devices: 141 us -> 40.7 us
  matrix products: 30.2 us -> 0 us
  Pallas kernels: 0 us -> 27.2 us
  other arithmetic: 24.9 us -> 1.07 us
  starting transfers between devices: 6.47 us -> 23.9 us
  between operations: 13.6 us -> 0.43 us
  local copies, waits for them, and re-layouts: 7.93 us -> 1.05 us
    all_gather x2 -> x0, waiting for transfers between devices: 137 us -> none  [the longest x1 68.8 us: on_device(): key_sum = add_rows(lax.all_gather(key_weight, 'dp', axis=0, tiled=True))]
    ppermute x0 -> x17, waiting for transfers between devices: none -> 40.7 us  [the longest x14 40 us: send(): return lax.ppermute(value, both, way)]
    dot_general x4 -> x0, matrix products: 30.2 us -> none  [the longest x2 14.8 us: add_rows(): return jnp.dot(normed, piece, preferred_element_type=jnp.float32)]
    pallas_call x0 -> x9, Pallas kernels: none -> 27.2 us  [the longest x4 13.6 us: project(): pl.pallas_call(functools.partial(project_kernel, len(weights), bool(befor...]
    sub x1 -> x0, other arithmetic: 18 us -> none  [on_device(): expd = jnp.where(allowed, jnp.exp(masked - largest), 0.0)]
    ppermute x0 -> x17, starting transfers between devices: none -> 16.1 us  [the longest x14 15.7 us: send(): return lax.ppermute(value, both, way)]
    ppermute x3, waiting for transfers between devices: 3.47 us -> 0.01 us  [from_behind(): lax.ppermute(value, axis, [(source, source + steps) for source in range(i...]
    reduce_sum x2 -> x1, other arithmetic: 3.35 us -> 0.22 us  [on_ring(): positions = jnp.sum(earlier.astype(jnp.int32), axis=1).astype(F32)]
  transfers between devices with their start and end apart: 5 -> 20, of which waited for: 3 -> 7; matrix products, arithmetic and copies ran while one was open for 11% -> 1% of each run, Pallas kernels for 0% -> 20%
where the time goes in v1:
time: 96.1 us; the launch traced here: 94.4 us
  waiting for transfers between devices  40.7 us (42%)
  Pallas kernels  27.2 us (28%)
  starting transfers between devices  23.9 us (25%)
  other arithmetic  1.07 us (1%)
  local copies, waits for them, and re-layouts  1.05 us (1%)
    ppermute x14, waiting for transfers between devices, send(): return lax.ppermute(value, both, way)  40 us
    ppermute x14, starting transfers between devices, send(): return lax.ppermute(value, both, way)  15.7 us
    pallas_call x4, Pallas kernels, project(): pl.pallas_call(functools.partial(project_kernel, len(weights), bool(befor...  13.6 us
    ppermute x3, starting transfers between devices, from_behind(): lax.ppermute(value, axis, [(source, source + steps) for source in range(i...  7.77 us
    pallas_call x1, Pallas kernels, normalise(): pl.pallas_call(norm_kernel, grid_spec=pltpu.PrefetchScalarGridSpec(num_sc...  5.43 us
    pallas_call x2, Pallas kernels, softmax_weights(): pl.pallas_call(scores_kernel, grid=(heads,), in_specs=[pl.BlockSpec((rows...  4.91 us
    pallas_call x1, Pallas kernels, contexts(): pl.pallas_call(context_kernel, grid=(heads,), in_specs=[weights, weights,...  2.99 us
  transfers between devices with their start and end apart: 20, of which 7 were waited for; matrix products, arithmetic and copies ran while one was open for 1% of the time, Pallas kernels for 20%

profile of v1, /device:TPU:8, one launch (start us, length us, event | category | flops | bytes accessed | tf_op | source)
XLA Modules:
  0.0 94.4 jit_solution(10676473948617336414)
XLA Ops:
  0.0 0.7 reshape.29.g_ref
  0.8 5.4 %norm.1 = (bf16[256,4096]{1,0:T(8,128)(2,1)S(1)}, bf16[256,4096]{1,0:T(8,128)(2,1)}) custom-call(s32[1]{0:T(128)} %bitcast.core_ref, bf16[256,8192]{1,0:T(8,128)(2,1)} %h_ref.1, bf16[1,8192]{1,0:T(2,128)(2,1)S(1)} %reshape.29.g_ref), custom_call_target="tpu_custom_call" | custom-call | flops 16777216 | bytes 8388608 | tf_op jit(solution)/shard_map/norm/pallas_call | solution.py:54
  6.4 2.0 %collective-permute-start.1 = (bf16[512,512]{1,0:T(8,128)(2,1)S(1)}, bf16[512,512]{1,0:T(8,128)(2,1)}, u32[]{:S(2)}, u32[]{:S(2)}) collective-permute-start(bf16[512,512]{1,0:T(8,128)(2,1)S(1)} %copy-done.4), channel_id=1, source_target_pairs={{0,4},{1,5},{4,8},{5,9},{8,12},{9,13},{12,14},{13,15},{14,10},{15,... | collective-permute-start | bytes 1572872 | tf_op jit(solution)/shard_map/ppermute | solution.py:219
  8.4 12.4 %collective-permute-done.11.refs_1_ = bf16[512,512]{1,0:T(8,128)(2,1)} collective-permute-done((bf16[512,512]{1,0:T(8,128)(2,1)S(1)}, bf16[512,512]{1,0:T(8,128)(2,1)}, u32[]{:S(2)}, u32[]{:S(2)}) %collective-permute-start.11) | collective-permute-done | bytes 524320 | tf_op jit(solution)/shard_map/ppermute | solution.py:219
  20.7 0.3 collective-permute-start.13
  21.0 1.7 %collective-permute-start.2 = (bf16[512,512]{1,0:T(8,128)(2,1)}, bf16[512,512]{1,0:T(8,128)(2,1)}, u32[]{:S(2)}, u32[]{:S(2)}) collective-permute-start(bf16[512,512]{1,0:T(8,128)(2,1)} %collective-permute-done.1.refs_1_), channel_id=1, source_target_pairs={{0,4},{1,5},{4,8},{5,9},{8,12},{9,13},{12,14},{13,15},{14,10},{15,... | collective-permute-start | bytes 1572872 | tf_op jit(solution)/shard_map/ppermute | solution.py:219
  22.7 1.5 %collective-permute-start.12 = (bf16[512,512]{1,0:T(8,128)(2,1)}, bf16[512,512]{1,0:T(8,128)(2,1)}, u32[]{:S(2)}, u32[]{:S(2)}) collective-permute-start(bf16[512,512]{1,0:T(8,128)(2,1)} %collective-permute-done.11.refs_1_), channel_id=1, source_target_pairs={{0,16},{1,17},{2,18},{3,19},{4,20},{5,21},{6,22},{7,23},{8,24},{9,... | collective-permute-start | bytes 1572872 | tf_op jit(solution)/shard_map/ppermute | solution.py:219
  24.3 1.9 %collective-permute-start.9 = (s32[128]{0:T(128)S(1)}, s32[128]{0:T(128)S(1)}, u32[]{:S(2)}, u32[]{:S(2)}) collective-permute-start(s32[128]{0:T(128)S(1)} %get-tuple-element.29), channel_id=1, source_target_pairs={{0,1},{1,2},{2,3},{3,4},{4,5},{5,6},{6,7},{7,8},{8,9},{9,10},{10,1... | collective-permute-start | bytes 1544 | tf_op jit(solution)/shard_map/ppermute | solution.py:30
  26.2 8.3 %collective-permute-done.13.refs_2_ = bf16[512,512]{1,0:T(8,128)(2,1)} collective-permute-done((bf16[512,512]{1,0:T(8,128)(2,1)}, bf16[512,512]{1,0:T(8,128)(2,1)}, u32[]{:S(2)}, u32[]{:S(2)}) %collective-permute-start.13) | collective-permute-done | bytes 524320 | tf_op jit(solution)/shard_map/ppermute | solution.py:219
  34.5 0.5 collective-permute-start.14
  35.0 2.6 %collective-permute-start.16 = (bf16[512,512]{1,0:T(8,128)(2,1)}, bf16[512,512]{1,0:T(8,128)(2,1)}, u32[]{:S(2)}, u32[]{:S(2)}) collective-permute-start(bf16[512,512]{1,0:T(8,128)(2,1)} %collective-permute-done.13.refs_2_), channel_id=1, source_target_pairs={{0,16},{1,17},{2,18},{3,19},{4,20},{5,21},{6,22},{7,23},{8,24},{9,... | collective-permute-start | bytes 1572872 | tf_op jit(solution)/shard_map/ppermute | solution.py:219
  37.7 1.6 %collective-permute-start.3 = (bf16[512,512]{1,0:T(8,128)(2,1)}, bf16[512,512]{1,0:T(8,128)(2,1)}, u32[]{:S(2)}, u32[]{:S(2)}) collective-permute-start(bf16[512,512]{1,0:T(8,128)(2,1)} %collective-permute-done.2.refs_3_), channel_id=1, source_target_pairs={{0,4},{1,5},{4,8},{5,9},{8,12},{9,13},{12,14},{13,15},{14,10},{15,... | collective-permute-start | bytes 1572872 | tf_op jit(solution)/shard_map/ppermute | solution.py:219
  39.4 8.0 %collective-permute-done.14.refs_3_ = bf16[512,512]{1,0:T(8,128)(2,1)} collective-permute-done((bf16[512,512]{1,0:T(8,128)(2,1)}, bf16[512,512]{1,0:T(8,128)(2,1)}, u32[]{:S(2)}, u32[]{:S(2)}) %collective-permute-start.14) | collective-permute-done | bytes 524320 | tf_op jit(solution)/shard_map/ppermute | solution.py:219
  47.4 0.7 collective-permute-start.15
  48.2 2.6 %collective-permute-done.16.refs_4_ = bf16[512,512]{1,0:T(8,128)(2,1)} collective-permute-done((bf16[512,512]{1,0:T(8,128)(2,1)}, bf16[512,512]{1,0:T(8,128)(2,1)}, u32[]{:S(2)}, u32[]{:S(2)}) %collective-permute-start.16) | collective-permute-done | bytes 524320 | tf_op jit(solution)/shard_map/ppermute | solution.py:219
  50.8 1.6 %collective-permute-start.17 = (bf16[512,512]{1,0:T(8,128)(2,1)}, bf16[512,512]{1,0:T(8,128)(2,1)}, u32[]{:S(2)}, u32[]{:S(2)}) collective-permute-start(bf16[512,512]{1,0:T(8,128)(2,1)} %collective-permute-done.16.refs_4_), channel_id=1, source_target_pairs={{0,4},{1,5},{4,8},{5,9},{8,12},{9,13},{12,14},{13,15},{14,10},{15,... | collective-permute-start | bytes 1572872 | tf_op jit(solution)/shard_map/ppermute | solution.py:219
  52.4 0.9 collective-permute-start.7
  53.4 8.7 %collective-permute-done.5.refs_5_ = bf16[512,512]{1,0:T(8,128)(2,1)} collective-permute-done((bf16[512,512]{1,0:T(8,128)(2,1)}, bf16[512,512]{1,0:T(8,128)(2,1)}, u32[]{:S(2)}, u32[]{:S(2)}) %collective-permute-start.5) | collective-permute-done | bytes 524320 | tf_op jit(solution)/shard_map/ppermute | solution.py:219
  62.0 1.6 %collective-permute-start.4 = (bf16[512,512]{1,0:T(8,128)(2,1)}, bf16[512,512]{1,0:T(8,128)(2,1)S(1)}, u32[]{:S(2)}, u32[]{:S(2)}) collective-permute-start(bf16[512,512]{1,0:T(8,128)(2,1)} %collective-permute-done.3.refs_4_), channel_id=1, source_target_pairs={{0,4},{1,5},{4,8},{5,9},{8,12},{9,13},{12,14},{13,15},{14,10},{15,... | collective-permute-start | bytes 1572872 | tf_op jit(solution)/shard_map/ppermute | solution.py:219
  63.6 0.5 collective-permute-start.6
  64.1 3.7 %project.6 = (f32[256,512]{1,0:T(8,128)S(1)}, f32[256,512]{1,0:T(8,128)S(1)}) custom-call(s32[5]{0:T(128)S(1)} %compare_select_fusion.8.index_ref, bf16[256,4096]{1,0:T(8,128)(2,1)S(1)} %get-tuple-element.15.xa_ref, bf16[256,4096]{1,0:T(8,128)(2,1)} %collective-permute-done.xb_ref, bf16[512,512]{1,0:T(8,128)(2,1)S(1)} %copy-done.3, ...), custom_call_target="tpu_custom_call" | custom-call | flops 1342177280 | bytes 6815744 | tf_op jit(solution)/shard_map/project/pallas_call | solution.py:96
  67.8 3.0 %project.7 = (f32[256,512]{1,0:T(8,128)S(1)}, f32[256,512]{1,0:T(8,128)S(1)}) custom-call(s32[3]{0:T(128)S(1)} %compare_select_fusion.9.index_ref, bf16[256,4096]{1,0:T(8,128)(2,1)S(1)} %get-tuple-element.15.xa_ref, bf16[256,4096]{1,0:T(8,128)(2,1)} %collective-permute-done.xb_ref, bf16[512,512]{1,0:T(8,128)(2,1)} %collective-permute-done.12.refs_0_, ...), custom_call_target="tpu_custom_call" | custom-call | flops 805306368 | bytes 5767168 | tf_op jit(solution)/shard_map/project/pallas_call | solution.py:96
  70.9 4.7 %project.4 = (f32[256,512]{1,0:T(8,128)S(1)}, f32[256,512]{1,0:T(8,128)S(1)}) custom-call(s32[6]{0:T(128)S(1)} %compare_select_fusion.10.index_ref, bf16[256,4096]{1,0:T(8,128)(2,1)} %copy-done, bf16[256,4096]{1,0:T(8,128)(2,1)} %collective-permute-done.xb_ref, bf16[512,512]{1,0:T(8,128)(2,1)S(1)} %copy-done.4, ...), custom_call_target="tpu_custom_call" | custom-call | flops 1610612736 | bytes 7340032 | tf_op jit(solution)/shard_map/project/pallas_call | solution.py:96
  75.6 2.3 %project.5 = (f32[256,512]{1,0:T(8,128)S(1)}, f32[256,512]{1,0:T(8,128)S(1)}) custom-call(s32[2]{0:T(128)S(1)} %compare_select_fusion.11.index_ref, bf16[256,4096]{1,0:T(8,128)(2,1)S(1)} %copy-done.1, bf16[256,4096]{1,0:T(8,128)(2,1)} %collective-permute-done.xb_ref, bf16[512,512]{1,0:T(8,128)(2,1)S(1)} %collective-permute-done.4.refs_0_, ...), custom_call_target="tpu_custom_call" | custom-call | flops 536870912 | bytes 5242880 | tf_op jit(solution)/shard_map/project/pallas_call | solution.py:96
  77.9 0.4 collective-permute-start.8
  78.6 0.5 fusion.1
  79.3 0.7 collective-permute-done.8.b_ref
  80.2 2.2 %collective-permute-start.10 = (bf16[128,512]{1,0:T(8,128)(2,1)S(1)}, bf16[128,512]{1,0:T(8,128)(2,1)S(1)}, u32[]{:S(2)}, u32[]{:S(2)}) collective-permute-start(bf16[128,512]{1,0:T(8,128)(2,1)S(1)} %slice.33), channel_id=1, source_target_pairs={{0,1},{1,2},{2,3},{3,4},{4,5},{5,6},{6,7},{7,8},{8,9},{9,10},{10,1... | collective-permute-start | bytes 393224 | tf_op jit(solution)/shard_map/ppermute | solution.py:30
  82.5 3.6 %collective-permute-start.19 = (bf16[128,512]{1,0:T(8,128)(2,1)S(1)}, bf16[128,512]{1,0:T(8,128)(2,1)S(1)}, u32[]{:S(2)}, u32[]{:S(2)}) collective-permute-start(bf16[128,512]{1,0:T(8,128)(2,1)S(1)} %slice.34), channel_id=1, source_target_pairs={{0,1},{1,2},{2,3},{3,4},{4,5},{5,6},{6,7},{7,8},{8,9},{9,10},{10,1... | collective-permute-start | bytes 393224 | tf_op jit(solution)/shard_map/ppermute | solution.py:30
  86.4 2.5 %scores.3.p1_ref = bf16[4,1024,256]{2,1,0:T(8,128)(2,1)S(1)} custom-call(bf16[256,4096]{1,0:T(8,128)(2,1)S(1)} %copy-done.2, bf16[256,512]{1,0:T(8,128)(2,1)S(1)} %keys.1.kb_ref.ka_ref, bf16[256,512]{1,0:T(8,128)(2,1)S(1)} %keys.1.kb_ref.ka_ref, s32[128,1]{1,0:T(8,128)S(1)} %copy.14.sq_ref, s32[1,256]{1,0:T(1,128)S(1)} %bitcast.7), custom_call_target="tpu_custom_call" | custom-call | flops 268435456 | bytes 3145728 | tf_op jit(solution)/shard_map/scores/pallas_call | solution.py:148
  88.9 2.5 %scores.2.p0_ref = bf16[4,1024,256]{2,1,0:T(8,128)(2,1)S(1)} custom-call(bf16[256,4096]{1,0:T(8,128)(2,1)S(1)} %copy-done.2, bf16[128,512]{1,0:T(8,128)(2,1)S(1)} %collective-permute-done.10.ka_ref, bf16[256,512]{1,0:T(8,128)(2,1)S(1)} %keys.1.kb_ref.ka_ref, s32[128,1]{1,0:T(8,128)S(1)} %copy.13.sq_ref, s32[1,256]{1,0:T(1,128)S(1)} %bitcast.8), custom_call_target="tpu_custom_call" | custom-call | flops 268435456 | bytes 3145728 | tf_op jit(solution)/shard_map/scores/pallas_call | solution.py:148
  91.4 3.0 %context.1 = bf16[256,4096]{1,0:T(8,128)(2,1)} custom-call(bf16[4,1024,256]{2,1,0:T(8,128)(2,1)S(1)} %scores.2.p0_ref, bf16[4,1024,256]{2,1,0:T(8,128)(2,1)S(1)} %scores.3.p1_ref, bf16[128,512]{1,0:T(8,128)(2,1)S(1)} %collective-permute-done.19.prev_ref, bf16[256,512]{1,0:T(8,128)(2,1)S(1)} %add_convert_fusion.own_ref), custom_call_target="tpu_custom_call" | custom-call | flops 536870912 | bytes 6291456 | tf_op jit(solution)/shard_map/context/pallas_call | solution.py:181
  (58 shorter events, 1.4 us)
Async XLA Ops:
  0.7 5.5 %copy-start.3 = (bf16[512,512]{1,0:T(8,128)(2,1)S(1)}, bf16[512,512]{1,0:T(8,128)(2,1)}, u32[]{:S(2)}) copy-start(bf16[512,512]{1,0:T(8,128)(2,1)} %refs_0_.3) | copy-start | bytes 1572868
  0.8 5.6 %copy-start.4 = (bf16[512,512]{1,0:T(8,128)(2,1)S(1)}, bf16[512,512]{1,0:T(8,128)(2,1)}, u32[]{:S(2)}) copy-start(bf16[512,512]{1,0:T(8,128)(2,1)} %refs_0_.2) | copy-start | bytes 1572868
  0.8 23.5 %copy-start.5 = (s32[256]{0:T(256)S(1)}, s32[256]{0:T(256)}, u32[]{:S(2)}) copy-start(s32[256]{0:T(256)} %param.15) | copy-start | bytes 3076
  0.8 36.8 %copy-start.9 = (s32[5]{0:T(128)S(1)}, s32[5]{0:T(128)}, u32[]{:S(2)}) copy-start(s32[5]{0:T(128)} %constant.120.clone) | copy-start | bytes 64
  0.8 38.5 %copy-start.8 = (s32[3]{0:T(128)S(1)}, s32[3]{0:T(128)}, u32[]{:S(2)}) copy-start(s32[3]{0:T(128)} %constant.121.clone) | copy-start | bytes 40
  0.8 38.6 %copy-start.7 = (s32[6]{0:T(128)S(1)}, s32[6]{0:T(128)}, u32[]{:S(2)}) copy-start(s32[6]{0:T(128)} %constant.118.clone) | copy-start | bytes 76
  0.8 51.6 %copy-start.6 = (s32[2]{0:T(128)S(1)}, s32[2]{0:T(128)}, u32[]{:S(2)}) copy-start(s32[2]{0:T(128)} %constant.119.clone) | copy-start | bytes 28
  6.3 61.5 %copy-start = (bf16[256,4096]{1,0:T(8,128)(2,1)}, bf16[256,4096]{1,0:T(8,128)(2,1)S(1)}, u32[]{:S(2)}) copy-start(bf16[256,4096]{1,0:T(8,128)(2,1)S(1)} %get-tuple-element.15.xa_ref) | copy-start | bytes 6291460
  6.3 57.4 %collective-permute-start = (bf16[256,4096]{1,0:T(8,128)(2,1)}, bf16[256,4096]{1,0:T(8,128)(2,1)}, u32[]{:S(2)}, u32[]{:S(2)}) collective-permute-start(bf16[256,4096]{1,0:T(8,128)(2,1)} %get-tuple-element.16), channel_id=1, source_target_pairs={{0,1},{1,0},{2,3},{3,2},{4,5},{5,4},{6,7},{7,6},{8,9},{9,8},{10,11... | collective-permute-start | bytes 6291464 | tf_op jit(solution)/shard_map/ppermute | solution.py:222
  6.3 14.4 %collective-permute-start.11 = (bf16[512,512]{1,0:T(8,128)(2,1)S(1)}, bf16[512,512]{1,0:T(8,128)(2,1)}, u32[]{:S(2)}, u32[]{:S(2)}) collective-permute-start(bf16[512,512]{1,0:T(8,128)(2,1)S(1)} %copy-done.3), channel_id=1, source_target_pairs={{0,2},{1,3},{4,0},{5,1},{8,4},{9,5},{12,8},{13,9},{14,12},{15,13},... | collective-permute-start | bytes 1572872 | tf_op jit(solution)/shard_map/ppermute | solution.py:219
  6.4 14.6 %collective-permute-start.1 = (bf16[512,512]{1,0:T(8,128)(2,1)S(1)}, bf16[512,512]{1,0:T(8,128)(2,1)}, u32[]{:S(2)}, u32[]{:S(2)}) collective-permute-start(bf16[512,512]{1,0:T(8,128)(2,1)S(1)} %copy-done.4), channel_id=1, source_target_pairs={{0,4},{1,5},{4,8},{5,9},{8,12},{9,13},{12,14},{13,15},{14,10},{15,... | collective-permute-start | bytes 1572872 | tf_op jit(solution)/shard_map/ppermute | solution.py:219
  20.7 13.8 %collective-permute-start.13 = (bf16[512,512]{1,0:T(8,128)(2,1)}, bf16[512,512]{1,0:T(8,128)(2,1)}, u32[]{:S(2)}, u32[]{:S(2)}) collective-permute-start(bf16[512,512]{1,0:T(8,128)(2,1)} %collective-permute-done.11.refs_1_), channel_id=1, source_target_pairs={{0,2},{1,3},{4,0},{5,1},{8,4},{9,5},{12,8},{13,9},{14,12},{15,13},... | collective-permute-start | bytes 1572872 | tf_op jit(solution)/shard_map/ppermute | solution.py:219
  21.0 16.6 %collective-permute-start.2 = (bf16[512,512]{1,0:T(8,128)(2,1)}, bf16[512,512]{1,0:T(8,128)(2,1)}, u32[]{:S(2)}, u32[]{:S(2)}) collective-permute-start(bf16[512,512]{1,0:T(8,128)(2,1)} %collective-permute-done.1.refs_1_), channel_id=1, source_target_pairs={{0,4},{1,5},{4,8},{5,9},{8,12},{9,13},{12,14},{13,15},{14,10},{15,... | collective-permute-start | bytes 1572872 | tf_op jit(solution)/shard_map/ppermute | solution.py:219
  22.7 16.6 %collective-permute-start.12 = (bf16[512,512]{1,0:T(8,128)(2,1)}, bf16[512,512]{1,0:T(8,128)(2,1)}, u32[]{:S(2)}, u32[]{:S(2)}) collective-permute-start(bf16[512,512]{1,0:T(8,128)(2,1)} %collective-permute-done.11.refs_1_), channel_id=1, source_target_pairs={{0,16},{1,17},{2,18},{3,19},{4,20},{5,21},{6,22},{7,23},{8,24},{9,... | collective-permute-start | bytes 1572872 | tf_op jit(solution)/shard_map/ppermute | solution.py:219
  24.3 10.7 %collective-permute-start.9 = (s32[128]{0:T(128)S(1)}, s32[128]{0:T(128)S(1)}, u32[]{:S(2)}, u32[]{:S(2)}) collective-permute-start(s32[128]{0:T(128)S(1)} %get-tuple-element.29), channel_id=1, source_target_pairs={{0,1},{1,2},{2,3},{3,4},{4,5},{5,6},{6,7},{7,8},{8,9},{9,10},{10,1... | collective-permute-start | bytes 1544 | tf_op jit(solution)/shard_map/ppermute | solution.py:30
  34.5 12.9 %collective-permute-start.14 = (bf16[512,512]{1,0:T(8,128)(2,1)}, bf16[512,512]{1,0:T(8,128)(2,1)}, u32[]{:S(2)}, u32[]{:S(2)}) collective-permute-start(bf16[512,512]{1,0:T(8,128)(2,1)} %collective-permute-done.13.refs_2_), channel_id=1, source_target_pairs={{0,2},{1,3},{4,0},{5,1},{8,4},{9,5},{12,8},{13,9},{14,12},{15,13},... | collective-permute-start | bytes 1572872 | tf_op jit(solution)/shard_map/ppermute | solution.py:219
  35.0 15.8 %collective-permute-start.16 = (bf16[512,512]{1,0:T(8,128)(2,1)}, bf16[512,512]{1,0:T(8,128)(2,1)}, u32[]{:S(2)}, u32[]{:S(2)}) collective-permute-start(bf16[512,512]{1,0:T(8,128)(2,1)} %collective-permute-done.13.refs_2_), channel_id=1, source_target_pairs={{0,16},{1,17},{2,18},{3,19},{4,20},{5,21},{6,22},{7,23},{8,24},{9,... | collective-permute-start | bytes 1572872 | tf_op jit(solution)/shard_map/ppermute | solution.py:219
  37.7 14.8 %collective-permute-start.3 = (bf16[512,512]{1,0:T(8,128)(2,1)}, bf16[512,512]{1,0:T(8,128)(2,1)}, u32[]{:S(2)}, u32[]{:S(2)}) collective-permute-start(bf16[512,512]{1,0:T(8,128)(2,1)} %collective-permute-done.2.refs_3_), channel_id=1, source_target_pairs={{0,4},{1,5},{4,8},{5,9},{8,12},{9,13},{12,14},{13,15},{14,10},{15,... | collective-permute-start | bytes 1572872 | tf_op jit(solution)/shard_map/ppermute | solution.py:219
  39.3 22.7 %collective-permute-start.5 = (bf16[512,512]{1,0:T(8,128)(2,1)}, bf16[512,512]{1,0:T(8,128)(2,1)}, u32[]{:S(2)}, u32[]{:S(2)}) collective-permute-start(bf16[512,512]{1,0:T(8,128)(2,1)} %collective-permute-done.2.refs_3_), channel_id=1, source_target_pairs={{0,16},{1,17},{2,18},{3,19},{4,20},{5,21},{6,22},{7,23},{8,24},{9,... | collective-permute-start | bytes 1572872 | tf_op jit(solution)/shard_map/ppermute | solution.py:219
  47.4 20.3 %collective-permute-start.15 = (bf16[512,512]{1,0:T(8,128)(2,1)}, bf16[512,512]{1,0:T(8,128)(2,1)}, u32[]{:S(2)}, u32[]{:S(2)}) collective-permute-start(bf16[512,512]{1,0:T(8,128)(2,1)} %collective-permute-done.14.refs_3_), channel_id=1, source_target_pairs={{0,2},{1,3},{4,0},{5,1},{8,4},{9,5},{12,8},{13,9},{14,12},{15,13},... | collective-permute-start | bytes 1572872 | tf_op jit(solution)/shard_map/ppermute | solution.py:219
  50.8 17.0 %collective-permute-start.17 = (bf16[512,512]{1,0:T(8,128)(2,1)}, bf16[512,512]{1,0:T(8,128)(2,1)}, u32[]{:S(2)}, u32[]{:S(2)}) collective-permute-start(bf16[512,512]{1,0:T(8,128)(2,1)} %collective-permute-done.16.refs_4_), channel_id=1, source_target_pairs={{0,4},{1,5},{4,8},{5,9},{8,12},{9,13},{12,14},{13,15},{14,10},{15,... | collective-permute-start | bytes 1572872 | tf_op jit(solution)/shard_map/ppermute | solution.py:219
  52.4 18.5 %collective-permute-start.7 = (bf16[512,512]{1,0:T(8,128)(2,1)}, bf16[512,512]{1,0:T(8,128)(2,1)S(1)}, u32[]{:S(2)}, u32[]{:S(2)}) collective-permute-start(bf16[512,512]{1,0:T(8,128)(2,1)} %collective-permute-done.1.refs_1_), channel_id=1, source_target_pairs={{0,16},{1,17},{2,18},{3,19},{4,20},{5,21},{6,22},{7,23},{8,24},{9,... | collective-permute-start | bytes 1572872 | tf_op jit(solution)/shard_map/ppermute | solution.py:219
  62.0 13.6 %collective-permute-start.4 = (bf16[512,512]{1,0:T(8,128)(2,1)}, bf16[512,512]{1,0:T(8,128)(2,1)S(1)}, u32[]{:S(2)}, u32[]{:S(2)}) collective-permute-start(bf16[512,512]{1,0:T(8,128)(2,1)} %collective-permute-done.3.refs_4_), channel_id=1, source_target_pairs={{0,4},{1,5},{4,8},{5,9},{8,12},{9,13},{12,14},{13,15},{14,10},{15,... | collective-permute-start | bytes 1572872 | tf_op jit(solution)/shard_map/ppermute | solution.py:219
  63.6 12.0 %collective-permute-start.6 = (bf16[512,512]{1,0:T(8,128)(2,1)}, bf16[512,512]{1,0:T(8,128)(2,1)S(1)}, u32[]{:S(2)}, u32[]{:S(2)}) collective-permute-start(bf16[512,512]{1,0:T(8,128)(2,1)} %collective-permute-done.5.refs_5_), channel_id=1, source_target_pairs={{0,2},{1,3},{4,0},{5,1},{8,4},{9,5},{12,8},{13,9},{14,12},{15,13},... | collective-permute-start | bytes 1572872 | tf_op jit(solution)/shard_map/ppermute | solution.py:219
  70.8 4.9 %copy-start.1 = (bf16[256,4096]{1,0:T(8,128)(2,1)S(1)}, bf16[256,4096]{1,0:T(8,128)(2,1)}, u32[]{:S(2)}) copy-start(bf16[256,4096]{1,0:T(8,128)(2,1)} %copy-done) | copy-start | bytes 6291460
  70.8 11.6 %collective-permute-start.18 = (f32[256,512]{1,0:T(8,128)S(1)}, f32[256,512]{1,0:T(8,128)S(1)}, u32[]{:S(2)}, u32[]{:S(2)}) collective-permute-start(f32[256,512]{1,0:T(8,128)S(1)} %get-tuple-element.24), channel_id=1, source_target_pairs={{0,1},{1,0},{2,3},{3,2},{4,5},{5,4},{6,7},{7,6},{8,9},{9,8},{10,11... | collective-permute-start | bytes 1572872 | tf_op jit(solution)/shard_map/ppermute | solution.py:222
  77.9 2.0 %collective-permute-start.8 = (f32[256,512]{1,0:T(8,128)S(1)}, f32[256,512]{1,0:T(8,128)S(1)}, u32[]{:S(2)}, u32[]{:S(2)}) collective-permute-start(f32[256,512]{1,0:T(8,128)S(1)} %get-tuple-element.20), channel_id=1, source_target_pairs={{0,1},{1,0},{2,3},{3,2},{4,5},{5,4},{6,7},{7,6},{8,9},{9,8},{10,11... | collective-permute-start | bytes 1572872 | tf_op jit(solution)/shard_map/ppermute | solution.py:222
  79.1 7.3 %copy-start.2 = (bf16[256,4096]{1,0:T(8,128)(2,1)S(1)}, bf16[256,4096]{1,0:T(8,128)(2,1)}, u32[]{:S(2)}) copy-start(bf16[256,4096]{1,0:T(8,128)(2,1)} %q_ref.3) | copy-start | bytes 6291460
  80.2 8.7 %collective-permute-start.10 = (bf16[128,512]{1,0:T(8,128)(2,1)S(1)}, bf16[128,512]{1,0:T(8,128)(2,1)S(1)}, u32[]{:S(2)}, u32[]{:S(2)}) collective-permute-start(bf16[128,512]{1,0:T(8,128)(2,1)S(1)} %slice.33), channel_id=1, source_target_pairs={{0,1},{1,2},{2,3},{3,4},{4,5},{5,6},{6,7},{7,8},{8,9},{9,10},{10,1... | collective-permute-start | bytes 393224 | tf_op jit(solution)/shard_map/ppermute | solution.py:30
  82.5 8.8 %collective-permute-start.19 = (bf16[128,512]{1,0:T(8,128)(2,1)S(1)}, bf16[128,512]{1,0:T(8,128)(2,1)S(1)}, u32[]{:S(2)}, u32[]{:S(2)}) collective-permute-start(bf16[128,512]{1,0:T(8,128)(2,1)S(1)} %slice.34), channel_id=1, source_target_pairs={{0,1},{1,2},{2,3},{3,4},{4,5},{5,6},{6,7},{7,8},{8,9},{9,10},{10,1... | collective-permute-start | bytes 393224 | tf_op jit(solution)/shard_map/ppermute | solution.py:30

commit v2 on v1

--- a/solution.py
+++ b/solution.py
@@ -21,7 +21,7 @@
 
 
 def cost(flops, nbytes, trans=0):
-    return pl.CostEstimate(flops=flops, bytes_accessed=nbytes, transcendentals=trans)
+    return pl.CostEstimate(flops=flops // 1000, bytes_accessed=nbytes // 1000, transcendentals=trans // 1000)
 
 
 def from_behind(value, axis, steps):
@@ -30,7 +30,7 @@
     return lax.ppermute(value, axis, [(source, source + steps) for source in range(initial, last)])
 
 
-def norm_kernel(core_ref, h_ref, g_ref, mine_ref, theirs_ref):
+def norm_kernel(core_ref, h_ref, g_ref, mine_ref, *theirs):
     width = h_ref.shape[1]
     half = width // 16
     x = h_ref[...].astype(F32)
@@ -44,14 +44,19 @@
         n_hi = h_ref[:, hi].astype(F32) * scale * g_ref[:, hi].astype(F32)
         out = slice(b * half, (b + 1) * half)
         mine_ref[:, out] = jnp.where(first, n_lo, n_hi).astype(BF16)
-        theirs_ref[:, out] = jnp.where(first, n_hi, n_lo).astype(BF16)
+        for step, theirs_ref in enumerate(theirs):
+
+            @pl.when(pl.program_id(0) == step)
+            def _():
+                theirs_ref[:, out] = jnp.where(first, n_hi, n_lo).astype(BF16)
 
 
 def normalise(core, hidden, gain):
     rows, width = hidden.shape
     step = 64
-    out = jax.ShapeDtypeStruct((rows, width // 2), BF16)
-    return pl.pallas_call(
+    mine = jax.ShapeDtypeStruct((rows, width // 2), BF16)
+    theirs = jax.ShapeDtypeStruct((step, width // 2), BF16)
+    mine, *theirs = pl.pallas_call(
         norm_kernel,
         grid_spec=pltpu.PrefetchScalarGridSpec(
             num_scalar_prefetch=1,
@@ -60,62 +65,67 @@
                 pl.BlockSpec((step, width), lambda i, c: (i, 0)),
                 pl.BlockSpec((1, width), lambda i, c: (0, 0)),
             ],
-            out_specs=[pl.BlockSpec((step, width // 2), lambda i, c: (i, 0))] * 2,
+            out_specs=[pl.BlockSpec((step, width // 2), lambda i, c: (i, 0))]
+            + [pl.BlockSpec((step, width // 2), lambda i, c: (0, 0))] * (rows // step),
         ),
-        out_shape=[out, out],
+        out_shape=[mine] + [theirs] * (rows // step),
         compiler_params=params(),
         cost_estimate=cost(8 * rows * width, 4 * rows * width),
         name="norm",
     )(core, hidden, gain.reshape(1, width))
-
-
-def project_kernel(count, carried, index_ref, xa_ref, xb_ref, *refs):
+    return mine, theirs
+
+
+def project_kernel(count, parts, carried, index_ref, xa_ref, *refs):
+    others, refs = refs[:parts], refs[parts:]
     weights, refs = refs[:count], refs[count:]
-    before, (oa_ref, ob_ref) = refs[:-2], refs[-2:]
-    rows = xa_ref.shape[0]
+    before, outs = refs[:carried], refs[carried:]
     total = None
     for j in range(count):
         depth = weights[j].shape[0]
         columns = pl.ds(pl.multiple_of(index_ref[j] * depth, depth), depth)
-        x = jnp.concatenate([xa_ref[:, columns], xb_ref[:, columns]], axis=0)
+        x = jnp.concatenate([ref[:, columns] for ref in (xa_ref, *others)], axis=0)
         part = jnp.dot(x, weights[j][...], preferred_element_type=F32)
         total = part if total is None else total + part
-    if carried:
-        oa_ref[...] = before[0][...] + total[:rows]
-        ob_ref[...] = before[1][...] + total[rows:]
-    else:
-        oa_ref[...] = total[:rows]
-        ob_ref[...] = total[rows:]
-
-
-def project(index, xa, xb, weights, before=()):
+    held = jnp.concatenate([ref[...] for ref in before], axis=0) if carried else None
+    total = held + total if carried else total
+    at = 0
+    for ref in outs:
+        ref[...] = total[at : at + ref.shape[0]]
+        at += ref.shape[0]
+
+
+def project(index, xa, others, weights, before=(), split=1):
     rows = xa.shape[0]
     depth, feats = weights[0].shape
-    out = jax.ShapeDtypeStruct((rows, feats), F32)
+    outs = [jax.ShapeDtypeStruct((rows, feats), F32)]
+    outs += [jax.ShapeDtypeStruct((rows // split, feats), F32)] * split
     whole = pl.BlockSpec(memory_space=pltpu.VMEM)
+    operands = [xa, *others, *weights, *before]
     return pl.pallas_call(
-        functools.partial(project_kernel, len(weights), bool(before)),
-        in_specs=[pl.BlockSpec(memory_space=pltpu.SMEM)]
-        + [whole] * (2 + len(weights) + len(before)),
-        out_specs=[whole, whole],
-        out_shape=[out, out],
+        functools.partial(project_kernel, len(weights), len(others), len(before)),
+        in_specs=[pl.BlockSpec(memory_space=pltpu.SMEM)] + [whole] * len(operands),
+        out_specs=[whole] * len(outs),
+        out_shape=outs,
         compiler_params=params(),
         cost_estimate=cost(
             4 * rows * depth * feats * len(weights), 2 * depth * feats * len(weights) + 4 * rows * 4096
         ),
         name="project",
-    )(index, xa, xb, *weights, *before)
-
-
-def keys_kernel(a_ref, b_ref, cos_ref, sin_ref, out_ref):
+    )(index, *operands)
+
+
+def keys_kernel(a_ref, cos_ref, sin_ref, *refs):
     cos, sin = cos_ref[...], sin_ref[...]
+    others, out_ref = refs[:-1], refs[-1]
     for h in range(a_ref.shape[1] // HD):
         at = slice(h * HD, (h + 1) * HD)
-        raw = (a_ref[:, at] + b_ref[:, at]).astype(BF16).astype(F32)
+        b = jnp.concatenate([ref[:, at] for ref in others], axis=0)
+        raw = (a_ref[:, at] + b).astype(BF16).astype(F32)
         out_ref[:, at] = (raw * cos + pltpu.roll(raw, HD // 2, 1) * sin).astype(BF16)
 
 
-def finish_keys(a, b, cos, sin):
+def finish_keys(a, others, cos, sin):
     rows, feats = a.shape
     return pl.pallas_call(
         keys_kernel,
@@ -123,7 +133,7 @@
         compiler_params=params(),
         cost_estimate=cost(6 * rows * feats, 10 * rows * feats),
         name="keys",
-    )(a, b, cos, sin)
+    )(a, cos, sin, *others)
 
 
 def scores_kernel(q_ref, ka_ref, kb_ref, sq_ref, sk_ref, out_ref):
@@ -195,6 +205,10 @@
     )(p0, p1, prev, own)
 
 
+def after(*values):
+    return lax.optimization_barrier(values)
+
+
 def place(p):
     z, x = (p, 0) if p < 4 else (7 - p, 1)
     return z * 2 + x
@@ -227,21 +241,24 @@
     position = jnp.where(x == 0, z, 7 - z)
     sign = jnp.where(lax.axis_index("groups") == 0, 1, -1)
 
+    def blocks(steps):
+        p = jnp.mod(position + sign * jnp.array(steps, jnp.int32), 8)
+        return jnp.where(p < 4, 2 * p, 2 * (7 - p) + 1).astype(jnp.int32)
+
+    rows = segment_ids.shape[0]
+    mine, theirs = normalise(core.reshape(1).astype(jnp.int32), hidden, norm_gain)
+    other = [swap(t) for t in theirs]
+
     k1, v1 = send(key_weight, key_way), send(value_weight, value_way)
+    k1, v1, mine = after(k1, v1, mine)
     yk1 = send(k1, other_group)
     k2, v2 = send(k1, key_way), send(v1, value_way)
+    behind = from_behind(segment_ids[rows - REACH :], "dp", 1)
+    k2, v2, yk1, behind = after(k2, v2, yk1, behind)
     yk2, yv2 = send(k2, other_group), send(v2, other_group)
     k3, v3 = send(k2, key_way), send(v2, value_way)
     yv1 = send(v1, other_group)
-    k4, k3b = send(k3, key_way), send(yk2, value_way)
-    v4, v3b = send(v3, value_way), send(yv2, key_way)
-
-    def blocks(steps):
-        p = jnp.mod(position + sign * jnp.array(steps, jnp.int32), 8)
-        return jnp.where(p < 4, 2 * p, 2 * (7 - p) + 1).astype(jnp.int32)
-
-    rows = segment_ids.shape[0]
-    behind = from_behind(segment_ids[rows - REACH :], "dp", 1)
+
     behind = jnp.where(me > 0, behind, -1)
     window = jnp.concatenate([behind, segment_ids], axis=0)
     index = jnp.arange(window.shape[0], dtype=jnp.int32)
@@ -254,26 +271,31 @@
     cos = jnp.concatenate([cos, cos], axis=1)
     sin = jnp.concatenate([-sin, sin], axis=1)
 
-    mine, theirs = normalise(core.reshape(1).astype(jnp.int32), hidden, norm_gain)
-    other = swap(theirs)
-
-    part = project(blocks([0, -1, 1, -2, -3, 2]), mine, other, [key_weight, k1, yk1, k2, k3, yk2])
-    own_k, other_k = project(blocks([-4, 3]), mine, other, [k4, k3b], part)
-    keys = finish_keys(own_k, swap(other_k), cos, sin)
+    key_part = project(blocks([0, -1, 1, -2]), mine, other, [key_weight, k1, yk1, k2])
+    k3, v3, yk2, key_part, cos, sin = after(k3, v3, yk2, key_part, cos, sin)
+    k4, k3b = send(k3, key_way), send(yk2, value_way)
+    v4 = send(v3, value_way)
+    key_part = project(blocks([-3, 2]), mine, other, [k3, yk2], key_part)
+    value_part = project(blocks([0, 1, 2, 3]), mine, other, [value_weight, v1, v2, v3])
+    yv2, key_part, value_part = after(yv2, key_part, value_part)
+    v3b = send(yv2, key_way)
+
+    own_k, *other_k = project(blocks([-4, 3]), mine, other, [k4, k3b], key_part, 2)
+    keys = finish_keys(own_k, [swap(o) for o in other_k], cos, sin)
     prev_keys = from_behind(keys[rows - REACH :], "dp", 1)
-
     segs_q = segment_ids.reshape(rows, 1)
     p1 = softmax_weights(
         queries, 1, keys, 0, keys, 1, segs_q[REACH:], segment_ids.reshape(1, rows)
     )
+    value_part, p1 = after(value_part, p1)
+    own_v, other_v = project(
+        blocks([-2, -1, 4, -3]), mine, other, [yv2, yv1, v4, v3b], value_part
+    )
+    values = (own_v + swap(other_v)).astype(BF16)
+    prev_values = from_behind(values[rows - REACH :], "dp", 1)
     p0 = softmax_weights(
         queries, 0, prev_keys, 0, keys, 0, segs_q[:REACH], window[: 2 * REACH].reshape(1, 2 * REACH)
     )
-
-    part = project(blocks([0, 1, 2, 3, -2]), mine, other, [value_weight, v1, v2, v3, yv2])
-    own_v, other_v = project(blocks([-1, 4, -3]), mine, other, [yv1, v4, v3b], part)
-    values = (own_v + swap(other_v)).astype(BF16)
-    prev_values = from_behind(values[rows - REACH :], "dp", 1)
     return contexts(p0, p1, prev_values, values)
 
 

time: 96.1 us -> 94.8 us (0.986)
  waiting for transfers between devices: 40.7 us -> 20.8 us
  local copies, waits for them, and re-layouts: 1.05 us -> 17 us
  starting transfers between devices: 23.9 us -> 26 us
  Pallas kernels: 27.2 us -> 28.7 us
    ppermute x14, waiting for transfers between devices: 40 us -> 15.1 us  [send(): return lax.ppermute(value, both, way)]
    unnamed x20 -> x56, local copies, waits for them, and re-layouts: 0.06 us -> 16 us
    ppermute x3, waiting for transfers between devices: 0.01 us -> 4.54 us  [from_behind(): lax.ppermute(value, axis, [(source, source + steps) for source in range(i...]
    ppermute x3 -> x7, starting transfers between devices: 0.45 us -> 3.74 us  [swap(): return lax.ppermute(value, 'dp', other_core)]
    pallas_call x4 -> x5, Pallas kernels: 13.6 us -> 15 us  [project(): pl.pallas_call(functools.partial(project_kernel, len(weights), len(others...]
    ppermute x14, starting transfers between devices: 15.7 us -> 14.6 us  [send(): return lax.ppermute(value, both, way)]
  transfers between devices with their start and end apart: 20 -> 24, of which waited for: 7 -> 11; matrix products, arithmetic and copies ran while one was open for 1% -> 2% of each run, Pallas kernels for 20% -> 24%
where the time goes in v2:
time: 94.8 us; the launch traced here: 93.9 us
  Pallas kernels  28.7 us (30%)
  starting transfers between devices  26 us (27%)
  waiting for transfers between devices  20.8 us (22%)
  local copies, waits for them, and re-layouts  17 us (18%)
  other arithmetic  1.07 us (1%)
    unnamed x56, local copies, waits for them, and re-layouts  16 us
    ppermute x14, waiting for transfers between devices, send(): return lax.ppermute(value, both, way)  15.1 us
    pallas_call x5, Pallas kernels, project(): pl.pallas_call(functools.partial(project_kernel, len(weights), len(others...  15 us
    ppermute x14, starting transfers between devices, send(): return lax.ppermute(value, both, way)  14.6 us
    ppermute x3, starting transfers between devices, from_behind(): lax.ppermute(value, axis, [(source, source + steps) for source in range(i...  7.65 us
    pallas_call x1, Pallas kernels, normalise(): pl.pallas_call(norm_kernel, grid_spec=pltpu.PrefetchScalarGridSpec(num_sc...  5.55 us
    pallas_call x2, Pallas kernels, softmax_weights(): pl.pallas_call(scores_kernel, grid=(heads,), in_specs=[pl.BlockSpec((rows...  4.89 us
    ppermute x3, waiting for transfers between devices, from_behind(): lax.ppermute(value, axis, [(source, source + steps) for source in range(i...  4.54 us
  transfers between devices with their start and end apart: 24, of which 11 were waited for; matrix products, arithmetic and copies ran while one was open for 2% of the time, Pallas kernels for 24%

profile of v2, /device:TPU:8, one launch (start us, length us, event | category | flops | bytes accessed | tf_op | source)
XLA Modules:
  0.0 93.9 jit_solution(11011087128896081117)
XLA Ops:
  0.0 1.6 %collective-permute-start = (bf16[512,512]{1,0:T(8,128)(2,1)}, bf16[512,512]{1,0:T(8,128)(2,1)}, u32[]{:S(2)}, u32[]{:S(2)}) collective-permute-start(bf16[512,512]{1,0:T(8,128)(2,1)} %refs_4_.2), channel_id=1, source_target_pairs={{0,4},{1,5},{4,8},{5,9},{8,12},{9,13},{12,14},{13,15},{14,10},{15,... | collective-permute-start | bytes 1572872 | tf_op jit(solution)/shard_map/ppermute | solution.py:233
  2.8 5.6 %norm.1 = (bf16[256,4096]{1,0:T(8,128)(2,1)S(1)}, bf16[64,4096]{1,0:T(8,128)(2,1)}, bf16[64,4096]{1,0:T(8,128)(2,1)S(1)}, bf16[64,4096]{1,0:T(8,128)(2,1)S(1)}, bf16[64,4096]{1,0:T(8,128)(2,1)S(1)}) custom-call(s32[1]{0:T(128)} %bitcast.core_ref, bf16[256,8192]{1,0:T(8,128)(2,1)} %h_ref.1, bf16[1,8192]{1,0:T(2,128)(2,1)S(1)} %reshape.29.g_ref), custom_call_target="tpu_custom_call" | custom-call | flops 16777 | bytes 8388 | tf_op jit(solution)/shard_map/norm/pallas_call | solution.py:59
  8.4 1.3 %copy-done = bf16[256,4096]{1,0:T(8,128)(2,1)} copy-done((bf16[256,4096]{1,0:T(8,128)(2,1)}, bf16[256,4096]{1,0:T(8,128)(2,1)S(1)}, u32[]{:S(2)}) %copy-start) | copy-done | bytes 2097176
  12.1 1.9 %collective-permute-done.refs_5_ = bf16[512,512]{1,0:T(8,128)(2,1)} collective-permute-done((bf16[512,512]{1,0:T(8,128)(2,1)}, bf16[512,512]{1,0:T(8,128)(2,1)}, u32[]{:S(2)}, u32[]{:S(2)}) %collective-permute-start) | collective-permute-done | bytes 524320 | tf_op jit(solution)/shard_map/ppermute | solution.py:233
  14.0 1.2 %collective-permute-done.1.refs_5_ = bf16[512,512]{1,0:T(8,128)(2,1)S(1)} collective-permute-done((bf16[512,512]{1,0:T(8,128)(2,1)}, bf16[512,512]{1,0:T(8,128)(2,1)S(1)}, u32[]{:S(2)}, u32[]{:S(2)}) %collective-permute-start.1) | collective-permute-done | bytes 524320 | tf_op jit(solution)/shard_map/ppermute | solution.py:233
  15.2 1.6 %collective-permute-start.6 = (bf16[512,512]{1,0:T(8,128)(2,1)}, bf16[512,512]{1,0:T(8,128)(2,1)S(1)}, u32[]{:S(2)}, u32[]{:S(2)}) collective-permute-start(bf16[512,512]{1,0:T(8,128)(2,1)} %collective-permute-done.refs_5_), channel_id=1, source_target_pairs={{0,4},{1,5},{4,8},{5,9},{8,12},{9,13},{12,14},{13,15},{14,10},{15,... | collective-permute-start | bytes 1572872 | tf_op jit(solution)/shard_map/ppermute | solution.py:233
  17.6 1.9 %collective-permute-start.9 = (s32[128]{0:T(128)S(1)}, s32[128]{0:T(128)S(1)}, u32[]{:S(2)}, u32[]{:S(2)}) collective-permute-start(s32[128]{0:T(128)S(1)} %get-tuple-element.85), channel_id=1, source_target_pairs={{0,1},{1,2},{2,3},{3,4},{4,5},{5,6},{6,7},{7,8},{8,9},{9,10},{10,1... | collective-permute-start | bytes 1544 | tf_op jit(solution)/shard_map/ppermute | solution.py:30
  19.5 2.8 %collective-permute-start.2 = (bf16[64,4096]{1,0:T(8,128)(2,1)}, bf16[64,4096]{1,0:T(8,128)(2,1)S(1)}, u32[]{:S(2)}, u32[]{:S(2)}) collective-permute-start(bf16[64,4096]{1,0:T(8,128)(2,1)} %get-tuple-element.45), channel_id=1, source_target_pairs={{0,1},{1,0},{2,3},{3,2},{4,5},{5,4},{6,7},{7,6},{8,9},{9,8},{10,11... | collective-permute-start | bytes 1572872 | tf_op jit(solution)/shard_map/ppermute | solution.py:236
  22.3 3.4 %collective-permute-done.9 = s32[128]{0:T(128)S(1)} collective-permute-done((s32[128]{0:T(128)S(1)}, s32[128]{0:T(128)S(1)}, u32[]{:S(2)}, u32[]{:S(2)}) %collective-permute-start.9) | collective-permute-done | bytes 544 | tf_op jit(solution)/shard_map/ppermute | solution.py:30
  25.7 2.3 %collective-permute-done.6.refs_7_ = bf16[512,512]{1,0:T(8,128)(2,1)S(1)} collective-permute-done((bf16[512,512]{1,0:T(8,128)(2,1)}, bf16[512,512]{1,0:T(8,128)(2,1)S(1)}, u32[]{:S(2)}, u32[]{:S(2)}) %collective-permute-start.6) | collective-permute-done | bytes 524320 | tf_op jit(solution)/shard_map/ppermute | solution.py:233
  30.1 1.6 %collective-permute-start.10 = (bf16[512,512]{1,0:T(8,128)(2,1)}, bf16[512,512]{1,0:T(8,128)(2,1)S(1)}, u32[]{:S(2)}, u32[]{:S(2)}) collective-permute-start(bf16[512,512]{1,0:T(8,128)(2,1)} %copy-done.9), channel_id=1, source_target_pairs={{0,4},{1,5},{4,8},{5,9},{8,12},{9,13},{12,14},{13,15},{14,10},{15,... | collective-permute-start | bytes 1572872 | tf_op jit(solution)/shard_map/ppermute | solution.py:233
  32.0 1.6 %collective-permute-start.11 = (bf16[512,512]{1,0:T(8,128)(2,1)}, bf16[512,512]{1,0:T(8,128)(2,1)}, u32[]{:S(2)}, u32[]{:S(2)}) collective-permute-start(bf16[512,512]{1,0:T(8,128)(2,1)} %copy-done.7), channel_id=1, source_target_pairs={{0,2},{1,3},{4,0},{5,1},{8,4},{9,5},{12,8},{13,9},{14,12},{15,13},... | collective-permute-start | bytes 1572872 | tf_op jit(solution)/shard_map/ppermute | solution.py:233
  33.9 1.7 %collective-permute-start.15 = (bf16[512,512]{1,0:T(8,128)(2,1)}, bf16[512,512]{1,0:T(8,128)(2,1)}, u32[]{:S(2)}, u32[]{:S(2)}) collective-permute-start(bf16[512,512]{1,0:T(8,128)(2,1)} %copy-done.7), channel_id=1, source_target_pairs={{0,16},{1,17},{2,18},{3,19},{4,20},{5,21},{6,22},{7,23},{8,24},{9,... | collective-permute-start | bytes 1572872 | tf_op jit(solution)/shard_map/ppermute | solution.py:233
  36.6 3.1 %project.5 = (f32[256,512]{1,0:T(8,128)S(1)}, f32[256,512]{1,0:T(8,128)S(1)}) custom-call(s32[4]{0:T(128)S(1)} %get-tuple-element.88.index_ref, bf16[256,4096]{1,0:T(8,128)(2,1)} %copy-done, bf16[64,4096]{1,0:T(8,128)(2,1)S(1)} %collective-permute-done.2.refs_0_, bf16[64,4096]{1,0:T(8,128)(2,1)S(1)} %collective-permute-done.3.refs_1_, ...), custom_call_target="tpu_custom_call" | custom-call | flops 1073741 | bytes 6291 | tf_op jit(solution)/shard_map/project/pallas_call | solution.py:105
  40.4 4.1 %collective-permute-done.10.refs_4_ = bf16[512,512]{1,0:T(8,128)(2,1)S(1)} collective-permute-done((bf16[512,512]{1,0:T(8,128)(2,1)}, bf16[512,512]{1,0:T(8,128)(2,1)S(1)}, u32[]{:S(2)}, u32[]{:S(2)}) %collective-permute-start.10) | collective-permute-done | bytes 524320 | tf_op jit(solution)/shard_map/ppermute | solution.py:233
  44.5 1.4 %collective-permute-done.11.refs_7_ = bf16[512,512]{1,0:T(8,128)(2,1)} collective-permute-done((bf16[512,512]{1,0:T(8,128)(2,1)}, bf16[512,512]{1,0:T(8,128)(2,1)}, u32[]{:S(2)}, u32[]{:S(2)}) %collective-permute-start.11) | collective-permute-done | bytes 524320 | tf_op jit(solution)/shard_map/ppermute | solution.py:233
  46.7 1.5 %collective-permute-start.13 = (bf16[512,512]{1,0:T(8,128)(2,1)S(1)}, bf16[512,512]{1,0:T(8,128)(2,1)S(1)}, u32[]{:S(2)}, u32[]{:S(2)}) collective-permute-start(bf16[512,512]{1,0:T(8,128)(2,1)S(1)} %collective-permute-done.10.refs_4_), channel_id=1, source_target_pairs={{0,4},{1,5},{4,8},{5,9},{8,12},{9,13},{12,14},{13,15},{14,10},{15,... | collective-permute-start | bytes 1572872 | tf_op jit(solution)/shard_map/ppermute | solution.py:233
  49.7 2.3 %project.6 = (f32[256,512]{1,0:T(8,128)S(1)}, f32[256,512]{1,0:T(8,128)S(1)}) custom-call(s32[2]{0:T(128)S(1)} %compare_select_fusion.12.index_ref, bf16[256,4096]{1,0:T(8,128)(2,1)} %copy-done, bf16[64,4096]{1,0:T(8,128)(2,1)S(1)} %collective-permute-done.2.refs_0_, bf16[64,4096]{1,0:T(8,128)(2,1)S(1)} %collective-permute-done.3.refs_1_, ...), custom_call_target="tpu_custom_call" | custom-call | flops 536870 | bytes 5242 | tf_op jit(solution)/shard_map/project/pallas_call | solution.py:105
  52.0 2.9 %project.7 = (f32[256,512]{1,0:T(8,128)S(1)}, f32[256,512]{1,0:T(8,128)S(1)}) custom-call(s32[4]{0:T(128)S(1)} %get-tuple-element.87.index_ref, bf16[256,4096]{1,0:T(8,128)(2,1)} %copy-done, bf16[64,4096]{1,0:T(8,128)(2,1)S(1)} %collective-permute-done.2.refs_0_, bf16[64,4096]{1,0:T(8,128)(2,1)S(1)} %collective-permute-done.3.refs_1_, ...), custom_call_target="tpu_custom_call" | custom-call | flops 1073741 | bytes 6291 | tf_op jit(solution)/shard_map/project/pallas_call | solution.py:105
  55.0 3.1 %collective-permute-done.15.refs_4_ = bf16[512,512]{1,0:T(8,128)(2,1)} collective-permute-done((bf16[512,512]{1,0:T(8,128)(2,1)}, bf16[512,512]{1,0:T(8,128)(2,1)}, u32[]{:S(2)}, u32[]{:S(2)}) %collective-permute-start.15) | collective-permute-done | bytes 524320 | tf_op jit(solution)/shard_map/ppermute | solution.py:233
  58.1 1.5 %collective-permute-start.21 = (bf16[512,512]{1,0:T(8,128)(2,1)}, bf16[512,512]{1,0:T(8,128)(2,1)}, u32[]{:S(2)}, u32[]{:S(2)}) collective-permute-start(bf16[512,512]{1,0:T(8,128)(2,1)} %collective-permute-done.15.refs_4_), channel_id=1, source_target_pairs={{0,4},{1,5},{4,8},{5,9},{8,12},{9,13},{12,14},{13,15},{14,10},{15,... | collective-permute-start | bytes 1572872 | tf_op jit(solution)/shard_map/ppermute | solution.py:233
  60.2 3.1 %project.8 = (f32[256,512]{1,0:T(8,128)S(1)}, f32[128,512]{1,0:T(8,128)}, f32[128,512]{1,0:T(8,128)}) custom-call(s32[2]{0:T(128)S(1)} %compare_select_fusion.14.index_ref, bf16[256,4096]{1,0:T(8,128)(2,1)} %copy-done, bf16[64,4096]{1,0:T(8,128)(2,1)S(1)} %collective-permute-done.2.refs_0_, bf16[64,4096]{1,0:T(8,128)(2,1)S(1)} %collective-permute-done.3.refs_1_, ...), custom_call_target="tpu_custom_call" | custom-call | flops 536870 | bytes 5242 | tf_op jit(solution)/shard_map/project/pallas_call | solution.py:105
  70.4 1.6 %copy-done.3 = bf16[256,4096]{1,0:T(8,128)(2,1)S(1)} copy-done((bf16[256,4096]{1,0:T(8,128)(2,1)S(1)}, bf16[256,4096]{1,0:T(8,128)(2,1)}, u32[]{:S(2)}) %copy-start.3) | copy-done | bytes 2097176
  72.0 2.4 %scores.3.p1_ref = bf16[4,1024,256]{2,1,0:T(8,128)(2,1)S(1)} custom-call(bf16[256,4096]{1,0:T(8,128)(2,1)S(1)} %copy-done.3, bf16[256,512]{1,0:T(8,128)(2,1)S(1)} %keys.1.kb_ref.ka_ref, bf16[256,512]{1,0:T(8,128)(2,1)S(1)} %keys.1.kb_ref.ka_ref, s32[128,1]{1,0:T(8,128)S(1)} %copy.15.sq_ref, s32[1,256]{1,0:T(1,128)S(1)} %bitcast.7), custom_call_target="tpu_custom_call" | custom-call | flops 268435 | bytes 3145 | tf_op jit(solution)/shard_map/scores/pallas_call | solution.py:158
  74.5 1.3 %copy-done.1 = bf16[4,1024,256]{2,1,0:T(8,128)(2,1)} copy-done((bf16[4,1024,256]{2,1,0:T(8,128)(2,1)}, bf16[4,1024,256]{2,1,0:T(8,128)(2,1)S(1)}, u32[]{:S(2)}) %copy-start.1) | copy-done | bytes 2097176
  75.8 3.6 %project.9 = (f32[256,512]{1,0:T(8,128)S(1)}, f32[256,512]{1,0:T(8,128)S(1)}) custom-call(s32[4]{0:T(128)S(1)} %compare_select_fusion.10.index_ref, bf16[256,4096]{1,0:T(8,128)(2,1)} %copy-done, bf16[64,4096]{1,0:T(8,128)(2,1)S(1)} %collective-permute-done.2.refs_0_, bf16[64,4096]{1,0:T(8,128)(2,1)S(1)} %collective-permute-done.3.refs_1_, ...), custom_call_target="tpu_custom_call" | custom-call | flops 1073741 | bytes 6291 | tf_op jit(solution)/shard_map/project/pallas_call | solution.py:105
  79.6 2.3 %collective-permute-start.18 = (bf16[128,512]{1,0:T(8,128)(2,1)S(1)}, bf16[128,512]{1,0:T(8,128)(2,1)S(1)}, u32[]{:S(2)}, u32[]{:S(2)}) collective-permute-start(bf16[128,512]{1,0:T(8,128)(2,1)S(1)} %slice.33), channel_id=1, source_target_pairs={{0,1},{1,2},{2,3},{3,4},{4,5},{5,6},{6,7},{7,8},{8,9},{9,10},{10,1... | collective-permute-start | bytes 393224 | tf_op jit(solution)/shard_map/ppermute | solution.py:30
  82.0 3.5 %collective-permute-start.23 = (bf16[128,512]{1,0:T(8,128)(2,1)S(1)}, bf16[128,512]{1,0:T(8,128)(2,1)S(1)}, u32[]{:S(2)}, u32[]{:S(2)}) collective-permute-start(bf16[128,512]{1,0:T(8,128)(2,1)S(1)} %slice.34), channel_id=1, source_target_pairs={{0,1},{1,2},{2,3},{3,4},{4,5},{5,6},{6,7},{7,8},{8,9},{9,10},{10,1... | collective-permute-start | bytes 393224 | tf_op jit(solution)/shard_map/ppermute | solution.py:30
  85.6 1.2 %collective-permute-done.18.ka_ref = bf16[128,512]{1,0:T(8,128)(2,1)S(1)} collective-permute-done((bf16[128,512]{1,0:T(8,128)(2,1)S(1)}, bf16[128,512]{1,0:T(8,128)(2,1)S(1)}, u32[]{:S(2)}, u32[]{:S(2)}) %collective-permute-start.18) | collective-permute-done | bytes 131104 | tf_op jit(solution)/shard_map/ppermute | solution.py:30
  86.8 1.6 %copy-done.4 = bf16[256,4096]{1,0:T(8,128)(2,1)S(1)} copy-done((bf16[256,4096]{1,0:T(8,128)(2,1)S(1)}, bf16[256,4096]{1,0:T(8,128)(2,1)}, u32[]{:S(2)}) %copy-start.4) | copy-done | bytes 2097176
  88.4 2.4 %scores.2.p0_ref = bf16[4,1024,256]{2,1,0:T(8,128)(2,1)S(1)} custom-call(bf16[256,4096]{1,0:T(8,128)(2,1)S(1)} %copy-done.4, bf16[128,512]{1,0:T(8,128)(2,1)S(1)} %collective-permute-done.18.ka_ref, bf16[256,512]{1,0:T(8,128)(2,1)S(1)} %keys.1.kb_ref.ka_ref, s32[128,1]{1,0:T(8,128)S(1)} %copy.14.sq_ref, s32[1,256]{1,0:T(1,128)S(1)} %bitcast.8), custom_call_target="tpu_custom_call" | custom-call | flops 268435 | bytes 3145 | tf_op jit(solution)/shard_map/scores/pallas_call | solution.py:158
  90.9 3.0 %context.1 = bf16[256,4096]{1,0:T(8,128)(2,1)} custom-call(bf16[4,1024,256]{2,1,0:T(8,128)(2,1)S(1)} %scores.2.p0_ref, bf16[4,1024,256]{2,1,0:T(8,128)(2,1)S(1)} %copy-done.2, bf16[128,512]{1,0:T(8,128)(2,1)S(1)} %collective-permute-done.23.prev_ref, bf16[256,512]{1,0:T(8,128)(2,1)S(1)} %add_convert_fusion.own_ref), custom_call_target="tpu_custom_call" | custom-call | flops 536870 | bytes 6291 | tf_op jit(solution)/shard_map/context/pallas_call | solution.py:191
  (103 shorter events, 19.2 us)
Async XLA Ops:
  0.0 14.0 %collective-permute-start = (bf16[512,512]{1,0:T(8,128)(2,1)}, bf16[512,512]{1,0:T(8,128)(2,1)}, u32[]{:S(2)}, u32[]{:S(2)}) collective-permute-start(bf16[512,512]{1,0:T(8,128)(2,1)} %refs_4_.2), channel_id=1, source_target_pairs={{0,4},{1,5},{4,8},{5,9},{8,12},{9,13},{12,14},{13,15},{14,10},{15,... | collective-permute-start | bytes 1572872 | tf_op jit(solution)/shard_map/ppermute | solution.py:233
  1.6 13.6 %collective-permute-start.1 = (bf16[512,512]{1,0:T(8,128)(2,1)}, bf16[512,512]{1,0:T(8,128)(2,1)S(1)}, u32[]{:S(2)}, u32[]{:S(2)}) collective-permute-start(bf16[512,512]{1,0:T(8,128)(2,1)} %refs_4_.3), channel_id=1, source_target_pairs={{0,2},{1,3},{4,0},{5,1},{8,4},{9,5},{12,8},{13,9},{14,12},{15,13},... | collective-permute-start | bytes 1572872 | tf_op jit(solution)/shard_map/ppermute | solution.py:233
  2.8 14.8 %copy-start.20 = (s32[256]{0:T(256)S(1)}, s32[256]{0:T(256)}, u32[]{:S(2)}) copy-start(s32[256]{0:T(256)} %param.16) | copy-start | bytes 3076
  2.8 22.9 %copy-start.24 = (s32[4]{0:T(128)S(1)}, s32[4]{0:T(128)}, u32[]{:S(2)}) copy-start(s32[4]{0:T(128)} %constant.111.clone) | copy-start | bytes 52
  2.8 32.8 %copy-start.5 = (bf16[512,512]{1,0:T(8,128)(2,1)S(1)}, bf16[512,512]{1,0:T(8,128)(2,1)}, u32[]{:S(2)}) copy-start(bf16[512,512]{1,0:T(8,128)(2,1)} %refs_4_.2) | copy-start | bytes 1572868
  15.2 12.8 %collective-permute-start.6 = (bf16[512,512]{1,0:T(8,128)(2,1)}, bf16[512,512]{1,0:T(8,128)(2,1)S(1)}, u32[]{:S(2)}, u32[]{:S(2)}) collective-permute-start(bf16[512,512]{1,0:T(8,128)(2,1)} %collective-permute-done.refs_5_), channel_id=1, source_target_pairs={{0,4},{1,5},{4,8},{5,9},{8,12},{9,13},{12,14},{13,15},{14,10},{15,... | collective-permute-start | bytes 1572872 | tf_op jit(solution)/shard_map/ppermute | solution.py:233
  16.7 12.3 %collective-permute-start.7 = (bf16[512,512]{1,0:T(8,128)(2,1)S(1)}, bf16[512,512]{1,0:T(8,128)(2,1)S(1)}, u32[]{:S(2)}, u32[]{:S(2)}) collective-permute-start(bf16[512,512]{1,0:T(8,128)(2,1)S(1)} %collective-permute-done.1.refs_5_), channel_id=1, source_target_pairs={{0,2},{1,3},{4,0},{5,1},{8,4},{9,5},{12,8},{13,9},{14,12},{15,13},... | collective-permute-start | bytes 1572872 | tf_op jit(solution)/shard_map/ppermute | solution.py:233
  17.2 12.9 %collective-permute-start.8 = (bf16[512,512]{1,0:T(8,128)(2,1)}, bf16[512,512]{1,0:T(8,128)(2,1)}, u32[]{:S(2)}, u32[]{:S(2)}) collective-permute-start(bf16[512,512]{1,0:T(8,128)(2,1)} %collective-permute-done.refs_5_), channel_id=1, source_target_pairs={{0,16},{1,17},{2,18},{3,19},{4,20},{5,21},{6,22},{7,23},{8,24},{9,... | collective-permute-start | bytes 1572872 | tf_op jit(solution)/shard_map/ppermute | solution.py:233
  17.6 8.1 %collective-permute-start.9 = (s32[128]{0:T(128)S(1)}, s32[128]{0:T(128)S(1)}, u32[]{:S(2)}, u32[]{:S(2)}) collective-permute-start(s32[128]{0:T(128)S(1)} %get-tuple-element.85), channel_id=1, source_target_pairs={{0,1},{1,2},{2,3},{3,4},{4,5},{5,6},{6,7},{7,8},{8,9},{9,10},{10,1... | collective-permute-start | bytes 1544 | tf_op jit(solution)/shard_map/ppermute | solution.py:30
  19.5 12.2 %collective-permute-start.2 = (bf16[64,4096]{1,0:T(8,128)(2,1)}, bf16[64,4096]{1,0:T(8,128)(2,1)S(1)}, u32[]{:S(2)}, u32[]{:S(2)}) collective-permute-start(bf16[64,4096]{1,0:T(8,128)(2,1)} %get-tuple-element.45), channel_id=1, source_target_pairs={{0,1},{1,0},{2,3},{3,2},{4,5},{5,4},{6,7},{7,6},{8,9},{9,8},{10,11... | collective-permute-start | bytes 1572872 | tf_op jit(solution)/shard_map/ppermute | solution.py:236
  25.7 6.4 %collective-permute-start.3 = (bf16[64,4096]{1,0:T(8,128)(2,1)}, bf16[64,4096]{1,0:T(8,128)(2,1)S(1)}, u32[]{:S(2)}, u32[]{:S(2)}) collective-permute-start(bf16[64,4096]{1,0:T(8,128)(2,1)} %copy-done.23), channel_id=1, source_target_pairs={{0,1},{1,0},{2,3},{3,2},{4,5},{5,4},{6,7},{7,6},{8,9},{9,8},{10,11... | collective-permute-start | bytes 1572872 | tf_op jit(solution)/shard_map/ppermute | solution.py:236
  28.8 5.1 %collective-permute-start.4 = (bf16[64,4096]{1,0:T(8,128)(2,1)}, bf16[64,4096]{1,0:T(8,128)(2,1)S(1)}, u32[]{:S(2)}, u32[]{:S(2)}) collective-permute-start(bf16[64,4096]{1,0:T(8,128)(2,1)} %copy-done.22), channel_id=1, source_target_pairs={{0,1},{1,0},{2,3},{3,2},{4,5},{5,4},{6,7},{7,6},{8,9},{9,8},{10,11... | collective-permute-start | bytes 1572872 | tf_op jit(solution)/shard_map/ppermute | solution.py:236
  29.8 5.7 %collective-permute-start.5 = (bf16[64,4096]{1,0:T(8,128)(2,1)}, bf16[64,4096]{1,0:T(8,128)(2,1)S(1)}, u32[]{:S(2)}, u32[]{:S(2)}) collective-permute-start(bf16[64,4096]{1,0:T(8,128)(2,1)} %copy-done.21), channel_id=1, source_target_pairs={{0,1},{1,0},{2,3},{3,2},{4,5},{5,4},{6,7},{7,6},{8,9},{9,8},{10,11... | collective-permute-start | bytes 1572872 | tf_op jit(solution)/shard_map/ppermute | solution.py:236
  30.1 14.4 %collective-permute-start.10 = (bf16[512,512]{1,0:T(8,128)(2,1)}, bf16[512,512]{1,0:T(8,128)(2,1)S(1)}, u32[]{:S(2)}, u32[]{:S(2)}) collective-permute-start(bf16[512,512]{1,0:T(8,128)(2,1)} %copy-done.9), channel_id=1, source_target_pairs={{0,4},{1,5},{4,8},{5,9},{8,12},{9,13},{12,14},{13,15},{14,10},{15,... | collective-permute-start | bytes 1572872 | tf_op jit(solution)/shard_map/ppermute | solution.py:233
  31.7 15.0 %collective-permute-start.12 = (bf16[512,512]{1,0:T(8,128)(2,1)}, bf16[512,512]{1,0:T(8,128)(2,1)S(1)}, u32[]{:S(2)}, u32[]{:S(2)}) collective-permute-start(bf16[512,512]{1,0:T(8,128)(2,1)} %copy-done.9), channel_id=1, source_target_pairs={{0,16},{1,17},{2,18},{3,19},{4,20},{5,21},{6,22},{7,23},{8,24},{9,... | collective-permute-start | bytes 1572872 | tf_op jit(solution)/shard_map/ppermute | solution.py:233
  32.0 13.9 %collective-permute-start.11 = (bf16[512,512]{1,0:T(8,128)(2,1)}, bf16[512,512]{1,0:T(8,128)(2,1)}, u32[]{:S(2)}, u32[]{:S(2)}) collective-permute-start(bf16[512,512]{1,0:T(8,128)(2,1)} %copy-done.7), channel_id=1, source_target_pairs={{0,2},{1,3},{4,0},{5,1},{8,4},{9,5},{12,8},{13,9},{14,12},{15,13},... | collective-permute-start | bytes 1572872 | tf_op jit(solution)/shard_map/ppermute | solution.py:233
  33.9 24.2 %collective-permute-start.15 = (bf16[512,512]{1,0:T(8,128)(2,1)}, bf16[512,512]{1,0:T(8,128)(2,1)}, u32[]{:S(2)}, u32[]{:S(2)}) collective-permute-start(bf16[512,512]{1,0:T(8,128)(2,1)} %copy-done.7), channel_id=1, source_target_pairs={{0,16},{1,17},{2,18},{3,19},{4,20},{5,21},{6,22},{7,23},{8,24},{9,... | collective-permute-start | bytes 1572872 | tf_op jit(solution)/shard_map/ppermute | solution.py:233
  36.6 12.2 %copy-start.27 = (s32[2]{0:T(128)S(1)}, s32[2]{0:T(128)}, u32[]{:S(2)}) copy-start(s32[2]{0:T(128)} %constant.112.clone) | copy-start | bytes 28
  46.7 13.4 %collective-permute-start.13 = (bf16[512,512]{1,0:T(8,128)(2,1)S(1)}, bf16[512,512]{1,0:T(8,128)(2,1)S(1)}, u32[]{:S(2)}, u32[]{:S(2)}) collective-permute-start(bf16[512,512]{1,0:T(8,128)(2,1)S(1)} %collective-permute-done.10.refs_4_), channel_id=1, source_target_pairs={{0,4},{1,5},{4,8},{5,9},{8,12},{9,13},{12,14},{13,15},{14,10},{15,... | collective-permute-start | bytes 1572872 | tf_op jit(solution)/shard_map/ppermute | solution.py:233
  48.3 11.9 %collective-permute-start.14 = (bf16[512,512]{1,0:T(8,128)(2,1)S(1)}, bf16[512,512]{1,0:T(8,128)(2,1)S(1)}, u32[]{:S(2)}, u32[]{:S(2)}) collective-permute-start(bf16[512,512]{1,0:T(8,128)(2,1)S(1)} %collective-permute-done.12.refs_5_), channel_id=1, source_target_pairs={{0,2},{1,3},{4,0},{5,1},{8,4},{9,5},{12,8},{13,9},{14,12},{15,13},... | collective-permute-start | bytes 1572872 | tf_op jit(solution)/shard_map/ppermute | solution.py:233
  48.8 27.0 %collective-permute-start.19 = (bf16[512,512]{1,0:T(8,128)(2,1)S(1)}, bf16[512,512]{1,0:T(8,128)(2,1)}, u32[]{:S(2)}, u32[]{:S(2)}) collective-permute-start(bf16[512,512]{1,0:T(8,128)(2,1)S(1)} %collective-permute-done.1.refs_5_), channel_id=1, source_target_pairs={{0,16},{1,17},{2,18},{3,19},{4,20},{5,21},{6,22},{7,23},{8,24},{9,... | collective-permute-start | bytes 1572872 | tf_op jit(solution)/shard_map/ppermute | solution.py:233
  52.0 8.1 %copy-start.26 = (s32[2]{0:T(128)S(1)}, s32[2]{0:T(128)}, u32[]{:S(2)}) copy-start(s32[2]{0:T(128)} %constant.113.clone) | copy-start | bytes 28
  55.0 8.3 %copy-start.13 = (f32[256,512]{1,0:T(8,128)}, f32[256,512]{1,0:T(8,128)S(1)}, u32[]{:S(2)}) copy-start(f32[256,512]{1,0:T(8,128)S(1)} %get-tuple-element.77.refs_8_) | copy-start | bytes 1572868
  55.0 8.3 %copy-start.15 = (f32[256,512]{1,0:T(8,128)}, f32[256,512]{1,0:T(8,128)S(1)}, u32[]{:S(2)}) copy-start(f32[256,512]{1,0:T(8,128)S(1)} %get-tuple-element.78.refs_9_) | copy-start | bytes 1572868
  58.1 17.7 %collective-permute-start.21 = (bf16[512,512]{1,0:T(8,128)(2,1)}, bf16[512,512]{1,0:T(8,128)(2,1)}, u32[]{:S(2)}, u32[]{:S(2)}) collective-permute-start(bf16[512,512]{1,0:T(8,128)(2,1)} %collective-permute-done.15.refs_4_), channel_id=1, source_target_pairs={{0,4},{1,5},{4,8},{5,9},{8,12},{9,13},{12,14},{13,15},{14,10},{15,... | collective-permute-start | bytes 1572872 | tf_op jit(solution)/shard_map/ppermute | solution.py:233
  59.6 16.2 %collective-permute-start.20 = (bf16[512,512]{1,0:T(8,128)(2,1)}, bf16[512,512]{1,0:T(8,128)(2,1)}, u32[]{:S(2)}, u32[]{:S(2)}) collective-permute-start(bf16[512,512]{1,0:T(8,128)(2,1)} %collective-permute-done.11.refs_7_), channel_id=1, source_target_pairs={{0,2},{1,3},{4,0},{5,1},{8,4},{9,5},{12,8},{13,9},{14,12},{15,13},... | collective-permute-start | bytes 1572872 | tf_op jit(solution)/shard_map/ppermute | solution.py:233
  60.1 4.6 %copy-start.25 = (s32[4]{0:T(128)S(1)}, s32[4]{0:T(128)}, u32[]{:S(2)}) copy-start(s32[4]{0:T(128)} %constant.114.clone) | copy-start | bytes 52
  64.1 1.7 %collective-permute-start.16 = (f32[128,512]{1,0:T(8,128)}, f32[128,512]{1,0:T(8,128)S(1)}, u32[]{:S(2)}, u32[]{:S(2)}) collective-permute-start(f32[128,512]{1,0:T(8,128)} %get-tuple-element.71), channel_id=1, source_target_pairs={{0,1},{1,0},{2,3},{3,2},{4,5},{5,4},{6,7},{7,6},{8,9},{9,8},{10,11... | collective-permute-start | bytes 786440 | tf_op jit(solution)/shard_map/ppermute | solution.py:236
  64.1 2.4 %collective-permute-start.17 = (f32[128,512]{1,0:T(8,128)}, f32[128,512]{1,0:T(8,128)S(1)}, u32[]{:S(2)}, u32[]{:S(2)}) collective-permute-start(f32[128,512]{1,0:T(8,128)} %get-tuple-element.72), channel_id=1, source_target_pairs={{0,1},{1,0},{2,3},{3,2},{4,5},{5,4},{6,7},{7,6},{8,9},{9,8},{10,11... | collective-permute-start | bytes 786440 | tf_op jit(solution)/shard_map/ppermute | solution.py:236
  79.4 2.5 %collective-permute-start.22 = (f32[256,512]{1,0:T(8,128)S(1)}, f32[256,512]{1,0:T(8,128)S(1)}, u32[]{:S(2)}, u32[]{:S(2)}) collective-permute-start(f32[256,512]{1,0:T(8,128)S(1)} %get-tuple-element.80), channel_id=1, source_target_pairs={{0,1},{1,0},{2,3},{3,2},{4,5},{5,4},{6,7},{7,6},{8,9},{9,8},{10,11... | collective-permute-start | bytes 1572872 | tf_op jit(solution)/shard_map/ppermute | solution.py:236
  79.6 7.2 %collective-permute-start.18 = (bf16[128,512]{1,0:T(8,128)(2,1)S(1)}, bf16[128,512]{1,0:T(8,128)(2,1)S(1)}, u32[]{:S(2)}, u32[]{:S(2)}) collective-permute-start(bf16[128,512]{1,0:T(8,128)(2,1)S(1)} %slice.33), channel_id=1, source_target_pairs={{0,1},{1,2},{2,3},{3,4},{4,5},{5,6},{6,7},{7,8},{8,9},{9,10},{10,1... | collective-permute-start | bytes 393224 | tf_op jit(solution)/shard_map/ppermute | solution.py:30
  82.0 8.8 %collective-permute-start.23 = (bf16[128,512]{1,0:T(8,128)(2,1)S(1)}, bf16[128,512]{1,0:T(8,128)(2,1)S(1)}, u32[]{:S(2)}, u32[]{:S(2)}) collective-permute-start(bf16[128,512]{1,0:T(8,128)(2,1)S(1)} %slice.34), channel_id=1, source_target_pairs={{0,1},{1,2},{2,3},{3,4},{4,5},{5,6},{6,7},{7,8},{8,9},{9,10},{10,1... | collective-permute-start | bytes 393224 | tf_op jit(solution)/shard_map/ppermute | solution.py:30
  (20 other events, 28.7 us)

commit v3 on v2

--- a/solution.py
+++ b/solution.py
@@ -2,6 +2,7 @@
 
 import jax
 import jax.numpy as jnp
+import numpy as np
 from jax import lax
 from jax.experimental import pallas as pl
 from jax.experimental.pallas import tpu as pltpu
@@ -13,7 +14,7 @@
 EPS = 1e-05
 F32 = jnp.float32
 BF16 = jnp.bfloat16
-VMEM_LIMIT = 48 * 1024 * 1024
+VMEM_LIMIT = 16 * 1024 * 1024
 
 
 def params():
@@ -21,7 +22,7 @@
 
 
 def cost(flops, nbytes, trans=0):
-    return pl.CostEstimate(flops=flops // 1000, bytes_accessed=nbytes // 1000, transcendentals=trans // 1000)
+    return pl.CostEstimate(flops=flops, bytes_accessed=nbytes, transcendentals=trans)
 
 
 def from_behind(value, axis, steps):
@@ -36,7 +37,7 @@
     x = h_ref[...].astype(F32)
     meansq = jnp.sum(x * x, axis=-1, keepdims=True) * (1.0 / width)
     scale = lax.rsqrt(meansq + EPS)
-    first = core_ref[0] == 0
+    first = lax.rem(core_ref[0], 2) == 0
     for b in range(8):
         lo = slice(2 * b * half, (2 * b + 1) * half)
         hi = slice((2 * b + 1) * half, (2 * b + 2) * half)
@@ -76,14 +77,23 @@
     return mine, theirs
 
 
-def project_kernel(count, parts, carried, index_ref, xa_ref, *refs):
+def block_at(ids_ref, step):
+    z, x = lax.div(ids_ref[0], 4), lax.rem(lax.div(ids_ref[0], 2), 2)
+    p = jnp.where(x == 0, z, 7 - z) + jnp.where(ids_ref[1] == 0, step, -step)
+    p = jnp.where(p < 0, p + 8, p)
+    p = jnp.where(p > 7, p - 8, p)
+    return jnp.where(p < 4, 2 * p, 15 - 2 * p)
+
+
+def project_kernel(steps, parts, carried, ids_ref, xa_ref, *refs):
+    count = len(steps)
     others, refs = refs[:parts], refs[parts:]
     weights, refs = refs[:count], refs[count:]
     before, outs = refs[:carried], refs[carried:]
     total = None
     for j in range(count):
         depth = weights[j].shape[0]
-        columns = pl.ds(pl.multiple_of(index_ref[j] * depth, depth), depth)
+        columns = pl.ds(pl.multiple_of(block_at(ids_ref, steps[j]) * depth, depth), depth)
         x = jnp.concatenate([ref[:, columns] for ref in (xa_ref, *others)], axis=0)
         part = jnp.dot(x, weights[j][...], preferred_element_type=F32)
         total = part if total is None else total + part
@@ -95,7 +105,7 @@
         at += ref.shape[0]
 
 
-def project(index, xa, others, weights, before=(), split=1):
+def project(ids, steps, xa, others, weights, before=(), split=1):
     rows = xa.shape[0]
     depth, feats = weights[0].shape
     outs = [jax.ShapeDtypeStruct((rows, feats), F32)]
@@ -103,7 +113,7 @@
     whole = pl.BlockSpec(memory_space=pltpu.VMEM)
     operands = [xa, *others, *weights, *before]
     return pl.pallas_call(
-        functools.partial(project_kernel, len(weights), len(others), len(before)),
+        functools.partial(project_kernel, steps, len(others), len(before)),
         in_specs=[pl.BlockSpec(memory_space=pltpu.SMEM)] + [whole] * len(operands),
         out_specs=[whole] * len(outs),
         out_shape=outs,
@@ -112,47 +122,101 @@
             4 * rows * depth * feats * len(weights), 2 * depth * feats * len(weights) + 4 * rows * 4096
         ),
         name="project",
-    )(index, *operands)
+    )(ids, *operands)
+
+
+def tables_kernel(ids_ref, own_ref, behind_ref, freq_ref, cos_ref, sin_ref, bias_ref):
+    own = own_ref[...]
+    rows = own.shape[1]
+    behind = jnp.where(ids_ref[0] > 0, behind_ref[:, rows - REACH :], -1)
+    window = jnp.concatenate([behind, own], axis=1)
+    shape = (REACH, 2 * REACH)
+    r, c = lax.broadcasted_iota(jnp.int32, shape, 0), lax.broadcasted_iota(jnp.int32, shape, 1)
+    freq = freq_ref[...]
+    for block in range(rows // REACH):
+        keys = window[:, block * REACH : (block + 2) * REACH]
+        mine = jnp.sum(jnp.where(c == r + REACH, keys, 0), axis=1, keepdims=True)
+        same = mine == keys
+        bias_ref[block] = jnp.where(same & (c <= r + REACH), 0.0, -1e30)
+        position = jnp.sum(jnp.where(same & (c < r + REACH), 1.0, 0.0), axis=1, keepdims=True)
+        angle = position * freq
+        at = slice(block * REACH, (block + 1) * REACH)
+        sign = jnp.where(lax.broadcasted_iota(jnp.int32, (REACH, HD), 1) < HD // 2, -1.0, 1.0)
+        cos_ref[at, :] = jnp.cos(angle)
+        sin_ref[at, :] = jnp.sin(angle) * sign
+
+
+def tables(ids, own, behind):
+    rows = own.shape[0]
+    half = np.arange(HD // 2, dtype=np.float32)
+    freq = np.float32(500000.0) ** (-(2.0 * half) / np.float32(HD))
+    freq = jnp.asarray(np.concatenate([freq, freq]).astype(np.float32).reshape(1, HD))
+    whole = pl.BlockSpec(memory_space=pltpu.VMEM)
+    return pl.pallas_call(
+        tables_kernel,
+        in_specs=[pl.BlockSpec(memory_space=pltpu.SMEM)] + [whole] * 3,
+        out_specs=[whole] * 3,
+        out_shape=[
+            jax.ShapeDtypeStruct((rows, HD), F32),
+            jax.ShapeDtypeStruct((rows, HD), F32),
+            jax.ShapeDtypeStruct((rows // REACH, REACH, 2 * REACH), F32),
+        ],
+        compiler_params=params(),
+        cost_estimate=cost(20 * rows * 2 * REACH, 16 * rows * REACH, 2 * rows * HD),
+        name="tables",
+    )(ids, own.reshape(1, rows), behind.reshape(1, rows), freq)
 
 
 def keys_kernel(a_ref, cos_ref, sin_ref, *refs):
     cos, sin = cos_ref[...], sin_ref[...]
-    others, out_ref = refs[:-1], refs[-1]
+    others, (out_ref, tail_ref) = refs[:-2], refs[-2:]
+    rows = out_ref.shape[0]
     for h in range(a_ref.shape[1] // HD):
         at = slice(h * HD, (h + 1) * HD)
         b = jnp.concatenate([ref[:, at] for ref in others], axis=0)
         raw = (a_ref[:, at] + b).astype(BF16).astype(F32)
-        out_ref[:, at] = (raw * cos + pltpu.roll(raw, HD // 2, 1) * sin).astype(BF16)
-
-
-def finish_keys(a, others, cos, sin):
-    rows, feats = a.shape
+        out = (raw * cos + pltpu.roll(raw, HD // 2, 1) * sin).astype(BF16)
+        out_ref[:, at] = out
+        tail_ref[:, at] = out[rows - REACH :]
+
+
+def values_kernel(a_ref, *refs):
+    others, (out_ref, tail_ref) = refs[:-2], refs[-2:]
+    rows = out_ref.shape[0]
+    out = (a_ref[...] + jnp.concatenate([ref[...] for ref in others], axis=0)).astype(BF16)
+    out_ref[...] = out
+    tail_ref[...] = out[rows - REACH :]
+
+
+def finish(kernel, name, *operands):
+    rows, feats = operands[0].shape
     return pl.pallas_call(
-        keys_kernel,
-        out_shape=jax.ShapeDtypeStruct((rows, feats), BF16),
+        kernel,
+        out_shape=[
+            jax.ShapeDtypeStruct((rows, feats), BF16),
+            jax.ShapeDtypeStruct((REACH, feats), BF16),
+        ],
         compiler_params=params(),
         cost_estimate=cost(6 * rows * feats, 10 * rows * feats),
-        name="keys",
-    )(a, cos, sin, *others)
-
-
-def scores_kernel(q_ref, ka_ref, kb_ref, sq_ref, sk_ref, out_ref):
-    rows, span = q_ref.shape[0], sk_ref.shape[1]
+        name=name,
+    )(*operands)
+
+
+def scores_kernel(q_ref, ka_ref, kb_ref, bias_ref, out_ref):
+    rows = q_ref.shape[0]
     keys = jnp.concatenate([ka_ref[...], kb_ref[...]], axis=0)
-    q_at = lax.broadcasted_iota(jnp.int32, (rows, span), 0) + (span - rows)
-    k_at = lax.broadcasted_iota(jnp.int32, (rows, span), 1)
-    allowed = (k_at <= q_at) & (sq_ref[...] == sk_ref[...])
+    bias = bias_ref[0]
     scale = 1.0 / HD**0.5
     for j in range(GROUP):
         q = q_ref[:, j * HD : (j + 1) * HD]
         s = lax.dot_general(q, keys, (((1,), (1,)), ((), ())), preferred_element_type=F32)
-        s = jnp.where(allowed, s * scale, -1e30)
+        s = s * scale + bias
         e = jnp.exp(s - jnp.max(s, axis=-1, keepdims=True))
         w = e * (1.0 / jnp.sum(e, axis=-1, keepdims=True))
         out_ref[0, j * rows : (j + 1) * rows, :] = w.astype(BF16)
 
 
-def softmax_weights(queries, block, keys_a, block_a, keys_b, block_b, segs_q, segs_k):
+def softmax_weights(queries, block, keys_a, block_a, keys_b, block_b, bias):
     rows = REACH
     heads = keys_a.shape[1] // HD
     return pl.pallas_call(
@@ -162,8 +226,7 @@
             pl.BlockSpec((rows, GROUP * HD), lambda h: (block, h)),
             pl.BlockSpec((rows, HD), lambda h: (block_a, h)),
             pl.BlockSpec((rows, HD), lambda h: (block_b, h)),
-            pl.BlockSpec((rows, 1), lambda h: (0, 0)),
-            pl.BlockSpec((1, 2 * rows), lambda h: (0, 0)),
+            pl.BlockSpec((1, rows, 2 * rows), lambda h: (block, 0, 0)),
         ],
         out_specs=pl.BlockSpec((1, GROUP * rows, 2 * rows), lambda h: (h, 0, 0)),
         out_shape=jax.ShapeDtypeStruct((heads, GROUP * rows, 2 * rows), BF16),
@@ -172,7 +235,7 @@
             4 * heads * GROUP * rows * rows * HD, 6 * rows * heads * GROUP * HD, 2 * heads * GROUP * rows * rows
         ),
         name="scores",
-    )(queries, keys_a, keys_b, segs_q, segs_k)
+    )(queries, keys_a, keys_b, bias)
 
 
 def context_kernel(p0_ref, p1_ref, prev_ref, own_ref, out_ref):
@@ -235,67 +298,41 @@
     def swap(value):
         return lax.ppermute(value, "dp", other_core)
 
-    me = lax.axis_index("dp")
-    chip, core = me // 2, me % 2
-    z, x = chip // 2, chip % 2
-    position = jnp.where(x == 0, z, 7 - z)
-    sign = jnp.where(lax.axis_index("groups") == 0, 1, -1)
-
-    def blocks(steps):
-        p = jnp.mod(position + sign * jnp.array(steps, jnp.int32), 8)
-        return jnp.where(p < 4, 2 * p, 2 * (7 - p) + 1).astype(jnp.int32)
-
-    rows = segment_ids.shape[0]
-    mine, theirs = normalise(core.reshape(1).astype(jnp.int32), hidden, norm_gain)
+    ids = jnp.stack([lax.axis_index("dp"), lax.axis_index("groups")]).astype(jnp.int32)
+    mine, theirs = normalise(ids, hidden, norm_gain)
     other = [swap(t) for t in theirs]
+    behind = from_behind(segment_ids, "dp", 1)
 
     k1, v1 = send(key_weight, key_way), send(value_weight, value_way)
     k1, v1, mine = after(k1, v1, mine)
     yk1 = send(k1, other_group)
     k2, v2 = send(k1, key_way), send(v1, value_way)
-    behind = from_behind(segment_ids[rows - REACH :], "dp", 1)
     k2, v2, yk1, behind = after(k2, v2, yk1, behind)
     yk2, yv2 = send(k2, other_group), send(v2, other_group)
     k3, v3 = send(k2, key_way), send(v2, value_way)
     yv1 = send(v1, other_group)
 
-    behind = jnp.where(me > 0, behind, -1)
-    window = jnp.concatenate([behind, segment_ids], axis=0)
-    index = jnp.arange(window.shape[0], dtype=jnp.int32)
-    earlier = (window[None, :] == segment_ids[:, None]) & (index[None, :] < index[REACH:, None])
-    positions = jnp.sum(earlier.astype(jnp.int32), axis=1).astype(F32)
-    half = HD // 2
-    freqs = 500000.0 ** (-(2.0 * jnp.arange(half, dtype=F32)) / HD)
-    angles = positions[:, None] * freqs[None, :]
-    cos, sin = jnp.cos(angles), jnp.sin(angles)
-    cos = jnp.concatenate([cos, cos], axis=1)
-    sin = jnp.concatenate([-sin, sin], axis=1)
-
-    key_part = project(blocks([0, -1, 1, -2]), mine, other, [key_weight, k1, yk1, k2])
-    k3, v3, yk2, key_part, cos, sin = after(k3, v3, yk2, key_part, cos, sin)
+    cos, sin, bias = tables(ids, segment_ids, behind)
+    key_part = project(ids, (0, -1, 1, -2), mine, other, [key_weight, k1, yk1, k2])
+    k3, v3, yk2, key_part, cos, sin, bias = after(k3, v3, yk2, key_part, cos, sin, bias)
     k4, k3b = send(k3, key_way), send(yk2, value_way)
     v4 = send(v3, value_way)
-    key_part = project(blocks([-3, 2]), mine, other, [k3, yk2], key_part)
-    value_part = project(blocks([0, 1, 2, 3]), mine, other, [value_weight, v1, v2, v3])
+    key_part = project(ids, (-3, 2), mine, other, [k3, yk2], key_part)
+    value_part = project(ids, (0, 1, 2, 3), mine, other, [value_weight, v1, v2, v3])
     yv2, key_part, value_part = after(yv2, key_part, value_part)
     v3b = send(yv2, key_way)
 
-    own_k, *other_k = project(blocks([-4, 3]), mine, other, [k4, k3b], key_part, 2)
-    keys = finish_keys(own_k, [swap(o) for o in other_k], cos, sin)
-    prev_keys = from_behind(keys[rows - REACH :], "dp", 1)
-    segs_q = segment_ids.reshape(rows, 1)
-    p1 = softmax_weights(
-        queries, 1, keys, 0, keys, 1, segs_q[REACH:], segment_ids.reshape(1, rows)
-    )
+    own_k, *other_k = project(ids, (-4, 3), mine, other, [k4, k3b], key_part, 2)
+    keys, tail = finish(keys_kernel, "keys", own_k, cos, sin, *[swap(o) for o in other_k])
+    prev_keys = from_behind(tail, "dp", 1)
+    p1 = softmax_weights(queries, 1, keys, 0, keys, 1, bias)
     value_part, p1 = after(value_part, p1)
     own_v, other_v = project(
-        blocks([-2, -1, 4, -3]), mine, other, [yv2, yv1, v4, v3b], value_part
-    )
-    values = (own_v + swap(other_v)).astype(BF16)
-    prev_values = from_behind(values[rows - REACH :], "dp", 1)
-    p0 = softmax_weights(
-        queries, 0, prev_keys, 0, keys, 0, segs_q[:REACH], window[: 2 * REACH].reshape(1, 2 * REACH)
-    )
+        ids, (-2, -1, 4, -3), mine, other, [yv2, yv1, v4, v3b], value_part
+    )
+    values, tail = finish(values_kernel, "values", own_v, swap(other_v))
+    prev_values = from_behind(tail, "dp", 1)
+    p0 = softmax_weights(queries, 0, prev_keys, 0, keys, 0, bias)
     return contexts(p0, p1, prev_values, values)
 
 

time: 94.8 us -> 88.9 us (0.938)
  waiting for transfers between devices: 20.8 us -> 43 us
  local copies, waits for them, and re-layouts: 17 us -> 2.94 us
  Pallas kernels: 28.7 us -> 20.6 us
  starting transfers between devices: 26 us -> 21.9 us
  other arithmetic: 1.07 us -> 0.08 us
    ppermute x14, waiting for transfers between devices: 15.1 us -> 35.2 us  [send(): return lax.ppermute(value, both, way)]
    unnamed x56 -> x12, local copies, waits for them, and re-layouts: 16 us -> 2.21 us
    pallas_call x6 -> x8, Pallas kernels: 15.2 us -> 9.35 us  [the longest x5 7.87 us: project(): pl.pallas_call(functools.partial(project_kernel, steps, len(others), len(...]
    pallas_call x1, Pallas kernels: 5.55 us -> 3.44 us  [normalise(): pl.pallas_call(norm_kernel, grid_spec=pltpu.PrefetchScalarGridSpec(num_sc...]
    ppermute x14, starting transfers between devices: 14.6 us -> 12.6 us  [send(): return lax.ppermute(value, both, way)]
    ppermute x3, waiting for transfers between devices: 4.54 us -> 6.36 us  [from_behind(): lax.ppermute(value, axis, [(source, source + steps) for source in range(i...]
    ppermute x3, starting transfers between devices: 7.65 us -> 6.22 us  [from_behind(): lax.ppermute(value, axis, [(source, source + steps) for source in range(i...]
  transfers between devices with their start and end apart: 24 -> 24, of which waited for: 11 -> 17; matrix products, arithmetic and copies ran while one was open for 2% -> 1% of each run, Pallas kernels for 24% -> 18%
where the time goes in v3:
time: 88.9 us; the launch traced here: 88.7 us
  waiting for transfers between devices  43 us (48%)
  starting transfers between devices  21.9 us (25%)
  Pallas kernels  20.6 us (23%)
  local copies, waits for them, and re-layouts  2.94 us (3%)
    ppermute x14, waiting for transfers between devices, send(): return lax.ppermute(value, both, way)  35.2 us
    ppermute x14, starting transfers between devices, send(): return lax.ppermute(value, both, way)  12.6 us
    pallas_call x5, Pallas kernels, project(): pl.pallas_call(functools.partial(project_kernel, steps, len(others), len(...  7.87 us
    ppermute x3, waiting for transfers between devices, from_behind(): lax.ppermute(value, axis, [(source, source + steps) for source in range(i...  6.36 us
    ppermute x3, starting transfers between devices, from_behind(): lax.ppermute(value, axis, [(source, source + steps) for source in range(i...  6.22 us
    pallas_call x2, Pallas kernels, softmax_weights(): pl.pallas_call(scores_kernel, grid=(heads,), in_specs=[pl.BlockSpec((rows...  4.77 us
    pallas_call x1, Pallas kernels, normalise(): pl.pallas_call(norm_kernel, grid_spec=pltpu.PrefetchScalarGridSpec(num_sc...  3.44 us
    ppermute x7, starting transfers between devices, swap(): return lax.ppermute(value, 'dp', other_core)  3.09 us
  transfers between devices with their start and end apart: 24, of which 17 were waited for; matrix products, arithmetic and copies ran while one was open for 1% of the time, Pallas kernels for 18%

profile of v3, /device:TPU:8, one launch (start us, length us, event | category | flops | bytes accessed | tf_op | source)
XLA Modules:
  0.0 88.7 jit_solution(6323291795801880647)
XLA Ops:
  0.0 1.6 %collective-permute-start = (bf16[512,512]{1,0:T(8,128)(2,1)}, bf16[512,512]{1,0:T(8,128)(2,1)S(1)}, u32[]{:S(2)}, u32[]{:S(2)}) collective-permute-start(bf16[512,512]{1,0:T(8,128)(2,1)} %refs_4_.2), channel_id=1, source_target_pairs={{0,4},{1,5},{4,8},{5,9},{8,12},{9,13},{12,14},{13,15},{14,10},{15,... | collective-permute-start | bytes 1572872 | tf_op jit(solution)/shard_map/ppermute | solution.py:296
  2.8 2.2 %copy-done.1 = bf16[256,8192]{1,0:T(8,128)(2,1)S(1)} copy-done((bf16[256,8192]{1,0:T(8,128)(2,1)S(1)}, bf16[256,8192]{1,0:T(8,128)(2,1)}, u32[]{:S(2)}) %copy-start.1) | copy-done | bytes 4194328
  5.0 3.4 %norm.1 = (bf16[256,4096]{1,0:T(8,128)(2,1)S(1)}, bf16[64,4096]{1,0:T(8,128)(2,1)S(1)}, bf16[64,4096]{1,0:T(8,128)(2,1)S(1)}, bf16[64,4096]{1,0:T(8,128)(2,1)S(1)}, bf16[64,4096]{1,0:T(8,128)(2,1)S(1)}) custom-call(s32[2]{0:T(128)S(1)} %pad_add_fusion.core_ref.ids_ref, bf16[256,8192]{1,0:T(8,128)(2,1)S(1)} %copy-done.1, bf16[1,8192]{1,0:T(2,128)(2,1)S(1)} %reshape.9.g_ref), custom_call_target="tpu_custom_call" | custom-call | flops 16777216 | bytes 8388608 | tf_op jit(solution)/shard_map/norm/pallas_call | solution.py:60
  8.5 5.4 %collective-permute-done.refs_5_ = bf16[512,512]{1,0:T(8,128)(2,1)S(1)} collective-permute-done((bf16[512,512]{1,0:T(8,128)(2,1)}, bf16[512,512]{1,0:T(8,128)(2,1)S(1)}, u32[]{:S(2)}, u32[]{:S(2)}) %collective-permute-start) | collective-permute-done | bytes 524320 | tf_op jit(solution)/shard_map/ppermute | solution.py:296
  13.9 1.3 %collective-permute-done.1.refs_5_ = bf16[512,512]{1,0:T(8,128)(2,1)S(1)} collective-permute-done((bf16[512,512]{1,0:T(8,128)(2,1)}, bf16[512,512]{1,0:T(8,128)(2,1)S(1)}, u32[]{:S(2)}, u32[]{:S(2)}) %collective-permute-start.1) | collective-permute-done | bytes 524320 | tf_op jit(solution)/shard_map/ppermute | solution.py:296
  15.2 1.6 %collective-permute-start.6 = (bf16[512,512]{1,0:T(8,128)(2,1)S(1)}, bf16[512,512]{1,0:T(8,128)(2,1)S(1)}, u32[]{:S(2)}, u32[]{:S(2)}) collective-permute-start(bf16[512,512]{1,0:T(8,128)(2,1)S(1)} %collective-permute-done.refs_5_), channel_id=1, source_target_pairs={{0,4},{1,5},{4,8},{5,9},{8,12},{9,13},{12,14},{13,15},{14,10},{15,... | collective-permute-start | bytes 1572872 | tf_op jit(solution)/shard_map/ppermute | solution.py:296
  17.2 1.9 %collective-permute-start.9 = (s32[256]{0:T(256)S(1)}, s32[256]{0:T(256)S(1)}, u32[]{:S(2)}, u32[]{:S(2)}) collective-permute-start(s32[256]{0:T(256)S(1)} %copy-done.4), channel_id=1, source_target_pairs={{0,1},{1,2},{2,3},{3,4},{4,5},{5,6},{6,7},{7,8},{8,9},{9,10},{10,1... | collective-permute-start | bytes 3080 | tf_op jit(solution)/shard_map/ppermute | solution.py:31
  19.6 2.4 %collective-permute-start.2 = (bf16[64,4096]{1,0:T(8,128)(2,1)S(1)}, bf16[64,4096]{1,0:T(8,128)(2,1)S(1)}, u32[]{:S(2)}, u32[]{:S(2)}) collective-permute-start(bf16[64,4096]{1,0:T(8,128)(2,1)S(1)} %get-tuple-element.53), channel_id=1, source_target_pairs={{0,1},{1,0},{2,3},{3,2},{4,5},{5,4},{6,7},{7,6},{8,9},{9,8},{10,11... | collective-permute-start | bytes 1572872 | tf_op jit(solution)/shard_map/ppermute | solution.py:299
  22.0 3.5 %collective-permute-done.9 = s32[256]{0:T(256)S(1)} collective-permute-done((s32[256]{0:T(256)S(1)}, s32[256]{0:T(256)S(1)}, u32[]{:S(2)}, u32[]{:S(2)}) %collective-permute-start.9) | collective-permute-done | bytes 1056 | tf_op jit(solution)/shard_map/ppermute | solution.py:31
  25.5 2.1 %collective-permute-done.6.refs_7_ = bf16[512,512]{1,0:T(8,128)(2,1)S(1)} collective-permute-done((bf16[512,512]{1,0:T(8,128)(2,1)S(1)}, bf16[512,512]{1,0:T(8,128)(2,1)S(1)}, u32[]{:S(2)}, u32[]{:S(2)}) %collective-permute-start.6) | collective-permute-done | bytes 524320 | tf_op jit(solution)/shard_map/ppermute | solution.py:296
  27.6 1.3 %collective-permute-done.7.refs_6_ = bf16[512,512]{1,0:T(8,128)(2,1)S(1)} collective-permute-done((bf16[512,512]{1,0:T(8,128)(2,1)S(1)}, bf16[512,512]{1,0:T(8,128)(2,1)S(1)}, u32[]{:S(2)}, u32[]{:S(2)}) %collective-permute-start.7) | collective-permute-done | bytes 524320 | tf_op jit(solution)/shard_map/ppermute | solution.py:296
  28.9 4.7 %collective-permute-done.8.refs_6_ = bf16[512,512]{1,0:T(8,128)(2,1)S(1)} collective-permute-done((bf16[512,512]{1,0:T(8,128)(2,1)S(1)}, bf16[512,512]{1,0:T(8,128)(2,1)S(1)}, u32[]{:S(2)}, u32[]{:S(2)}) %collective-permute-start.8) | collective-permute-done | bytes 524320 | tf_op jit(solution)/shard_map/ppermute | solution.py:296
  33.7 1.6 %collective-permute-start.10 = (bf16[512,512]{1,0:T(8,128)(2,1)S(1)}, bf16[512,512]{1,0:T(8,128)(2,1)S(1)}, u32[]{:S(2)}, u32[]{:S(2)}) collective-permute-start(bf16[512,512]{1,0:T(8,128)(2,1)S(1)} %collective-permute-done.6.refs_7_), channel_id=1, source_target_pairs={{0,4},{1,5},{4,8},{5,9},{8,12},{9,13},{12,14},{13,15},{14,10},{15,... | collective-permute-start | bytes 1572872 | tf_op jit(solution)/shard_map/ppermute | solution.py:296
  35.7 2.0 %collective-permute-start.15 = (bf16[512,512]{1,0:T(8,128)(2,1)S(1)}, bf16[512,512]{1,0:T(8,128)(2,1)S(1)}, u32[]{:S(2)}, u32[]{:S(2)}) collective-permute-start(bf16[512,512]{1,0:T(8,128)(2,1)S(1)} %collective-permute-done.7.refs_6_), channel_id=1, source_target_pairs={{0,16},{1,17},{2,18},{3,19},{4,20},{5,21},{6,22},{7,23},{8,24},{9,... | collective-permute-start | bytes 1572872 | tf_op jit(solution)/shard_map/ppermute | solution.py:296
  39.0 1.8 %project.5 = (f32[256,512]{1,0:T(8,128)S(1)}, f32[256,512]{1,0:T(8,128)S(1)}) custom-call(s32[2]{0:T(128)S(1)} %pad_add_fusion.core_ref.ids_ref, bf16[256,4096]{1,0:T(8,128)(2,1)S(1)} %get-tuple-element.52.xa_ref, bf16[64,4096]{1,0:T(8,128)(2,1)S(1)} %collective-permute-done.2.refs_0_, bf16[64,4096]{1,0:T(8,128)(2,1)S(1)} %collective-permute-done.3.refs_1_, ...), custom_call_target="tpu_custom_call" | custom-call | flops 1073741824 | bytes 6291456 | tf_op jit(solution)/shard_map/project/pallas_call | solution.py:115
  40.7 6.9 %collective-permute-done.10.refs_4_ = bf16[512,512]{1,0:T(8,128)(2,1)S(1)} collective-permute-done((bf16[512,512]{1,0:T(8,128)(2,1)S(1)}, bf16[512,512]{1,0:T(8,128)(2,1)S(1)}, u32[]{:S(2)}, u32[]{:S(2)}) %collective-permute-start.10) | collective-permute-done | bytes 524320 | tf_op jit(solution)/shard_map/ppermute | solution.py:296
  47.6 1.3 %collective-permute-done.11.refs_7_ = bf16[512,512]{1,0:T(8,128)(2,1)S(1)} collective-permute-done((bf16[512,512]{1,0:T(8,128)(2,1)S(1)}, bf16[512,512]{1,0:T(8,128)(2,1)S(1)}, u32[]{:S(2)}, u32[]{:S(2)}) %collective-permute-start.11) | collective-permute-done | bytes 524320 | tf_op jit(solution)/shard_map/ppermute | solution.py:296
  48.9 1.6 %collective-permute-done.12.refs_5_ = bf16[512,512]{1,0:T(8,128)(2,1)S(1)} collective-permute-done((bf16[512,512]{1,0:T(8,128)(2,1)S(1)}, bf16[512,512]{1,0:T(8,128)(2,1)S(1)}, u32[]{:S(2)}, u32[]{:S(2)}) %collective-permute-start.12) | collective-permute-done | bytes 524320 | tf_op jit(solution)/shard_map/ppermute | solution.py:296
  50.6 1.6 %collective-permute-start.13 = (bf16[512,512]{1,0:T(8,128)(2,1)S(1)}, bf16[512,512]{1,0:T(8,128)(2,1)S(1)}, u32[]{:S(2)}, u32[]{:S(2)}) collective-permute-start(bf16[512,512]{1,0:T(8,128)(2,1)S(1)} %collective-permute-done.10.refs_4_), channel_id=1, source_target_pairs={{0,4},{1,5},{4,8},{5,9},{8,12},{9,13},{12,14},{13,15},{14,10},{15,... | collective-permute-start | bytes 1572872 | tf_op jit(solution)/shard_map/ppermute | solution.py:296
  53.9 1.8 %project.7 = (f32[256,512]{1,0:T(8,128)S(1)}, f32[256,512]{1,0:T(8,128)S(1)}) custom-call(s32[2]{0:T(128)S(1)} %pad_add_fusion.core_ref.ids_ref, bf16[256,4096]{1,0:T(8,128)(2,1)S(1)} %get-tuple-element.52.xa_ref, bf16[64,4096]{1,0:T(8,128)(2,1)S(1)} %collective-permute-done.2.refs_0_, bf16[64,4096]{1,0:T(8,128)(2,1)S(1)} %collective-permute-done.3.refs_1_, ...), custom_call_target="tpu_custom_call" | custom-call | flops 1073741824 | bytes 6291456 | tf_op jit(solution)/shard_map/project/pallas_call | solution.py:115
  55.6 6.1 %collective-permute-done.15.refs_4_ = bf16[512,512]{1,0:T(8,128)(2,1)S(1)} collective-permute-done((bf16[512,512]{1,0:T(8,128)(2,1)S(1)}, bf16[512,512]{1,0:T(8,128)(2,1)S(1)}, u32[]{:S(2)}, u32[]{:S(2)}) %collective-permute-start.15) | collective-permute-done | bytes 524320 | tf_op jit(solution)/shard_map/ppermute | solution.py:296
  61.8 1.6 %collective-permute-start.21 = (bf16[512,512]{1,0:T(8,128)(2,1)S(1)}, bf16[512,512]{1,0:T(8,128)(2,1)S(1)}, u32[]{:S(2)}, u32[]{:S(2)}) collective-permute-start(bf16[512,512]{1,0:T(8,128)(2,1)S(1)} %collective-permute-done.15.refs_4_), channel_id=1, source_target_pairs={{0,4},{1,5},{4,8},{5,9},{8,12},{9,13},{12,14},{13,15},{14,10},{15,... | collective-permute-start | bytes 1572872 | tf_op jit(solution)/shard_map/ppermute | solution.py:296
  63.8 1.3 %project.8 = (f32[256,512]{1,0:T(8,128)S(1)}, f32[128,512]{1,0:T(8,128)S(1)}, f32[128,512]{1,0:T(8,128)S(1)}) custom-call(s32[2]{0:T(128)S(1)} %pad_add_fusion.core_ref.ids_ref, bf16[256,4096]{1,0:T(8,128)(2,1)S(1)} %get-tuple-element.52.xa_ref, bf16[64,4096]{1,0:T(8,128)(2,1)S(1)} %collective-permute-done.2.refs_0_, ...), custom_call_target="tpu_custom_call" | custom-call | flops 536870912 | bytes 5242880 | tf_op jit(solution)/shard_map/project/pallas_call | solution.py:115
  67.3 2.4 %scores.3.p1_ref = bf16[4,1024,256]{2,1,0:T(8,128)(2,1)S(1)} custom-call(bf16[256,4096]{1,0:T(8,128)(2,1)S(1)} %copy-done, bf16[256,512]{1,0:T(8,128)(2,1)S(1)} %get-tuple-element.85.kb_ref.ka_ref, bf16[256,512]{1,0:T(8,128)(2,1)S(1)} %get-tuple-element.85.kb_ref.ka_ref, f32[2,128,256]{2,1,0:T(8,128)S(1)} %get-tuple-element.86.bias_ref), custom_call_target="tpu_custom_call" | custom-call | flops 268435456 | bytes 3145728 | tf_op jit(solution)/shard_map/scores/pallas_call | solution.py:222
  69.7 1.9 %collective-permute-done.19.refs_5_ = bf16[512,512]{1,0:T(8,128)(2,1)S(1)} collective-permute-done((bf16[512,512]{1,0:T(8,128)(2,1)S(1)}, bf16[512,512]{1,0:T(8,128)(2,1)S(1)}, u32[]{:S(2)}, u32[]{:S(2)}) %collective-permute-start.19) | collective-permute-done | bytes 524320 | tf_op jit(solution)/shard_map/ppermute | solution.py:296
  71.6 1.4 %collective-permute-done.21.refs_7_ = bf16[512,512]{1,0:T(8,128)(2,1)S(1)} collective-permute-done((bf16[512,512]{1,0:T(8,128)(2,1)S(1)}, bf16[512,512]{1,0:T(8,128)(2,1)S(1)}, u32[]{:S(2)}, u32[]{:S(2)}) %collective-permute-start.21) | collective-permute-done | bytes 524320 | tf_op jit(solution)/shard_map/ppermute | solution.py:296
  74.1 1.8 %project.9 = (f32[256,512]{1,0:T(8,128)S(1)}, f32[256,512]{1,0:T(8,128)S(1)}) custom-call(s32[2]{0:T(128)S(1)} %pad_add_fusion.core_ref.ids_ref, bf16[256,4096]{1,0:T(8,128)(2,1)S(1)} %get-tuple-element.52.xa_ref, bf16[64,4096]{1,0:T(8,128)(2,1)S(1)} %collective-permute-done.2.refs_0_, bf16[64,4096]{1,0:T(8,128)(2,1)S(1)} %collective-permute-done.3.refs_1_, ...), custom_call_target="tpu_custom_call" | custom-call | flops 1073741824 | bytes 6291456 | tf_op jit(solution)/shard_map/project/pallas_call | solution.py:115
  76.0 2.4 %collective-permute-start.18 = (bf16[128,512]{1,0:T(8,128)(2,1)S(1)}, bf16[128,512]{1,0:T(8,128)(2,1)S(1)}, u32[]{:S(2)}, u32[]{:S(2)}) collective-permute-start(bf16[128,512]{1,0:T(8,128)(2,1)S(1)} %get-tuple-element.84), channel_id=1, source_target_pairs={{0,1},{1,2},{2,3},{3,4},{4,5},{5,6},{6,7},{7,8},{8,9},{9,10},{10,1... | collective-permute-start | bytes 393224 | tf_op jit(solution)/shard_map/ppermute | solution.py:31
  78.5 1.9 %collective-permute-start.23 = (bf16[128,512]{1,0:T(8,128)(2,1)S(1)}, bf16[128,512]{1,0:T(8,128)(2,1)S(1)}, u32[]{:S(2)}, u32[]{:S(2)}) collective-permute-start(bf16[128,512]{1,0:T(8,128)(2,1)S(1)} %get-tuple-element.95), channel_id=1, source_target_pairs={{0,1},{1,2},{2,3},{3,4},{4,5},{5,6},{6,7},{7,8},{8,9},{9,10},{10,1... | collective-permute-start | bytes 393224 | tf_op jit(solution)/shard_map/ppermute | solution.py:31
  80.4 2.8 %collective-permute-done.18.ka_ref = bf16[128,512]{1,0:T(8,128)(2,1)S(1)} collective-permute-done((bf16[128,512]{1,0:T(8,128)(2,1)S(1)}, bf16[128,512]{1,0:T(8,128)(2,1)S(1)}, u32[]{:S(2)}, u32[]{:S(2)}) %collective-permute-start.18) | collective-permute-done | bytes 131104 | tf_op jit(solution)/shard_map/ppermute | solution.py:31
  83.2 2.4 %scores.2.p0_ref = bf16[4,1024,256]{2,1,0:T(8,128)(2,1)S(1)} custom-call(bf16[256,4096]{1,0:T(8,128)(2,1)S(1)} %copy-done, bf16[128,512]{1,0:T(8,128)(2,1)S(1)} %collective-permute-done.18.ka_ref, bf16[256,512]{1,0:T(8,128)(2,1)S(1)} %get-tuple-element.85.kb_ref.ka_ref, f32[2,128,256]{2,1,0:T(8,128)S(1)} %get-tuple-element.86.bias_ref), custom_call_target="tpu_custom_call" | custom-call | flops 268435456 | bytes 3145728 | tf_op jit(solution)/shard_map/scores/pallas_call | solution.py:222
  85.7 3.0 %context.1 = bf16[256,4096]{1,0:T(8,128)(2,1)} custom-call(bf16[4,1024,256]{2,1,0:T(8,128)(2,1)S(1)} %scores.2.p0_ref, bf16[4,1024,256]{2,1,0:T(8,128)(2,1)S(1)} %scores.3.p1_ref, bf16[128,512]{1,0:T(8,128)(2,1)S(1)} %collective-permute-done.23.prev_ref, bf16[256,512]{1,0:T(8,128)(2,1)S(1)} %get-tuple-element.96.own_ref), custom_call_target="tpu_custom_call" | custom-call | flops 536870912 | bytes 6291456 | tf_op jit(solution)/shard_map/context/pallas_call | solution.py:254
  (42 shorter events, 9.6 us)
Async XLA Ops:
  0.0 13.9 %collective-permute-start = (bf16[512,512]{1,0:T(8,128)(2,1)}, bf16[512,512]{1,0:T(8,128)(2,1)S(1)}, u32[]{:S(2)}, u32[]{:S(2)}) collective-permute-start(bf16[512,512]{1,0:T(8,128)(2,1)} %refs_4_.2), channel_id=1, source_target_pairs={{0,4},{1,5},{4,8},{5,9},{8,12},{9,13},{12,14},{13,15},{14,10},{15,... | collective-permute-start | bytes 1572872 | tf_op jit(solution)/shard_map/ppermute | solution.py:296
  1.6 13.6 %collective-permute-start.1 = (bf16[512,512]{1,0:T(8,128)(2,1)}, bf16[512,512]{1,0:T(8,128)(2,1)S(1)}, u32[]{:S(2)}, u32[]{:S(2)}) collective-permute-start(bf16[512,512]{1,0:T(8,128)(2,1)} %refs_4_.3), channel_id=1, source_target_pairs={{0,2},{1,3},{4,0},{5,1},{8,4},{9,5},{12,8},{13,9},{14,12},{15,13},... | collective-permute-start | bytes 1572872 | tf_op jit(solution)/shard_map/ppermute | solution.py:296
  2.8 2.2 %copy-start.1 = (bf16[256,8192]{1,0:T(8,128)(2,1)S(1)}, bf16[256,8192]{1,0:T(8,128)(2,1)}, u32[]{:S(2)}) copy-start(bf16[256,8192]{1,0:T(8,128)(2,1)} %h_ref.1) | copy-start | bytes 12582916
  5.0 12.2 %copy-start.4 = (s32[256]{0:T(256)S(1)}, s32[256]{0:T(256)}, u32[]{:S(2)}) copy-start(s32[256]{0:T(256)} %param.12) | copy-start | bytes 3076
  5.0 32.7 %copy-start.5 = (f32[1,128]{1,0:T(1,128)S(1)}, f32[1,128]{1,0:T(1,128)}, u32[]{:S(2)}) copy-start(f32[1,128]{1,0:T(1,128)} %constant.11.clone.freq_ref) | copy-start | bytes 1540
  5.0 33.9 %copy-start.2 = (bf16[512,512]{1,0:T(8,128)(2,1)S(1)}, bf16[512,512]{1,0:T(8,128)(2,1)}, u32[]{:S(2)}) copy-start(bf16[512,512]{1,0:T(8,128)(2,1)} %refs_4_.2) | copy-start | bytes 1572868
  15.2 12.5 %collective-permute-start.6 = (bf16[512,512]{1,0:T(8,128)(2,1)S(1)}, bf16[512,512]{1,0:T(8,128)(2,1)S(1)}, u32[]{:S(2)}, u32[]{:S(2)}) collective-permute-start(bf16[512,512]{1,0:T(8,128)(2,1)S(1)} %collective-permute-done.refs_5_), channel_id=1, source_target_pairs={{0,4},{1,5},{4,8},{5,9},{8,12},{9,13},{12,14},{13,15},{14,10},{15,... | collective-permute-start | bytes 1572872 | tf_op jit(solution)/shard_map/ppermute | solution.py:296
  16.7 12.2 %collective-permute-start.7 = (bf16[512,512]{1,0:T(8,128)(2,1)S(1)}, bf16[512,512]{1,0:T(8,128)(2,1)S(1)}, u32[]{:S(2)}, u32[]{:S(2)}) collective-permute-start(bf16[512,512]{1,0:T(8,128)(2,1)S(1)} %collective-permute-done.1.refs_5_), channel_id=1, source_target_pairs={{0,2},{1,3},{4,0},{5,1},{8,4},{9,5},{12,8},{13,9},{14,12},{15,13},... | collective-permute-start | bytes 1572872 | tf_op jit(solution)/shard_map/ppermute | solution.py:296
  17.2 8.3 %collective-permute-start.9 = (s32[256]{0:T(256)S(1)}, s32[256]{0:T(256)S(1)}, u32[]{:S(2)}, u32[]{:S(2)}) collective-permute-start(s32[256]{0:T(256)S(1)} %copy-done.4), channel_id=1, source_target_pairs={{0,1},{1,2},{2,3},{3,4},{4,5},{5,6},{6,7},{7,8},{8,9},{9,10},{10,1... | collective-permute-start | bytes 3080 | tf_op jit(solution)/shard_map/ppermute | solution.py:31
  19.1 14.5 %collective-permute-start.8 = (bf16[512,512]{1,0:T(8,128)(2,1)S(1)}, bf16[512,512]{1,0:T(8,128)(2,1)S(1)}, u32[]{:S(2)}, u32[]{:S(2)}) collective-permute-start(bf16[512,512]{1,0:T(8,128)(2,1)S(1)} %collective-permute-done.refs_5_), channel_id=1, source_target_pairs={{0,16},{1,17},{2,18},{3,19},{4,20},{5,21},{6,22},{7,23},{8,24},{9,... | collective-permute-start | bytes 1572872 | tf_op jit(solution)/shard_map/ppermute | solution.py:296
  19.6 15.7 %collective-permute-start.2 = (bf16[64,4096]{1,0:T(8,128)(2,1)S(1)}, bf16[64,4096]{1,0:T(8,128)(2,1)S(1)}, u32[]{:S(2)}, u32[]{:S(2)}) collective-permute-start(bf16[64,4096]{1,0:T(8,128)(2,1)S(1)} %get-tuple-element.53), channel_id=1, source_target_pairs={{0,1},{1,0},{2,3},{3,2},{4,5},{5,4},{6,7},{7,6},{8,9},{9,8},{10,11... | collective-permute-start | bytes 1572872 | tf_op jit(solution)/shard_map/ppermute | solution.py:299
  25.5 10.2 %collective-permute-start.3 = (bf16[64,4096]{1,0:T(8,128)(2,1)S(1)}, bf16[64,4096]{1,0:T(8,128)(2,1)S(1)}, u32[]{:S(2)}, u32[]{:S(2)}) collective-permute-start(bf16[64,4096]{1,0:T(8,128)(2,1)S(1)} %get-tuple-element.54), channel_id=1, source_target_pairs={{0,1},{1,0},{2,3},{3,2},{4,5},{5,4},{6,7},{7,6},{8,9},{9,8},{10,11... | collective-permute-start | bytes 1572872 | tf_op jit(solution)/shard_map/ppermute | solution.py:299
  27.6 8.1 %collective-permute-start.4 = (bf16[64,4096]{1,0:T(8,128)(2,1)S(1)}, bf16[64,4096]{1,0:T(8,128)(2,1)S(1)}, u32[]{:S(2)}, u32[]{:S(2)}) collective-permute-start(bf16[64,4096]{1,0:T(8,128)(2,1)S(1)} %get-tuple-element.55), channel_id=1, source_target_pairs={{0,1},{1,0},{2,3},{3,2},{4,5},{5,4},{6,7},{7,6},{8,9},{9,8},{10,11... | collective-permute-start | bytes 1572872 | tf_op jit(solution)/shard_map/ppermute | solution.py:299
  28.9 10.0 %collective-permute-start.5 = (bf16[64,4096]{1,0:T(8,128)(2,1)S(1)}, bf16[64,4096]{1,0:T(8,128)(2,1)S(1)}, u32[]{:S(2)}, u32[]{:S(2)}) collective-permute-start(bf16[64,4096]{1,0:T(8,128)(2,1)S(1)} %get-tuple-element.56), channel_id=1, source_target_pairs={{0,1},{1,0},{2,3},{3,2},{4,5},{5,4},{6,7},{7,6},{8,9},{9,8},{10,11... | collective-permute-start | bytes 1572872 | tf_op jit(solution)/shard_map/ppermute | solution.py:299
  33.7 14.0 %collective-permute-start.10 = (bf16[512,512]{1,0:T(8,128)(2,1)S(1)}, bf16[512,512]{1,0:T(8,128)(2,1)S(1)}, u32[]{:S(2)}, u32[]{:S(2)}) collective-permute-start(bf16[512,512]{1,0:T(8,128)(2,1)S(1)} %collective-permute-done.6.refs_7_), channel_id=1, source_target_pairs={{0,4},{1,5},{4,8},{5,9},{8,12},{9,13},{12,14},{13,15},{14,10},{15,... | collective-permute-start | bytes 1572872 | tf_op jit(solution)/shard_map/ppermute | solution.py:296
  35.2 13.7 %collective-permute-start.11 = (bf16[512,512]{1,0:T(8,128)(2,1)S(1)}, bf16[512,512]{1,0:T(8,128)(2,1)S(1)}, u32[]{:S(2)}, u32[]{:S(2)}) collective-permute-start(bf16[512,512]{1,0:T(8,128)(2,1)S(1)} %collective-permute-done.7.refs_6_), channel_id=1, source_target_pairs={{0,2},{1,3},{4,0},{5,1},{8,4},{9,5},{12,8},{13,9},{14,12},{15,13},... | collective-permute-start | bytes 1572872 | tf_op jit(solution)/shard_map/ppermute | solution.py:296
  35.7 14.9 %collective-permute-start.12 = (bf16[512,512]{1,0:T(8,128)(2,1)S(1)}, bf16[512,512]{1,0:T(8,128)(2,1)S(1)}, u32[]{:S(2)}, u32[]{:S(2)}) collective-permute-start(bf16[512,512]{1,0:T(8,128)(2,1)S(1)} %collective-permute-done.6.refs_7_), channel_id=1, source_target_pairs={{0,16},{1,17},{2,18},{3,19},{4,20},{5,21},{6,22},{7,23},{8,24},{9,... | collective-permute-start | bytes 1572872 | tf_op jit(solution)/shard_map/ppermute | solution.py:296
  35.7 26.1 %collective-permute-start.15 = (bf16[512,512]{1,0:T(8,128)(2,1)S(1)}, bf16[512,512]{1,0:T(8,128)(2,1)S(1)}, u32[]{:S(2)}, u32[]{:S(2)}) collective-permute-start(bf16[512,512]{1,0:T(8,128)(2,1)S(1)} %collective-permute-done.7.refs_6_), channel_id=1, source_target_pairs={{0,16},{1,17},{2,18},{3,19},{4,20},{5,21},{6,22},{7,23},{8,24},{9,... | collective-permute-start | bytes 1572872 | tf_op jit(solution)/shard_map/ppermute | solution.py:296
  50.5 3.3 %copy-start.3 = (bf16[512,512]{1,0:T(8,128)(2,1)S(1)}, bf16[512,512]{1,0:T(8,128)(2,1)}, u32[]{:S(2)}) copy-start(bf16[512,512]{1,0:T(8,128)(2,1)} %refs_4_.3) | copy-start | bytes 1572868
  50.6 13.3 %collective-permute-start.13 = (bf16[512,512]{1,0:T(8,128)(2,1)S(1)}, bf16[512,512]{1,0:T(8,128)(2,1)S(1)}, u32[]{:S(2)}, u32[]{:S(2)}) collective-permute-start(bf16[512,512]{1,0:T(8,128)(2,1)S(1)} %collective-permute-done.10.refs_4_), channel_id=1, source_target_pairs={{0,4},{1,5},{4,8},{5,9},{8,12},{9,13},{12,14},{13,15},{14,10},{15,... | collective-permute-start | bytes 1572872 | tf_op jit(solution)/shard_map/ppermute | solution.py:296
  52.1 11.7 %collective-permute-start.14 = (bf16[512,512]{1,0:T(8,128)(2,1)S(1)}, bf16[512,512]{1,0:T(8,128)(2,1)S(1)}, u32[]{:S(2)}, u32[]{:S(2)}) collective-permute-start(bf16[512,512]{1,0:T(8,128)(2,1)S(1)} %collective-permute-done.12.refs_5_), channel_id=1, source_target_pairs={{0,2},{1,3},{4,0},{5,1},{8,4},{9,5},{12,8},{13,9},{14,12},{15,13},... | collective-permute-start | bytes 1572872 | tf_op jit(solution)/shard_map/ppermute | solution.py:296
  52.6 19.0 %collective-permute-start.19 = (bf16[512,512]{1,0:T(8,128)(2,1)S(1)}, bf16[512,512]{1,0:T(8,128)(2,1)S(1)}, u32[]{:S(2)}, u32[]{:S(2)}) collective-permute-start(bf16[512,512]{1,0:T(8,128)(2,1)S(1)} %collective-permute-done.1.refs_5_), channel_id=1, source_target_pairs={{0,16},{1,17},{2,18},{3,19},{4,20},{5,21},{6,22},{7,23},{8,24},{9,... | collective-permute-start | bytes 1572872 | tf_op jit(solution)/shard_map/ppermute | solution.py:296
  61.8 11.2 %collective-permute-start.21 = (bf16[512,512]{1,0:T(8,128)(2,1)S(1)}, bf16[512,512]{1,0:T(8,128)(2,1)S(1)}, u32[]{:S(2)}, u32[]{:S(2)}) collective-permute-start(bf16[512,512]{1,0:T(8,128)(2,1)S(1)} %collective-permute-done.15.refs_4_), channel_id=1, source_target_pairs={{0,4},{1,5},{4,8},{5,9},{8,12},{9,13},{12,14},{13,15},{14,10},{15,... | collective-permute-start | bytes 1572872 | tf_op jit(solution)/shard_map/ppermute | solution.py:296
  63.4 10.8 %collective-permute-start.20 = (bf16[512,512]{1,0:T(8,128)(2,1)S(1)}, bf16[512,512]{1,0:T(8,128)(2,1)S(1)}, u32[]{:S(2)}, u32[]{:S(2)}) collective-permute-start(bf16[512,512]{1,0:T(8,128)(2,1)S(1)} %collective-permute-done.11.refs_7_), channel_id=1, source_target_pairs={{0,2},{1,3},{4,0},{5,1},{8,4},{9,5},{12,8},{13,9},{14,12},{15,13},... | collective-permute-start | bytes 1572872 | tf_op jit(solution)/shard_map/ppermute | solution.py:296
  63.8 3.5 %copy-start = (bf16[256,4096]{1,0:T(8,128)(2,1)S(1)}, bf16[256,4096]{1,0:T(8,128)(2,1)}, u32[]{:S(2)}) copy-start(bf16[256,4096]{1,0:T(8,128)(2,1)} %q_ref.3) | copy-start | bytes 6291460
  65.1 1.6 %collective-permute-start.16 = (f32[128,512]{1,0:T(8,128)S(1)}, f32[128,512]{1,0:T(8,128)S(1)}, u32[]{:S(2)}, u32[]{:S(2)}) collective-permute-start(f32[128,512]{1,0:T(8,128)S(1)} %get-tuple-element.82), channel_id=1, source_target_pairs={{0,1},{1,0},{2,3},{3,2},{4,5},{5,4},{6,7},{7,6},{8,9},{9,8},{10,11... | collective-permute-start | bytes 786440 | tf_op jit(solution)/shard_map/ppermute | solution.py:299
  65.2 1.9 %collective-permute-start.17 = (f32[128,512]{1,0:T(8,128)S(1)}, f32[128,512]{1,0:T(8,128)S(1)}, u32[]{:S(2)}, u32[]{:S(2)}) collective-permute-start(f32[128,512]{1,0:T(8,128)S(1)} %get-tuple-element.83), channel_id=1, source_target_pairs={{0,1},{1,0},{2,3},{3,2},{4,5},{5,4},{6,7},{7,6},{8,9},{9,8},{10,11... | collective-permute-start | bytes 786440 | tf_op jit(solution)/shard_map/ppermute | solution.py:299
  75.9 2.5 %collective-permute-start.22 = (f32[256,512]{1,0:T(8,128)S(1)}, f32[256,512]{1,0:T(8,128)S(1)}, u32[]{:S(2)}, u32[]{:S(2)}) collective-permute-start(f32[256,512]{1,0:T(8,128)S(1)} %get-tuple-element.94), channel_id=1, source_target_pairs={{0,1},{1,0},{2,3},{3,2},{4,5},{5,4},{6,7},{7,6},{8,9},{9,8},{10,11... | collective-permute-start | bytes 1572872 | tf_op jit(solution)/shard_map/ppermute | solution.py:299
  76.0 7.2 %collective-permute-start.18 = (bf16[128,512]{1,0:T(8,128)(2,1)S(1)}, bf16[128,512]{1,0:T(8,128)(2,1)S(1)}, u32[]{:S(2)}, u32[]{:S(2)}) collective-permute-start(bf16[128,512]{1,0:T(8,128)(2,1)S(1)} %get-tuple-element.84), channel_id=1, source_target_pairs={{0,1},{1,2},{2,3},{3,4},{4,5},{5,6},{6,7},{7,8},{8,9},{9,10},{10,1... | collective-permute-start | bytes 393224 | tf_op jit(solution)/shard_map/ppermute | solution.py:31
  78.5 7.2 %collective-permute-start.23 = (bf16[128,512]{1,0:T(8,128)(2,1)S(1)}, bf16[128,512]{1,0:T(8,128)(2,1)S(1)}, u32[]{:S(2)}, u32[]{:S(2)}) collective-permute-start(bf16[128,512]{1,0:T(8,128)(2,1)S(1)} %get-tuple-element.95), channel_id=1, source_target_pairs={{0,1},{1,2},{2,3},{3,4},{4,5},{5,6},{6,7},{7,8},{8,9},{9,10},{10,1... | collective-permute-start | bytes 393224 | tf_op jit(solution)/shard_map/ppermute | solution.py:31

commit v4 on v3

--- a/solution.py
+++ b/solution.py
@@ -45,18 +45,21 @@
         n_hi = h_ref[:, hi].astype(F32) * scale * g_ref[:, hi].astype(F32)
         out = slice(b * half, (b + 1) * half)
         mine_ref[:, out] = jnp.where(first, n_lo, n_hi).astype(BF16)
-        for step, theirs_ref in enumerate(theirs):
-
-            @pl.when(pl.program_id(0) == step)
+        other = jnp.where(first, n_hi, n_lo).astype(BF16)
+        for part, theirs_ref in enumerate(theirs):
+
+            @pl.when(pl.program_id(0) // (pl.num_programs(0) // len(theirs)) == part)
             def _():
-                theirs_ref[:, out] = jnp.where(first, n_hi, n_lo).astype(BF16)
+                theirs_ref[:, out] = other
 
 
 def normalise(core, hidden, gain):
     rows, width = hidden.shape
     step = 64
     mine = jax.ShapeDtypeStruct((rows, width // 2), BF16)
-    theirs = jax.ShapeDtypeStruct((step, width // 2), BF16)
+    parts = 2
+    theirs = jax.ShapeDtypeStruct((rows // parts, width // 2), BF16)
+    last = rows // step // parts - 1
     mine, *theirs = pl.pallas_call(
         norm_kernel,
         grid_spec=pltpu.PrefetchScalarGridSpec(
@@ -67,9 +70,15 @@
                 pl.BlockSpec((1, width), lambda i, c: (0, 0)),
             ],
             out_specs=[pl.BlockSpec((step, width // 2), lambda i, c: (i, 0))]
-            + [pl.BlockSpec((step, width // 2), lambda i, c: (0, 0))] * (rows // step),
+            + [
+                pl.BlockSpec(
+                    (step, width // 2),
+                    functools.partial(lambda p, i, c: (jnp.clip(i - p * (last + 1), 0, last), 0), p),
+                )
+                for p in range(parts)
+            ],
         ),
-        out_shape=[mine] + [theirs] * (rows // step),
+        out_shape=[mine] + [theirs] * parts,
         compiler_params=params(),
         cost_estimate=cost(8 * rows * width, 4 * rows * width),
         name="norm",
@@ -238,34 +247,35 @@
     )(queries, keys_a, keys_b, bias)
 
 
-def context_kernel(p0_ref, p1_ref, prev_ref, own_ref, out_ref):
-    rows = prev_ref.shape[0]
-    first = jnp.concatenate([prev_ref[...], own_ref[:rows, :]], axis=0)
-    for block, (p_ref, values) in enumerate(((p0_ref, first), (p1_ref, own_ref[...]))):
-        c = jnp.dot(p_ref[0], values, preferred_element_type=F32).astype(BF16)
-        for j in range(GROUP):
-            out_ref[block * rows : (block + 1) * rows, j * HD : (j + 1) * HD] = c[j * rows : (j + 1) * rows]
-
-
-def contexts(p0, p1, prev, own):
-    heads, _, span = p0.shape
-    rows = prev.shape[0]
-    weights = pl.BlockSpec((1, GROUP * rows, span), lambda h: (h, 0, 0))
+def context_kernel(p_ref, va_ref, vb_ref, *refs):
+    out_ref = refs[-1]
+    rows = va_ref.shape[0]
+    values = jnp.concatenate([va_ref[...], vb_ref[...]], axis=0)
+    c = jnp.dot(p_ref[0], values, preferred_element_type=F32).astype(BF16)
+    for j in range(GROUP):
+        out_ref[:, j * HD : (j + 1) * HD] = c[j * rows : (j + 1) * rows]
+
+
+def contexts(block, weights, values_a, block_a, values_b, block_b, out=None):
+    heads, _, span = weights.shape
+    rows = REACH
+    more = () if out is None else (out,)
     return pl.pallas_call(
         context_kernel,
         grid=(heads,),
         in_specs=[
-            weights,
-            weights,
-            pl.BlockSpec((rows, HD), lambda h: (0, h)),
-            pl.BlockSpec((2 * rows, HD), lambda h: (0, h)),
-        ],
-        out_specs=pl.BlockSpec((2 * rows, GROUP * HD), lambda h: (0, h)),
+            pl.BlockSpec((1, GROUP * rows, span), lambda h: (h, 0, 0)),
+            pl.BlockSpec((rows, HD), lambda h: (block_a, h)),
+            pl.BlockSpec((rows, HD), lambda h: (block_b, h)),
+        ]
+        + [pl.BlockSpec(memory_space=pl.ANY)] * len(more),
+        out_specs=pl.BlockSpec((rows, GROUP * HD), lambda h: (block, h)),
         out_shape=jax.ShapeDtypeStruct((2 * rows, heads * GROUP * HD), BF16),
-        compiler_params=params(),
-        cost_estimate=cost(4 * heads * GROUP * rows * span * HD, 12 * rows * heads * GROUP * HD),
+        input_output_aliases={3: 0} if more else {},
+        compiler_params=params(),
+        cost_estimate=cost(2 * heads * GROUP * rows * span * HD, 6 * rows * heads * GROUP * HD),
         name="context",
-    )(p0, p1, prev, own)
+    )(weights, values_a, values_b, *more)
 
 
 def after(*values):
@@ -301,39 +311,40 @@
     ids = jnp.stack([lax.axis_index("dp"), lax.axis_index("groups")]).astype(jnp.int32)
     mine, theirs = normalise(ids, hidden, norm_gain)
     other = [swap(t) for t in theirs]
-    behind = from_behind(segment_ids, "dp", 1)
-
     k1, v1 = send(key_weight, key_way), send(value_weight, value_way)
     k1, v1, mine = after(k1, v1, mine)
     yk1 = send(k1, other_group)
     k2, v2 = send(k1, key_way), send(v1, value_way)
-    k2, v2, yk1, behind = after(k2, v2, yk1, behind)
+    k2, v2, yk1 = after(k2, v2, yk1)
     yk2, yv2 = send(k2, other_group), send(v2, other_group)
     k3, v3 = send(k2, key_way), send(v2, value_way)
     yv1 = send(v1, other_group)
 
-    cos, sin, bias = tables(ids, segment_ids, behind)
+    behind = from_behind(segment_ids, "dp", 1)
     key_part = project(ids, (0, -1, 1, -2), mine, other, [key_weight, k1, yk1, k2])
-    k3, v3, yk2, key_part, cos, sin, bias = after(k3, v3, yk2, key_part, cos, sin, bias)
+    k3, v3, yk2, key_part, behind = after(k3, v3, yk2, key_part, behind)
     k4, k3b = send(k3, key_way), send(yk2, value_way)
     v4 = send(v3, value_way)
     key_part = project(ids, (-3, 2), mine, other, [k3, yk2], key_part)
     value_part = project(ids, (0, 1, 2, 3), mine, other, [value_weight, v1, v2, v3])
-    yv2, key_part, value_part = after(yv2, key_part, value_part)
+    cos, sin, bias = tables(ids, segment_ids, behind)
+    yv2, key_part, value_part, cos, sin, bias = after(yv2, key_part, value_part, cos, sin, bias)
     v3b = send(yv2, key_way)
 
     own_k, *other_k = project(ids, (-4, 3), mine, other, [k4, k3b], key_part, 2)
     keys, tail = finish(keys_kernel, "keys", own_k, cos, sin, *[swap(o) for o in other_k])
     prev_keys = from_behind(tail, "dp", 1)
     p1 = softmax_weights(queries, 1, keys, 0, keys, 1, bias)
-    value_part, p1 = after(value_part, p1)
+    value_part, p1, prev_keys = after(value_part, p1, prev_keys)
     own_v, other_v = project(
         ids, (-2, -1, 4, -3), mine, other, [yv2, yv1, v4, v3b], value_part
     )
-    values, tail = finish(values_kernel, "values", own_v, swap(other_v))
+    p0 = softmax_weights(queries, 0, prev_keys, 0, keys, 0, bias)
+    other_v, p0 = after(swap(other_v), p0)
+    values, tail = finish(values_kernel, "values", own_v, other_v)
     prev_values = from_behind(tail, "dp", 1)
-    p0 = softmax_weights(queries, 0, prev_keys, 0, keys, 0, bias)
-    return contexts(p0, p1, prev_values, values)
+    later = contexts(1, p1, values, 0, values, 1)
+    return contexts(0, p0, prev_values, 0, values, 0, later)
 
 
 def rotary(block, positions):

time: 88.9 us -> 83.5 us (0.939)
  the two profiles are of different devices: /device:TPU:8 before, /device:TPU:24 now
where the time goes in v4:
time: 83.5 us; the launch traced here: 83.3 us
  waiting for transfers between devices  36.5 us (44%)
  Pallas kernels  22.1 us (26%)
  starting transfers between devices  21.4 us (26%)
  local copies, waits for them, and re-layouts  2.94 us (4%)
    ppermute x14, waiting for transfers between devices, send(): return lax.ppermute(value, both, way)  28.4 us
    ppermute x14, starting transfers between devices, send(): return lax.ppermute(value, both, way)  13.9 us
    pallas_call x5, Pallas kernels, project(): pl.pallas_call(functools.partial(project_kernel, steps, len(others), len(...  7.86 us
    ppermute x3, waiting for transfers between devices, from_behind(): lax.ppermute(value, axis, [(source, source + steps) for source in range(i...  6.72 us
    ppermute x3, starting transfers between devices, from_behind(): lax.ppermute(value, axis, [(source, source + steps) for source in range(i...  6.35 us
    pallas_call x2, Pallas kernels, softmax_weights(): pl.pallas_call(scores_kernel, grid=(heads,), in_specs=[pl.BlockSpec((rows...  4.78 us
    pallas_call x2, Pallas kernels, contexts(): pl.pallas_call(context_kernel, grid=(heads,), in_specs=[pl.BlockSpec((1,...  4.75 us
    pallas_call x1, Pallas kernels, normalise(): pl.pallas_call(norm_kernel, grid_spec=pltpu.PrefetchScalarGridSpec(num_sc...  3.22 us
  transfers between devices with their start and end apart: 22, of which 14 were waited for; matrix products, arithmetic and copies ran while one was open for 1% of the time, Pallas kernels for 21%

profile of v4, /device:TPU:24, one launch (start us, length us, event | category | flops | bytes accessed | tf_op | source)
XLA Modules:
  0.0 83.3 jit_solution(2997945381190444954)
XLA Ops:
  0.0 1.5 %collective-permute-start = (bf16[512,512]{1,0:T(8,128)(2,1)}, bf16[512,512]{1,0:T(8,128)(2,1)S(1)}, u32[]{:S(2)}, u32[]{:S(2)}) collective-permute-start(bf16[512,512]{1,0:T(8,128)(2,1)} %refs_2_.2), channel_id=1, source_target_pairs={{0,4},{1,5},{4,8},{5,9},{8,12},{9,13},{12,14},{13,15},{14,10},{15,... | collective-permute-start | bytes 1572872 | tf_op jit(solution)/shard_map/ppermute | solution.py:306
  2.8 2.2 %copy-done.1 = bf16[256,8192]{1,0:T(8,128)(2,1)S(1)} copy-done((bf16[256,8192]{1,0:T(8,128)(2,1)S(1)}, bf16[256,8192]{1,0:T(8,128)(2,1)}, u32[]{:S(2)}) %copy-start.1) | copy-done | bytes 4194328
  5.0 3.2 %norm.1 = (bf16[256,4096]{1,0:T(8,128)(2,1)S(1)}, bf16[128,4096]{1,0:T(8,128)(2,1)S(1)}, bf16[128,4096]{1,0:T(8,128)(2,1)S(1)}) custom-call(s32[2]{0:T(128)S(1)} %pad_add_fusion.core_ref.ids_ref, bf16[256,8192]{1,0:T(8,128)(2,1)S(1)} %copy-done.1, bf16[1,8192]{1,0:T(2,128)(2,1)S(1)} %reshape.9.g_ref), custom_call_target="tpu_custom_call" | custom-call | flops 16777216 | bytes 8388608 | tf_op jit(solution)/shard_map/norm/pallas_call | solution.py:63
  8.8 5.0 %collective-permute-done.refs_3_ = bf16[512,512]{1,0:T(8,128)(2,1)S(1)} collective-permute-done((bf16[512,512]{1,0:T(8,128)(2,1)}, bf16[512,512]{1,0:T(8,128)(2,1)S(1)}, u32[]{:S(2)}, u32[]{:S(2)}) %collective-permute-start) | collective-permute-done | bytes 524320 | tf_op jit(solution)/shard_map/ppermute | solution.py:306
  13.9 1.2 %collective-permute-done.1.refs_3_ = bf16[512,512]{1,0:T(8,128)(2,1)S(1)} collective-permute-done((bf16[512,512]{1,0:T(8,128)(2,1)}, bf16[512,512]{1,0:T(8,128)(2,1)S(1)}, u32[]{:S(2)}, u32[]{:S(2)}) %collective-permute-start.1) | collective-permute-done | bytes 524320 | tf_op jit(solution)/shard_map/ppermute | solution.py:306
  15.6 1.6 %collective-permute-start.4 = (bf16[512,512]{1,0:T(8,128)(2,1)S(1)}, bf16[512,512]{1,0:T(8,128)(2,1)S(1)}, u32[]{:S(2)}, u32[]{:S(2)}) collective-permute-start(bf16[512,512]{1,0:T(8,128)(2,1)S(1)} %collective-permute-done.refs_3_), channel_id=1, source_target_pairs={{0,4},{1,5},{4,8},{5,9},{8,12},{9,13},{12,14},{13,15},{14,10},{15,... | collective-permute-start | bytes 1572872 | tf_op jit(solution)/shard_map/ppermute | solution.py:306
  17.6 10.0 %collective-permute-done.6.refs_4_ = bf16[512,512]{1,0:T(8,128)(2,1)S(1)} collective-permute-done((bf16[512,512]{1,0:T(8,128)(2,1)S(1)}, bf16[512,512]{1,0:T(8,128)(2,1)S(1)}, u32[]{:S(2)}, u32[]{:S(2)}) %collective-permute-start.6) | collective-permute-done | bytes 524320 | tf_op jit(solution)/shard_map/ppermute | solution.py:306
  27.9 1.3 %collective-permute-done.5.refs_4_ = bf16[512,512]{1,0:T(8,128)(2,1)S(1)} collective-permute-done((bf16[512,512]{1,0:T(8,128)(2,1)S(1)}, bf16[512,512]{1,0:T(8,128)(2,1)S(1)}, u32[]{:S(2)}, u32[]{:S(2)}) %collective-permute-start.5) | collective-permute-done | bytes 524320 | tf_op jit(solution)/shard_map/ppermute | solution.py:306
  29.7 1.5 %collective-permute-start.10 = (bf16[512,512]{1,0:T(8,128)(2,1)S(1)}, bf16[512,512]{1,0:T(8,128)(2,1)S(1)}, u32[]{:S(2)}, u32[]{:S(2)}) collective-permute-start(bf16[512,512]{1,0:T(8,128)(2,1)S(1)} %collective-permute-done.4.refs_5_), channel_id=1, source_target_pairs={{0,16},{1,17},{2,18},{3,19},{4,20},{5,21},{6,22},{7,23},{8,24},{9,... | collective-permute-start | bytes 1572872 | tf_op jit(solution)/shard_map/ppermute | solution.py:306
  31.7 1.9 %collective-permute-start.11 = (s32[256]{0:T(256)S(1)}, s32[256]{0:T(256)S(1)}, u32[]{:S(2)}, u32[]{:S(2)}) collective-permute-start(s32[256]{0:T(256)S(1)} %copy-done.4), channel_id=1, source_target_pairs={{0,1},{1,2},{2,3},{3,4},{4,5},{5,6},{6,7},{7,8},{8,9},{9,10},{10,1... | collective-permute-start | bytes 3080 | tf_op jit(solution)/shard_map/ppermute | solution.py:31
  34.2 1.8 %project.5 = (f32[256,512]{1,0:T(8,128)S(1)}, f32[256,512]{1,0:T(8,128)S(1)}) custom-call(s32[2]{0:T(128)S(1)} %pad_add_fusion.core_ref.ids_ref, bf16[256,4096]{1,0:T(8,128)(2,1)S(1)} %get-tuple-element.53.xa_ref, bf16[128,4096]{1,0:T(8,128)(2,1)S(1)} %collective-permute-done.2.refs_0_, bf16[128,4096]{1,0:T(8,128)(2,1)S(1)} %collective-permute-done.3.refs_1_, ...), custom_call_target="tpu_custom_call" | custom-call | flops 1073741824 | bytes 6291456 | tf_op jit(solution)/shard_map/project/pallas_call | solution.py:124
  36.0 1.6 %collective-permute-done.11 = s32[256]{0:T(256)S(1)} collective-permute-done((s32[256]{0:T(256)S(1)}, s32[256]{0:T(256)S(1)}, u32[]{:S(2)}, u32[]{:S(2)}) %collective-permute-start.11) | collective-permute-done | bytes 1056 | tf_op jit(solution)/shard_map/ppermute | solution.py:31
  37.5 2.8 %collective-permute-done.9.refs_5_ = bf16[512,512]{1,0:T(8,128)(2,1)S(1)} collective-permute-done((bf16[512,512]{1,0:T(8,128)(2,1)S(1)}, bf16[512,512]{1,0:T(8,128)(2,1)S(1)}, u32[]{:S(2)}, u32[]{:S(2)}) %collective-permute-start.9) | collective-permute-done | bytes 524320 | tf_op jit(solution)/shard_map/ppermute | solution.py:306
  40.4 3.0 %collective-permute-done.10.refs_3_ = bf16[512,512]{1,0:T(8,128)(2,1)S(1)} collective-permute-done((bf16[512,512]{1,0:T(8,128)(2,1)S(1)}, bf16[512,512]{1,0:T(8,128)(2,1)S(1)}, u32[]{:S(2)}, u32[]{:S(2)}) %collective-permute-start.10) | collective-permute-done | bytes 524320 | tf_op jit(solution)/shard_map/ppermute | solution.py:306
  43.4 2.7 %collective-permute-start.15 = (bf16[512,512]{1,0:T(8,128)(2,1)S(1)}, bf16[512,512]{1,0:T(8,128)(2,1)S(1)}, u32[]{:S(2)}, u32[]{:S(2)}) collective-permute-start(bf16[512,512]{1,0:T(8,128)(2,1)S(1)} %collective-permute-done.8.refs_2_), channel_id=1, source_target_pairs={{0,4},{1,5},{4,8},{5,9},{8,12},{9,13},{12,14},{13,15},{14,10},{15,... | collective-permute-start | bytes 1572872 | tf_op jit(solution)/shard_map/ppermute | solution.py:306
  47.1 1.2 %tables.1 = (f32[256,128]{1,0:T(8,128)S(1)}, f32[256,128]{1,0:T(8,128)S(1)}, f32[2,128,256]{2,1,0:T(8,128)S(1)}) custom-call(s32[2]{0:T(128)S(1)} %pad_add_fusion.core_ref.ids_ref, s32[1,256]{1,0:T(1,128)S(1)} %bitcast.4, s32[1,256]{1,0:T(1,128)S(1)} %bitcast.5, f32[1,128]{1,0:T(1,128)S(1)} %copy-done.5), custom_call_target="tpu_custom_call" | custom-call | flops 1310720 | bytes 524288 | tf_op jit(solution)/shard_map/tables/pallas_call | solution.py:164
  48.3 1.3 %project.6 = (f32[256,512]{1,0:T(8,128)S(1)}, f32[256,512]{1,0:T(8,128)S(1)}) custom-call(s32[2]{0:T(128)S(1)} %pad_add_fusion.core_ref.ids_ref, bf16[256,4096]{1,0:T(8,128)(2,1)S(1)} %get-tuple-element.53.xa_ref, bf16[128,4096]{1,0:T(8,128)(2,1)S(1)} %collective-permute-done.2.refs_0_, bf16[128,4096]{1,0:T(8,128)(2,1)S(1)} %collective-permute-done.3.refs_1_, ...), custom_call_target="tpu_custom_call" | custom-call | flops 536870912 | bytes 5242880 | tf_op jit(solution)/shard_map/project/pallas_call | solution.py:124
  49.6 1.8 %project.7 = (f32[256,512]{1,0:T(8,128)S(1)}, f32[256,512]{1,0:T(8,128)S(1)}) custom-call(s32[2]{0:T(128)S(1)} %pad_add_fusion.core_ref.ids_ref, bf16[256,4096]{1,0:T(8,128)(2,1)S(1)} %get-tuple-element.53.xa_ref, bf16[128,4096]{1,0:T(8,128)(2,1)S(1)} %collective-permute-done.2.refs_0_, bf16[128,4096]{1,0:T(8,128)(2,1)S(1)} %collective-permute-done.3.refs_1_, ...), custom_call_target="tpu_custom_call" | custom-call | flops 1073741824 | bytes 6291456 | tf_op jit(solution)/shard_map/project/pallas_call | solution.py:124
  51.4 3.3 %collective-permute-done.7.refs_2_ = bf16[512,512]{1,0:T(8,128)(2,1)S(1)} collective-permute-done((bf16[512,512]{1,0:T(8,128)(2,1)S(1)}, bf16[512,512]{1,0:T(8,128)(2,1)S(1)}, u32[]{:S(2)}, u32[]{:S(2)}) %collective-permute-start.7) | collective-permute-done | bytes 524320 | tf_op jit(solution)/shard_map/ppermute | solution.py:306
  54.7 2.7 %collective-permute-start.14 = (bf16[512,512]{1,0:T(8,128)(2,1)S(1)}, bf16[512,512]{1,0:T(8,128)(2,1)S(1)}, u32[]{:S(2)}, u32[]{:S(2)}) collective-permute-start(bf16[512,512]{1,0:T(8,128)(2,1)S(1)} %collective-permute-done.7.refs_2_), channel_id=1, source_target_pairs={{0,4},{1,5},{4,8},{5,9},{8,12},{9,13},{12,14},{13,15},{14,10},{15,... | collective-permute-start | bytes 1572872 | tf_op jit(solution)/shard_map/ppermute | solution.py:306
  57.4 1.3 %collective-permute-done.16.refs_3_ = bf16[512,512]{1,0:T(8,128)(2,1)S(1)} collective-permute-done((bf16[512,512]{1,0:T(8,128)(2,1)S(1)}, bf16[512,512]{1,0:T(8,128)(2,1)S(1)}, u32[]{:S(2)}, u32[]{:S(2)}) %collective-permute-start.16) | collective-permute-done | bytes 524320 | tf_op jit(solution)/shard_map/ppermute | solution.py:306
  58.7 1.2 %project.8 = (f32[256,512]{1,0:T(8,128)S(1)}, f32[128,512]{1,0:T(8,128)S(1)}, f32[128,512]{1,0:T(8,128)S(1)}) custom-call(s32[2]{0:T(128)S(1)} %pad_add_fusion.core_ref.ids_ref, bf16[256,4096]{1,0:T(8,128)(2,1)S(1)} %get-tuple-element.53.xa_ref, bf16[128,4096]{1,0:T(8,128)(2,1)S(1)} %collective-permute-done.2.refs_0_, ...), custom_call_target="tpu_custom_call" | custom-call | flops 536870912 | bytes 5242880 | tf_op jit(solution)/shard_map/project/pallas_call | solution.py:124
  60.5 1.0 %collective-permute-done.17.refs_0_ = f32[128,512]{1,0:T(8,128)S(1)} collective-permute-done((f32[128,512]{1,0:T(8,128)S(1)}, f32[128,512]{1,0:T(8,128)S(1)}, u32[]{:S(2)}, u32[]{:S(2)}) %collective-permute-start.17) | collective-permute-done | bytes 262176 | tf_op jit(solution)/shard_map/ppermute | solution.py:309
  62.2 2.0 %collective-permute-start.19 = (bf16[128,512]{1,0:T(8,128)(2,1)S(1)}, bf16[128,512]{1,0:T(8,128)(2,1)S(1)}, u32[]{:S(2)}, u32[]{:S(2)}) collective-permute-start(bf16[128,512]{1,0:T(8,128)(2,1)S(1)} %get-tuple-element.88), channel_id=1, source_target_pairs={{0,1},{1,2},{2,3},{3,4},{4,5},{5,6},{6,7},{7,8},{8,9},{9,10},{10,1... | collective-permute-start | bytes 393224 | tf_op jit(solution)/shard_map/ppermute | solution.py:31
  64.2 2.4 %scores.2.p_ref = bf16[4,1024,256]{2,1,0:T(8,128)(2,1)S(1)} custom-call(bf16[256,4096]{1,0:T(8,128)(2,1)S(1)} %copy-done, bf16[256,512]{1,0:T(8,128)(2,1)S(1)} %get-tuple-element.86.ka_ref.kb_ref, bf16[256,512]{1,0:T(8,128)(2,1)S(1)} %get-tuple-element.86.ka_ref.kb_ref, f32[2,128,256]{2,1,0:T(8,128)S(1)} %get-tuple-element.87.bias_ref), custom_call_target="tpu_custom_call" | custom-call | flops 268435456 | bytes 3145728 | tf_op jit(solution)/shard_map/scores/pallas_call | solution.py:231
  66.6 2.7 %collective-permute-done.19.ka_ref = bf16[128,512]{1,0:T(8,128)(2,1)S(1)} collective-permute-done((bf16[128,512]{1,0:T(8,128)(2,1)S(1)}, bf16[128,512]{1,0:T(8,128)(2,1)S(1)}, u32[]{:S(2)}, u32[]{:S(2)}) %collective-permute-start.19) | collective-permute-done | bytes 131104 | tf_op jit(solution)/shard_map/ppermute | solution.py:31
  69.4 1.8 %project.9 = (f32[256,512]{1,0:T(8,128)S(1)}, f32[256,512]{1,0:T(8,128)S(1)}) custom-call(s32[2]{0:T(128)S(1)} %pad_add_fusion.core_ref.ids_ref, bf16[256,4096]{1,0:T(8,128)(2,1)S(1)} %get-tuple-element.53.xa_ref, bf16[128,4096]{1,0:T(8,128)(2,1)S(1)} %collective-permute-done.2.refs_0_, bf16[128,4096]{1,0:T(8,128)(2,1)S(1)} %collective-permute-done.3.refs_1_, ...), custom_call_target="tpu_custom_call" | custom-call | flops 1073741824 | bytes 6291456 | tf_op jit(solution)/shard_map/project/pallas_call | solution.py:124
  71.2 2.4 %scores.3.p_ref = bf16[4,1024,256]{2,1,0:T(8,128)(2,1)S(1)} custom-call(bf16[256,4096]{1,0:T(8,128)(2,1)S(1)} %copy-done, bf16[128,512]{1,0:T(8,128)(2,1)S(1)} %collective-permute-done.19.ka_ref, bf16[256,512]{1,0:T(8,128)(2,1)S(1)} %get-tuple-element.86.ka_ref.kb_ref, f32[2,128,256]{2,1,0:T(8,128)S(1)} %get-tuple-element.87.bias_ref), custom_call_target="tpu_custom_call" | custom-call | flops 268435456 | bytes 3145728 | tf_op jit(solution)/shard_map/scores/pallas_call | solution.py:231
  73.7 2.4 %collective-permute-start.21 = (bf16[128,512]{1,0:T(8,128)(2,1)S(1)}, bf16[128,512]{1,0:T(8,128)(2,1)S(1)}, u32[]{:S(2)}, u32[]{:S(2)}) collective-permute-start(bf16[128,512]{1,0:T(8,128)(2,1)S(1)} %get-tuple-element.96), channel_id=1, source_target_pairs={{0,1},{1,2},{2,3},{3,4},{4,5},{5,6},{6,7},{7,8},{8,9},{9,10},{10,1... | collective-permute-start | bytes 393224 | tf_op jit(solution)/shard_map/ppermute | solution.py:31
  76.1 2.4 %context.2.refs_0_ = bf16[256,4096]{1,0:T(8,128)(2,1)} custom-call(bf16[4,1024,256]{2,1,0:T(8,128)(2,1)S(1)} %scores.2.p_ref, bf16[256,512]{1,0:T(8,128)(2,1)S(1)} %get-tuple-element.97.va_ref.vb_ref, bf16[256,512]{1,0:T(8,128)(2,1)S(1)} %get-tuple-element.97.va_ref.vb_ref), custom_call_target="tpu_custom_call" | custom-call | flops 268435456 | bytes 3145728 | tf_op jit(solution)/shard_map/context/pallas_call | solution.py:263
  78.5 2.4 %collective-permute-done.21.va_ref = bf16[128,512]{1,0:T(8,128)(2,1)S(1)} collective-permute-done((bf16[128,512]{1,0:T(8,128)(2,1)S(1)}, bf16[128,512]{1,0:T(8,128)(2,1)S(1)}, u32[]{:S(2)}, u32[]{:S(2)}) %collective-permute-start.21) | collective-permute-done | bytes 131104 | tf_op jit(solution)/shard_map/ppermute | solution.py:31
  80.9 2.4 %context.3 = bf16[256,4096]{1,0:T(8,128)(2,1)} custom-call(bf16[4,1024,256]{2,1,0:T(8,128)(2,1)S(1)} %scores.3.p_ref, bf16[128,512]{1,0:T(8,128)(2,1)S(1)} %collective-permute-done.21.va_ref, bf16[256,512]{1,0:T(8,128)(2,1)S(1)} %get-tuple-element.97.va_ref.vb_ref, bf16[256,4096]{1,0:T(8,128)(2,1)} %context.2.refs_0_), custom_call_target="tpu_custom_call", output_to_operand_aliasing={{}: (3, {})} | custom-call | flops 268435456 | bytes 3145728 | tf_op jit(solution)/shard_map/context/pallas_call | solution.py:263
  (39 shorter events, 6.9 us)
Async XLA Ops:
  0.0 13.9 %collective-permute-start = (bf16[512,512]{1,0:T(8,128)(2,1)}, bf16[512,512]{1,0:T(8,128)(2,1)S(1)}, u32[]{:S(2)}, u32[]{:S(2)}) collective-permute-start(bf16[512,512]{1,0:T(8,128)(2,1)} %refs_2_.2), channel_id=1, source_target_pairs={{0,4},{1,5},{4,8},{5,9},{8,12},{9,13},{12,14},{13,15},{14,10},{15,... | collective-permute-start | bytes 1572872 | tf_op jit(solution)/shard_map/ppermute | solution.py:306
  1.5 13.6 %collective-permute-start.1 = (bf16[512,512]{1,0:T(8,128)(2,1)}, bf16[512,512]{1,0:T(8,128)(2,1)S(1)}, u32[]{:S(2)}, u32[]{:S(2)}) collective-permute-start(bf16[512,512]{1,0:T(8,128)(2,1)} %refs_2_.3), channel_id=1, source_target_pairs={{0,2},{1,3},{4,0},{5,1},{8,4},{9,5},{12,8},{13,9},{14,12},{15,13},... | collective-permute-start | bytes 1572872 | tf_op jit(solution)/shard_map/ppermute | solution.py:306
  2.8 2.2 %copy-start.1 = (bf16[256,8192]{1,0:T(8,128)(2,1)S(1)}, bf16[256,8192]{1,0:T(8,128)(2,1)}, u32[]{:S(2)}) copy-start(bf16[256,8192]{1,0:T(8,128)(2,1)} %h_ref.1) | copy-start | bytes 12582916
  5.0 26.7 %copy-start.4 = (s32[256]{0:T(256)S(1)}, s32[256]{0:T(256)}, u32[]{:S(2)}) copy-start(s32[256]{0:T(256)} %param.12) | copy-start | bytes 3076
  5.0 29.1 %copy-start.2 = (bf16[512,512]{1,0:T(8,128)(2,1)S(1)}, bf16[512,512]{1,0:T(8,128)(2,1)}, u32[]{:S(2)}) copy-start(bf16[512,512]{1,0:T(8,128)(2,1)} %refs_2_.2) | copy-start | bytes 1572868
  8.3 23.4 %collective-permute-start.2 = (bf16[128,4096]{1,0:T(8,128)(2,1)S(1)}, bf16[128,4096]{1,0:T(8,128)(2,1)S(1)}, u32[]{:S(2)}, u32[]{:S(2)}) collective-permute-start(bf16[128,4096]{1,0:T(8,128)(2,1)S(1)} %get-tuple-element.54), channel_id=1, source_target_pairs={{0,1},{1,0},{2,3},{3,2},{4,5},{5,4},{6,7},{7,6},{8,9},{9,8},{10,11... | collective-permute-start | bytes 3145736 | tf_op jit(solution)/shard_map/ppermute | solution.py:309
  8.3 25.3 %collective-permute-start.3 = (bf16[128,4096]{1,0:T(8,128)(2,1)S(1)}, bf16[128,4096]{1,0:T(8,128)(2,1)S(1)}, u32[]{:S(2)}, u32[]{:S(2)}) collective-permute-start(bf16[128,4096]{1,0:T(8,128)(2,1)S(1)} %get-tuple-element.55), channel_id=1, source_target_pairs={{0,1},{1,0},{2,3},{3,2},{4,5},{5,4},{6,7},{7,6},{8,9},{9,8},{10,11... | collective-permute-start | bytes 3145736 | tf_op jit(solution)/shard_map/ppermute | solution.py:309
  15.1 32.0 %copy-start.5 = (f32[1,128]{1,0:T(1,128)S(1)}, f32[1,128]{1,0:T(1,128)}, u32[]{:S(2)}) copy-start(f32[1,128]{1,0:T(1,128)} %constant.11.clone.freq_ref) | copy-start | bytes 1540
  15.1 12.5 %collective-permute-start.6 = (bf16[512,512]{1,0:T(8,128)(2,1)S(1)}, bf16[512,512]{1,0:T(8,128)(2,1)S(1)}, u32[]{:S(2)}, u32[]{:S(2)}) collective-permute-start(bf16[512,512]{1,0:T(8,128)(2,1)S(1)} %collective-permute-done.refs_3_), channel_id=1, source_target_pairs={{0,16},{1,17},{2,18},{3,19},{4,20},{5,21},{6,22},{7,23},{8,24},{9,... | collective-permute-start | bytes 1572872 | tf_op jit(solution)/shard_map/ppermute | solution.py:306
  15.6 12.3 %collective-permute-start.4 = (bf16[512,512]{1,0:T(8,128)(2,1)S(1)}, bf16[512,512]{1,0:T(8,128)(2,1)S(1)}, u32[]{:S(2)}, u32[]{:S(2)}) collective-permute-start(bf16[512,512]{1,0:T(8,128)(2,1)S(1)} %collective-permute-done.refs_3_), channel_id=1, source_target_pairs={{0,4},{1,5},{4,8},{5,9},{8,12},{9,13},{12,14},{13,15},{14,10},{15,... | collective-permute-start | bytes 1572872 | tf_op jit(solution)/shard_map/ppermute | solution.py:306
  17.1 12.1 %collective-permute-start.5 = (bf16[512,512]{1,0:T(8,128)(2,1)S(1)}, bf16[512,512]{1,0:T(8,128)(2,1)S(1)}, u32[]{:S(2)}, u32[]{:S(2)}) collective-permute-start(bf16[512,512]{1,0:T(8,128)(2,1)S(1)} %collective-permute-done.1.refs_3_), channel_id=1, source_target_pairs={{0,2},{1,3},{4,0},{5,1},{8,4},{9,5},{12,8},{13,9},{14,12},{15,13},... | collective-permute-start | bytes 1572872 | tf_op jit(solution)/shard_map/ppermute | solution.py:306
  29.2 11.1 %collective-permute-start.9 = (bf16[512,512]{1,0:T(8,128)(2,1)S(1)}, bf16[512,512]{1,0:T(8,128)(2,1)S(1)}, u32[]{:S(2)}, u32[]{:S(2)}) collective-permute-start(bf16[512,512]{1,0:T(8,128)(2,1)S(1)} %collective-permute-done.5.refs_4_), channel_id=1, source_target_pairs={{0,2},{1,3},{4,0},{5,1},{8,4},{9,5},{12,8},{13,9},{14,12},{15,13},... | collective-permute-start | bytes 1572872 | tf_op jit(solution)/shard_map/ppermute | solution.py:306
  29.7 13.7 %collective-permute-start.10 = (bf16[512,512]{1,0:T(8,128)(2,1)S(1)}, bf16[512,512]{1,0:T(8,128)(2,1)S(1)}, u32[]{:S(2)}, u32[]{:S(2)}) collective-permute-start(bf16[512,512]{1,0:T(8,128)(2,1)S(1)} %collective-permute-done.4.refs_5_), channel_id=1, source_target_pairs={{0,16},{1,17},{2,18},{3,19},{4,20},{5,21},{6,22},{7,23},{8,24},{9,... | collective-permute-start | bytes 1572872 | tf_op jit(solution)/shard_map/ppermute | solution.py:306
  31.2 12.2 %collective-permute-start.8 = (bf16[512,512]{1,0:T(8,128)(2,1)S(1)}, bf16[512,512]{1,0:T(8,128)(2,1)S(1)}, u32[]{:S(2)}, u32[]{:S(2)}) collective-permute-start(bf16[512,512]{1,0:T(8,128)(2,1)S(1)} %collective-permute-done.4.refs_5_), channel_id=1, source_target_pairs={{0,4},{1,5},{4,8},{5,9},{8,12},{9,13},{12,14},{13,15},{14,10},{15,... | collective-permute-start | bytes 1572872 | tf_op jit(solution)/shard_map/ppermute | solution.py:306
  31.7 5.9 %collective-permute-start.11 = (s32[256]{0:T(256)S(1)}, s32[256]{0:T(256)S(1)}, u32[]{:S(2)}, u32[]{:S(2)}) collective-permute-start(s32[256]{0:T(256)S(1)} %copy-done.4), channel_id=1, source_target_pairs={{0,1},{1,2},{2,3},{3,4},{4,5},{5,6},{6,7},{7,8},{8,9},{9,10},{10,1... | collective-permute-start | bytes 3080 | tf_op jit(solution)/shard_map/ppermute | solution.py:31
  33.6 21.0 %collective-permute-start.7 = (bf16[512,512]{1,0:T(8,128)(2,1)S(1)}, bf16[512,512]{1,0:T(8,128)(2,1)S(1)}, u32[]{:S(2)}, u32[]{:S(2)}) collective-permute-start(bf16[512,512]{1,0:T(8,128)(2,1)S(1)} %collective-permute-done.5.refs_4_), channel_id=1, source_target_pairs={{0,16},{1,17},{2,18},{3,19},{4,20},{5,21},{6,22},{7,23},{8,24},{9,... | collective-permute-start | bytes 1572872 | tf_op jit(solution)/shard_map/ppermute | solution.py:306
  43.4 13.9 %collective-permute-start.15 = (bf16[512,512]{1,0:T(8,128)(2,1)S(1)}, bf16[512,512]{1,0:T(8,128)(2,1)S(1)}, u32[]{:S(2)}, u32[]{:S(2)}) collective-permute-start(bf16[512,512]{1,0:T(8,128)(2,1)S(1)} %collective-permute-done.8.refs_2_), channel_id=1, source_target_pairs={{0,4},{1,5},{4,8},{5,9},{8,12},{9,13},{12,14},{13,15},{14,10},{15,... | collective-permute-start | bytes 1572872 | tf_op jit(solution)/shard_map/ppermute | solution.py:306
  46.1 12.6 %collective-permute-start.16 = (bf16[512,512]{1,0:T(8,128)(2,1)S(1)}, bf16[512,512]{1,0:T(8,128)(2,1)S(1)}, u32[]{:S(2)}, u32[]{:S(2)}) collective-permute-start(bf16[512,512]{1,0:T(8,128)(2,1)S(1)} %collective-permute-done.10.refs_3_), channel_id=1, source_target_pairs={{0,2},{1,3},{4,0},{5,1},{8,4},{9,5},{12,8},{13,9},{14,12},{15,13},... | collective-permute-start | bytes 1572872 | tf_op jit(solution)/shard_map/ppermute | solution.py:306
  46.1 23.2 %collective-permute-start.12 = (bf16[512,512]{1,0:T(8,128)(2,1)S(1)}, bf16[512,512]{1,0:T(8,128)(2,1)S(1)}, u32[]{:S(2)}, u32[]{:S(2)}) collective-permute-start(bf16[512,512]{1,0:T(8,128)(2,1)S(1)} %collective-permute-done.1.refs_3_), channel_id=1, source_target_pairs={{0,16},{1,17},{2,18},{3,19},{4,20},{5,21},{6,22},{7,23},{8,24},{9,... | collective-permute-start | bytes 1572872 | tf_op jit(solution)/shard_map/ppermute | solution.py:306
  48.3 1.3 %copy-start.3 = (bf16[512,512]{1,0:T(8,128)(2,1)S(1)}, bf16[512,512]{1,0:T(8,128)(2,1)}, u32[]{:S(2)}) copy-start(bf16[512,512]{1,0:T(8,128)(2,1)} %refs_2_.3) | copy-start | bytes 1572868
  54.7 14.7 %collective-permute-start.14 = (bf16[512,512]{1,0:T(8,128)(2,1)S(1)}, bf16[512,512]{1,0:T(8,128)(2,1)S(1)}, u32[]{:S(2)}, u32[]{:S(2)}) collective-permute-start(bf16[512,512]{1,0:T(8,128)(2,1)S(1)} %collective-permute-done.7.refs_2_), channel_id=1, source_target_pairs={{0,4},{1,5},{4,8},{5,9},{8,12},{9,13},{12,14},{13,15},{14,10},{15,... | collective-permute-start | bytes 1572872 | tf_op jit(solution)/shard_map/ppermute | solution.py:306
  57.4 12.0 %collective-permute-start.13 = (bf16[512,512]{1,0:T(8,128)(2,1)S(1)}, bf16[512,512]{1,0:T(8,128)(2,1)S(1)}, u32[]{:S(2)}, u32[]{:S(2)}) collective-permute-start(bf16[512,512]{1,0:T(8,128)(2,1)S(1)} %collective-permute-done.9.refs_5_), channel_id=1, source_target_pairs={{0,2},{1,3},{4,0},{5,1},{8,4},{9,5},{12,8},{13,9},{14,12},{15,13},... | collective-permute-start | bytes 1572872 | tf_op jit(solution)/shard_map/ppermute | solution.py:306
  58.7 5.5 %copy-start = (bf16[256,4096]{1,0:T(8,128)(2,1)S(1)}, bf16[256,4096]{1,0:T(8,128)(2,1)}, u32[]{:S(2)}) copy-start(bf16[256,4096]{1,0:T(8,128)(2,1)} %q_ref.3) | copy-start | bytes 6291460
  59.9 1.6 %collective-permute-start.17 = (f32[128,512]{1,0:T(8,128)S(1)}, f32[128,512]{1,0:T(8,128)S(1)}, u32[]{:S(2)}, u32[]{:S(2)}) collective-permute-start(f32[128,512]{1,0:T(8,128)S(1)} %get-tuple-element.84), channel_id=1, source_target_pairs={{0,1},{1,0},{2,3},{3,2},{4,5},{5,4},{6,7},{7,6},{8,9},{9,8},{10,11... | collective-permute-start | bytes 786440 | tf_op jit(solution)/shard_map/ppermute | solution.py:309
  60.0 1.9 %collective-permute-start.18 = (f32[128,512]{1,0:T(8,128)S(1)}, f32[128,512]{1,0:T(8,128)S(1)}, u32[]{:S(2)}, u32[]{:S(2)}) collective-permute-start(f32[128,512]{1,0:T(8,128)S(1)} %get-tuple-element.85), channel_id=1, source_target_pairs={{0,1},{1,0},{2,3},{3,2},{4,5},{5,4},{6,7},{7,6},{8,9},{9,8},{10,11... | collective-permute-start | bytes 786440 | tf_op jit(solution)/shard_map/ppermute | solution.py:309
  62.2 7.2 %collective-permute-start.19 = (bf16[128,512]{1,0:T(8,128)(2,1)S(1)}, bf16[128,512]{1,0:T(8,128)(2,1)S(1)}, u32[]{:S(2)}, u32[]{:S(2)}) collective-permute-start(bf16[128,512]{1,0:T(8,128)(2,1)S(1)} %get-tuple-element.88), channel_id=1, source_target_pairs={{0,1},{1,2},{2,3},{3,4},{4,5},{5,6},{6,7},{7,8},{8,9},{9,10},{10,1... | collective-permute-start | bytes 393224 | tf_op jit(solution)/shard_map/ppermute | solution.py:31
  71.1 2.5 %collective-permute-start.20 = (f32[256,512]{1,0:T(8,128)S(1)}, f32[256,512]{1,0:T(8,128)S(1)}, u32[]{:S(2)}, u32[]{:S(2)}) collective-permute-start(f32[256,512]{1,0:T(8,128)S(1)} %get-tuple-element.91), channel_id=1, source_target_pairs={{0,1},{1,0},{2,3},{3,2},{4,5},{5,4},{6,7},{7,6},{8,9},{9,8},{10,11... | collective-permute-start | bytes 1572872 | tf_op jit(solution)/shard_map/ppermute | solution.py:309
  73.7 7.2 %collective-permute-start.21 = (bf16[128,512]{1,0:T(8,128)(2,1)S(1)}, bf16[128,512]{1,0:T(8,128)(2,1)S(1)}, u32[]{:S(2)}, u32[]{:S(2)}) collective-permute-start(bf16[128,512]{1,0:T(8,128)(2,1)S(1)} %get-tuple-element.96), channel_id=1, source_target_pairs={{0,1},{1,2},{2,3},{3,4},{4,5},{5,6},{6,7},{7,8},{8,9},{9,10},{10,1... | collective-permute-start | bytes 393224 | tf_op jit(solution)/shard_map/ppermute | solution.py:31

commit v5 on v4

--- a/solution.py
+++ b/solution.py
@@ -247,30 +247,45 @@
     )(queries, keys_a, keys_b, bias)
 
 
-def context_kernel(p_ref, va_ref, vb_ref, *refs):
-    out_ref = refs[-1]
+def context_kernel(block, p_ref, va_ref, vb_ref, *refs):
+    out_ref, held, sems = refs[-3:]
     rows = va_ref.shape[0]
-    values = jnp.concatenate([va_ref[...], vb_ref[...]], axis=0)
-    c = jnp.dot(p_ref[0], values, preferred_element_type=F32).astype(BF16)
-    for j in range(GROUP):
-        out_ref[:, j * HD : (j + 1) * HD] = c[j * rows : (j + 1) * rows]
+    width = GROUP * HD
+    copies = []
+    for h in range(p_ref.shape[0]):
+        at = slice(h * HD, (h + 1) * HD)
+        values = jnp.concatenate([va_ref[:, at], vb_ref[:, at]], axis=0)
+        c = jnp.dot(p_ref[h], values, preferred_element_type=F32).astype(BF16)
+        for j in range(GROUP):
+            held[:, h * width + j * HD : h * width + (j + 1) * HD] = c[j * rows : (j + 1) * rows]
+        here = (pl.ds(0, rows), pl.ds(h * width, width))
+        there = (pl.ds(block * rows, rows), pl.ds(h * width, width))
+        copies.append(pltpu.make_async_copy(held.at[here], out_ref.at[there], sems.at[h]))
+        copies[-1].start()
+    for copy in copies:
+        copy.wait()
 
 
 def contexts(block, weights, values_a, block_a, values_b, block_b, out=None):
     heads, _, span = weights.shape
     rows = REACH
+    feats = heads * HD
     more = () if out is None else (out,)
     return pl.pallas_call(
-        context_kernel,
-        grid=(heads,),
+        functools.partial(context_kernel, block),
+        grid=(1,),
         in_specs=[
-            pl.BlockSpec((1, GROUP * rows, span), lambda h: (h, 0, 0)),
-            pl.BlockSpec((rows, HD), lambda h: (block_a, h)),
-            pl.BlockSpec((rows, HD), lambda h: (block_b, h)),
+            pl.BlockSpec(memory_space=pltpu.VMEM),
+            pl.BlockSpec((rows, feats), lambda i: (block_a, 0)),
+            pl.BlockSpec((rows, feats), lambda i: (block_b, 0)),
         ]
         + [pl.BlockSpec(memory_space=pl.ANY)] * len(more),
-        out_specs=pl.BlockSpec((rows, GROUP * HD), lambda h: (block, h)),
-        out_shape=jax.ShapeDtypeStruct((2 * rows, heads * GROUP * HD), BF16),
+        out_specs=pl.BlockSpec(memory_space=pl.ANY),
+        out_shape=jax.ShapeDtypeStruct((2 * rows, GROUP * feats), BF16),
+        scratch_shapes=[
+            pltpu.VMEM((rows, GROUP * feats), BF16),
+            pltpu.SemaphoreType.DMA((heads,)),
+        ],
         input_output_aliases={3: 0} if more else {},
         compiler_params=params(),
         cost_estimate=cost(2 * heads * GROUP * rows * span * HD, 6 * rows * heads * GROUP * HD),
@@ -313,16 +328,16 @@
     other = [swap(t) for t in theirs]
     k1, v1 = send(key_weight, key_way), send(value_weight, value_way)
     k1, v1, mine = after(k1, v1, mine)
+    k2, v2 = send(k1, key_way), send(v1, value_way)
     yk1 = send(k1, other_group)
-    k2, v2 = send(k1, key_way), send(v1, value_way)
-    k2, v2, yk1 = after(k2, v2, yk1)
+    k2, v2 = after(k2, v2)
+    k3, v3 = send(k2, key_way), send(v2, value_way)
     yk2, yv2 = send(k2, other_group), send(v2, other_group)
-    k3, v3 = send(k2, key_way), send(v2, value_way)
     yv1 = send(v1, other_group)
 
     behind = from_behind(segment_ids, "dp", 1)
     key_part = project(ids, (0, -1, 1, -2), mine, other, [key_weight, k1, yk1, k2])
-    k3, v3, yk2, key_part, behind = after(k3, v3, yk2, key_part, behind)
+    k3, v3, key_part, behind = after(k3, v3, key_part, behind)
     k4, k3b = send(k3, key_way), send(yk2, value_way)
     v4 = send(v3, value_way)
     key_part = project(ids, (-3, 2), mine, other, [k3, yk2], key_part)
@@ -335,10 +350,9 @@
     keys, tail = finish(keys_kernel, "keys", own_k, cos, sin, *[swap(o) for o in other_k])
     prev_keys = from_behind(tail, "dp", 1)
     p1 = softmax_weights(queries, 1, keys, 0, keys, 1, bias)
+    value_part = project(ids, (-2,), mine, other, [yv2], value_part)
     value_part, p1, prev_keys = after(value_part, p1, prev_keys)
-    own_v, other_v = project(
-        ids, (-2, -1, 4, -3), mine, other, [yv2, yv1, v4, v3b], value_part
-    )
+    own_v, other_v = project(ids, (-1, 4, -3), mine, other, [yv1, v4, v3b], value_part)
     p0 = softmax_weights(queries, 0, prev_keys, 0, keys, 0, bias)
     other_v, p0 = after(swap(other_v), p0)
     values, tail = finish(values_kernel, "values", own_v, other_v)

time: 83.5 us -> 82.2 us (0.984)
  the two profiles are of different devices: /device:TPU:24 before, /device:TPU:8 now
where the time goes in v5:
time: 82.2 us; the launch traced here: 82 us
  waiting for transfers between devices  35 us (43%)
  starting transfers between devices  22.4 us (27%)
  Pallas kernels  21.3 us (26%)
  local copies, waits for them, and re-layouts  2.95 us (4%)
    ppermute x14, waiting for transfers between devices, send(): return lax.ppermute(value, both, way)  28.4 us
    ppermute x14, starting transfers between devices, send(): return lax.ppermute(value, both, way)  14.7 us
    pallas_call x6, Pallas kernels, project(): pl.pallas_call(functools.partial(project_kernel, steps, len(others), len(...  8.57 us
    ppermute x3, starting transfers between devices, from_behind(): lax.ppermute(value, axis, [(source, source + steps) for source in range(i...  6.48 us
    ppermute x3, waiting for transfers between devices, from_behind(): lax.ppermute(value, axis, [(source, source + steps) for source in range(i...  5.24 us
    pallas_call x2, Pallas kernels, softmax_weights(): pl.pallas_call(scores_kernel, grid=(heads,), in_specs=[pl.BlockSpec((rows...  4.83 us
    pallas_call x1, Pallas kernels, normalise(): pl.pallas_call(norm_kernel, grid_spec=pltpu.PrefetchScalarGridSpec(num_sc...  3.22 us
    pallas_call x2, Pallas kernels, contexts(): pl.pallas_call(functools.partial(context_kernel, block), grid=(1,), in_sp...  3.21 us
  transfers between devices with their start and end apart: 22, of which 13 were waited for; matrix products, arithmetic and copies ran while one was open for 1% of the time, Pallas kernels for 22%

profile of v5, /device:TPU:8, one launch (start us, length us, event | category | flops | bytes accessed | tf_op | source)
XLA Modules:
  0.0 82.0 jit_solution(6117504085816404525)
XLA Ops:
  0.0 1.6 %collective-permute-start = (bf16[512,512]{1,0:T(8,128)(2,1)}, bf16[512,512]{1,0:T(8,128)(2,1)S(1)}, u32[]{:S(2)}, u32[]{:S(2)}) collective-permute-start(bf16[512,512]{1,0:T(8,128)(2,1)} %refs_2_.2), channel_id=1, source_target_pairs={{0,4},{1,5},{4,8},{5,9},{8,12},{9,13},{12,14},{13,15},{14,10},{15,... | collective-permute-start | bytes 1572872 | tf_op jit(solution)/shard_map/ppermute | solution.py:321
  2.8 2.2 %copy-done.1 = bf16[256,8192]{1,0:T(8,128)(2,1)S(1)} copy-done((bf16[256,8192]{1,0:T(8,128)(2,1)S(1)}, bf16[256,8192]{1,0:T(8,128)(2,1)}, u32[]{:S(2)}) %copy-start.1) | copy-done | bytes 4194328
  5.0 3.2 %norm.1 = (bf16[256,4096]{1,0:T(8,128)(2,1)S(1)}, bf16[128,4096]{1,0:T(8,128)(2,1)S(1)}, bf16[128,4096]{1,0:T(8,128)(2,1)S(1)}) custom-call(s32[2]{0:T(128)S(1)} %pad_add_fusion.core_ref.ids_ref, bf16[256,8192]{1,0:T(8,128)(2,1)S(1)} %copy-done.1, bf16[1,8192]{1,0:T(2,128)(2,1)S(1)} %reshape.9.g_ref), custom_call_target="tpu_custom_call" | custom-call | flops 16777216 | bytes 8388608 | tf_op jit(solution)/shard_map/norm/pallas_call | solution.py:63
  8.8 5.0 %collective-permute-done.refs_3_ = bf16[512,512]{1,0:T(8,128)(2,1)S(1)} collective-permute-done((bf16[512,512]{1,0:T(8,128)(2,1)}, bf16[512,512]{1,0:T(8,128)(2,1)S(1)}, u32[]{:S(2)}, u32[]{:S(2)}) %collective-permute-start) | collective-permute-done | bytes 524320 | tf_op jit(solution)/shard_map/ppermute | solution.py:321
  13.9 1.3 %collective-permute-done.1.refs_3_ = bf16[512,512]{1,0:T(8,128)(2,1)S(1)} collective-permute-done((bf16[512,512]{1,0:T(8,128)(2,1)}, bf16[512,512]{1,0:T(8,128)(2,1)S(1)}, u32[]{:S(2)}, u32[]{:S(2)}) %collective-permute-start.1) | collective-permute-done | bytes 524320 | tf_op jit(solution)/shard_map/ppermute | solution.py:321
  15.2 1.6 %collective-permute-start.5 = (bf16[512,512]{1,0:T(8,128)(2,1)S(1)}, bf16[512,512]{1,0:T(8,128)(2,1)S(1)}, u32[]{:S(2)}, u32[]{:S(2)}) collective-permute-start(bf16[512,512]{1,0:T(8,128)(2,1)S(1)} %collective-permute-done.refs_3_), channel_id=1, source_target_pairs={{0,4},{1,5},{4,8},{5,9},{8,12},{9,13},{12,14},{13,15},{14,10},{15,... | collective-permute-start | bytes 1572872 | tf_op jit(solution)/shard_map/ppermute | solution.py:321
  17.6 10.1 %collective-permute-done.5.refs_5_ = bf16[512,512]{1,0:T(8,128)(2,1)S(1)} collective-permute-done((bf16[512,512]{1,0:T(8,128)(2,1)S(1)}, bf16[512,512]{1,0:T(8,128)(2,1)S(1)}, u32[]{:S(2)}, u32[]{:S(2)}) %collective-permute-start.5) | collective-permute-done | bytes 524320 | tf_op jit(solution)/shard_map/ppermute | solution.py:321
  27.6 1.3 %collective-permute-done.6.refs_4_ = bf16[512,512]{1,0:T(8,128)(2,1)S(1)} collective-permute-done((bf16[512,512]{1,0:T(8,128)(2,1)S(1)}, bf16[512,512]{1,0:T(8,128)(2,1)S(1)}, u32[]{:S(2)}, u32[]{:S(2)}) %collective-permute-start.6) | collective-permute-done | bytes 524320 | tf_op jit(solution)/shard_map/ppermute | solution.py:321
  28.9 1.5 %collective-permute-start.7 = (bf16[512,512]{1,0:T(8,128)(2,1)S(1)}, bf16[512,512]{1,0:T(8,128)(2,1)S(1)}, u32[]{:S(2)}, u32[]{:S(2)}) collective-permute-start(bf16[512,512]{1,0:T(8,128)(2,1)S(1)} %collective-permute-done.5.refs_5_), channel_id=1, source_target_pairs={{0,4},{1,5},{4,8},{5,9},{8,12},{9,13},{12,14},{13,15},{14,10},{15,... | collective-permute-start | bytes 1572872 | tf_op jit(solution)/shard_map/ppermute | solution.py:321
  31.3 1.9 %collective-permute-start.10 = (s32[256]{0:T(256)S(1)}, s32[256]{0:T(256)S(1)}, u32[]{:S(2)}, u32[]{:S(2)}) collective-permute-start(s32[256]{0:T(256)S(1)} %copy-done.4), channel_id=1, source_target_pairs={{0,1},{1,2},{2,3},{3,4},{4,5},{5,6},{6,7},{7,8},{8,9},{9,10},{10,1... | collective-permute-start | bytes 3080 | tf_op jit(solution)/shard_map/ppermute | solution.py:31
  33.2 1.8 %collective-permute-start.12 = (bf16[512,512]{1,0:T(8,128)(2,1)S(1)}, bf16[512,512]{1,0:T(8,128)(2,1)S(1)}, u32[]{:S(2)}, u32[]{:S(2)}) collective-permute-start(bf16[512,512]{1,0:T(8,128)(2,1)S(1)} %collective-permute-done.6.refs_4_), channel_id=1, source_target_pairs={{0,16},{1,17},{2,18},{3,19},{4,20},{5,21},{6,22},{7,23},{8,24},{9,... | collective-permute-start | bytes 1572872 | tf_op jit(solution)/shard_map/ppermute | solution.py:321
  35.0 1.8 %project.6 = (f32[256,512]{1,0:T(8,128)S(1)}, f32[256,512]{1,0:T(8,128)S(1)}) custom-call(s32[2]{0:T(128)S(1)} %pad_add_fusion.core_ref.ids_ref, bf16[256,4096]{1,0:T(8,128)(2,1)S(1)} %get-tuple-element.53.xa_ref, bf16[128,4096]{1,0:T(8,128)(2,1)S(1)} %collective-permute-done.2.refs_0_, bf16[128,4096]{1,0:T(8,128)(2,1)S(1)} %collective-permute-done.3.refs_1_, ...), custom_call_target="tpu_custom_call" | custom-call | flops 1073741824 | bytes 6291456 | tf_op jit(solution)/shard_map/project/pallas_call | solution.py:124
  37.1 3.1 %collective-permute-done.7.refs_2_ = bf16[512,512]{1,0:T(8,128)(2,1)S(1)} collective-permute-done((bf16[512,512]{1,0:T(8,128)(2,1)S(1)}, bf16[512,512]{1,0:T(8,128)(2,1)S(1)}, u32[]{:S(2)}, u32[]{:S(2)}) %collective-permute-start.7) | collective-permute-done | bytes 524320 | tf_op jit(solution)/shard_map/ppermute | solution.py:321
  40.2 1.7 %collective-permute-done.8.refs_5_ = bf16[512,512]{1,0:T(8,128)(2,1)S(1)} collective-permute-done((bf16[512,512]{1,0:T(8,128)(2,1)S(1)}, bf16[512,512]{1,0:T(8,128)(2,1)S(1)}, u32[]{:S(2)}, u32[]{:S(2)}) %collective-permute-start.8) | collective-permute-done | bytes 524320 | tf_op jit(solution)/shard_map/ppermute | solution.py:321
  42.6 2.1 %collective-permute-done.13.refs_3_ = bf16[512,512]{1,0:T(8,128)(2,1)S(1)} collective-permute-done((bf16[512,512]{1,0:T(8,128)(2,1)S(1)}, bf16[512,512]{1,0:T(8,128)(2,1)S(1)}, u32[]{:S(2)}, u32[]{:S(2)}) %collective-permute-start.13) | collective-permute-done | bytes 524320 | tf_op jit(solution)/shard_map/ppermute | solution.py:321
  45.2 2.1 %collective-permute-start.4 = (bf16[512,512]{1,0:T(8,128)(2,1)S(1)}, bf16[512,512]{1,0:T(8,128)(2,1)S(1)}, u32[]{:S(2)}, u32[]{:S(2)}) collective-permute-start(bf16[512,512]{1,0:T(8,128)(2,1)S(1)} %collective-permute-done.1.refs_3_), channel_id=1, source_target_pairs={{0,16},{1,17},{2,18},{3,19},{4,20},{5,21},{6,22},{7,23},{8,24},{9,... | collective-permute-start | bytes 1572872 | tf_op jit(solution)/shard_map/ppermute | solution.py:321
  47.7 1.2 %tables.1 = (f32[256,128]{1,0:T(8,128)S(1)}, f32[256,128]{1,0:T(8,128)S(1)}, f32[2,128,256]{2,1,0:T(8,128)S(1)}) custom-call(s32[2]{0:T(128)S(1)} %pad_add_fusion.core_ref.ids_ref, s32[1,256]{1,0:T(1,128)S(1)} %bitcast.4, s32[1,256]{1,0:T(1,128)S(1)} %bitcast.5, f32[1,128]{1,0:T(1,128)S(1)} %copy-done.5), custom_call_target="tpu_custom_call" | custom-call | flops 1310720 | bytes 524288 | tf_op jit(solution)/shard_map/tables/pallas_call | solution.py:164
  48.9 1.3 %project.7 = (f32[256,512]{1,0:T(8,128)S(1)}, f32[256,512]{1,0:T(8,128)S(1)}) custom-call(s32[2]{0:T(128)S(1)} %pad_add_fusion.core_ref.ids_ref, bf16[256,4096]{1,0:T(8,128)(2,1)S(1)} %get-tuple-element.53.xa_ref, bf16[128,4096]{1,0:T(8,128)(2,1)S(1)} %collective-permute-done.2.refs_0_, bf16[128,4096]{1,0:T(8,128)(2,1)S(1)} %collective-permute-done.3.refs_1_, ...), custom_call_target="tpu_custom_call" | custom-call | flops 536870912 | bytes 5242880 | tf_op jit(solution)/shard_map/project/pallas_call | solution.py:124
  50.2 1.8 %project.8 = (f32[256,512]{1,0:T(8,128)S(1)}, f32[256,512]{1,0:T(8,128)S(1)}) custom-call(s32[2]{0:T(128)S(1)} %pad_add_fusion.core_ref.ids_ref, bf16[256,4096]{1,0:T(8,128)(2,1)S(1)} %get-tuple-element.53.xa_ref, bf16[128,4096]{1,0:T(8,128)(2,1)S(1)} %collective-permute-done.2.refs_0_, bf16[128,4096]{1,0:T(8,128)(2,1)S(1)} %collective-permute-done.3.refs_1_, ...), custom_call_target="tpu_custom_call" | custom-call | flops 1073741824 | bytes 6291456 | tf_op jit(solution)/shard_map/project/pallas_call | solution.py:124
  52.0 3.8 %collective-permute-done.12.refs_2_ = bf16[512,512]{1,0:T(8,128)(2,1)S(1)} collective-permute-done((bf16[512,512]{1,0:T(8,128)(2,1)S(1)}, bf16[512,512]{1,0:T(8,128)(2,1)S(1)}, u32[]{:S(2)}, u32[]{:S(2)}) %collective-permute-start.12) | collective-permute-done | bytes 524320 | tf_op jit(solution)/shard_map/ppermute | solution.py:321
  55.9 2.4 %collective-permute-start.14 = (bf16[512,512]{1,0:T(8,128)(2,1)S(1)}, bf16[512,512]{1,0:T(8,128)(2,1)S(1)}, u32[]{:S(2)}, u32[]{:S(2)}) collective-permute-start(bf16[512,512]{1,0:T(8,128)(2,1)S(1)} %collective-permute-done.12.refs_2_), channel_id=1, source_target_pairs={{0,4},{1,5},{4,8},{5,9},{8,12},{9,13},{12,14},{13,15},{14,10},{15,... | collective-permute-start | bytes 1572872 | tf_op jit(solution)/shard_map/ppermute | solution.py:321
  58.3 1.2 %project.10 = (f32[256,512]{1,0:T(8,128)S(1)}, f32[128,512]{1,0:T(8,128)S(1)}, f32[128,512]{1,0:T(8,128)S(1)}) custom-call(s32[2]{0:T(128)S(1)} %pad_add_fusion.core_ref.ids_ref, bf16[256,4096]{1,0:T(8,128)(2,1)S(1)} %get-tuple-element.53.xa_ref, bf16[128,4096]{1,0:T(8,128)(2,1)S(1)} %collective-permute-done.2.refs_0_, ...), custom_call_target="tpu_custom_call" | custom-call | flops 536870912 | bytes 5242880 | tf_op jit(solution)/shard_map/project/pallas_call | solution.py:124
  60.1 1.0 %collective-permute-done.17.refs_0_ = f32[128,512]{1,0:T(8,128)S(1)} collective-permute-done((f32[128,512]{1,0:T(8,128)S(1)}, f32[128,512]{1,0:T(8,128)S(1)}, u32[]{:S(2)}, u32[]{:S(2)}) %collective-permute-start.17) | collective-permute-done | bytes 262176 | tf_op jit(solution)/shard_map/ppermute | solution.py:324
  61.8 2.2 %collective-permute-start.19 = (bf16[128,512]{1,0:T(8,128)(2,1)S(1)}, bf16[128,512]{1,0:T(8,128)(2,1)S(1)}, u32[]{:S(2)}, u32[]{:S(2)}) collective-permute-start(bf16[128,512]{1,0:T(8,128)(2,1)S(1)} %get-tuple-element.88), channel_id=1, source_target_pairs={{0,1},{1,2},{2,3},{3,4},{4,5},{5,6},{6,7},{7,8},{8,9},{9,10},{10,1... | collective-permute-start | bytes 393224 | tf_op jit(solution)/shard_map/ppermute | solution.py:31
  64.9 2.4 %scores.2.p_ref = bf16[4,1024,256]{2,1,0:T(8,128)(2,1)S(1)} custom-call(bf16[256,4096]{1,0:T(8,128)(2,1)S(1)} %copy-done, bf16[256,512]{1,0:T(8,128)(2,1)S(1)} %get-tuple-element.86.ka_ref.kb_ref, bf16[256,512]{1,0:T(8,128)(2,1)S(1)} %get-tuple-element.86.ka_ref.kb_ref, f32[2,128,256]{2,1,0:T(8,128)S(1)} %get-tuple-element.87.bias_ref), custom_call_target="tpu_custom_call" | custom-call | flops 268435456 | bytes 3145728 | tf_op jit(solution)/shard_map/scores/pallas_call | solution.py:231
  67.4 1.7 %collective-permute-done.19.ka_ref = bf16[128,512]{1,0:T(8,128)(2,1)S(1)} collective-permute-done((bf16[128,512]{1,0:T(8,128)(2,1)S(1)}, bf16[128,512]{1,0:T(8,128)(2,1)S(1)}, u32[]{:S(2)}, u32[]{:S(2)}) %collective-permute-start.19) | collective-permute-done | bytes 131104 | tf_op jit(solution)/shard_map/ppermute | solution.py:31
  69.1 1.5 %project.11 = (f32[256,512]{1,0:T(8,128)S(1)}, f32[256,512]{1,0:T(8,128)S(1)}) custom-call(s32[2]{0:T(128)S(1)} %pad_add_fusion.core_ref.ids_ref, bf16[256,4096]{1,0:T(8,128)(2,1)S(1)} %get-tuple-element.53.xa_ref, bf16[128,4096]{1,0:T(8,128)(2,1)S(1)} %collective-permute-done.2.refs_0_, bf16[128,4096]{1,0:T(8,128)(2,1)S(1)} %collective-permute-done.3.refs_1_, ...), custom_call_target="tpu_custom_call" | custom-call | flops 805306368 | bytes 5767168 | tf_op jit(solution)/shard_map/project/pallas_call | solution.py:124
  70.7 2.4 %scores.3.p_ref = bf16[4,1024,256]{2,1,0:T(8,128)(2,1)S(1)} custom-call(bf16[256,4096]{1,0:T(8,128)(2,1)S(1)} %copy-done, bf16[128,512]{1,0:T(8,128)(2,1)S(1)} %collective-permute-done.19.ka_ref, bf16[256,512]{1,0:T(8,128)(2,1)S(1)} %get-tuple-element.86.ka_ref.kb_ref, f32[2,128,256]{2,1,0:T(8,128)S(1)} %get-tuple-element.87.bias_ref), custom_call_target="tpu_custom_call" | custom-call | flops 268435456 | bytes 3145728 | tf_op jit(solution)/shard_map/scores/pallas_call | solution.py:231
  73.2 2.4 %collective-permute-start.21 = (bf16[128,512]{1,0:T(8,128)(2,1)S(1)}, bf16[128,512]{1,0:T(8,128)(2,1)S(1)}, u32[]{:S(2)}, u32[]{:S(2)}) collective-permute-start(bf16[128,512]{1,0:T(8,128)(2,1)S(1)} %get-tuple-element.96), channel_id=1, source_target_pairs={{0,1},{1,2},{2,3},{3,4},{4,5},{5,6},{6,7},{7,8},{8,9},{9,10},{10,1... | collective-permute-start | bytes 393224 | tf_op jit(solution)/shard_map/ppermute | solution.py:31
  75.6 1.6 %context.2.refs_0_ = bf16[256,4096]{1,0:T(8,128)(2,1)} custom-call(bf16[4,1024,256]{2,1,0:T(8,128)(2,1)S(1)} %scores.2.p_ref, bf16[256,512]{1,0:T(8,128)(2,1)S(1)} %get-tuple-element.97.va_ref.vb_ref, bf16[256,512]{1,0:T(8,128)(2,1)S(1)} %get-tuple-element.97.va_ref.vb_ref), custom_call_target="tpu_custom_call" | custom-call | flops 268435456 | bytes 3145728 | tf_op jit(solution)/shard_map/context/pallas_call | solution.py:274
  77.2 3.2 %collective-permute-done.21.va_ref = bf16[128,512]{1,0:T(8,128)(2,1)S(1)} collective-permute-done((bf16[128,512]{1,0:T(8,128)(2,1)S(1)}, bf16[128,512]{1,0:T(8,128)(2,1)S(1)}, u32[]{:S(2)}, u32[]{:S(2)}) %collective-permute-start.21) | collective-permute-done | bytes 131104 | tf_op jit(solution)/shard_map/ppermute | solution.py:31
  80.4 1.6 %context.3 = bf16[256,4096]{1,0:T(8,128)(2,1)} custom-call(bf16[4,1024,256]{2,1,0:T(8,128)(2,1)S(1)} %scores.3.p_ref, bf16[128,512]{1,0:T(8,128)(2,1)S(1)} %collective-permute-done.21.va_ref, bf16[256,512]{1,0:T(8,128)(2,1)S(1)} %get-tuple-element.97.va_ref.vb_ref, bf16[256,4096]{1,0:T(8,128)(2,1)} %context.2.refs_0_), custom_call_target="tpu_custom_call", output_to_operand_aliasing={{}: (3, {})} | custom-call | flops 268435456 | bytes 3145728 | tf_op jit(solution)/shard_map/context/pallas_call | solution.py:274
  (40 shorter events, 7.9 us)
Async XLA Ops:
  0.0 13.9 %collective-permute-start = (bf16[512,512]{1,0:T(8,128)(2,1)}, bf16[512,512]{1,0:T(8,128)(2,1)S(1)}, u32[]{:S(2)}, u32[]{:S(2)}) collective-permute-start(bf16[512,512]{1,0:T(8,128)(2,1)} %refs_2_.2), channel_id=1, source_target_pairs={{0,4},{1,5},{4,8},{5,9},{8,12},{9,13},{12,14},{13,15},{14,10},{15,... | collective-permute-start | bytes 1572872 | tf_op jit(solution)/shard_map/ppermute | solution.py:321
  1.6 13.6 %collective-permute-start.1 = (bf16[512,512]{1,0:T(8,128)(2,1)}, bf16[512,512]{1,0:T(8,128)(2,1)S(1)}, u32[]{:S(2)}, u32[]{:S(2)}) collective-permute-start(bf16[512,512]{1,0:T(8,128)(2,1)} %refs_2_.3), channel_id=1, source_target_pairs={{0,2},{1,3},{4,0},{5,1},{8,4},{9,5},{12,8},{13,9},{14,12},{15,13},... | collective-permute-start | bytes 1572872 | tf_op jit(solution)/shard_map/ppermute | solution.py:321
  2.8 2.2 %copy-start.1 = (bf16[256,8192]{1,0:T(8,128)(2,1)S(1)}, bf16[256,8192]{1,0:T(8,128)(2,1)}, u32[]{:S(2)}) copy-start(bf16[256,8192]{1,0:T(8,128)(2,1)} %h_ref.1) | copy-start | bytes 12582916
  5.0 26.3 %copy-start.4 = (s32[256]{0:T(256)S(1)}, s32[256]{0:T(256)}, u32[]{:S(2)}) copy-start(s32[256]{0:T(256)} %param.12) | copy-start | bytes 3076
  5.0 30.0 %copy-start.2 = (bf16[512,512]{1,0:T(8,128)(2,1)S(1)}, bf16[512,512]{1,0:T(8,128)(2,1)}, u32[]{:S(2)}) copy-start(bf16[512,512]{1,0:T(8,128)(2,1)} %refs_2_.2) | copy-start | bytes 1572868
  8.3 22.7 %collective-permute-start.2 = (bf16[128,4096]{1,0:T(8,128)(2,1)S(1)}, bf16[128,4096]{1,0:T(8,128)(2,1)S(1)}, u32[]{:S(2)}, u32[]{:S(2)}) collective-permute-start(bf16[128,4096]{1,0:T(8,128)(2,1)S(1)} %get-tuple-element.54), channel_id=1, source_target_pairs={{0,1},{1,0},{2,3},{3,2},{4,5},{5,4},{6,7},{7,6},{8,9},{9,8},{10,11... | collective-permute-start | bytes 3145736 | tf_op jit(solution)/shard_map/ppermute | solution.py:324
  8.3 22.9 %collective-permute-start.3 = (bf16[128,4096]{1,0:T(8,128)(2,1)S(1)}, bf16[128,4096]{1,0:T(8,128)(2,1)S(1)}, u32[]{:S(2)}, u32[]{:S(2)}) collective-permute-start(bf16[128,4096]{1,0:T(8,128)(2,1)S(1)} %get-tuple-element.55), channel_id=1, source_target_pairs={{0,1},{1,0},{2,3},{3,2},{4,5},{5,4},{6,7},{7,6},{8,9},{9,8},{10,11... | collective-permute-start | bytes 3145736 | tf_op jit(solution)/shard_map/ppermute | solution.py:324
  15.2 32.6 %copy-start.5 = (f32[1,128]{1,0:T(1,128)S(1)}, f32[1,128]{1,0:T(1,128)}, u32[]{:S(2)}) copy-start(f32[1,128]{1,0:T(1,128)} %constant.11.clone.freq_ref) | copy-start | bytes 1540
  15.2 12.5 %collective-permute-start.5 = (bf16[512,512]{1,0:T(8,128)(2,1)S(1)}, bf16[512,512]{1,0:T(8,128)(2,1)S(1)}, u32[]{:S(2)}, u32[]{:S(2)}) collective-permute-start(bf16[512,512]{1,0:T(8,128)(2,1)S(1)} %collective-permute-done.refs_3_), channel_id=1, source_target_pairs={{0,4},{1,5},{4,8},{5,9},{8,12},{9,13},{12,14},{13,15},{14,10},{15,... | collective-permute-start | bytes 1572872 | tf_op jit(solution)/shard_map/ppermute | solution.py:321
  16.8 12.2 %collective-permute-start.6 = (bf16[512,512]{1,0:T(8,128)(2,1)S(1)}, bf16[512,512]{1,0:T(8,128)(2,1)S(1)}, u32[]{:S(2)}, u32[]{:S(2)}) collective-permute-start(bf16[512,512]{1,0:T(8,128)(2,1)S(1)} %collective-permute-done.1.refs_3_), channel_id=1, source_target_pairs={{0,2},{1,3},{4,0},{5,1},{8,4},{9,5},{12,8},{13,9},{14,12},{15,13},... | collective-permute-start | bytes 1572872 | tf_op jit(solution)/shard_map/ppermute | solution.py:321
  17.2 16.0 %collective-permute-start.9 = (bf16[512,512]{1,0:T(8,128)(2,1)S(1)}, bf16[512,512]{1,0:T(8,128)(2,1)S(1)}, u32[]{:S(2)}, u32[]{:S(2)}) collective-permute-start(bf16[512,512]{1,0:T(8,128)(2,1)S(1)} %collective-permute-done.refs_3_), channel_id=1, source_target_pairs={{0,16},{1,17},{2,18},{3,19},{4,20},{5,21},{6,22},{7,23},{8,24},{9,... | collective-permute-start | bytes 1572872 | tf_op jit(solution)/shard_map/ppermute | solution.py:321
  28.9 11.3 %collective-permute-start.7 = (bf16[512,512]{1,0:T(8,128)(2,1)S(1)}, bf16[512,512]{1,0:T(8,128)(2,1)S(1)}, u32[]{:S(2)}, u32[]{:S(2)}) collective-permute-start(bf16[512,512]{1,0:T(8,128)(2,1)S(1)} %collective-permute-done.5.refs_5_), channel_id=1, source_target_pairs={{0,4},{1,5},{4,8},{5,9},{8,12},{9,13},{12,14},{13,15},{14,10},{15,... | collective-permute-start | bytes 1572872 | tf_op jit(solution)/shard_map/ppermute | solution.py:321
  30.4 11.4 %collective-permute-start.8 = (bf16[512,512]{1,0:T(8,128)(2,1)S(1)}, bf16[512,512]{1,0:T(8,128)(2,1)S(1)}, u32[]{:S(2)}, u32[]{:S(2)}) collective-permute-start(bf16[512,512]{1,0:T(8,128)(2,1)S(1)} %collective-permute-done.6.refs_4_), channel_id=1, source_target_pairs={{0,2},{1,3},{4,0},{5,1},{8,4},{9,5},{12,8},{13,9},{14,12},{15,13},... | collective-permute-start | bytes 1572872 | tf_op jit(solution)/shard_map/ppermute | solution.py:321
  31.0 13.6 %collective-permute-start.13 = (bf16[512,512]{1,0:T(8,128)(2,1)S(1)}, bf16[512,512]{1,0:T(8,128)(2,1)S(1)}, u32[]{:S(2)}, u32[]{:S(2)}) collective-permute-start(bf16[512,512]{1,0:T(8,128)(2,1)S(1)} %collective-permute-done.5.refs_5_), channel_id=1, source_target_pairs={{0,16},{1,17},{2,18},{3,19},{4,20},{5,21},{6,22},{7,23},{8,24},{9,... | collective-permute-start | bytes 1572872 | tf_op jit(solution)/shard_map/ppermute | solution.py:321
  31.3 5.9 %collective-permute-start.10 = (s32[256]{0:T(256)S(1)}, s32[256]{0:T(256)S(1)}, u32[]{:S(2)}, u32[]{:S(2)}) collective-permute-start(s32[256]{0:T(256)S(1)} %copy-done.4), channel_id=1, source_target_pairs={{0,1},{1,2},{2,3},{3,4},{4,5},{5,6},{6,7},{7,8},{8,9},{9,10},{10,1... | collective-permute-start | bytes 3080 | tf_op jit(solution)/shard_map/ppermute | solution.py:31
  33.2 22.6 %collective-permute-start.12 = (bf16[512,512]{1,0:T(8,128)(2,1)S(1)}, bf16[512,512]{1,0:T(8,128)(2,1)S(1)}, u32[]{:S(2)}, u32[]{:S(2)}) collective-permute-start(bf16[512,512]{1,0:T(8,128)(2,1)S(1)} %collective-permute-done.6.refs_4_), channel_id=1, source_target_pairs={{0,16},{1,17},{2,18},{3,19},{4,20},{5,21},{6,22},{7,23},{8,24},{9,... | collective-permute-start | bytes 1572872 | tf_op jit(solution)/shard_map/ppermute | solution.py:321
  41.9 16.4 %collective-permute-start.15 = (bf16[512,512]{1,0:T(8,128)(2,1)S(1)}, bf16[512,512]{1,0:T(8,128)(2,1)S(1)}, u32[]{:S(2)}, u32[]{:S(2)}) collective-permute-start(bf16[512,512]{1,0:T(8,128)(2,1)S(1)} %collective-permute-done.7.refs_2_), channel_id=1, source_target_pairs={{0,4},{1,5},{4,8},{5,9},{8,12},{9,13},{12,14},{13,15},{14,10},{15,... | collective-permute-start | bytes 1572872 | tf_op jit(solution)/shard_map/ppermute | solution.py:321
  44.6 13.7 %collective-permute-start.16 = (bf16[512,512]{1,0:T(8,128)(2,1)S(1)}, bf16[512,512]{1,0:T(8,128)(2,1)S(1)}, u32[]{:S(2)}, u32[]{:S(2)}) collective-permute-start(bf16[512,512]{1,0:T(8,128)(2,1)S(1)} %collective-permute-done.13.refs_3_), channel_id=1, source_target_pairs={{0,2},{1,3},{4,0},{5,1},{8,4},{9,5},{12,8},{13,9},{14,12},{15,13},... | collective-permute-start | bytes 1572872 | tf_op jit(solution)/shard_map/ppermute | solution.py:321
  45.2 23.8 %collective-permute-start.4 = (bf16[512,512]{1,0:T(8,128)(2,1)S(1)}, bf16[512,512]{1,0:T(8,128)(2,1)S(1)}, u32[]{:S(2)}, u32[]{:S(2)}) collective-permute-start(bf16[512,512]{1,0:T(8,128)(2,1)S(1)} %collective-permute-done.1.refs_3_), channel_id=1, source_target_pairs={{0,16},{1,17},{2,18},{3,19},{4,20},{5,21},{6,22},{7,23},{8,24},{9,... | collective-permute-start | bytes 1572872 | tf_op jit(solution)/shard_map/ppermute | solution.py:321
  47.3 21.7 %collective-permute-start.11 = (bf16[512,512]{1,0:T(8,128)(2,1)S(1)}, bf16[512,512]{1,0:T(8,128)(2,1)S(1)}, u32[]{:S(2)}, u32[]{:S(2)}) collective-permute-start(bf16[512,512]{1,0:T(8,128)(2,1)S(1)} %collective-permute-done.8.refs_5_), channel_id=1, source_target_pairs={{0,2},{1,3},{4,0},{5,1},{8,4},{9,5},{12,8},{13,9},{14,12},{15,13},... | collective-permute-start | bytes 1572872 | tf_op jit(solution)/shard_map/ppermute | solution.py:321
  48.9 1.3 %copy-start.3 = (bf16[512,512]{1,0:T(8,128)(2,1)S(1)}, bf16[512,512]{1,0:T(8,128)(2,1)}, u32[]{:S(2)}) copy-start(bf16[512,512]{1,0:T(8,128)(2,1)} %refs_2_.3) | copy-start | bytes 1572868
  55.9 13.2 %collective-permute-start.14 = (bf16[512,512]{1,0:T(8,128)(2,1)S(1)}, bf16[512,512]{1,0:T(8,128)(2,1)S(1)}, u32[]{:S(2)}, u32[]{:S(2)}) collective-permute-start(bf16[512,512]{1,0:T(8,128)(2,1)S(1)} %collective-permute-done.12.refs_2_), channel_id=1, source_target_pairs={{0,4},{1,5},{4,8},{5,9},{8,12},{9,13},{12,14},{13,15},{14,10},{15,... | collective-permute-start | bytes 1572872 | tf_op jit(solution)/shard_map/ppermute | solution.py:321
  59.5 1.6 %collective-permute-start.17 = (f32[128,512]{1,0:T(8,128)S(1)}, f32[128,512]{1,0:T(8,128)S(1)}, u32[]{:S(2)}, u32[]{:S(2)}) collective-permute-start(f32[128,512]{1,0:T(8,128)S(1)} %get-tuple-element.84), channel_id=1, source_target_pairs={{0,1},{1,0},{2,3},{3,2},{4,5},{5,4},{6,7},{7,6},{8,9},{9,8},{10,11... | collective-permute-start | bytes 786440 | tf_op jit(solution)/shard_map/ppermute | solution.py:324
  59.6 1.9 %collective-permute-start.18 = (f32[128,512]{1,0:T(8,128)S(1)}, f32[128,512]{1,0:T(8,128)S(1)}, u32[]{:S(2)}, u32[]{:S(2)}) collective-permute-start(f32[128,512]{1,0:T(8,128)S(1)} %get-tuple-element.85), channel_id=1, source_target_pairs={{0,1},{1,0},{2,3},{3,2},{4,5},{5,4},{6,7},{7,6},{8,9},{9,8},{10,11... | collective-permute-start | bytes 786440 | tf_op jit(solution)/shard_map/ppermute | solution.py:324
  61.7 3.2 %copy-start = (bf16[256,4096]{1,0:T(8,128)(2,1)S(1)}, bf16[256,4096]{1,0:T(8,128)(2,1)}, u32[]{:S(2)}) copy-start(bf16[256,4096]{1,0:T(8,128)(2,1)} %q_ref.3) | copy-start | bytes 6291460
  61.8 7.3 %collective-permute-start.19 = (bf16[128,512]{1,0:T(8,128)(2,1)S(1)}, bf16[128,512]{1,0:T(8,128)(2,1)S(1)}, u32[]{:S(2)}, u32[]{:S(2)}) collective-permute-start(bf16[128,512]{1,0:T(8,128)(2,1)S(1)} %get-tuple-element.88), channel_id=1, source_target_pairs={{0,1},{1,2},{2,3},{3,4},{4,5},{5,6},{6,7},{7,8},{8,9},{9,10},{10,1... | collective-permute-start | bytes 393224 | tf_op jit(solution)/shard_map/ppermute | solution.py:31
  70.6 2.5 %collective-permute-start.20 = (f32[256,512]{1,0:T(8,128)S(1)}, f32[256,512]{1,0:T(8,128)S(1)}, u32[]{:S(2)}, u32[]{:S(2)}) collective-permute-start(f32[256,512]{1,0:T(8,128)S(1)} %get-tuple-element.91), channel_id=1, source_target_pairs={{0,1},{1,0},{2,3},{3,2},{4,5},{5,4},{6,7},{7,6},{8,9},{9,8},{10,11... | collective-permute-start | bytes 1572872 | tf_op jit(solution)/shard_map/ppermute | solution.py:324
  73.2 7.2 %collective-permute-start.21 = (bf16[128,512]{1,0:T(8,128)(2,1)S(1)}, bf16[128,512]{1,0:T(8,128)(2,1)S(1)}, u32[]{:S(2)}, u32[]{:S(2)}) collective-permute-start(bf16[128,512]{1,0:T(8,128)(2,1)S(1)} %get-tuple-element.96), channel_id=1, source_target_pairs={{0,1},{1,2},{2,3},{3,4},{4,5},{5,6},{6,7},{7,8},{8,9},{9,10},{10,1... | collective-permute-start | bytes 393224 | tf_op jit(solution)/shard_map/ppermute | solution.py:31

commit v6 on v5

--- a/solution.py
+++ b/solution.py
@@ -327,32 +327,32 @@
     mine, theirs = normalise(ids, hidden, norm_gain)
     other = [swap(t) for t in theirs]
     k1, v1 = send(key_weight, key_way), send(value_weight, value_way)
-    k1, v1, mine = after(k1, v1, mine)
+    behind = from_behind(segment_ids, "dp", 1)
+    k1, mine, behind = after(k1, mine, behind)
     k2, v2 = send(k1, key_way), send(v1, value_way)
-    yk1 = send(k1, other_group)
-    k2, v2 = after(k2, v2)
+    k1b, yv1 = send(key_weight, value_way), send(v1, other_group)
     k3, v3 = send(k2, key_way), send(v2, value_way)
-    yk2, yv2 = send(k2, other_group), send(v2, other_group)
-    yv1 = send(v1, other_group)
-
-    behind = from_behind(segment_ids, "dp", 1)
-    key_part = project(ids, (0, -1, 1, -2), mine, other, [key_weight, k1, yk1, k2])
-    k3, v3, key_part, behind = after(k3, v3, key_part, behind)
-    k4, k3b = send(k3, key_way), send(yk2, value_way)
+    yk2 = send(k2, other_group)
+
+    key_part = project(ids, (0, -1, -2), mine, other, [key_weight, k1, k2])
+    k3, yv1, key_part = after(k3, yv1, key_part)
+    k4, yk3 = send(k3, key_way), send(k3, other_group)
+    cos, sin, bias = tables(ids, segment_ids, behind)
+    key_part = project(ids, (-3, 2, 1), mine, other, [k3, yk2, k1b], key_part)
+    v3, key_part, cos, sin, bias = after(v3, key_part, cos, sin, bias)
     v4 = send(v3, value_way)
-    key_part = project(ids, (-3, 2), mine, other, [k3, yk2], key_part)
-    value_part = project(ids, (0, 1, 2, 3), mine, other, [value_weight, v1, v2, v3])
-    cos, sin, bias = tables(ids, segment_ids, behind)
-    yv2, key_part, value_part, cos, sin, bias = after(yv2, key_part, value_part, cos, sin, bias)
-    v3b = send(yv2, key_way)
-
-    own_k, *other_k = project(ids, (-4, 3), mine, other, [k4, k3b], key_part, 2)
-    keys, tail = finish(keys_kernel, "keys", own_k, cos, sin, *[swap(o) for o in other_k])
+    yk3, v3y = after(yk3, v3)
+    yv3 = send(v3y, other_group)
+    v2b = send(yv1, key_way)
+    value_part = project(ids, (0, 1, 2, -1, 3), mine, other, [value_weight, v1, v2, yv1, v3])
+
+    own_k, *other_k = project(ids, (-4, 3), mine, other, [k4, yk3], key_part, 2)
+    *other_k, value_part = after(*[swap(o) for o in other_k], value_part)
+    keys, tail = finish(keys_kernel, "keys", own_k, cos, sin, *other_k)
     prev_keys = from_behind(tail, "dp", 1)
     p1 = softmax_weights(queries, 1, keys, 0, keys, 1, bias)
-    value_part = project(ids, (-2,), mine, other, [yv2], value_part)
     value_part, p1, prev_keys = after(value_part, p1, prev_keys)
-    own_v, other_v = project(ids, (-1, 4, -3), mine, other, [yv1, v4, v3b], value_part)
+    own_v, other_v = project(ids, (4, -2, -3), mine, other, [v4, v2b, yv3], value_part)
     p0 = softmax_weights(queries, 0, prev_keys, 0, keys, 0, bias)
     other_v, p0 = after(swap(other_v), p0)
     values, tail = finish(values_kernel, "values", own_v, other_v)

time: 82.2 us -> 78.8 us (0.959)
  waiting for transfers between devices: 35 us -> 31.5 us
    ppermute x14, waiting for transfers between devices: 28.4 us -> 21.6 us  [send(): return lax.ppermute(value, both, way)]
    ppermute x3, waiting for transfers between devices: 5.24 us -> 9.94 us  [from_behind(): lax.ppermute(value, axis, [(source, source + steps) for source in range(i...]
    ppermute x5, waiting for transfers between devices: 1.41 us -> 0.01 us  [swap(): return lax.ppermute(value, 'dp', other_core)]
    pallas_call x6 -> x5, Pallas kernels: 8.57 us -> 7.87 us  [project(): pl.pallas_call(functools.partial(project_kernel, steps, len(others), len(...]
  transfers between devices with their start and end apart: 22 -> 22, of which waited for: 13 -> 7; matrix products, arithmetic and copies ran while one was open for 1% -> 1% of each run, Pallas kernels for 22% -> 22%
where the time goes in v6:
time: 78.8 us; the launch traced here: 78.4 us
  waiting for transfers between devices  31.5 us (40%)
  starting transfers between devices  23.1 us (29%)
  Pallas kernels  20.6 us (26%)
  local copies, waits for them, and re-layouts  2.94 us (4%)
    ppermute x14, waiting for transfers between devices, send(): return lax.ppermute(value, both, way)  21.6 us
    ppermute x14, starting transfers between devices, send(): return lax.ppermute(value, both, way)  15.5 us
    ppermute x3, waiting for transfers between devices, from_behind(): lax.ppermute(value, axis, [(source, source + steps) for source in range(i...  9.94 us
    pallas_call x5, Pallas kernels, project(): pl.pallas_call(functools.partial(project_kernel, steps, len(others), len(...  7.87 us
    ppermute x3, starting transfers between devices, from_behind(): lax.ppermute(value, axis, [(source, source + steps) for source in range(i...  6.2 us
    pallas_call x2, Pallas kernels, softmax_weights(): pl.pallas_call(scores_kernel, grid=(heads,), in_specs=[pl.BlockSpec((rows...  4.84 us
    pallas_call x1, Pallas kernels, normalise(): pl.pallas_call(norm_kernel, grid_spec=pltpu.PrefetchScalarGridSpec(num_sc...  3.22 us
    pallas_call x2, Pallas kernels, contexts(): pl.pallas_call(functools.partial(context_kernel, block), grid=(1,), in_sp...  3.2 us
  transfers between devices with their start and end apart: 22, of which 7 were waited for; matrix products, arithmetic and copies ran while one was open for 1% of the time, Pallas kernels for 22%

profile of v6, /device:TPU:8, one launch (start us, length us, event | category | flops | bytes accessed | tf_op | source)
XLA Modules:
  0.0 78.4 jit_solution(17421809106311222972)
XLA Ops:
  0.0 1.6 %collective-permute-start = (bf16[512,512]{1,0:T(8,128)(2,1)}, bf16[512,512]{1,0:T(8,128)(2,1)S(1)}, u32[]{:S(2)}, u32[]{:S(2)}) collective-permute-start(bf16[512,512]{1,0:T(8,128)(2,1)} %refs_2_.2), channel_id=1, source_target_pairs={{0,4},{1,5},{4,8},{5,9},{8,12},{9,13},{12,14},{13,15},{14,10},{15,... | collective-permute-start | bytes 1572872 | tf_op jit(solution)/shard_map/ppermute | solution.py:321
  2.0 0.7 reshape.9.g_ref
  2.8 2.2 %copy-done.1 = bf16[256,8192]{1,0:T(8,128)(2,1)S(1)} copy-done((bf16[256,8192]{1,0:T(8,128)(2,1)S(1)}, bf16[256,8192]{1,0:T(8,128)(2,1)}, u32[]{:S(2)}) %copy-start.1) | copy-done | bytes 4194328
  5.0 3.2 %norm.1 = (bf16[256,4096]{1,0:T(8,128)(2,1)S(1)}, bf16[128,4096]{1,0:T(8,128)(2,1)S(1)}, bf16[128,4096]{1,0:T(8,128)(2,1)S(1)}) custom-call(s32[2]{0:T(128)S(1)} %pad_add_fusion.core_ref.ids_ref, bf16[256,8192]{1,0:T(8,128)(2,1)S(1)} %copy-done.1, bf16[1,8192]{1,0:T(2,128)(2,1)S(1)} %reshape.9.g_ref), custom_call_target="tpu_custom_call" | custom-call | flops 16777216 | bytes 8388608 | tf_op jit(solution)/shard_map/norm/pallas_call | solution.py:63
  8.3 0.5 collective-permute-start.3
  8.8 2.0 %collective-permute-start.1 = (s32[256]{0:T(256)S(1)}, s32[256]{0:T(256)S(1)}, u32[]{:S(2)}, u32[]{:S(2)}) collective-permute-start(s32[256]{0:T(256)S(1)} %copy-done.4), channel_id=1, source_target_pairs={{0,1},{1,2},{2,3},{3,4},{4,5},{5,6},{6,7},{7,8},{8,9},{9,10},{10,1... | collective-permute-start | bytes 3080 | tf_op jit(solution)/shard_map/ppermute | solution.py:31
  10.8 3.9 %collective-permute-done.1 = s32[256]{0:T(256)S(1)} collective-permute-done((s32[256]{0:T(256)S(1)}, s32[256]{0:T(256)S(1)}, u32[]{:S(2)}, u32[]{:S(2)}) %collective-permute-start.1) | collective-permute-done | bytes 1056 | tf_op jit(solution)/shard_map/ppermute | solution.py:31
  14.7 1.6 %collective-permute-start.7 = (bf16[512,512]{1,0:T(8,128)(2,1)S(1)}, bf16[512,512]{1,0:T(8,128)(2,1)S(1)}, u32[]{:S(2)}, u32[]{:S(2)}) collective-permute-start(bf16[512,512]{1,0:T(8,128)(2,1)S(1)} %collective-permute-done.refs_3_), channel_id=1, source_target_pairs={{0,4},{1,5},{4,8},{5,9},{8,12},{9,13},{12,14},{13,15},{14,10},{15,... | collective-permute-start | bytes 1572872 | tf_op jit(solution)/shard_map/ppermute | solution.py:321
  16.7 1.5 %collective-permute-start.9 = (bf16[512,512]{1,0:T(8,128)(2,1)S(1)}, bf16[512,512]{1,0:T(8,128)(2,1)S(1)}, u32[]{:S(2)}, u32[]{:S(2)}) collective-permute-start(bf16[512,512]{1,0:T(8,128)(2,1)S(1)} %collective-permute-done.4.refs_3_), channel_id=1, source_target_pairs={{0,16},{1,17},{2,18},{3,19},{4,20},{5,21},{6,22},{7,23},{8,24},{9,... | collective-permute-start | bytes 1572872 | tf_op jit(solution)/shard_map/ppermute | solution.py:321
  18.3 8.6 %collective-permute-done.7.refs_4_ = bf16[512,512]{1,0:T(8,128)(2,1)S(1)} collective-permute-done((bf16[512,512]{1,0:T(8,128)(2,1)S(1)}, bf16[512,512]{1,0:T(8,128)(2,1)S(1)}, u32[]{:S(2)}, u32[]{:S(2)}) %collective-permute-start.7) | collective-permute-done | bytes 524320 | tf_op jit(solution)/shard_map/ppermute | solution.py:321
  26.9 1.6 %collective-permute-start.8 = (bf16[512,512]{1,0:T(8,128)(2,1)S(1)}, bf16[512,512]{1,0:T(8,128)(2,1)S(1)}, u32[]{:S(2)}, u32[]{:S(2)}) collective-permute-start(bf16[512,512]{1,0:T(8,128)(2,1)S(1)} %collective-permute-done.7.refs_4_), channel_id=1, source_target_pairs={{0,4},{1,5},{4,8},{5,9},{8,12},{9,13},{12,14},{13,15},{14,10},{15,... | collective-permute-start | bytes 1572872 | tf_op jit(solution)/shard_map/ppermute | solution.py:321
  28.9 1.5 %collective-permute-start.10 = (bf16[512,512]{1,0:T(8,128)(2,1)S(1)}, bf16[512,512]{1,0:T(8,128)(2,1)S(1)}, u32[]{:S(2)}, u32[]{:S(2)}) collective-permute-start(bf16[512,512]{1,0:T(8,128)(2,1)S(1)} %collective-permute-done.7.refs_4_), channel_id=1, source_target_pairs={{0,16},{1,17},{2,18},{3,19},{4,20},{5,21},{6,22},{7,23},{8,24},{9,... | collective-permute-start | bytes 1572872 | tf_op jit(solution)/shard_map/ppermute | solution.py:321
  30.9 1.5 %project.5 = (f32[256,512]{1,0:T(8,128)S(1)}, f32[256,512]{1,0:T(8,128)S(1)}) custom-call(s32[2]{0:T(128)S(1)} %pad_add_fusion.core_ref.ids_ref, bf16[256,4096]{1,0:T(8,128)(2,1)S(1)} %get-tuple-element.52.xa_ref, bf16[128,4096]{1,0:T(8,128)(2,1)S(1)} %collective-permute-done.2.refs_0_, bf16[128,4096]{1,0:T(8,128)(2,1)S(1)} %collective-permute-done.3.refs_1_, ...), custom_call_target="tpu_custom_call" | custom-call | flops 805306368 | bytes 5767168 | tf_op jit(solution)/shard_map/project/pallas_call | solution.py:124
  32.4 5.7 %collective-permute-done.8.refs_2_ = bf16[512,512]{1,0:T(8,128)(2,1)S(1)} collective-permute-done((bf16[512,512]{1,0:T(8,128)(2,1)S(1)}, bf16[512,512]{1,0:T(8,128)(2,1)S(1)}, u32[]{:S(2)}, u32[]{:S(2)}) %collective-permute-start.8) | collective-permute-done | bytes 524320 | tf_op jit(solution)/shard_map/ppermute | solution.py:321
  38.2 2.1 %collective-permute-start.14 = (bf16[512,512]{1,0:T(8,128)(2,1)S(1)}, bf16[512,512]{1,0:T(8,128)(2,1)S(1)}, u32[]{:S(2)}, u32[]{:S(2)}) collective-permute-start(bf16[512,512]{1,0:T(8,128)(2,1)S(1)} %collective-permute-done.8.refs_2_), channel_id=1, source_target_pairs={{0,16},{1,17},{2,18},{3,19},{4,20},{5,21},{6,22},{7,23},{8,24},{9,... | collective-permute-start | bytes 1572872 | tf_op jit(solution)/shard_map/ppermute | solution.py:321
  40.3 1.6 %collective-permute-start.16 = (bf16[512,512]{1,0:T(8,128)(2,1)S(1)}, bf16[512,512]{1,0:T(8,128)(2,1)S(1)}, u32[]{:S(2)}, u32[]{:S(2)}) collective-permute-start(bf16[512,512]{1,0:T(8,128)(2,1)S(1)} %collective-permute-done.8.refs_2_), channel_id=1, source_target_pairs={{0,4},{1,5},{4,8},{5,9},{8,12},{9,13},{12,14},{13,15},{14,10},{15,... | collective-permute-start | bytes 1572872 | tf_op jit(solution)/shard_map/ppermute | solution.py:321
  41.9 1.2 %tables.1 = (f32[256,128]{1,0:T(8,128)S(1)}, f32[256,128]{1,0:T(8,128)S(1)}, f32[2,128,256]{2,1,0:T(8,128)S(1)}) custom-call(s32[2]{0:T(128)S(1)} %pad_add_fusion.core_ref.ids_ref, s32[1,256]{1,0:T(1,128)S(1)} %bitcast.4, s32[1,256]{1,0:T(1,128)S(1)} %bitcast.5, f32[1,128]{1,0:T(1,128)S(1)} %copy-done.5), custom_call_target="tpu_custom_call" | custom-call | flops 1310720 | bytes 524288 | tf_op jit(solution)/shard_map/tables/pallas_call | solution.py:164
  43.3 1.5 %project.6 = (f32[256,512]{1,0:T(8,128)S(1)}, f32[256,512]{1,0:T(8,128)S(1)}) custom-call(s32[2]{0:T(128)S(1)} %pad_add_fusion.core_ref.ids_ref, bf16[256,4096]{1,0:T(8,128)(2,1)S(1)} %get-tuple-element.52.xa_ref, bf16[128,4096]{1,0:T(8,128)(2,1)S(1)} %collective-permute-done.2.refs_0_, bf16[128,4096]{1,0:T(8,128)(2,1)S(1)} %collective-permute-done.3.refs_1_, ...), custom_call_target="tpu_custom_call" | custom-call | flops 805306368 | bytes 5767168 | tf_op jit(solution)/shard_map/project/pallas_call | solution.py:124
  44.9 6.9 %collective-permute-done.6.refs_6_ = bf16[512,512]{1,0:T(8,128)(2,1)S(1)} collective-permute-done((bf16[512,512]{1,0:T(8,128)(2,1)S(1)}, bf16[512,512]{1,0:T(8,128)(2,1)S(1)}, u32[]{:S(2)}, u32[]{:S(2)}) %collective-permute-start.6) | collective-permute-done | bytes 524320 | tf_op jit(solution)/shard_map/ppermute | solution.py:321
  52.1 1.7 %collective-permute-start.13 = (bf16[512,512]{1,0:T(8,128)(2,1)S(1)}, bf16[512,512]{1,0:T(8,128)(2,1)S(1)}, u32[]{:S(2)}, u32[]{:S(2)}) collective-permute-start(bf16[512,512]{1,0:T(8,128)(2,1)S(1)} %collective-permute-done.9.refs_5_), channel_id=1, source_target_pairs={{0,4},{1,5},{4,8},{5,9},{8,12},{9,13},{12,14},{13,15},{14,10},{15,... | collective-permute-start | bytes 1572872 | tf_op jit(solution)/shard_map/ppermute | solution.py:321
  54.0 1.3 %project.7 = (f32[256,512]{1,0:T(8,128)S(1)}, f32[128,512]{1,0:T(8,128)S(1)}, f32[128,512]{1,0:T(8,128)S(1)}) custom-call(s32[2]{0:T(128)S(1)} %pad_add_fusion.core_ref.ids_ref, bf16[256,4096]{1,0:T(8,128)(2,1)S(1)} %get-tuple-element.52.xa_ref, bf16[128,4096]{1,0:T(8,128)(2,1)S(1)} %collective-permute-done.2.refs_0_, ...), custom_call_target="tpu_custom_call" | custom-call | flops 536870912 | bytes 5242880 | tf_op jit(solution)/shard_map/project/pallas_call | solution.py:124
  55.4 0.5 collective-permute-start.18
  55.9 2.1 %project.8 = (f32[256,512]{1,0:T(8,128)S(1)}, f32[256,512]{1,0:T(8,128)S(1)}) custom-call(s32[2]{0:T(128)S(1)} %pad_add_fusion.core_ref.ids_ref, bf16[256,4096]{1,0:T(8,128)(2,1)S(1)} %get-tuple-element.52.xa_ref, bf16[128,4096]{1,0:T(8,128)(2,1)S(1)} %collective-permute-done.2.refs_0_, bf16[128,4096]{1,0:T(8,128)(2,1)S(1)} %collective-permute-done.3.refs_1_, ...), custom_call_target="tpu_custom_call" | custom-call | flops 1342177280 | bytes 6815744 | tf_op jit(solution)/shard_map/project/pallas_call | solution.py:124
  58.2 2.0 %collective-permute-start.19 = (bf16[128,512]{1,0:T(8,128)(2,1)S(1)}, bf16[128,512]{1,0:T(8,128)(2,1)S(1)}, u32[]{:S(2)}, u32[]{:S(2)}) collective-permute-start(bf16[128,512]{1,0:T(8,128)(2,1)S(1)} %get-tuple-element.86), channel_id=1, source_target_pairs={{0,1},{1,2},{2,3},{3,4},{4,5},{5,6},{6,7},{7,8},{8,9},{9,10},{10,1... | collective-permute-start | bytes 393224 | tf_op jit(solution)/shard_map/ppermute | solution.py:31
  60.2 2.4 %scores.2.p_ref = bf16[4,1024,256]{2,1,0:T(8,128)(2,1)S(1)} custom-call(bf16[256,4096]{1,0:T(8,128)(2,1)S(1)} %copy-done, bf16[256,512]{1,0:T(8,128)(2,1)S(1)} %get-tuple-element.84.ka_ref.kb_ref, bf16[256,512]{1,0:T(8,128)(2,1)S(1)} %get-tuple-element.84.ka_ref.kb_ref, f32[2,128,256]{2,1,0:T(8,128)S(1)} %get-tuple-element.85.bias_ref), custom_call_target="tpu_custom_call" | custom-call | flops 268435456 | bytes 3145728 | tf_op jit(solution)/shard_map/scores/pallas_call | solution.py:231
  62.6 2.7 %collective-permute-done.19.ka_ref = bf16[128,512]{1,0:T(8,128)(2,1)S(1)} collective-permute-done((bf16[128,512]{1,0:T(8,128)(2,1)S(1)}, bf16[128,512]{1,0:T(8,128)(2,1)S(1)}, u32[]{:S(2)}, u32[]{:S(2)}) %collective-permute-start.19) | collective-permute-done | bytes 131104 | tf_op jit(solution)/shard_map/ppermute | solution.py:31
  65.4 1.5 %project.9 = (f32[256,512]{1,0:T(8,128)S(1)}, f32[256,512]{1,0:T(8,128)S(1)}) custom-call(s32[2]{0:T(128)S(1)} %pad_add_fusion.core_ref.ids_ref, bf16[256,4096]{1,0:T(8,128)(2,1)S(1)} %get-tuple-element.52.xa_ref, bf16[128,4096]{1,0:T(8,128)(2,1)S(1)} %collective-permute-done.2.refs_0_, bf16[128,4096]{1,0:T(8,128)(2,1)S(1)} %collective-permute-done.3.refs_1_, ...), custom_call_target="tpu_custom_call" | custom-call | flops 805306368 | bytes 5767168 | tf_op jit(solution)/shard_map/project/pallas_call | solution.py:124
  67.2 2.4 %scores.3.p_ref = bf16[4,1024,256]{2,1,0:T(8,128)(2,1)S(1)} custom-call(bf16[256,4096]{1,0:T(8,128)(2,1)S(1)} %copy-done, bf16[128,512]{1,0:T(8,128)(2,1)S(1)} %collective-permute-done.19.ka_ref, bf16[256,512]{1,0:T(8,128)(2,1)S(1)} %get-tuple-element.84.ka_ref.kb_ref, f32[2,128,256]{2,1,0:T(8,128)S(1)} %get-tuple-element.85.bias_ref), custom_call_target="tpu_custom_call" | custom-call | flops 268435456 | bytes 3145728 | tf_op jit(solution)/shard_map/scores/pallas_call | solution.py:231
  69.7 2.2 %collective-permute-start.21 = (bf16[128,512]{1,0:T(8,128)(2,1)S(1)}, bf16[128,512]{1,0:T(8,128)(2,1)S(1)}, u32[]{:S(2)}, u32[]{:S(2)}) collective-permute-start(bf16[128,512]{1,0:T(8,128)(2,1)S(1)} %get-tuple-element.94), channel_id=1, source_target_pairs={{0,1},{1,2},{2,3},{3,4},{4,5},{5,6},{6,7},{7,8},{8,9},{9,10},{10,1... | collective-permute-start | bytes 393224 | tf_op jit(solution)/shard_map/ppermute | solution.py:31
  71.9 1.6 %context.2.refs_0_ = bf16[256,4096]{1,0:T(8,128)(2,1)} custom-call(bf16[4,1024,256]{2,1,0:T(8,128)(2,1)S(1)} %scores.2.p_ref, bf16[256,512]{1,0:T(8,128)(2,1)S(1)} %get-tuple-element.95.va_ref.vb_ref, bf16[256,512]{1,0:T(8,128)(2,1)S(1)} %get-tuple-element.95.va_ref.vb_ref), custom_call_target="tpu_custom_call" | custom-call | flops 268435456 | bytes 3145728 | tf_op jit(solution)/shard_map/context/pallas_call | solution.py:274
  73.5 3.3 %collective-permute-done.21.va_ref = bf16[128,512]{1,0:T(8,128)(2,1)S(1)} collective-permute-done((bf16[128,512]{1,0:T(8,128)(2,1)S(1)}, bf16[128,512]{1,0:T(8,128)(2,1)S(1)}, u32[]{:S(2)}, u32[]{:S(2)}) %collective-permute-start.21) | collective-permute-done | bytes 131104 | tf_op jit(solution)/shard_map/ppermute | solution.py:31
  76.8 1.6 %context.3 = bf16[256,4096]{1,0:T(8,128)(2,1)} custom-call(bf16[4,1024,256]{2,1,0:T(8,128)(2,1)S(1)} %scores.3.p_ref, bf16[128,512]{1,0:T(8,128)(2,1)S(1)} %collective-permute-done.21.va_ref, bf16[256,512]{1,0:T(8,128)(2,1)S(1)} %get-tuple-element.95.va_ref.vb_ref, bf16[256,4096]{1,0:T(8,128)(2,1)} %context.2.refs_0_), custom_call_target="tpu_custom_call", output_to_operand_aliasing={{}: (3, {})} | custom-call | flops 268435456 | bytes 3145728 | tf_op jit(solution)/shard_map/context/pallas_call | solution.py:274
  (39 shorter events, 3.5 us)
Async XLA Ops:
  0.0 14.7 %collective-permute-start = (bf16[512,512]{1,0:T(8,128)(2,1)}, bf16[512,512]{1,0:T(8,128)(2,1)S(1)}, u32[]{:S(2)}, u32[]{:S(2)}) collective-permute-start(bf16[512,512]{1,0:T(8,128)(2,1)} %refs_2_.2), channel_id=1, source_target_pairs={{0,4},{1,5},{4,8},{5,9},{8,12},{9,13},{12,14},{13,15},{14,10},{15,... | collective-permute-start | bytes 1572872 | tf_op jit(solution)/shard_map/ppermute | solution.py:321
  1.6 14.7 %collective-permute-start.4 = (bf16[512,512]{1,0:T(8,128)(2,1)}, bf16[512,512]{1,0:T(8,128)(2,1)S(1)}, u32[]{:S(2)}, u32[]{:S(2)}) collective-permute-start(bf16[512,512]{1,0:T(8,128)(2,1)} %refs_2_.3), channel_id=1, source_target_pairs={{0,2},{1,3},{4,0},{5,1},{8,4},{9,5},{12,8},{13,9},{14,12},{15,13},... | collective-permute-start | bytes 1572872 | tf_op jit(solution)/shard_map/ppermute | solution.py:321
  2.8 2.2 %copy-start.1 = (bf16[256,8192]{1,0:T(8,128)(2,1)S(1)}, bf16[256,8192]{1,0:T(8,128)(2,1)}, u32[]{:S(2)}) copy-start(bf16[256,8192]{1,0:T(8,128)(2,1)} %h_ref.1) | copy-start | bytes 12582916
  5.0 3.8 %copy-start.4 = (s32[256]{0:T(256)S(1)}, s32[256]{0:T(256)}, u32[]{:S(2)}) copy-start(s32[256]{0:T(256)} %param.12) | copy-start | bytes 3076
  5.0 23.4 %copy-start.2 = (bf16[512,512]{1,0:T(8,128)(2,1)S(1)}, bf16[512,512]{1,0:T(8,128)(2,1)}, u32[]{:S(2)}) copy-start(bf16[512,512]{1,0:T(8,128)(2,1)} %refs_2_.2) | copy-start | bytes 1572868
  8.3 20.7 %collective-permute-start.2 = (bf16[128,4096]{1,0:T(8,128)(2,1)S(1)}, bf16[128,4096]{1,0:T(8,128)(2,1)S(1)}, u32[]{:S(2)}, u32[]{:S(2)}) collective-permute-start(bf16[128,4096]{1,0:T(8,128)(2,1)S(1)} %get-tuple-element.53), channel_id=1, source_target_pairs={{0,1},{1,0},{2,3},{3,2},{4,5},{5,4},{6,7},{7,6},{8,9},{9,8},{10,11... | collective-permute-start | bytes 3145736 | tf_op jit(solution)/shard_map/ppermute | solution.py:324
  8.3 22.1 %collective-permute-start.3 = (bf16[128,4096]{1,0:T(8,128)(2,1)S(1)}, bf16[128,4096]{1,0:T(8,128)(2,1)S(1)}, u32[]{:S(2)}, u32[]{:S(2)}) collective-permute-start(bf16[128,4096]{1,0:T(8,128)(2,1)S(1)} %get-tuple-element.54), channel_id=1, source_target_pairs={{0,1},{1,0},{2,3},{3,2},{4,5},{5,4},{6,7},{7,6},{8,9},{9,8},{10,11... | collective-permute-start | bytes 3145736 | tf_op jit(solution)/shard_map/ppermute | solution.py:324
  8.8 5.8 %collective-permute-start.1 = (s32[256]{0:T(256)S(1)}, s32[256]{0:T(256)S(1)}, u32[]{:S(2)}, u32[]{:S(2)}) collective-permute-start(s32[256]{0:T(256)S(1)} %copy-done.4), channel_id=1, source_target_pairs={{0,1},{1,2},{2,3},{3,4},{4,5},{5,6},{6,7},{7,8},{8,9},{9,10},{10,1... | collective-permute-start | bytes 3080 | tf_op jit(solution)/shard_map/ppermute | solution.py:31
  14.7 27.2 %copy-start.5 = (f32[1,128]{1,0:T(1,128)S(1)}, f32[1,128]{1,0:T(1,128)}, u32[]{:S(2)}) copy-start(f32[1,128]{1,0:T(1,128)} %constant.11.clone.freq_ref) | copy-start | bytes 1540
  14.7 12.2 %collective-permute-start.7 = (bf16[512,512]{1,0:T(8,128)(2,1)S(1)}, bf16[512,512]{1,0:T(8,128)(2,1)S(1)}, u32[]{:S(2)}, u32[]{:S(2)}) collective-permute-start(bf16[512,512]{1,0:T(8,128)(2,1)S(1)} %collective-permute-done.refs_3_), channel_id=1, source_target_pairs={{0,4},{1,5},{4,8},{5,9},{8,12},{9,13},{12,14},{13,15},{14,10},{15,... | collective-permute-start | bytes 1572872 | tf_op jit(solution)/shard_map/ppermute | solution.py:321
  16.3 12.2 %collective-permute-start.5 = (bf16[512,512]{1,0:T(8,128)(2,1)S(1)}, bf16[512,512]{1,0:T(8,128)(2,1)S(1)}, u32[]{:S(2)}, u32[]{:S(2)}) collective-permute-start(bf16[512,512]{1,0:T(8,128)(2,1)S(1)} %collective-permute-done.4.refs_3_), channel_id=1, source_target_pairs={{0,2},{1,3},{4,0},{5,1},{8,4},{9,5},{12,8},{13,9},{14,12},{15,13},... | collective-permute-start | bytes 1572872 | tf_op jit(solution)/shard_map/ppermute | solution.py:321
  16.7 15.7 %collective-permute-start.9 = (bf16[512,512]{1,0:T(8,128)(2,1)S(1)}, bf16[512,512]{1,0:T(8,128)(2,1)S(1)}, u32[]{:S(2)}, u32[]{:S(2)}) collective-permute-start(bf16[512,512]{1,0:T(8,128)(2,1)S(1)} %collective-permute-done.4.refs_3_), channel_id=1, source_target_pairs={{0,16},{1,17},{2,18},{3,19},{4,20},{5,21},{6,22},{7,23},{8,24},{9,... | collective-permute-start | bytes 1572872 | tf_op jit(solution)/shard_map/ppermute | solution.py:321
  26.9 11.3 %collective-permute-start.8 = (bf16[512,512]{1,0:T(8,128)(2,1)S(1)}, bf16[512,512]{1,0:T(8,128)(2,1)S(1)}, u32[]{:S(2)}, u32[]{:S(2)}) collective-permute-start(bf16[512,512]{1,0:T(8,128)(2,1)S(1)} %collective-permute-done.7.refs_4_), channel_id=1, source_target_pairs={{0,4},{1,5},{4,8},{5,9},{8,12},{9,13},{12,14},{13,15},{14,10},{15,... | collective-permute-start | bytes 1572872 | tf_op jit(solution)/shard_map/ppermute | solution.py:321
  28.5 14.9 %collective-permute-start.11 = (bf16[512,512]{1,0:T(8,128)(2,1)S(1)}, bf16[512,512]{1,0:T(8,128)(2,1)S(1)}, u32[]{:S(2)}, u32[]{:S(2)}) collective-permute-start(bf16[512,512]{1,0:T(8,128)(2,1)S(1)} %copy-done.2), channel_id=1, source_target_pairs={{0,2},{1,3},{4,0},{5,1},{8,4},{9,5},{12,8},{13,9},{14,12},{15,13},... | collective-permute-start | bytes 1572872 | tf_op jit(solution)/shard_map/ppermute | solution.py:321
  28.9 14.4 %collective-permute-start.10 = (bf16[512,512]{1,0:T(8,128)(2,1)S(1)}, bf16[512,512]{1,0:T(8,128)(2,1)S(1)}, u32[]{:S(2)}, u32[]{:S(2)}) collective-permute-start(bf16[512,512]{1,0:T(8,128)(2,1)S(1)} %collective-permute-done.7.refs_4_), channel_id=1, source_target_pairs={{0,16},{1,17},{2,18},{3,19},{4,20},{5,21},{6,22},{7,23},{8,24},{9,... | collective-permute-start | bytes 1572872 | tf_op jit(solution)/shard_map/ppermute | solution.py:321
  30.5 21.3 %collective-permute-start.6 = (bf16[512,512]{1,0:T(8,128)(2,1)S(1)}, bf16[512,512]{1,0:T(8,128)(2,1)S(1)}, u32[]{:S(2)}, u32[]{:S(2)}) collective-permute-start(bf16[512,512]{1,0:T(8,128)(2,1)S(1)} %collective-permute-done.5.refs_4_), channel_id=1, source_target_pairs={{0,2},{1,3},{4,0},{5,1},{8,4},{9,5},{12,8},{13,9},{14,12},{15,13},... | collective-permute-start | bytes 1572872 | tf_op jit(solution)/shard_map/ppermute | solution.py:321
  38.2 15.6 %collective-permute-start.14 = (bf16[512,512]{1,0:T(8,128)(2,1)S(1)}, bf16[512,512]{1,0:T(8,128)(2,1)S(1)}, u32[]{:S(2)}, u32[]{:S(2)}) collective-permute-start(bf16[512,512]{1,0:T(8,128)(2,1)S(1)} %collective-permute-done.8.refs_2_), channel_id=1, source_target_pairs={{0,16},{1,17},{2,18},{3,19},{4,20},{5,21},{6,22},{7,23},{8,24},{9,... | collective-permute-start | bytes 1572872 | tf_op jit(solution)/shard_map/ppermute | solution.py:321
  40.3 13.8 %collective-permute-start.16 = (bf16[512,512]{1,0:T(8,128)(2,1)S(1)}, bf16[512,512]{1,0:T(8,128)(2,1)S(1)}, u32[]{:S(2)}, u32[]{:S(2)}) collective-permute-start(bf16[512,512]{1,0:T(8,128)(2,1)S(1)} %collective-permute-done.8.refs_2_), channel_id=1, source_target_pairs={{0,4},{1,5},{4,8},{5,9},{8,12},{9,13},{12,14},{13,15},{14,10},{15,... | collective-permute-start | bytes 1572872 | tf_op jit(solution)/shard_map/ppermute | solution.py:321
  51.8 4.1 %copy-start.3 = (bf16[512,512]{1,0:T(8,128)(2,1)S(1)}, bf16[512,512]{1,0:T(8,128)(2,1)}, u32[]{:S(2)}) copy-start(bf16[512,512]{1,0:T(8,128)(2,1)} %refs_2_.3) | copy-start | bytes 1572868
  51.8 13.6 %collective-permute-start.12 = (bf16[512,512]{1,0:T(8,128)(2,1)S(1)}, bf16[512,512]{1,0:T(8,128)(2,1)S(1)}, u32[]{:S(2)}, u32[]{:S(2)}) collective-permute-start(bf16[512,512]{1,0:T(8,128)(2,1)S(1)} %collective-permute-done.6.refs_6_), channel_id=1, source_target_pairs={{0,2},{1,3},{4,0},{5,1},{8,4},{9,5},{12,8},{13,9},{14,12},{15,13},... | collective-permute-start | bytes 1572872 | tf_op jit(solution)/shard_map/ppermute | solution.py:321
  52.1 13.3 %collective-permute-start.13 = (bf16[512,512]{1,0:T(8,128)(2,1)S(1)}, bf16[512,512]{1,0:T(8,128)(2,1)S(1)}, u32[]{:S(2)}, u32[]{:S(2)}) collective-permute-start(bf16[512,512]{1,0:T(8,128)(2,1)S(1)} %collective-permute-done.9.refs_5_), channel_id=1, source_target_pairs={{0,4},{1,5},{4,8},{5,9},{8,12},{9,13},{12,14},{13,15},{14,10},{15,... | collective-permute-start | bytes 1572872 | tf_op jit(solution)/shard_map/ppermute | solution.py:321
  53.8 11.6 %collective-permute-start.15 = (bf16[512,512]{1,0:T(8,128)(2,1)S(1)}, bf16[512,512]{1,0:T(8,128)(2,1)S(1)}, u32[]{:S(2)}, u32[]{:S(2)}) collective-permute-start(bf16[512,512]{1,0:T(8,128)(2,1)S(1)} %collective-permute-done.6.refs_6_), channel_id=1, source_target_pairs={{0,16},{1,17},{2,18},{3,19},{4,20},{5,21},{6,22},{7,23},{8,24},{9,... | collective-permute-start | bytes 1572872 | tf_op jit(solution)/shard_map/ppermute | solution.py:321
  55.3 2.6 %collective-permute-start.17 = (f32[128,512]{1,0:T(8,128)S(1)}, f32[128,512]{1,0:T(8,128)S(1)}, u32[]{:S(2)}, u32[]{:S(2)}) collective-permute-start(f32[128,512]{1,0:T(8,128)S(1)} %get-tuple-element.73), channel_id=1, source_target_pairs={{0,1},{1,0},{2,3},{3,2},{4,5},{5,4},{6,7},{7,6},{8,9},{9,8},{10,11... | collective-permute-start | bytes 786440 | tf_op jit(solution)/shard_map/ppermute | solution.py:324
  55.4 2.6 %collective-permute-start.18 = (f32[128,512]{1,0:T(8,128)S(1)}, f32[128,512]{1,0:T(8,128)S(1)}, u32[]{:S(2)}, u32[]{:S(2)}) collective-permute-start(f32[128,512]{1,0:T(8,128)S(1)} %get-tuple-element.74), channel_id=1, source_target_pairs={{0,1},{1,0},{2,3},{3,2},{4,5},{5,4},{6,7},{7,6},{8,9},{9,8},{10,11... | collective-permute-start | bytes 786440 | tf_op jit(solution)/shard_map/ppermute | solution.py:324
  55.9 4.3 %copy-start = (bf16[256,4096]{1,0:T(8,128)(2,1)S(1)}, bf16[256,4096]{1,0:T(8,128)(2,1)}, u32[]{:S(2)}) copy-start(bf16[256,4096]{1,0:T(8,128)(2,1)} %q_ref.3) | copy-start | bytes 6291460
  58.2 7.2 %collective-permute-start.19 = (bf16[128,512]{1,0:T(8,128)(2,1)S(1)}, bf16[128,512]{1,0:T(8,128)(2,1)S(1)}, u32[]{:S(2)}, u32[]{:S(2)}) collective-permute-start(bf16[128,512]{1,0:T(8,128)(2,1)S(1)} %get-tuple-element.86), channel_id=1, source_target_pairs={{0,1},{1,2},{2,3},{3,4},{4,5},{5,6},{6,7},{7,8},{8,9},{9,10},{10,1... | collective-permute-start | bytes 393224 | tf_op jit(solution)/shard_map/ppermute | solution.py:31
  66.9 2.7 %collective-permute-start.20 = (f32[256,512]{1,0:T(8,128)S(1)}, f32[256,512]{1,0:T(8,128)S(1)}, u32[]{:S(2)}, u32[]{:S(2)}) collective-permute-start(f32[256,512]{1,0:T(8,128)S(1)} %get-tuple-element.89), channel_id=1, source_target_pairs={{0,1},{1,0},{2,3},{3,2},{4,5},{5,4},{6,7},{7,6},{8,9},{9,8},{10,11... | collective-permute-start | bytes 1572872 | tf_op jit(solution)/shard_map/ppermute | solution.py:324
  69.7 7.2 %collective-permute-start.21 = (bf16[128,512]{1,0:T(8,128)(2,1)S(1)}, bf16[128,512]{1,0:T(8,128)(2,1)S(1)}, u32[]{:S(2)}, u32[]{:S(2)}) collective-permute-start(bf16[128,512]{1,0:T(8,128)(2,1)S(1)} %get-tuple-element.94), channel_id=1, source_target_pairs={{0,1},{1,2},{2,3},{3,4},{4,5},{5,6},{6,7},{7,8},{8,9},{9,10},{10,1... | collective-permute-start | bytes 393224 | tf_op jit(solution)/shard_map/ppermute | solution.py:31

commit v7 on v6

--- a/solution.py
+++ b/solution.py
@@ -1,4 +1,5 @@
 import functools
+import math
 
 import jax
 import jax.numpy as jnp
@@ -99,13 +100,11 @@
     others, refs = refs[:parts], refs[parts:]
     weights, refs = refs[:count], refs[count:]
     before, outs = refs[:carried], refs[carried:]
-    total = None
-    for j in range(count):
-        depth = weights[j].shape[0]
-        columns = pl.ds(pl.multiple_of(block_at(ids_ref, steps[j]) * depth, depth), depth)
-        x = jnp.concatenate([ref[:, columns] for ref in (xa_ref, *others)], axis=0)
-        part = jnp.dot(x, weights[j][...], preferred_element_type=F32)
-        total = part if total is None else total + part
+    depth = weights[0].shape[0]
+    columns = [pl.ds(pl.multiple_of(block_at(ids_ref, step) * depth, depth), depth) for step in steps]
+    x = [jnp.concatenate([ref[:, c] for c in columns], axis=1) for ref in (xa_ref, *others)]
+    w = jnp.concatenate([ref[...] for ref in weights], axis=0)
+    total = jnp.dot(jnp.concatenate(x, axis=0), w, preferred_element_type=F32)
     held = jnp.concatenate([ref[...] for ref in before], axis=0) if carried else None
     total = held + total if carried else total
     at = 0
@@ -178,7 +177,7 @@
 
 def keys_kernel(a_ref, cos_ref, sin_ref, *refs):
     cos, sin = cos_ref[...], sin_ref[...]
-    others, (out_ref, tail_ref) = refs[:-2], refs[-2:]
+    others, (out_ref, head_ref, tail_ref) = refs[:-3], refs[-3:]
     rows = out_ref.shape[0]
     for h in range(a_ref.shape[1] // HD):
         at = slice(h * HD, (h + 1) * HD)
@@ -186,14 +185,16 @@
         raw = (a_ref[:, at] + b).astype(BF16).astype(F32)
         out = (raw * cos + pltpu.roll(raw, HD // 2, 1) * sin).astype(BF16)
         out_ref[:, at] = out
+        head_ref[:, at] = out[:REACH]
         tail_ref[:, at] = out[rows - REACH :]
 
 
 def values_kernel(a_ref, *refs):
-    others, (out_ref, tail_ref) = refs[:-2], refs[-2:]
+    others, (out_ref, head_ref, tail_ref) = refs[:-3], refs[-3:]
     rows = out_ref.shape[0]
     out = (a_ref[...] + jnp.concatenate([ref[...] for ref in others], axis=0)).astype(BF16)
     out_ref[...] = out
+    head_ref[...] = out[:REACH]
     tail_ref[...] = out[rows - REACH :]
 
 
@@ -204,6 +205,7 @@
         out_shape=[
             jax.ShapeDtypeStruct((rows, feats), BF16),
             jax.ShapeDtypeStruct((REACH, feats), BF16),
+            jax.ShapeDtypeStruct((REACH, feats), BF16),
         ],
         compiler_params=params(),
         cost_estimate=cost(6 * rows * feats, 10 * rows * feats),
@@ -211,33 +213,34 @@
     )(*operands)
 
 
-def scores_kernel(q_ref, ka_ref, kb_ref, bias_ref, out_ref):
-    rows = q_ref.shape[0]
-    keys = jnp.concatenate([ka_ref[...], kb_ref[...]], axis=0)
-    bias = bias_ref[0]
-    scale = 1.0 / HD**0.5
-    for j in range(GROUP):
-        q = q_ref[:, j * HD : (j + 1) * HD]
-        s = lax.dot_general(q, keys, (((1,), (1,)), ((), ())), preferred_element_type=F32)
-        s = s * scale + bias
-        e = jnp.exp(s - jnp.max(s, axis=-1, keepdims=True))
-        w = e * (1.0 / jnp.sum(e, axis=-1, keepdims=True))
-        out_ref[0, j * rows : (j + 1) * rows, :] = w.astype(BF16)
-
-
-def softmax_weights(queries, block, keys_a, block_a, keys_b, block_b, bias):
+def scores_kernel(block, q_ref, ka_ref, kb_ref, bias_ref, out_ref):
+    rows = REACH
+    bias = bias_ref[block]
+    ones = jnp.ones((2 * rows, rows), BF16)
+    scale = math.log2(math.e) / HD**0.5
+    for h in range(out_ref.shape[0]):
+        at = slice(h * HD, (h + 1) * HD)
+        keys = jnp.concatenate([ka_ref[:rows, at], kb_ref[-rows:, at]], axis=0)
+        for j in range(GROUP):
+            column = (h * GROUP + j) * HD
+            q = q_ref[block * rows : (block + 1) * rows, column : column + HD]
+            s = lax.dot_general(q, keys, (((1,), (1,)), ((), ())), preferred_element_type=F32)
+            s = s * scale + bias
+            e = jnp.exp2(s - jnp.max(s, axis=-1, keepdims=True))
+            total = jnp.dot(e.astype(BF16), ones, preferred_element_type=F32)
+            inverse = 1.0 / total
+            w = e * jnp.concatenate([inverse, inverse], axis=1)
+            out_ref[h, j * rows : (j + 1) * rows, :] = w.astype(BF16)
+
+
+def softmax_weights(block, queries, keys_a, keys_b, bias):
     rows = REACH
     heads = keys_a.shape[1] // HD
+    whole = pl.BlockSpec(memory_space=pltpu.VMEM)
     return pl.pallas_call(
-        scores_kernel,
-        grid=(heads,),
-        in_specs=[
-            pl.BlockSpec((rows, GROUP * HD), lambda h: (block, h)),
-            pl.BlockSpec((rows, HD), lambda h: (block_a, h)),
-            pl.BlockSpec((rows, HD), lambda h: (block_b, h)),
-            pl.BlockSpec((1, rows, 2 * rows), lambda h: (block, 0, 0)),
-        ],
-        out_specs=pl.BlockSpec((1, GROUP * rows, 2 * rows), lambda h: (h, 0, 0)),
+        functools.partial(scores_kernel, block),
+        in_specs=[whole] * 4,
+        out_specs=whole,
         out_shape=jax.ShapeDtypeStruct((heads, GROUP * rows, 2 * rows), BF16),
         compiler_params=params(),
         cost_estimate=cost(
@@ -249,12 +252,12 @@
 
 def context_kernel(block, p_ref, va_ref, vb_ref, *refs):
     out_ref, held, sems = refs[-3:]
-    rows = va_ref.shape[0]
+    rows = held.shape[0]
     width = GROUP * HD
     copies = []
     for h in range(p_ref.shape[0]):
         at = slice(h * HD, (h + 1) * HD)
-        values = jnp.concatenate([va_ref[:, at], vb_ref[:, at]], axis=0)
+        values = jnp.concatenate([va_ref[:rows, at], vb_ref[-rows:, at]], axis=0)
         c = jnp.dot(p_ref[h], values, preferred_element_type=F32).astype(BF16)
         for j in range(GROUP):
             held[:, h * width + j * HD : h * width + (j + 1) * HD] = c[j * rows : (j + 1) * rows]
@@ -266,20 +269,15 @@
         copy.wait()
 
 
-def contexts(block, weights, values_a, block_a, values_b, block_b, out=None):
+def contexts(block, weights, values_a, values_b, out=None):
     heads, _, span = weights.shape
     rows = REACH
     feats = heads * HD
+    whole = pl.BlockSpec(memory_space=pltpu.VMEM)
     more = () if out is None else (out,)
     return pl.pallas_call(
         functools.partial(context_kernel, block),
-        grid=(1,),
-        in_specs=[
-            pl.BlockSpec(memory_space=pltpu.VMEM),
-            pl.BlockSpec((rows, feats), lambda i: (block_a, 0)),
-            pl.BlockSpec((rows, feats), lambda i: (block_b, 0)),
-        ]
-        + [pl.BlockSpec(memory_space=pl.ANY)] * len(more),
+        in_specs=[whole] * 3 + [pl.BlockSpec(memory_space=pl.ANY)] * len(more),
         out_specs=pl.BlockSpec(memory_space=pl.ANY),
         out_shape=jax.ShapeDtypeStruct((2 * rows, GROUP * feats), BF16),
         scratch_shapes=[
@@ -348,17 +346,17 @@
 
     own_k, *other_k = project(ids, (-4, 3), mine, other, [k4, yk3], key_part, 2)
     *other_k, value_part = after(*[swap(o) for o in other_k], value_part)
-    keys, tail = finish(keys_kernel, "keys", own_k, cos, sin, *other_k)
+    keys, head_keys, tail = finish(keys_kernel, "keys", own_k, cos, sin, *other_k)
     prev_keys = from_behind(tail, "dp", 1)
-    p1 = softmax_weights(queries, 1, keys, 0, keys, 1, bias)
+    p1 = softmax_weights(1, queries, keys, keys, bias)
     value_part, p1, prev_keys = after(value_part, p1, prev_keys)
     own_v, other_v = project(ids, (4, -2, -3), mine, other, [v4, v2b, yv3], value_part)
-    p0 = softmax_weights(queries, 0, prev_keys, 0, keys, 0, bias)
+    p0 = softmax_weights(0, queries, prev_keys, head_keys, bias)
     other_v, p0 = after(swap(other_v), p0)
-    values, tail = finish(values_kernel, "values", own_v, other_v)
+    values, head_values, tail = finish(values_kernel, "values", own_v, other_v)
     prev_values = from_behind(tail, "dp", 1)
-    later = contexts(1, p1, values, 0, values, 1)
-    return contexts(0, p0, prev_values, 0, values, 0, later)
+    later = contexts(1, p1, values, values)
+    return contexts(0, p0, prev_values, head_values, later)
 
 
 def rotary(block, positions):

time: 78.8 us -> 78.3 us (level)
  Pallas kernels: 20.6 us -> 19.4 us
    pallas_call x4, Pallas kernels: 8.04 us -> 6.8 us  [the longest x2 3.6 us: softmax_weights(): pl.pallas_call(functools.partial(scores_kernel, block), in_specs=[whole]...]
  transfers between devices with their start and end apart: 22 -> 22, of which waited for: 7 -> 8; matrix products, arithmetic and copies ran while one was open for 1% -> 1% of each run, Pallas kernels for 22% -> 21%
where the time goes in v7:
time: 78.3 us; the launch traced here: 77.7 us
  waiting for transfers between devices  32.1 us (41%)
  starting transfers between devices  23 us (29%)
  Pallas kernels  19.4 us (25%)
  local copies, waits for them, and re-layouts  2.94 us (4%)
    ppermute x14, waiting for transfers between devices, send(): return lax.ppermute(value, both, way)  21.6 us
    ppermute x14, starting transfers between devices, send(): return lax.ppermute(value, both, way)  15.5 us
    ppermute x3, waiting for transfers between devices, from_behind(): lax.ppermute(value, axis, [(source, source + steps) for source in range(i...  10.5 us
    pallas_call x5, Pallas kernels, project(): pl.pallas_call(functools.partial(project_kernel, steps, len(others), len(...  7.87 us
    ppermute x3, starting transfers between devices, from_behind(): lax.ppermute(value, axis, [(source, source + steps) for source in range(i...  6.3 us
    pallas_call x2, Pallas kernels, softmax_weights(): pl.pallas_call(functools.partial(scores_kernel, block), in_specs=[whole]...  3.6 us
    pallas_call x1, Pallas kernels, normalise(): pl.pallas_call(norm_kernel, grid_spec=pltpu.PrefetchScalarGridSpec(num_sc...  3.22 us
    pallas_call x2, Pallas kernels, contexts(): pl.pallas_call(functools.partial(context_kernel, block), in_specs=[whole]...  3.2 us
  transfers between devices with their start and end apart: 22, of which 8 were waited for; matrix products, arithmetic and copies ran while one was open for 1% of the time, Pallas kernels for 21%

profile of v7, /device:TPU:8, one launch (start us, length us, event | category | flops | bytes accessed | tf_op | source)
XLA Modules:
  0.0 77.7 jit_solution(16542181085511878590)
XLA Ops:
  0.0 1.6 %collective-permute-start = (bf16[512,512]{1,0:T(8,128)(2,1)}, bf16[512,512]{1,0:T(8,128)(2,1)S(1)}, u32[]{:S(2)}, u32[]{:S(2)}) collective-permute-start(bf16[512,512]{1,0:T(8,128)(2,1)} %refs_2_.2), channel_id=1, source_target_pairs={{0,4},{1,5},{4,8},{5,9},{8,12},{9,13},{12,14},{13,15},{14,10},{15,... | collective-permute-start | bytes 1572872 | tf_op jit(solution)/shard_map/ppermute | solution.py:319
  2.0 0.7 reshape.9.g_ref
  2.8 2.2 %copy-done.1 = bf16[256,8192]{1,0:T(8,128)(2,1)S(1)} copy-done((bf16[256,8192]{1,0:T(8,128)(2,1)S(1)}, bf16[256,8192]{1,0:T(8,128)(2,1)}, u32[]{:S(2)}) %copy-start.1) | copy-done | bytes 4194328
  5.0 3.2 %norm.1 = (bf16[256,4096]{1,0:T(8,128)(2,1)S(1)}, bf16[128,4096]{1,0:T(8,128)(2,1)S(1)}, bf16[128,4096]{1,0:T(8,128)(2,1)S(1)}) custom-call(s32[2]{0:T(128)S(1)} %pad_add_fusion.core_ref.ids_ref, bf16[256,8192]{1,0:T(8,128)(2,1)S(1)} %copy-done.1, bf16[1,8192]{1,0:T(2,128)(2,1)S(1)} %reshape.9.g_ref), custom_call_target="tpu_custom_call" | custom-call | flops 16777216 | bytes 8388608 | tf_op jit(solution)/shard_map/norm/pallas_call | solution.py:64
  8.3 0.5 collective-permute-start.3
  8.8 2.0 %collective-permute-start.1 = (s32[256]{0:T(256)S(1)}, s32[256]{0:T(256)S(1)}, u32[]{:S(2)}, u32[]{:S(2)}) collective-permute-start(s32[256]{0:T(256)S(1)} %copy-done.4), channel_id=1, source_target_pairs={{0,1},{1,2},{2,3},{3,4},{4,5},{5,6},{6,7},{7,8},{8,9},{9,10},{10,1... | collective-permute-start | bytes 3080 | tf_op jit(solution)/shard_map/ppermute | solution.py:32
  10.8 3.9 %collective-permute-done.1 = s32[256]{0:T(256)S(1)} collective-permute-done((s32[256]{0:T(256)S(1)}, s32[256]{0:T(256)S(1)}, u32[]{:S(2)}, u32[]{:S(2)}) %collective-permute-start.1) | collective-permute-done | bytes 1056 | tf_op jit(solution)/shard_map/ppermute | solution.py:32
  14.7 1.6 %collective-permute-start.7 = (bf16[512,512]{1,0:T(8,128)(2,1)S(1)}, bf16[512,512]{1,0:T(8,128)(2,1)S(1)}, u32[]{:S(2)}, u32[]{:S(2)}) collective-permute-start(bf16[512,512]{1,0:T(8,128)(2,1)S(1)} %collective-permute-done.refs_3_), channel_id=1, source_target_pairs={{0,4},{1,5},{4,8},{5,9},{8,12},{9,13},{12,14},{13,15},{14,10},{15,... | collective-permute-start | bytes 1572872 | tf_op jit(solution)/shard_map/ppermute | solution.py:319
  16.7 1.5 %collective-permute-start.9 = (bf16[512,512]{1,0:T(8,128)(2,1)S(1)}, bf16[512,512]{1,0:T(8,128)(2,1)S(1)}, u32[]{:S(2)}, u32[]{:S(2)}) collective-permute-start(bf16[512,512]{1,0:T(8,128)(2,1)S(1)} %collective-permute-done.4.refs_3_), channel_id=1, source_target_pairs={{0,16},{1,17},{2,18},{3,19},{4,20},{5,21},{6,22},{7,23},{8,24},{9,... | collective-permute-start | bytes 1572872 | tf_op jit(solution)/shard_map/ppermute | solution.py:319
  18.3 8.6 %collective-permute-done.7.refs_4_ = bf16[512,512]{1,0:T(8,128)(2,1)S(1)} collective-permute-done((bf16[512,512]{1,0:T(8,128)(2,1)S(1)}, bf16[512,512]{1,0:T(8,128)(2,1)S(1)}, u32[]{:S(2)}, u32[]{:S(2)}) %collective-permute-start.7) | collective-permute-done | bytes 524320 | tf_op jit(solution)/shard_map/ppermute | solution.py:319
  26.9 1.6 %collective-permute-start.8 = (bf16[512,512]{1,0:T(8,128)(2,1)S(1)}, bf16[512,512]{1,0:T(8,128)(2,1)S(1)}, u32[]{:S(2)}, u32[]{:S(2)}) collective-permute-start(bf16[512,512]{1,0:T(8,128)(2,1)S(1)} %collective-permute-done.7.refs_4_), channel_id=1, source_target_pairs={{0,4},{1,5},{4,8},{5,9},{8,12},{9,13},{12,14},{13,15},{14,10},{15,... | collective-permute-start | bytes 1572872 | tf_op jit(solution)/shard_map/ppermute | solution.py:319
  28.9 1.5 %collective-permute-start.10 = (bf16[512,512]{1,0:T(8,128)(2,1)S(1)}, bf16[512,512]{1,0:T(8,128)(2,1)S(1)}, u32[]{:S(2)}, u32[]{:S(2)}) collective-permute-start(bf16[512,512]{1,0:T(8,128)(2,1)S(1)} %collective-permute-done.7.refs_4_), channel_id=1, source_target_pairs={{0,16},{1,17},{2,18},{3,19},{4,20},{5,21},{6,22},{7,23},{8,24},{9,... | collective-permute-start | bytes 1572872 | tf_op jit(solution)/shard_map/ppermute | solution.py:319
  30.9 1.5 %project.5 = (f32[256,512]{1,0:T(8,128)S(1)}, f32[256,512]{1,0:T(8,128)S(1)}) custom-call(s32[2]{0:T(128)S(1)} %pad_add_fusion.core_ref.ids_ref, bf16[256,4096]{1,0:T(8,128)(2,1)S(1)} %get-tuple-element.54.xa_ref, bf16[128,4096]{1,0:T(8,128)(2,1)S(1)} %collective-permute-done.2.refs_0_, bf16[128,4096]{1,0:T(8,128)(2,1)S(1)} %collective-permute-done.3.refs_1_, ...), custom_call_target="tpu_custom_call" | custom-call | flops 805306368 | bytes 5767168 | tf_op jit(solution)/shard_map/project/pallas_call | solution.py:123
  32.4 5.7 %collective-permute-done.8.refs_2_ = bf16[512,512]{1,0:T(8,128)(2,1)S(1)} collective-permute-done((bf16[512,512]{1,0:T(8,128)(2,1)S(1)}, bf16[512,512]{1,0:T(8,128)(2,1)S(1)}, u32[]{:S(2)}, u32[]{:S(2)}) %collective-permute-start.8) | collective-permute-done | bytes 524320 | tf_op jit(solution)/shard_map/ppermute | solution.py:319
  38.2 2.1 %collective-permute-start.14 = (bf16[512,512]{1,0:T(8,128)(2,1)S(1)}, bf16[512,512]{1,0:T(8,128)(2,1)S(1)}, u32[]{:S(2)}, u32[]{:S(2)}) collective-permute-start(bf16[512,512]{1,0:T(8,128)(2,1)S(1)} %collective-permute-done.8.refs_2_), channel_id=1, source_target_pairs={{0,16},{1,17},{2,18},{3,19},{4,20},{5,21},{6,22},{7,23},{8,24},{9,... | collective-permute-start | bytes 1572872 | tf_op jit(solution)/shard_map/ppermute | solution.py:319
  40.3 1.6 %collective-permute-start.16 = (bf16[512,512]{1,0:T(8,128)(2,1)S(1)}, bf16[512,512]{1,0:T(8,128)(2,1)S(1)}, u32[]{:S(2)}, u32[]{:S(2)}) collective-permute-start(bf16[512,512]{1,0:T(8,128)(2,1)S(1)} %collective-permute-done.8.refs_2_), channel_id=1, source_target_pairs={{0,4},{1,5},{4,8},{5,9},{8,12},{9,13},{12,14},{13,15},{14,10},{15,... | collective-permute-start | bytes 1572872 | tf_op jit(solution)/shard_map/ppermute | solution.py:319
  41.9 1.2 %tables.1 = (f32[256,128]{1,0:T(8,128)S(1)}, f32[256,128]{1,0:T(8,128)S(1)}, f32[2,128,256]{2,1,0:T(8,128)S(1)}) custom-call(s32[2]{0:T(128)S(1)} %pad_add_fusion.core_ref.ids_ref, s32[1,256]{1,0:T(1,128)S(1)} %bitcast.4, s32[1,256]{1,0:T(1,128)S(1)} %bitcast.5, f32[1,128]{1,0:T(1,128)S(1)} %copy-done.5), custom_call_target="tpu_custom_call" | custom-call | flops 1310720 | bytes 524288 | tf_op jit(solution)/shard_map/tables/pallas_call | solution.py:163
  43.3 1.5 %project.6 = (f32[256,512]{1,0:T(8,128)S(1)}, f32[256,512]{1,0:T(8,128)S(1)}) custom-call(s32[2]{0:T(128)S(1)} %pad_add_fusion.core_ref.ids_ref, bf16[256,4096]{1,0:T(8,128)(2,1)S(1)} %get-tuple-element.54.xa_ref, bf16[128,4096]{1,0:T(8,128)(2,1)S(1)} %collective-permute-done.2.refs_0_, bf16[128,4096]{1,0:T(8,128)(2,1)S(1)} %collective-permute-done.3.refs_1_, ...), custom_call_target="tpu_custom_call" | custom-call | flops 805306368 | bytes 5767168 | tf_op jit(solution)/shard_map/project/pallas_call | solution.py:123
  44.9 6.9 %collective-permute-done.6.refs_6_ = bf16[512,512]{1,0:T(8,128)(2,1)S(1)} collective-permute-done((bf16[512,512]{1,0:T(8,128)(2,1)S(1)}, bf16[512,512]{1,0:T(8,128)(2,1)S(1)}, u32[]{:S(2)}, u32[]{:S(2)}) %collective-permute-start.6) | collective-permute-done | bytes 524320 | tf_op jit(solution)/shard_map/ppermute | solution.py:319
  52.1 1.7 %collective-permute-start.13 = (bf16[512,512]{1,0:T(8,128)(2,1)S(1)}, bf16[512,512]{1,0:T(8,128)(2,1)S(1)}, u32[]{:S(2)}, u32[]{:S(2)}) collective-permute-start(bf16[512,512]{1,0:T(8,128)(2,1)S(1)} %collective-permute-done.9.refs_5_), channel_id=1, source_target_pairs={{0,4},{1,5},{4,8},{5,9},{8,12},{9,13},{12,14},{13,15},{14,10},{15,... | collective-permute-start | bytes 1572872 | tf_op jit(solution)/shard_map/ppermute | solution.py:319
  54.0 1.3 %project.7 = (f32[256,512]{1,0:T(8,128)S(1)}, f32[128,512]{1,0:T(8,128)S(1)}, f32[128,512]{1,0:T(8,128)S(1)}) custom-call(s32[2]{0:T(128)S(1)} %pad_add_fusion.core_ref.ids_ref, bf16[256,4096]{1,0:T(8,128)(2,1)S(1)} %get-tuple-element.54.xa_ref, bf16[128,4096]{1,0:T(8,128)(2,1)S(1)} %collective-permute-done.2.refs_0_, ...), custom_call_target="tpu_custom_call" | custom-call | flops 536870912 | bytes 5242880 | tf_op jit(solution)/shard_map/project/pallas_call | solution.py:123
  55.4 0.5 collective-permute-start.18
  55.9 2.1 %project.8 = (f32[256,512]{1,0:T(8,128)S(1)}, f32[256,512]{1,0:T(8,128)S(1)}) custom-call(s32[2]{0:T(128)S(1)} %pad_add_fusion.core_ref.ids_ref, bf16[256,4096]{1,0:T(8,128)(2,1)S(1)} %get-tuple-element.54.xa_ref, bf16[128,4096]{1,0:T(8,128)(2,1)S(1)} %collective-permute-done.2.refs_0_, bf16[128,4096]{1,0:T(8,128)(2,1)S(1)} %collective-permute-done.3.refs_1_, ...), custom_call_target="tpu_custom_call" | custom-call | flops 1342177280 | bytes 6815744 | tf_op jit(solution)/shard_map/project/pallas_call | solution.py:123
  58.2 2.0 %collective-permute-start.19 = (bf16[128,512]{1,0:T(8,128)(2,1)S(1)}, bf16[128,512]{1,0:T(8,128)(2,1)S(1)}, u32[]{:S(2)}, u32[]{:S(2)}) collective-permute-start(bf16[128,512]{1,0:T(8,128)(2,1)S(1)} %get-tuple-element.88), channel_id=1, source_target_pairs={{0,1},{1,2},{2,3},{3,4},{4,5},{5,6},{6,7},{7,8},{8,9},{9,10},{10,1... | collective-permute-start | bytes 393224 | tf_op jit(solution)/shard_map/ppermute | solution.py:32
  60.2 1.8 %scores.2.p_ref = bf16[4,1024,256]{2,1,0:T(8,128)(2,1)S(1)} custom-call(bf16[256,4096]{1,0:T(8,128)(2,1)S(1)} %copy-done, bf16[256,512]{1,0:T(8,128)(2,1)S(1)} %get-tuple-element.86.ka_ref.kb_ref, bf16[256,512]{1,0:T(8,128)(2,1)S(1)} %get-tuple-element.86.ka_ref.kb_ref, f32[2,128,256]{2,1,0:T(8,128)S(1)} %get-tuple-element.87.bias_ref), custom_call_target="tpu_custom_call" | custom-call | flops 268435456 | bytes 3145728 | tf_op jit(solution)/shard_map/scores/pallas_call | solution.py:240
  62.0 3.4 %collective-permute-done.19.ka_ref = bf16[128,512]{1,0:T(8,128)(2,1)S(1)} collective-permute-done((bf16[128,512]{1,0:T(8,128)(2,1)S(1)}, bf16[128,512]{1,0:T(8,128)(2,1)S(1)}, u32[]{:S(2)}, u32[]{:S(2)}) %collective-permute-start.19) | collective-permute-done | bytes 131104 | tf_op jit(solution)/shard_map/ppermute | solution.py:32
  65.4 1.5 %project.9 = (f32[256,512]{1,0:T(8,128)S(1)}, f32[256,512]{1,0:T(8,128)S(1)}) custom-call(s32[2]{0:T(128)S(1)} %pad_add_fusion.core_ref.ids_ref, bf16[256,4096]{1,0:T(8,128)(2,1)S(1)} %get-tuple-element.54.xa_ref, bf16[128,4096]{1,0:T(8,128)(2,1)S(1)} %collective-permute-done.2.refs_0_, bf16[128,4096]{1,0:T(8,128)(2,1)S(1)} %collective-permute-done.3.refs_1_, ...), custom_call_target="tpu_custom_call" | custom-call | flops 805306368 | bytes 5767168 | tf_op jit(solution)/shard_map/project/pallas_call | solution.py:123
  67.0 1.8 %scores.3.p_ref = bf16[4,1024,256]{2,1,0:T(8,128)(2,1)S(1)} custom-call(bf16[256,4096]{1,0:T(8,128)(2,1)S(1)} %copy-done, bf16[128,512]{1,0:T(8,128)(2,1)S(1)} %collective-permute-done.19.ka_ref, bf16[128,512]{1,0:T(8,128)(2,1)S(1)} %get-tuple-element.93.kb_ref, f32[2,128,256]{2,1,0:T(8,128)S(1)} %get-tuple-element.87.bias_ref), custom_call_target="tpu_custom_call" | custom-call | flops 268435456 | bytes 3145728 | tf_op jit(solution)/shard_map/scores/pallas_call | solution.py:240
  69.0 2.3 %collective-permute-start.21 = (bf16[128,512]{1,0:T(8,128)(2,1)S(1)}, bf16[128,512]{1,0:T(8,128)(2,1)S(1)}, u32[]{:S(2)}, u32[]{:S(2)}) collective-permute-start(bf16[128,512]{1,0:T(8,128)(2,1)S(1)} %get-tuple-element.97), channel_id=1, source_target_pairs={{0,1},{1,2},{2,3},{3,4},{4,5},{5,6},{6,7},{7,8},{8,9},{9,10},{10,1... | collective-permute-start | bytes 393224 | tf_op jit(solution)/shard_map/ppermute | solution.py:32
  71.3 1.6 %context.2.refs_0_ = bf16[256,4096]{1,0:T(8,128)(2,1)} custom-call(bf16[4,1024,256]{2,1,0:T(8,128)(2,1)S(1)} %scores.2.p_ref, bf16[256,512]{1,0:T(8,128)(2,1)S(1)} %get-tuple-element.100.va_ref.vb_ref, bf16[256,512]{1,0:T(8,128)(2,1)S(1)} %get-tuple-element.100.va_ref.vb_ref), custom_call_target="tpu_custom_call" | custom-call | flops 268435456 | bytes 3145728 | tf_op jit(solution)/shard_map/context/pallas_call | solution.py:278
  72.9 3.2 %collective-permute-done.21.va_ref = bf16[128,512]{1,0:T(8,128)(2,1)S(1)} collective-permute-done((bf16[128,512]{1,0:T(8,128)(2,1)S(1)}, bf16[128,512]{1,0:T(8,128)(2,1)S(1)}, u32[]{:S(2)}, u32[]{:S(2)}) %collective-permute-start.21) | collective-permute-done | bytes 131104 | tf_op jit(solution)/shard_map/ppermute | solution.py:32
  76.1 1.6 %context.3 = bf16[256,4096]{1,0:T(8,128)(2,1)} custom-call(bf16[4,1024,256]{2,1,0:T(8,128)(2,1)S(1)} %scores.3.p_ref, bf16[128,512]{1,0:T(8,128)(2,1)S(1)} %collective-permute-done.21.va_ref, bf16[128,512]{1,0:T(8,128)(2,1)S(1)} %get-tuple-element.98.vb_ref, bf16[256,4096]{1,0:T(8,128)(2,1)} %context.2.refs_0_), custom_call_target="tpu_custom_call", output_to_operand_aliasing={{}: (3, {})} | custom-call | flops 268435456 | bytes 3145728 | tf_op jit(solution)/shard_map/context/pallas_call | solution.py:278
  (39 shorter events, 3.4 us)
Async XLA Ops:
  0.0 14.7 %collective-permute-start = (bf16[512,512]{1,0:T(8,128)(2,1)}, bf16[512,512]{1,0:T(8,128)(2,1)S(1)}, u32[]{:S(2)}, u32[]{:S(2)}) collective-permute-start(bf16[512,512]{1,0:T(8,128)(2,1)} %refs_2_.2), channel_id=1, source_target_pairs={{0,4},{1,5},{4,8},{5,9},{8,12},{9,13},{12,14},{13,15},{14,10},{15,... | collective-permute-start | bytes 1572872 | tf_op jit(solution)/shard_map/ppermute | solution.py:319
  1.6 14.7 %collective-permute-start.4 = (bf16[512,512]{1,0:T(8,128)(2,1)}, bf16[512,512]{1,0:T(8,128)(2,1)S(1)}, u32[]{:S(2)}, u32[]{:S(2)}) collective-permute-start(bf16[512,512]{1,0:T(8,128)(2,1)} %refs_2_.3), channel_id=1, source_target_pairs={{0,2},{1,3},{4,0},{5,1},{8,4},{9,5},{12,8},{13,9},{14,12},{15,13},... | collective-permute-start | bytes 1572872 | tf_op jit(solution)/shard_map/ppermute | solution.py:319
  2.8 2.2 %copy-start.1 = (bf16[256,8192]{1,0:T(8,128)(2,1)S(1)}, bf16[256,8192]{1,0:T(8,128)(2,1)}, u32[]{:S(2)}) copy-start(bf16[256,8192]{1,0:T(8,128)(2,1)} %h_ref.1) | copy-start | bytes 12582916
  5.0 3.8 %copy-start.4 = (s32[256]{0:T(256)S(1)}, s32[256]{0:T(256)}, u32[]{:S(2)}) copy-start(s32[256]{0:T(256)} %param.12) | copy-start | bytes 3076
  5.0 23.4 %copy-start.2 = (bf16[512,512]{1,0:T(8,128)(2,1)S(1)}, bf16[512,512]{1,0:T(8,128)(2,1)}, u32[]{:S(2)}) copy-start(bf16[512,512]{1,0:T(8,128)(2,1)} %refs_2_.2) | copy-start | bytes 1572868
  8.3 20.7 %collective-permute-start.2 = (bf16[128,4096]{1,0:T(8,128)(2,1)S(1)}, bf16[128,4096]{1,0:T(8,128)(2,1)S(1)}, u32[]{:S(2)}, u32[]{:S(2)}) collective-permute-start(bf16[128,4096]{1,0:T(8,128)(2,1)S(1)} %get-tuple-element.55), channel_id=1, source_target_pairs={{0,1},{1,0},{2,3},{3,2},{4,5},{5,4},{6,7},{7,6},{8,9},{9,8},{10,11... | collective-permute-start | bytes 3145736 | tf_op jit(solution)/shard_map/ppermute | solution.py:322
  8.3 22.1 %collective-permute-start.3 = (bf16[128,4096]{1,0:T(8,128)(2,1)S(1)}, bf16[128,4096]{1,0:T(8,128)(2,1)S(1)}, u32[]{:S(2)}, u32[]{:S(2)}) collective-permute-start(bf16[128,4096]{1,0:T(8,128)(2,1)S(1)} %get-tuple-element.56), channel_id=1, source_target_pairs={{0,1},{1,0},{2,3},{3,2},{4,5},{5,4},{6,7},{7,6},{8,9},{9,8},{10,11... | collective-permute-start | bytes 3145736 | tf_op jit(solution)/shard_map/ppermute | solution.py:322
  8.8 5.8 %collective-permute-start.1 = (s32[256]{0:T(256)S(1)}, s32[256]{0:T(256)S(1)}, u32[]{:S(2)}, u32[]{:S(2)}) collective-permute-start(s32[256]{0:T(256)S(1)} %copy-done.4), channel_id=1, source_target_pairs={{0,1},{1,2},{2,3},{3,4},{4,5},{5,6},{6,7},{7,8},{8,9},{9,10},{10,1... | collective-permute-start | bytes 3080 | tf_op jit(solution)/shard_map/ppermute | solution.py:32
  14.7 27.2 %copy-start.5 = (f32[1,128]{1,0:T(1,128)S(1)}, f32[1,128]{1,0:T(1,128)}, u32[]{:S(2)}) copy-start(f32[1,128]{1,0:T(1,128)} %constant.11.clone.freq_ref) | copy-start | bytes 1540
  14.7 12.2 %collective-permute-start.7 = (bf16[512,512]{1,0:T(8,128)(2,1)S(1)}, bf16[512,512]{1,0:T(8,128)(2,1)S(1)}, u32[]{:S(2)}, u32[]{:S(2)}) collective-permute-start(bf16[512,512]{1,0:T(8,128)(2,1)S(1)} %collective-permute-done.refs_3_), channel_id=1, source_target_pairs={{0,4},{1,5},{4,8},{5,9},{8,12},{9,13},{12,14},{13,15},{14,10},{15,... | collective-permute-start | bytes 1572872 | tf_op jit(solution)/shard_map/ppermute | solution.py:319
  16.3 12.2 %collective-permute-start.5 = (bf16[512,512]{1,0:T(8,128)(2,1)S(1)}, bf16[512,512]{1,0:T(8,128)(2,1)S(1)}, u32[]{:S(2)}, u32[]{:S(2)}) collective-permute-start(bf16[512,512]{1,0:T(8,128)(2,1)S(1)} %collective-permute-done.4.refs_3_), channel_id=1, source_target_pairs={{0,2},{1,3},{4,0},{5,1},{8,4},{9,5},{12,8},{13,9},{14,12},{15,13},... | collective-permute-start | bytes 1572872 | tf_op jit(solution)/shard_map/ppermute | solution.py:319
  16.7 15.7 %collective-permute-start.9 = (bf16[512,512]{1,0:T(8,128)(2,1)S(1)}, bf16[512,512]{1,0:T(8,128)(2,1)S(1)}, u32[]{:S(2)}, u32[]{:S(2)}) collective-permute-start(bf16[512,512]{1,0:T(8,128)(2,1)S(1)} %collective-permute-done.4.refs_3_), channel_id=1, source_target_pairs={{0,16},{1,17},{2,18},{3,19},{4,20},{5,21},{6,22},{7,23},{8,24},{9,... | collective-permute-start | bytes 1572872 | tf_op jit(solution)/shard_map/ppermute | solution.py:319
  26.9 11.3 %collective-permute-start.8 = (bf16[512,512]{1,0:T(8,128)(2,1)S(1)}, bf16[512,512]{1,0:T(8,128)(2,1)S(1)}, u32[]{:S(2)}, u32[]{:S(2)}) collective-permute-start(bf16[512,512]{1,0:T(8,128)(2,1)S(1)} %collective-permute-done.7.refs_4_), channel_id=1, source_target_pairs={{0,4},{1,5},{4,8},{5,9},{8,12},{9,13},{12,14},{13,15},{14,10},{15,... | collective-permute-start | bytes 1572872 | tf_op jit(solution)/shard_map/ppermute | solution.py:319
  28.5 14.9 %collective-permute-start.11 = (bf16[512,512]{1,0:T(8,128)(2,1)S(1)}, bf16[512,512]{1,0:T(8,128)(2,1)S(1)}, u32[]{:S(2)}, u32[]{:S(2)}) collective-permute-start(bf16[512,512]{1,0:T(8,128)(2,1)S(1)} %copy-done.2), channel_id=1, source_target_pairs={{0,2},{1,3},{4,0},{5,1},{8,4},{9,5},{12,8},{13,9},{14,12},{15,13},... | collective-permute-start | bytes 1572872 | tf_op jit(solution)/shard_map/ppermute | solution.py:319
  28.9 14.4 %collective-permute-start.10 = (bf16[512,512]{1,0:T(8,128)(2,1)S(1)}, bf16[512,512]{1,0:T(8,128)(2,1)S(1)}, u32[]{:S(2)}, u32[]{:S(2)}) collective-permute-start(bf16[512,512]{1,0:T(8,128)(2,1)S(1)} %collective-permute-done.7.refs_4_), channel_id=1, source_target_pairs={{0,16},{1,17},{2,18},{3,19},{4,20},{5,21},{6,22},{7,23},{8,24},{9,... | collective-permute-start | bytes 1572872 | tf_op jit(solution)/shard_map/ppermute | solution.py:319
  30.5 21.3 %collective-permute-start.6 = (bf16[512,512]{1,0:T(8,128)(2,1)S(1)}, bf16[512,512]{1,0:T(8,128)(2,1)S(1)}, u32[]{:S(2)}, u32[]{:S(2)}) collective-permute-start(bf16[512,512]{1,0:T(8,128)(2,1)S(1)} %collective-permute-done.5.refs_4_), channel_id=1, source_target_pairs={{0,2},{1,3},{4,0},{5,1},{8,4},{9,5},{12,8},{13,9},{14,12},{15,13},... | collective-permute-start | bytes 1572872 | tf_op jit(solution)/shard_map/ppermute | solution.py:319
  38.2 15.6 %collective-permute-start.14 = (bf16[512,512]{1,0:T(8,128)(2,1)S(1)}, bf16[512,512]{1,0:T(8,128)(2,1)S(1)}, u32[]{:S(2)}, u32[]{:S(2)}) collective-permute-start(bf16[512,512]{1,0:T(8,128)(2,1)S(1)} %collective-permute-done.8.refs_2_), channel_id=1, source_target_pairs={{0,16},{1,17},{2,18},{3,19},{4,20},{5,21},{6,22},{7,23},{8,24},{9,... | collective-permute-start | bytes 1572872 | tf_op jit(solution)/shard_map/ppermute | solution.py:319
  40.3 13.8 %collective-permute-start.16 = (bf16[512,512]{1,0:T(8,128)(2,1)S(1)}, bf16[512,512]{1,0:T(8,128)(2,1)S(1)}, u32[]{:S(2)}, u32[]{:S(2)}) collective-permute-start(bf16[512,512]{1,0:T(8,128)(2,1)S(1)} %collective-permute-done.8.refs_2_), channel_id=1, source_target_pairs={{0,4},{1,5},{4,8},{5,9},{8,12},{9,13},{12,14},{13,15},{14,10},{15,... | collective-permute-start | bytes 1572872 | tf_op jit(solution)/shard_map/ppermute | solution.py:319
  51.8 4.1 %copy-start.3 = (bf16[512,512]{1,0:T(8,128)(2,1)S(1)}, bf16[512,512]{1,0:T(8,128)(2,1)}, u32[]{:S(2)}) copy-start(bf16[512,512]{1,0:T(8,128)(2,1)} %refs_2_.3) | copy-start | bytes 1572868
  51.8 13.6 %collective-permute-start.12 = (bf16[512,512]{1,0:T(8,128)(2,1)S(1)}, bf16[512,512]{1,0:T(8,128)(2,1)S(1)}, u32[]{:S(2)}, u32[]{:S(2)}) collective-permute-start(bf16[512,512]{1,0:T(8,128)(2,1)S(1)} %collective-permute-done.6.refs_6_), channel_id=1, source_target_pairs={{0,2},{1,3},{4,0},{5,1},{8,4},{9,5},{12,8},{13,9},{14,12},{15,13},... | collective-permute-start | bytes 1572872 | tf_op jit(solution)/shard_map/ppermute | solution.py:319
  52.1 13.3 %collective-permute-start.13 = (bf16[512,512]{1,0:T(8,128)(2,1)S(1)}, bf16[512,512]{1,0:T(8,128)(2,1)S(1)}, u32[]{:S(2)}, u32[]{:S(2)}) collective-permute-start(bf16[512,512]{1,0:T(8,128)(2,1)S(1)} %collective-permute-done.9.refs_5_), channel_id=1, source_target_pairs={{0,4},{1,5},{4,8},{5,9},{8,12},{9,13},{12,14},{13,15},{14,10},{15,... | collective-permute-start | bytes 1572872 | tf_op jit(solution)/shard_map/ppermute | solution.py:319
  53.8 11.6 %collective-permute-start.15 = (bf16[512,512]{1,0:T(8,128)(2,1)S(1)}, bf16[512,512]{1,0:T(8,128)(2,1)S(1)}, u32[]{:S(2)}, u32[]{:S(2)}) collective-permute-start(bf16[512,512]{1,0:T(8,128)(2,1)S(1)} %collective-permute-done.6.refs_6_), channel_id=1, source_target_pairs={{0,16},{1,17},{2,18},{3,19},{4,20},{5,21},{6,22},{7,23},{8,24},{9,... | collective-permute-start | bytes 1572872 | tf_op jit(solution)/shard_map/ppermute | solution.py:319
  55.3 2.6 %collective-permute-start.17 = (f32[128,512]{1,0:T(8,128)S(1)}, f32[128,512]{1,0:T(8,128)S(1)}, u32[]{:S(2)}, u32[]{:S(2)}) collective-permute-start(f32[128,512]{1,0:T(8,128)S(1)} %get-tuple-element.75), channel_id=1, source_target_pairs={{0,1},{1,0},{2,3},{3,2},{4,5},{5,4},{6,7},{7,6},{8,9},{9,8},{10,11... | collective-permute-start | bytes 786440 | tf_op jit(solution)/shard_map/ppermute | solution.py:322
  55.4 2.6 %collective-permute-start.18 = (f32[128,512]{1,0:T(8,128)S(1)}, f32[128,512]{1,0:T(8,128)S(1)}, u32[]{:S(2)}, u32[]{:S(2)}) collective-permute-start(f32[128,512]{1,0:T(8,128)S(1)} %get-tuple-element.76), channel_id=1, source_target_pairs={{0,1},{1,0},{2,3},{3,2},{4,5},{5,4},{6,7},{7,6},{8,9},{9,8},{10,11... | collective-permute-start | bytes 786440 | tf_op jit(solution)/shard_map/ppermute | solution.py:322
  55.9 4.3 %copy-start = (bf16[256,4096]{1,0:T(8,128)(2,1)S(1)}, bf16[256,4096]{1,0:T(8,128)(2,1)}, u32[]{:S(2)}) copy-start(bf16[256,4096]{1,0:T(8,128)(2,1)} %q_ref.3) | copy-start | bytes 6291460
  58.2 7.2 %collective-permute-start.19 = (bf16[128,512]{1,0:T(8,128)(2,1)S(1)}, bf16[128,512]{1,0:T(8,128)(2,1)S(1)}, u32[]{:S(2)}, u32[]{:S(2)}) collective-permute-start(bf16[128,512]{1,0:T(8,128)(2,1)S(1)} %get-tuple-element.88), channel_id=1, source_target_pairs={{0,1},{1,2},{2,3},{3,4},{4,5},{5,6},{6,7},{7,8},{8,9},{9,10},{10,1... | collective-permute-start | bytes 393224 | tf_op jit(solution)/shard_map/ppermute | solution.py:32
  66.9 2.0 %collective-permute-start.20 = (f32[256,512]{1,0:T(8,128)S(1)}, f32[256,512]{1,0:T(8,128)S(1)}, u32[]{:S(2)}, u32[]{:S(2)}) collective-permute-start(f32[256,512]{1,0:T(8,128)S(1)} %get-tuple-element.91), channel_id=1, source_target_pairs={{0,1},{1,0},{2,3},{3,2},{4,5},{5,4},{6,7},{7,6},{8,9},{9,8},{10,11... | collective-permute-start | bytes 1572872 | tf_op jit(solution)/shard_map/ppermute | solution.py:322
  69.0 7.2 %collective-permute-start.21 = (bf16[128,512]{1,0:T(8,128)(2,1)S(1)}, bf16[128,512]{1,0:T(8,128)(2,1)S(1)}, u32[]{:S(2)}, u32[]{:S(2)}) collective-permute-start(bf16[128,512]{1,0:T(8,128)(2,1)S(1)} %get-tuple-element.97), channel_id=1, source_target_pairs={{0,1},{1,2},{2,3},{3,4},{4,5},{5,6},{6,7},{7,8},{8,9},{9,10},{10,1... | collective-permute-start | bytes 393224 | tf_op jit(solution)/shard_map/ppermute | solution.py:32

commit v8 on v7

--- a/solution.py
+++ b/solution.py
@@ -87,21 +87,22 @@
     return mine, theirs
 
 
-def block_at(ids_ref, step):
-    z, x = lax.div(ids_ref[0], 4), lax.rem(lax.div(ids_ref[0], 2), 2)
-    p = jnp.where(x == 0, z, 7 - z) + jnp.where(ids_ref[1] == 0, step, -step)
+def block_at(step):
+    me = lax.axis_index("dp")
+    z, x = lax.div(me, 4), lax.rem(lax.div(me, 2), 2)
+    p = jnp.where(x == 0, z, 7 - z) + jnp.where(lax.axis_index("groups") == 0, step, -step)
     p = jnp.where(p < 0, p + 8, p)
     p = jnp.where(p > 7, p - 8, p)
     return jnp.where(p < 4, 2 * p, 15 - 2 * p)
 
 
-def project_kernel(steps, parts, carried, ids_ref, xa_ref, *refs):
+def project_kernel(steps, parts, carried, xa_ref, *refs):
     count = len(steps)
     others, refs = refs[:parts], refs[parts:]
     weights, refs = refs[:count], refs[count:]
     before, outs = refs[:carried], refs[carried:]
     depth = weights[0].shape[0]
-    columns = [pl.ds(pl.multiple_of(block_at(ids_ref, step) * depth, depth), depth) for step in steps]
+    columns = [pl.ds(pl.multiple_of(block_at(step) * depth, depth), depth) for step in steps]
     x = [jnp.concatenate([ref[:, c] for c in columns], axis=1) for ref in (xa_ref, *others)]
     w = jnp.concatenate([ref[...] for ref in weights], axis=0)
     total = jnp.dot(jnp.concatenate(x, axis=0), w, preferred_element_type=F32)
@@ -113,7 +114,7 @@
         at += ref.shape[0]
 
 
-def project(ids, steps, xa, others, weights, before=(), split=1):
+def project(steps, xa, others, weights, before=(), split=1):
     rows = xa.shape[0]
     depth, feats = weights[0].shape
     outs = [jax.ShapeDtypeStruct((rows, feats), F32)]
@@ -122,7 +123,7 @@
     operands = [xa, *others, *weights, *before]
     return pl.pallas_call(
         functools.partial(project_kernel, steps, len(others), len(before)),
-        in_specs=[pl.BlockSpec(memory_space=pltpu.SMEM)] + [whole] * len(operands),
+        in_specs=[whole] * len(operands),
         out_specs=[whole] * len(outs),
         out_shape=outs,
         compiler_params=params(),
@@ -130,7 +131,7 @@
             4 * rows * depth * feats * len(weights), 2 * depth * feats * len(weights) + 4 * rows * 4096
         ),
         name="project",
-    )(ids, *operands)
+    )(*operands)
 
 
 def tables_kernel(ids_ref, own_ref, behind_ref, freq_ref, cos_ref, sin_ref, bias_ref):
@@ -332,25 +333,25 @@
     k3, v3 = send(k2, key_way), send(v2, value_way)
     yk2 = send(k2, other_group)
 
-    key_part = project(ids, (0, -1, -2), mine, other, [key_weight, k1, k2])
+    key_part = project((0, -1, -2), mine, other, [key_weight, k1, k2])
     k3, yv1, key_part = after(k3, yv1, key_part)
     k4, yk3 = send(k3, key_way), send(k3, other_group)
     cos, sin, bias = tables(ids, segment_ids, behind)
-    key_part = project(ids, (-3, 2, 1), mine, other, [k3, yk2, k1b], key_part)
+    key_part = project((-3, 2, 1), mine, other, [k3, yk2, k1b], key_part)
     v3, key_part, cos, sin, bias = after(v3, key_part, cos, sin, bias)
     v4 = send(v3, value_way)
     yk3, v3y = after(yk3, v3)
     yv3 = send(v3y, other_group)
     v2b = send(yv1, key_way)
-    value_part = project(ids, (0, 1, 2, -1, 3), mine, other, [value_weight, v1, v2, yv1, v3])
-
-    own_k, *other_k = project(ids, (-4, 3), mine, other, [k4, yk3], key_part, 2)
+    value_part = project((0, 1, 2, -1, 3), mine, other, [value_weight, v1, v2, yv1, v3])
+
+    own_k, *other_k = project((-4, 3), mine, other, [k4, yk3], key_part, 2)
     *other_k, value_part = after(*[swap(o) for o in other_k], value_part)
     keys, head_keys, tail = finish(keys_kernel, "keys", own_k, cos, sin, *other_k)
     prev_keys = from_behind(tail, "dp", 1)
     p1 = softmax_weights(1, queries, keys, keys, bias)
     value_part, p1, prev_keys = after(value_part, p1, prev_keys)
-    own_v, other_v = project(ids, (4, -2, -3), mine, other, [v4, v2b, yv3], value_part)
+    own_v, other_v = project((4, -2, -3), mine, other, [v4, v2b, yv3], value_part)
     p0 = softmax_weights(0, queries, prev_keys, head_keys, bias)
     other_v, p0 = after(swap(other_v), p0)
     values, head_values, tail = finish(values_kernel, "values", own_v, other_v)

time: 78.3 us -> 77.2 us (0.986)
  Pallas kernels: 19.4 us -> 16.6 us
  waiting for transfers between devices: 32.1 us -> 33.4 us
    pallas_call x5, Pallas kernels: 7.87 us -> 5.17 us  [project(): pl.pallas_call(functools.partial(project_kernel, steps, len(others), len(...]
    ppermute x14, waiting for transfers between devices: 21.6 us -> 22.6 us  [send(): return lax.ppermute(value, both, way)]
  transfers between devices with their start and end apart: 22 -> 22, of which waited for: 8 -> 8; matrix products, arithmetic and copies ran while one was open for 1% -> 1% of each run, Pallas kernels for 21% -> 18%
where the time goes in v8:
time: 77.2 us; the launch traced here: 76.1 us
  waiting for transfers between devices  33.4 us (43%)
  starting transfers between devices  23 us (30%)
  Pallas kernels  16.6 us (22%)
  local copies, waits for them, and re-layouts  2.94 us (4%)
    ppermute x14, waiting for transfers between devices, send(): return lax.ppermute(value, both, way)  22.6 us
    ppermute x14, starting transfers between devices, send(): return lax.ppermute(value, both, way)  15.5 us
    ppermute x3, waiting for transfers between devices, from_behind(): lax.ppermute(value, axis, [(source, source + steps) for source in range(i...  10.6 us
    ppermute x3, starting transfers between devices, from_behind(): lax.ppermute(value, axis, [(source, source + steps) for source in range(i...  6.25 us
    pallas_call x5, Pallas kernels, project(): pl.pallas_call(functools.partial(project_kernel, steps, len(others), len(...  5.17 us
    pallas_call x2, Pallas kernels, softmax_weights(): pl.pallas_call(functools.partial(scores_kernel, block), in_specs=[whole]...  3.51 us
    pallas_call x1, Pallas kernels, normalise(): pl.pallas_call(norm_kernel, grid_spec=pltpu.PrefetchScalarGridSpec(num_sc...  3.22 us
    pallas_call x2, Pallas kernels, contexts(): pl.pallas_call(functools.partial(context_kernel, block), in_specs=[whole]...  3.2 us
  transfers between devices with their start and end apart: 22, of which 8 were waited for; matrix products, arithmetic and copies ran while one was open for 1% of the time, Pallas kernels for 18%

profile of v8, /device:TPU:8, one launch (start us, length us, event | category | flops | bytes accessed | tf_op | source)
XLA Modules:
  0.0 76.1 jit_solution(18284033184422160011)
XLA Ops:
  0.0 1.6 %collective-permute-start = (bf16[512,512]{1,0:T(8,128)(2,1)}, bf16[512,512]{1,0:T(8,128)(2,1)S(1)}, u32[]{:S(2)}, u32[]{:S(2)}) collective-permute-start(bf16[512,512]{1,0:T(8,128)(2,1)} %refs_2_.2), channel_id=1, source_target_pairs={{0,4},{1,5},{4,8},{5,9},{8,12},{9,13},{12,14},{13,15},{14,10},{15,... | collective-permute-start | bytes 1572872 | tf_op jit(solution)/shard_map/ppermute | solution.py:320
  2.0 0.7 reshape.9.g_ref
  2.8 2.2 %copy-done.1 = bf16[256,8192]{1,0:T(8,128)(2,1)S(1)} copy-done((bf16[256,8192]{1,0:T(8,128)(2,1)S(1)}, bf16[256,8192]{1,0:T(8,128)(2,1)}, u32[]{:S(2)}) %copy-start.1) | copy-done | bytes 4194328
  5.0 3.2 %norm.1 = (bf16[256,4096]{1,0:T(8,128)(2,1)S(1)}, bf16[128,4096]{1,0:T(8,128)(2,1)S(1)}, bf16[128,4096]{1,0:T(8,128)(2,1)S(1)}) custom-call(s32[2]{0:T(128)S(1)} %pad_add_fusion.core_ref.ids_ref, bf16[256,8192]{1,0:T(8,128)(2,1)S(1)} %copy-done.1, bf16[1,8192]{1,0:T(2,128)(2,1)S(1)} %reshape.9.g_ref), custom_call_target="tpu_custom_call" | custom-call | flops 16777216 | bytes 8388608 | tf_op jit(solution)/shard_map/norm/pallas_call | solution.py:64
  8.3 0.5 collective-permute-start.3
  8.8 2.0 %collective-permute-start.1 = (s32[256]{0:T(256)S(1)}, s32[256]{0:T(256)S(1)}, u32[]{:S(2)}, u32[]{:S(2)}) collective-permute-start(s32[256]{0:T(256)S(1)} %copy-done.4), channel_id=1, source_target_pairs={{0,1},{1,2},{2,3},{3,4},{4,5},{5,6},{6,7},{7,8},{8,9},{9,10},{10,1... | collective-permute-start | bytes 3080 | tf_op jit(solution)/shard_map/ppermute | solution.py:32
  10.8 3.9 %collective-permute-done.1 = s32[256]{0:T(256)S(1)} collective-permute-done((s32[256]{0:T(256)S(1)}, s32[256]{0:T(256)S(1)}, u32[]{:S(2)}, u32[]{:S(2)}) %collective-permute-start.1) | collective-permute-done | bytes 1056 | tf_op jit(solution)/shard_map/ppermute | solution.py:32
  14.7 1.6 %collective-permute-start.7 = (bf16[512,512]{1,0:T(8,128)(2,1)S(1)}, bf16[512,512]{1,0:T(8,128)(2,1)S(1)}, u32[]{:S(2)}, u32[]{:S(2)}) collective-permute-start(bf16[512,512]{1,0:T(8,128)(2,1)S(1)} %collective-permute-done.refs_3_), channel_id=1, source_target_pairs={{0,4},{1,5},{4,8},{5,9},{8,12},{9,13},{12,14},{13,15},{14,10},{15,... | collective-permute-start | bytes 1572872 | tf_op jit(solution)/shard_map/ppermute | solution.py:320
  16.7 1.5 %collective-permute-start.9 = (bf16[512,512]{1,0:T(8,128)(2,1)S(1)}, bf16[512,512]{1,0:T(8,128)(2,1)S(1)}, u32[]{:S(2)}, u32[]{:S(2)}) collective-permute-start(bf16[512,512]{1,0:T(8,128)(2,1)S(1)} %collective-permute-done.4.refs_3_), channel_id=1, source_target_pairs={{0,16},{1,17},{2,18},{3,19},{4,20},{5,21},{6,22},{7,23},{8,24},{9,... | collective-permute-start | bytes 1572872 | tf_op jit(solution)/shard_map/ppermute | solution.py:320
  18.3 8.6 %collective-permute-done.7.refs_4_ = bf16[512,512]{1,0:T(8,128)(2,1)S(1)} collective-permute-done((bf16[512,512]{1,0:T(8,128)(2,1)S(1)}, bf16[512,512]{1,0:T(8,128)(2,1)S(1)}, u32[]{:S(2)}, u32[]{:S(2)}) %collective-permute-start.7) | collective-permute-done | bytes 524320 | tf_op jit(solution)/shard_map/ppermute | solution.py:320
  26.9 1.6 %collective-permute-start.8 = (bf16[512,512]{1,0:T(8,128)(2,1)S(1)}, bf16[512,512]{1,0:T(8,128)(2,1)S(1)}, u32[]{:S(2)}, u32[]{:S(2)}) collective-permute-start(bf16[512,512]{1,0:T(8,128)(2,1)S(1)} %collective-permute-done.7.refs_4_), channel_id=1, source_target_pairs={{0,4},{1,5},{4,8},{5,9},{8,12},{9,13},{12,14},{13,15},{14,10},{15,... | collective-permute-start | bytes 1572872 | tf_op jit(solution)/shard_map/ppermute | solution.py:320
  28.9 1.5 %collective-permute-start.10 = (bf16[512,512]{1,0:T(8,128)(2,1)S(1)}, bf16[512,512]{1,0:T(8,128)(2,1)S(1)}, u32[]{:S(2)}, u32[]{:S(2)}) collective-permute-start(bf16[512,512]{1,0:T(8,128)(2,1)S(1)} %collective-permute-done.7.refs_4_), channel_id=1, source_target_pairs={{0,16},{1,17},{2,18},{3,19},{4,20},{5,21},{6,22},{7,23},{8,24},{9,... | collective-permute-start | bytes 1572872 | tf_op jit(solution)/shard_map/ppermute | solution.py:320
  30.9 1.0 %project.5 = (f32[256,512]{1,0:T(8,128)S(1)}, f32[256,512]{1,0:T(8,128)S(1)}) custom-call(bf16[256,4096]{1,0:T(8,128)(2,1)S(1)} %get-tuple-element.54.xa_ref, bf16[128,4096]{1,0:T(8,128)(2,1)S(1)} %collective-permute-done.2.refs_0_, bf16[128,4096]{1,0:T(8,128)(2,1)S(1)} %collective-permute-done.3.refs_1_, bf16[512,512]{1,0:T(8,128)(2,1)S(1)} %copy-done.2, ...), custom_call_target="tpu_custom_call" | custom-call | flops 805306368 | bytes 5767168 | tf_op jit(solution)/shard_map/project/pallas_call | solution.py:124
  31.9 6.3 %collective-permute-done.8.refs_2_ = bf16[512,512]{1,0:T(8,128)(2,1)S(1)} collective-permute-done((bf16[512,512]{1,0:T(8,128)(2,1)S(1)}, bf16[512,512]{1,0:T(8,128)(2,1)S(1)}, u32[]{:S(2)}, u32[]{:S(2)}) %collective-permute-start.8) | collective-permute-done | bytes 524320 | tf_op jit(solution)/shard_map/ppermute | solution.py:320
  38.2 2.1 %collective-permute-start.14 = (bf16[512,512]{1,0:T(8,128)(2,1)S(1)}, bf16[512,512]{1,0:T(8,128)(2,1)S(1)}, u32[]{:S(2)}, u32[]{:S(2)}) collective-permute-start(bf16[512,512]{1,0:T(8,128)(2,1)S(1)} %collective-permute-done.8.refs_2_), channel_id=1, source_target_pairs={{0,16},{1,17},{2,18},{3,19},{4,20},{5,21},{6,22},{7,23},{8,24},{9,... | collective-permute-start | bytes 1572872 | tf_op jit(solution)/shard_map/ppermute | solution.py:320
  40.3 1.6 %collective-permute-start.16 = (bf16[512,512]{1,0:T(8,128)(2,1)S(1)}, bf16[512,512]{1,0:T(8,128)(2,1)S(1)}, u32[]{:S(2)}, u32[]{:S(2)}) collective-permute-start(bf16[512,512]{1,0:T(8,128)(2,1)S(1)} %collective-permute-done.8.refs_2_), channel_id=1, source_target_pairs={{0,4},{1,5},{4,8},{5,9},{8,12},{9,13},{12,14},{13,15},{14,10},{15,... | collective-permute-start | bytes 1572872 | tf_op jit(solution)/shard_map/ppermute | solution.py:320
  41.9 1.2 %tables.1 = (f32[256,128]{1,0:T(8,128)S(1)}, f32[256,128]{1,0:T(8,128)S(1)}, f32[2,128,256]{2,1,0:T(8,128)S(1)}) custom-call(s32[2]{0:T(128)S(1)} %pad_add_fusion.core_ref.ids_ref, s32[1,256]{1,0:T(1,128)S(1)} %bitcast.4, s32[1,256]{1,0:T(1,128)S(1)} %bitcast.5, f32[1,128]{1,0:T(1,128)S(1)} %copy-done.5), custom_call_target="tpu_custom_call" | custom-call | flops 1310720 | bytes 524288 | tf_op jit(solution)/shard_map/tables/pallas_call | solution.py:164
  43.3 1.0 %project.6 = (f32[256,512]{1,0:T(8,128)S(1)}, f32[256,512]{1,0:T(8,128)S(1)}) custom-call(bf16[256,4096]{1,0:T(8,128)(2,1)S(1)} %get-tuple-element.54.xa_ref, bf16[128,4096]{1,0:T(8,128)(2,1)S(1)} %collective-permute-done.2.refs_0_, bf16[128,4096]{1,0:T(8,128)(2,1)S(1)} %collective-permute-done.3.refs_1_, ...), custom_call_target="tpu_custom_call" | custom-call | flops 805306368 | bytes 5767168 | tf_op jit(solution)/shard_map/project/pallas_call | solution.py:124
  44.3 7.4 %collective-permute-done.6.refs_6_ = bf16[512,512]{1,0:T(8,128)(2,1)S(1)} collective-permute-done((bf16[512,512]{1,0:T(8,128)(2,1)S(1)}, bf16[512,512]{1,0:T(8,128)(2,1)S(1)}, u32[]{:S(2)}, u32[]{:S(2)}) %collective-permute-start.6) | collective-permute-done | bytes 524320 | tf_op jit(solution)/shard_map/ppermute | solution.py:320
  52.1 1.7 %collective-permute-start.13 = (bf16[512,512]{1,0:T(8,128)(2,1)S(1)}, bf16[512,512]{1,0:T(8,128)(2,1)S(1)}, u32[]{:S(2)}, u32[]{:S(2)}) collective-permute-start(bf16[512,512]{1,0:T(8,128)(2,1)S(1)} %collective-permute-done.9.refs_5_), channel_id=1, source_target_pairs={{0,4},{1,5},{4,8},{5,9},{8,12},{9,13},{12,14},{13,15},{14,10},{15,... | collective-permute-start | bytes 1572872 | tf_op jit(solution)/shard_map/ppermute | solution.py:320
  54.0 0.7 project.7
  54.8 0.5 collective-permute-start.18
  55.3 1.5 %project.8 = (f32[256,512]{1,0:T(8,128)S(1)}, f32[256,512]{1,0:T(8,128)S(1)}) custom-call(bf16[256,4096]{1,0:T(8,128)(2,1)S(1)} %get-tuple-element.54.xa_ref, bf16[128,4096]{1,0:T(8,128)(2,1)S(1)} %collective-permute-done.2.refs_0_, bf16[128,4096]{1,0:T(8,128)(2,1)S(1)} %collective-permute-done.3.refs_1_, bf16[512,512]{1,0:T(8,128)(2,1)S(1)} %copy-done.3, ...), custom_call_target="tpu_custom_call" | custom-call | flops 1342177280 | bytes 6815744 | tf_op jit(solution)/shard_map/project/pallas_call | solution.py:124
  57.1 2.0 %collective-permute-start.19 = (bf16[128,512]{1,0:T(8,128)(2,1)S(1)}, bf16[128,512]{1,0:T(8,128)(2,1)S(1)}, u32[]{:S(2)}, u32[]{:S(2)}) collective-permute-start(bf16[128,512]{1,0:T(8,128)(2,1)S(1)} %get-tuple-element.88), channel_id=1, source_target_pairs={{0,1},{1,2},{2,3},{3,4},{4,5},{5,6},{6,7},{7,8},{8,9},{9,10},{10,1... | collective-permute-start | bytes 393224 | tf_op jit(solution)/shard_map/ppermute | solution.py:32
  59.1 1.8 %scores.2.p_ref = bf16[4,1024,256]{2,1,0:T(8,128)(2,1)S(1)} custom-call(bf16[256,4096]{1,0:T(8,128)(2,1)S(1)} %copy-done, bf16[256,512]{1,0:T(8,128)(2,1)S(1)} %get-tuple-element.86.ka_ref.kb_ref, bf16[256,512]{1,0:T(8,128)(2,1)S(1)} %get-tuple-element.86.ka_ref.kb_ref, f32[2,128,256]{2,1,0:T(8,128)S(1)} %get-tuple-element.87.bias_ref), custom_call_target="tpu_custom_call" | custom-call | flops 268435456 | bytes 3145728 | tf_op jit(solution)/shard_map/scores/pallas_call | solution.py:241
  60.9 3.4 %collective-permute-done.19.ka_ref = bf16[128,512]{1,0:T(8,128)(2,1)S(1)} collective-permute-done((bf16[128,512]{1,0:T(8,128)(2,1)S(1)}, bf16[128,512]{1,0:T(8,128)(2,1)S(1)}, u32[]{:S(2)}, u32[]{:S(2)}) %collective-permute-start.19) | collective-permute-done | bytes 131104 | tf_op jit(solution)/shard_map/ppermute | solution.py:32
  64.3 1.0 %project.9 = (f32[256,512]{1,0:T(8,128)S(1)}, f32[256,512]{1,0:T(8,128)S(1)}) custom-call(bf16[256,4096]{1,0:T(8,128)(2,1)S(1)} %get-tuple-element.54.xa_ref, bf16[128,4096]{1,0:T(8,128)(2,1)S(1)} %collective-permute-done.2.refs_0_, bf16[128,4096]{1,0:T(8,128)(2,1)S(1)} %collective-permute-done.3.refs_1_, ...), custom_call_target="tpu_custom_call" | custom-call | flops 805306368 | bytes 5767168 | tf_op jit(solution)/shard_map/project/pallas_call | solution.py:124
  65.4 1.8 %scores.3.p_ref = bf16[4,1024,256]{2,1,0:T(8,128)(2,1)S(1)} custom-call(bf16[256,4096]{1,0:T(8,128)(2,1)S(1)} %copy-done, bf16[128,512]{1,0:T(8,128)(2,1)S(1)} %collective-permute-done.19.ka_ref, bf16[128,512]{1,0:T(8,128)(2,1)S(1)} %get-tuple-element.93.kb_ref, f32[2,128,256]{2,1,0:T(8,128)S(1)} %get-tuple-element.87.bias_ref), custom_call_target="tpu_custom_call" | custom-call | flops 268435456 | bytes 3145728 | tf_op jit(solution)/shard_map/scores/pallas_call | solution.py:241
  67.3 2.3 %collective-permute-start.21 = (bf16[128,512]{1,0:T(8,128)(2,1)S(1)}, bf16[128,512]{1,0:T(8,128)(2,1)S(1)}, u32[]{:S(2)}, u32[]{:S(2)}) collective-permute-start(bf16[128,512]{1,0:T(8,128)(2,1)S(1)} %get-tuple-element.97), channel_id=1, source_target_pairs={{0,1},{1,2},{2,3},{3,4},{4,5},{5,6},{6,7},{7,8},{8,9},{9,10},{10,1... | collective-permute-start | bytes 393224 | tf_op jit(solution)/shard_map/ppermute | solution.py:32
  69.6 1.6 %context.2.refs_0_ = bf16[256,4096]{1,0:T(8,128)(2,1)} custom-call(bf16[4,1024,256]{2,1,0:T(8,128)(2,1)S(1)} %scores.2.p_ref, bf16[256,512]{1,0:T(8,128)(2,1)S(1)} %get-tuple-element.100.va_ref.vb_ref, bf16[256,512]{1,0:T(8,128)(2,1)S(1)} %get-tuple-element.100.va_ref.vb_ref), custom_call_target="tpu_custom_call" | custom-call | flops 268435456 | bytes 3145728 | tf_op jit(solution)/shard_map/context/pallas_call | solution.py:279
  71.2 3.3 %collective-permute-done.21.va_ref = bf16[128,512]{1,0:T(8,128)(2,1)S(1)} collective-permute-done((bf16[128,512]{1,0:T(8,128)(2,1)S(1)}, bf16[128,512]{1,0:T(8,128)(2,1)S(1)}, u32[]{:S(2)}, u32[]{:S(2)}) %collective-permute-start.21) | collective-permute-done | bytes 131104 | tf_op jit(solution)/shard_map/ppermute | solution.py:32
  74.5 1.6 %context.3 = bf16[256,4096]{1,0:T(8,128)(2,1)} custom-call(bf16[4,1024,256]{2,1,0:T(8,128)(2,1)S(1)} %scores.3.p_ref, bf16[128,512]{1,0:T(8,128)(2,1)S(1)} %collective-permute-done.21.va_ref, bf16[128,512]{1,0:T(8,128)(2,1)S(1)} %get-tuple-element.98.vb_ref, bf16[256,4096]{1,0:T(8,128)(2,1)} %context.2.refs_0_), custom_call_target="tpu_custom_call", output_to_operand_aliasing={{}: (3, {})} | custom-call | flops 268435456 | bytes 3145728 | tf_op jit(solution)/shard_map/context/pallas_call | solution.py:279
  (39 shorter events, 3.4 us)
Async XLA Ops:
  0.0 14.7 %collective-permute-start = (bf16[512,512]{1,0:T(8,128)(2,1)}, bf16[512,512]{1,0:T(8,128)(2,1)S(1)}, u32[]{:S(2)}, u32[]{:S(2)}) collective-permute-start(bf16[512,512]{1,0:T(8,128)(2,1)} %refs_2_.2), channel_id=1, source_target_pairs={{0,4},{1,5},{4,8},{5,9},{8,12},{9,13},{12,14},{13,15},{14,10},{15,... | collective-permute-start | bytes 1572872 | tf_op jit(solution)/shard_map/ppermute | solution.py:320
  1.6 14.7 %collective-permute-start.4 = (bf16[512,512]{1,0:T(8,128)(2,1)}, bf16[512,512]{1,0:T(8,128)(2,1)S(1)}, u32[]{:S(2)}, u32[]{:S(2)}) collective-permute-start(bf16[512,512]{1,0:T(8,128)(2,1)} %refs_2_.3), channel_id=1, source_target_pairs={{0,2},{1,3},{4,0},{5,1},{8,4},{9,5},{12,8},{13,9},{14,12},{15,13},... | collective-permute-start | bytes 1572872 | tf_op jit(solution)/shard_map/ppermute | solution.py:320
  2.8 2.2 %copy-start.1 = (bf16[256,8192]{1,0:T(8,128)(2,1)S(1)}, bf16[256,8192]{1,0:T(8,128)(2,1)}, u32[]{:S(2)}) copy-start(bf16[256,8192]{1,0:T(8,128)(2,1)} %h_ref.1) | copy-start | bytes 12582916
  5.0 3.8 %copy-start.4 = (s32[256]{0:T(256)S(1)}, s32[256]{0:T(256)}, u32[]{:S(2)}) copy-start(s32[256]{0:T(256)} %param.12) | copy-start | bytes 3076
  5.0 23.4 %copy-start.2 = (bf16[512,512]{1,0:T(8,128)(2,1)S(1)}, bf16[512,512]{1,0:T(8,128)(2,1)}, u32[]{:S(2)}) copy-start(bf16[512,512]{1,0:T(8,128)(2,1)} %refs_2_.2) | copy-start | bytes 1572868
  8.3 20.7 %collective-permute-start.2 = (bf16[128,4096]{1,0:T(8,128)(2,1)S(1)}, bf16[128,4096]{1,0:T(8,128)(2,1)S(1)}, u32[]{:S(2)}, u32[]{:S(2)}) collective-permute-start(bf16[128,4096]{1,0:T(8,128)(2,1)S(1)} %get-tuple-element.55), channel_id=1, source_target_pairs={{0,1},{1,0},{2,3},{3,2},{4,5},{5,4},{6,7},{7,6},{8,9},{9,8},{10,11... | collective-permute-start | bytes 3145736 | tf_op jit(solution)/shard_map/ppermute | solution.py:323
  8.3 22.1 %collective-permute-start.3 = (bf16[128,4096]{1,0:T(8,128)(2,1)S(1)}, bf16[128,4096]{1,0:T(8,128)(2,1)S(1)}, u32[]{:S(2)}, u32[]{:S(2)}) collective-permute-start(bf16[128,4096]{1,0:T(8,128)(2,1)S(1)} %get-tuple-element.56), channel_id=1, source_target_pairs={{0,1},{1,0},{2,3},{3,2},{4,5},{5,4},{6,7},{7,6},{8,9},{9,8},{10,11... | collective-permute-start | bytes 3145736 | tf_op jit(solution)/shard_map/ppermute | solution.py:323
  8.8 5.8 %collective-permute-start.1 = (s32[256]{0:T(256)S(1)}, s32[256]{0:T(256)S(1)}, u32[]{:S(2)}, u32[]{:S(2)}) collective-permute-start(s32[256]{0:T(256)S(1)} %copy-done.4), channel_id=1, source_target_pairs={{0,1},{1,2},{2,3},{3,4},{4,5},{5,6},{6,7},{7,8},{8,9},{9,10},{10,1... | collective-permute-start | bytes 3080 | tf_op jit(solution)/shard_map/ppermute | solution.py:32
  14.7 27.2 %copy-start.5 = (f32[1,128]{1,0:T(1,128)S(1)}, f32[1,128]{1,0:T(1,128)}, u32[]{:S(2)}) copy-start(f32[1,128]{1,0:T(1,128)} %constant.11.clone.freq_ref) | copy-start | bytes 1540
  14.7 12.2 %collective-permute-start.7 = (bf16[512,512]{1,0:T(8,128)(2,1)S(1)}, bf16[512,512]{1,0:T(8,128)(2,1)S(1)}, u32[]{:S(2)}, u32[]{:S(2)}) collective-permute-start(bf16[512,512]{1,0:T(8,128)(2,1)S(1)} %collective-permute-done.refs_3_), channel_id=1, source_target_pairs={{0,4},{1,5},{4,8},{5,9},{8,12},{9,13},{12,14},{13,15},{14,10},{15,... | collective-permute-start | bytes 1572872 | tf_op jit(solution)/shard_map/ppermute | solution.py:320
  16.3 12.2 %collective-permute-start.5 = (bf16[512,512]{1,0:T(8,128)(2,1)S(1)}, bf16[512,512]{1,0:T(8,128)(2,1)S(1)}, u32[]{:S(2)}, u32[]{:S(2)}) collective-permute-start(bf16[512,512]{1,0:T(8,128)(2,1)S(1)} %collective-permute-done.4.refs_3_), channel_id=1, source_target_pairs={{0,2},{1,3},{4,0},{5,1},{8,4},{9,5},{12,8},{13,9},{14,12},{15,13},... | collective-permute-start | bytes 1572872 | tf_op jit(solution)/shard_map/ppermute | solution.py:320
  16.7 15.2 %collective-permute-start.9 = (bf16[512,512]{1,0:T(8,128)(2,1)S(1)}, bf16[512,512]{1,0:T(8,128)(2,1)S(1)}, u32[]{:S(2)}, u32[]{:S(2)}) collective-permute-start(bf16[512,512]{1,0:T(8,128)(2,1)S(1)} %collective-permute-done.4.refs_3_), channel_id=1, source_target_pairs={{0,16},{1,17},{2,18},{3,19},{4,20},{5,21},{6,22},{7,23},{8,24},{9,... | collective-permute-start | bytes 1572872 | tf_op jit(solution)/shard_map/ppermute | solution.py:320
  26.9 11.3 %collective-permute-start.8 = (bf16[512,512]{1,0:T(8,128)(2,1)S(1)}, bf16[512,512]{1,0:T(8,128)(2,1)S(1)}, u32[]{:S(2)}, u32[]{:S(2)}) collective-permute-start(bf16[512,512]{1,0:T(8,128)(2,1)S(1)} %collective-permute-done.7.refs_4_), channel_id=1, source_target_pairs={{0,4},{1,5},{4,8},{5,9},{8,12},{9,13},{12,14},{13,15},{14,10},{15,... | collective-permute-start | bytes 1572872 | tf_op jit(solution)/shard_map/ppermute | solution.py:320
  28.5 14.9 %collective-permute-start.11 = (bf16[512,512]{1,0:T(8,128)(2,1)S(1)}, bf16[512,512]{1,0:T(8,128)(2,1)S(1)}, u32[]{:S(2)}, u32[]{:S(2)}) collective-permute-start(bf16[512,512]{1,0:T(8,128)(2,1)S(1)} %copy-done.2), channel_id=1, source_target_pairs={{0,2},{1,3},{4,0},{5,1},{8,4},{9,5},{12,8},{13,9},{14,12},{15,13},... | collective-permute-start | bytes 1572872 | tf_op jit(solution)/shard_map/ppermute | solution.py:320
  28.9 14.4 %collective-permute-start.10 = (bf16[512,512]{1,0:T(8,128)(2,1)S(1)}, bf16[512,512]{1,0:T(8,128)(2,1)S(1)}, u32[]{:S(2)}, u32[]{:S(2)}) collective-permute-start(bf16[512,512]{1,0:T(8,128)(2,1)S(1)} %collective-permute-done.7.refs_4_), channel_id=1, source_target_pairs={{0,16},{1,17},{2,18},{3,19},{4,20},{5,21},{6,22},{7,23},{8,24},{9,... | collective-permute-start | bytes 1572872 | tf_op jit(solution)/shard_map/ppermute | solution.py:320
  30.5 21.3 %collective-permute-start.6 = (bf16[512,512]{1,0:T(8,128)(2,1)S(1)}, bf16[512,512]{1,0:T(8,128)(2,1)S(1)}, u32[]{:S(2)}, u32[]{:S(2)}) collective-permute-start(bf16[512,512]{1,0:T(8,128)(2,1)S(1)} %collective-permute-done.5.refs_4_), channel_id=1, source_target_pairs={{0,2},{1,3},{4,0},{5,1},{8,4},{9,5},{12,8},{13,9},{14,12},{15,13},... | collective-permute-start | bytes 1572872 | tf_op jit(solution)/shard_map/ppermute | solution.py:320
  38.2 15.6 %collective-permute-start.14 = (bf16[512,512]{1,0:T(8,128)(2,1)S(1)}, bf16[512,512]{1,0:T(8,128)(2,1)S(1)}, u32[]{:S(2)}, u32[]{:S(2)}) collective-permute-start(bf16[512,512]{1,0:T(8,128)(2,1)S(1)} %collective-permute-done.8.refs_2_), channel_id=1, source_target_pairs={{0,16},{1,17},{2,18},{3,19},{4,20},{5,21},{6,22},{7,23},{8,24},{9,... | collective-permute-start | bytes 1572872 | tf_op jit(solution)/shard_map/ppermute | solution.py:320
  40.3 13.8 %collective-permute-start.16 = (bf16[512,512]{1,0:T(8,128)(2,1)S(1)}, bf16[512,512]{1,0:T(8,128)(2,1)S(1)}, u32[]{:S(2)}, u32[]{:S(2)}) collective-permute-start(bf16[512,512]{1,0:T(8,128)(2,1)S(1)} %collective-permute-done.8.refs_2_), channel_id=1, source_target_pairs={{0,4},{1,5},{4,8},{5,9},{8,12},{9,13},{12,14},{13,15},{14,10},{15,... | collective-permute-start | bytes 1572872 | tf_op jit(solution)/shard_map/ppermute | solution.py:320
  51.8 3.6 %copy-start.3 = (bf16[512,512]{1,0:T(8,128)(2,1)S(1)}, bf16[512,512]{1,0:T(8,128)(2,1)}, u32[]{:S(2)}) copy-start(bf16[512,512]{1,0:T(8,128)(2,1)} %refs_2_.3) | copy-start | bytes 1572868
  51.8 12.5 %collective-permute-start.12 = (bf16[512,512]{1,0:T(8,128)(2,1)S(1)}, bf16[512,512]{1,0:T(8,128)(2,1)S(1)}, u32[]{:S(2)}, u32[]{:S(2)}) collective-permute-start(bf16[512,512]{1,0:T(8,128)(2,1)S(1)} %collective-permute-done.6.refs_6_), channel_id=1, source_target_pairs={{0,2},{1,3},{4,0},{5,1},{8,4},{9,5},{12,8},{13,9},{14,12},{15,13},... | collective-permute-start | bytes 1572872 | tf_op jit(solution)/shard_map/ppermute | solution.py:320
  52.1 12.2 %collective-permute-start.13 = (bf16[512,512]{1,0:T(8,128)(2,1)S(1)}, bf16[512,512]{1,0:T(8,128)(2,1)S(1)}, u32[]{:S(2)}, u32[]{:S(2)}) collective-permute-start(bf16[512,512]{1,0:T(8,128)(2,1)S(1)} %collective-permute-done.9.refs_5_), channel_id=1, source_target_pairs={{0,4},{1,5},{4,8},{5,9},{8,12},{9,13},{12,14},{13,15},{14,10},{15,... | collective-permute-start | bytes 1572872 | tf_op jit(solution)/shard_map/ppermute | solution.py:320
  53.8 10.5 %collective-permute-start.15 = (bf16[512,512]{1,0:T(8,128)(2,1)S(1)}, bf16[512,512]{1,0:T(8,128)(2,1)S(1)}, u32[]{:S(2)}, u32[]{:S(2)}) collective-permute-start(bf16[512,512]{1,0:T(8,128)(2,1)S(1)} %collective-permute-done.6.refs_6_), channel_id=1, source_target_pairs={{0,16},{1,17},{2,18},{3,19},{4,20},{5,21},{6,22},{7,23},{8,24},{9,... | collective-permute-start | bytes 1572872 | tf_op jit(solution)/shard_map/ppermute | solution.py:320
  54.8 2.1 %collective-permute-start.17 = (f32[128,512]{1,0:T(8,128)S(1)}, f32[128,512]{1,0:T(8,128)S(1)}, u32[]{:S(2)}, u32[]{:S(2)}) collective-permute-start(f32[128,512]{1,0:T(8,128)S(1)} %get-tuple-element.75), channel_id=1, source_target_pairs={{0,1},{1,0},{2,3},{3,2},{4,5},{5,4},{6,7},{7,6},{8,9},{9,8},{10,11... | collective-permute-start | bytes 786440 | tf_op jit(solution)/shard_map/ppermute | solution.py:323
  54.8 2.0 %collective-permute-start.18 = (f32[128,512]{1,0:T(8,128)S(1)}, f32[128,512]{1,0:T(8,128)S(1)}, u32[]{:S(2)}, u32[]{:S(2)}) collective-permute-start(f32[128,512]{1,0:T(8,128)S(1)} %get-tuple-element.76), channel_id=1, source_target_pairs={{0,1},{1,0},{2,3},{3,2},{4,5},{5,4},{6,7},{7,6},{8,9},{9,8},{10,11... | collective-permute-start | bytes 786440 | tf_op jit(solution)/shard_map/ppermute | solution.py:323
  55.3 3.8 %copy-start = (bf16[256,4096]{1,0:T(8,128)(2,1)S(1)}, bf16[256,4096]{1,0:T(8,128)(2,1)}, u32[]{:S(2)}) copy-start(bf16[256,4096]{1,0:T(8,128)(2,1)} %q_ref.3) | copy-start | bytes 6291460
  57.1 7.2 %collective-permute-start.19 = (bf16[128,512]{1,0:T(8,128)(2,1)S(1)}, bf16[128,512]{1,0:T(8,128)(2,1)S(1)}, u32[]{:S(2)}, u32[]{:S(2)}) collective-permute-start(bf16[128,512]{1,0:T(8,128)(2,1)S(1)} %get-tuple-element.88), channel_id=1, source_target_pairs={{0,1},{1,2},{2,3},{3,4},{4,5},{5,6},{6,7},{7,8},{8,9},{9,10},{10,1... | collective-permute-start | bytes 393224 | tf_op jit(solution)/shard_map/ppermute | solution.py:32
  65.3 2.0 %collective-permute-start.20 = (f32[256,512]{1,0:T(8,128)S(1)}, f32[256,512]{1,0:T(8,128)S(1)}, u32[]{:S(2)}, u32[]{:S(2)}) collective-permute-start(f32[256,512]{1,0:T(8,128)S(1)} %get-tuple-element.91), channel_id=1, source_target_pairs={{0,1},{1,0},{2,3},{3,2},{4,5},{5,4},{6,7},{7,6},{8,9},{9,8},{10,11... | collective-permute-start | bytes 1572872 | tf_op jit(solution)/shard_map/ppermute | solution.py:323
  67.3 7.2 %collective-permute-start.21 = (bf16[128,512]{1,0:T(8,128)(2,1)S(1)}, bf16[128,512]{1,0:T(8,128)(2,1)S(1)}, u32[]{:S(2)}, u32[]{:S(2)}) collective-permute-start(bf16[128,512]{1,0:T(8,128)(2,1)S(1)} %get-tuple-element.97), channel_id=1, source_target_pairs={{0,1},{1,2},{2,3},{3,4},{4,5},{5,6},{6,7},{7,8},{8,9},{9,10},{10,1... | collective-permute-start | bytes 393224 | tf_op jit(solution)/shard_map/ppermute | solution.py:32

commit v9 on v8

--- a/solution.py
+++ b/solution.py
@@ -32,13 +32,13 @@
     return lax.ppermute(value, axis, [(source, source + steps) for source in range(initial, last)])
 
 
-def norm_kernel(core_ref, h_ref, g_ref, mine_ref, *theirs):
+def norm_kernel(h_ref, g_ref, mine_ref, *theirs):
     width = h_ref.shape[1]
     half = width // 16
     x = h_ref[...].astype(F32)
     meansq = jnp.sum(x * x, axis=-1, keepdims=True) * (1.0 / width)
     scale = lax.rsqrt(meansq + EPS)
-    first = lax.rem(core_ref[0], 2) == 0
+    first = lax.rem(lax.axis_index("dp"), 2) == 0
     for b in range(8):
         lo = slice(2 * b * half, (2 * b + 1) * half)
         hi = slice((2 * b + 1) * half, (2 * b + 2) * half)
@@ -54,7 +54,7 @@
                 theirs_ref[:, out] = other
 
 
-def normalise(core, hidden, gain):
+def normalise(hidden, gain):
     rows, width = hidden.shape
     step = 64
     mine = jax.ShapeDtypeStruct((rows, width // 2), BF16)
@@ -63,27 +63,24 @@
     last = rows // step // parts - 1
     mine, *theirs = pl.pallas_call(
         norm_kernel,
-        grid_spec=pltpu.PrefetchScalarGridSpec(
-            num_scalar_prefetch=1,
-            grid=(rows // step,),
-            in_specs=[
-                pl.BlockSpec((step, width), lambda i, c: (i, 0)),
-                pl.BlockSpec((1, width), lambda i, c: (0, 0)),
-            ],
-            out_specs=[pl.BlockSpec((step, width // 2), lambda i, c: (i, 0))]
-            + [
-                pl.BlockSpec(
-                    (step, width // 2),
-                    functools.partial(lambda p, i, c: (jnp.clip(i - p * (last + 1), 0, last), 0), p),
-                )
-                for p in range(parts)
-            ],
-        ),
+        grid=(rows // step,),
+        in_specs=[
+            pl.BlockSpec((step, width), lambda i: (i, 0)),
+            pl.BlockSpec((1, width), lambda i: (0, 0)),
+        ],
+        out_specs=[pl.BlockSpec((step, width // 2), lambda i: (i, 0))]
+        + [
+            pl.BlockSpec(
+                (step, width // 2),
+                functools.partial(lambda p, i: (jnp.clip(i - p * (last + 1), 0, last), 0), p),
+            )
+            for p in range(parts)
+        ],
         out_shape=[mine] + [theirs] * parts,
         compiler_params=params(),
         cost_estimate=cost(8 * rows * width, 4 * rows * width),
         name="norm",
-    )(core, hidden, gain.reshape(1, width))
+    )(hidden, gain.reshape(1, width))
     return mine, theirs
 
 
@@ -134,10 +131,10 @@
     )(*operands)
 
 
-def tables_kernel(ids_ref, own_ref, behind_ref, freq_ref, cos_ref, sin_ref, bias_ref):
+def tables_kernel(own_ref, behind_ref, freq_ref, cos_ref, sin_ref, bias_ref):
     own = own_ref[...]
     rows = own.shape[1]
-    behind = jnp.where(ids_ref[0] > 0, behind_ref[:, rows - REACH :], -1)
+    behind = jnp.where(lax.axis_index("dp") > 0, behind_ref[:, rows - REACH :], -1)
     window = jnp.concatenate([behind, own], axis=1)
     shape = (REACH, 2 * REACH)
     r, c = lax.broadcasted_iota(jnp.int32, shape, 0), lax.broadcasted_iota(jnp.int32, shape, 1)
@@ -155,7 +152,7 @@
         sin_ref[at, :] = jnp.sin(angle) * sign
 
 
-def tables(ids, own, behind):
+def tables(own, behind):
     rows = own.shape[0]
     half = np.arange(HD // 2, dtype=np.float32)
     freq = np.float32(500000.0) ** (-(2.0 * half) / np.float32(HD))
@@ -163,7 +160,7 @@
     whole = pl.BlockSpec(memory_space=pltpu.VMEM)
     return pl.pallas_call(
         tables_kernel,
-        in_specs=[pl.BlockSpec(memory_space=pltpu.SMEM)] + [whole] * 3,
+        in_specs=[whole] * 3,
         out_specs=[whole] * 3,
         out_shape=[
             jax.ShapeDtypeStruct((rows, HD), F32),
@@ -173,7 +170,7 @@
         compiler_params=params(),
         cost_estimate=cost(20 * rows * 2 * REACH, 16 * rows * REACH, 2 * rows * HD),
         name="tables",
-    )(ids, own.reshape(1, rows), behind.reshape(1, rows), freq)
+    )(own.reshape(1, rows), behind.reshape(1, rows), freq)
 
 
 def keys_kernel(a_ref, cos_ref, sin_ref, *refs):
@@ -322,8 +319,7 @@
     def swap(value):
         return lax.ppermute(value, "dp", other_core)
 
-    ids = jnp.stack([lax.axis_index("dp"), lax.axis_index("groups")]).astype(jnp.int32)
-    mine, theirs = normalise(ids, hidden, norm_gain)
+    mine, theirs = normalise(hidden, norm_gain)
     other = [swap(t) for t in theirs]
     k1, v1 = send(key_weight, key_way), send(value_weight, value_way)
     behind = from_behind(segment_ids, "dp", 1)
@@ -336,7 +332,7 @@
     key_part = project((0, -1, -2), mine, other, [key_weight, k1, k2])
     k3, yv1, key_part = after(k3, yv1, key_part)
     k4, yk3 = send(k3, key_way), send(k3, other_group)
-    cos, sin, bias = tables(ids, segment_ids, behind)
+    cos, sin, bias = tables(segment_ids, behind)
     key_part = project((-3, 2, 1), mine, other, [k3, yk2, k1b], key_part)
     v3, key_part, cos, sin, bias = after(v3, key_part, cos, sin, bias)
     v4 = send(v3, value_way)

time: 77.2 us -> 76.5 us (level)
  waiting for transfers between devices: 33.4 us -> 34.9 us
  Pallas kernels: 16.6 us -> 15.4 us
    ppermute x14, waiting for transfers between devices: 22.6 us -> 24.1 us  [send(): return lax.ppermute(value, both, way)]
    pallas_call x2, Pallas kernels: 4.42 us -> 3.32 us  [the longest x1 2.66 us: normalise(): pl.pallas_call(norm_kernel, grid=(rows // step,), in_specs=[pl.BlockSpec(...]
  transfers between devices with their start and end apart: 22 -> 22, of which waited for: 8 -> 8; matrix products, arithmetic and copies ran while one was open for 1% -> 1% of each run, Pallas kernels for 18% -> 17%
where the time goes in v9:
time: 76.5 us; the launch traced here: 76.1 us
  waiting for transfers between devices  34.9 us (46%)
  starting transfers between devices  22.7 us (30%)
  Pallas kernels  15.4 us (20%)
  local copies, waits for them, and re-layouts  2.94 us (4%)
    ppermute x14, waiting for transfers between devices, send(): return lax.ppermute(value, both, way)  24.1 us
    ppermute x14, starting transfers between devices, send(): return lax.ppermute(value, both, way)  15.3 us
    ppermute x3, waiting for transfers between devices, from_behind(): lax.ppermute(value, axis, [(source, source + steps) for source in range(i...  10.7 us
    ppermute x3, starting transfers between devices, from_behind(): lax.ppermute(value, axis, [(source, source + steps) for source in range(i...  6.2 us
    pallas_call x5, Pallas kernels, project(): pl.pallas_call(functools.partial(project_kernel, steps, len(others), len(...  5.16 us
    pallas_call x2, Pallas kernels, softmax_weights(): pl.pallas_call(functools.partial(scores_kernel, block), in_specs=[whole]...  3.42 us
    pallas_call x2, Pallas kernels, contexts(): pl.pallas_call(functools.partial(context_kernel, block), in_specs=[whole]...  3.2 us
    pallas_call x1, Pallas kernels, normalise(): pl.pallas_call(norm_kernel, grid=(rows // step,), in_specs=[pl.BlockSpec(...  2.66 us
  transfers between devices with their start and end apart: 22, of which 8 were waited for; matrix products, arithmetic and copies ran while one was open for 1% of the time, Pallas kernels for 17%

profile of v9, /device:TPU:8, one launch (start us, length us, event | category | flops | bytes accessed | tf_op | source)
XLA Modules:
  0.0 76.1 jit_solution(11961264152964011331)
XLA Ops:
  0.0 1.6 %collective-permute-start = (bf16[512,512]{1,0:T(8,128)(2,1)}, bf16[512,512]{1,0:T(8,128)(2,1)S(1)}, u32[]{:S(2)}, u32[]{:S(2)}) collective-permute-start(bf16[512,512]{1,0:T(8,128)(2,1)} %refs_2_.2), channel_id=1, source_target_pairs={{0,4},{1,5},{4,8},{5,9},{8,12},{9,13},{12,14},{13,15},{14,10},{15,... | collective-permute-start | bytes 1572872 | tf_op jit(solution)/shard_map/ppermute | solution.py:317
  2.0 0.7 reshape.9.g_ref
  2.8 2.2 %copy-done.1 = bf16[256,8192]{1,0:T(8,128)(2,1)S(1)} copy-done((bf16[256,8192]{1,0:T(8,128)(2,1)S(1)}, bf16[256,8192]{1,0:T(8,128)(2,1)}, u32[]{:S(2)}) %copy-start.1) | copy-done | bytes 4194328
  5.0 2.7 %norm.1 = (bf16[256,4096]{1,0:T(8,128)(2,1)S(1)}, bf16[128,4096]{1,0:T(8,128)(2,1)S(1)}, bf16[128,4096]{1,0:T(8,128)(2,1)S(1)}) custom-call(bf16[256,8192]{1,0:T(8,128)(2,1)S(1)} %copy-done.1, bf16[1,8192]{1,0:T(2,128)(2,1)S(1)} %reshape.9.g_ref), custom_call_target="tpu_custom_call" | custom-call | flops 16777216 | bytes 8388608 | tf_op jit(solution)/shard_map/norm/pallas_call | solution.py:64
  7.7 0.5 collective-permute-start.3
  8.2 2.0 %collective-permute-start.1 = (s32[256]{0:T(256)S(1)}, s32[256]{0:T(256)S(1)}, u32[]{:S(2)}, u32[]{:S(2)}) collective-permute-start(s32[256]{0:T(256)S(1)} %copy-done.4), channel_id=1, source_target_pairs={{0,1},{1,2},{2,3},{3,4},{4,5},{5,6},{6,7},{7,8},{8,9},{9,10},{10,1... | collective-permute-start | bytes 3080 | tf_op jit(solution)/shard_map/ppermute | solution.py:32
  10.2 3.9 %collective-permute-done.1 = s32[256]{0:T(256)S(1)} collective-permute-done((s32[256]{0:T(256)S(1)}, s32[256]{0:T(256)S(1)}, u32[]{:S(2)}, u32[]{:S(2)}) %collective-permute-start.1) | collective-permute-done | bytes 1056 | tf_op jit(solution)/shard_map/ppermute | solution.py:32
  14.1 1.6 %collective-permute-start.7 = (bf16[512,512]{1,0:T(8,128)(2,1)S(1)}, bf16[512,512]{1,0:T(8,128)(2,1)S(1)}, u32[]{:S(2)}, u32[]{:S(2)}) collective-permute-start(bf16[512,512]{1,0:T(8,128)(2,1)S(1)} %collective-permute-done.refs_3_), channel_id=1, source_target_pairs={{0,4},{1,5},{4,8},{5,9},{8,12},{9,13},{12,14},{13,15},{14,10},{15,... | collective-permute-start | bytes 1572872 | tf_op jit(solution)/shard_map/ppermute | solution.py:317
  16.1 1.5 %collective-permute-start.9 = (bf16[512,512]{1,0:T(8,128)(2,1)S(1)}, bf16[512,512]{1,0:T(8,128)(2,1)S(1)}, u32[]{:S(2)}, u32[]{:S(2)}) collective-permute-start(bf16[512,512]{1,0:T(8,128)(2,1)S(1)} %collective-permute-done.4.refs_3_), channel_id=1, source_target_pairs={{0,16},{1,17},{2,18},{3,19},{4,20},{5,21},{6,22},{7,23},{8,24},{9,... | collective-permute-start | bytes 1572872 | tf_op jit(solution)/shard_map/ppermute | solution.py:317
  17.6 9.1 %collective-permute-done.7.refs_4_ = bf16[512,512]{1,0:T(8,128)(2,1)S(1)} collective-permute-done((bf16[512,512]{1,0:T(8,128)(2,1)S(1)}, bf16[512,512]{1,0:T(8,128)(2,1)S(1)}, u32[]{:S(2)}, u32[]{:S(2)}) %collective-permute-start.7) | collective-permute-done | bytes 524320 | tf_op jit(solution)/shard_map/ppermute | solution.py:317
  26.7 1.6 %collective-permute-start.8 = (bf16[512,512]{1,0:T(8,128)(2,1)S(1)}, bf16[512,512]{1,0:T(8,128)(2,1)S(1)}, u32[]{:S(2)}, u32[]{:S(2)}) collective-permute-start(bf16[512,512]{1,0:T(8,128)(2,1)S(1)} %collective-permute-done.7.refs_4_), channel_id=1, source_target_pairs={{0,4},{1,5},{4,8},{5,9},{8,12},{9,13},{12,14},{13,15},{14,10},{15,... | collective-permute-start | bytes 1572872 | tf_op jit(solution)/shard_map/ppermute | solution.py:317
  28.7 1.5 %collective-permute-start.10 = (bf16[512,512]{1,0:T(8,128)(2,1)S(1)}, bf16[512,512]{1,0:T(8,128)(2,1)S(1)}, u32[]{:S(2)}, u32[]{:S(2)}) collective-permute-start(bf16[512,512]{1,0:T(8,128)(2,1)S(1)} %collective-permute-done.7.refs_4_), channel_id=1, source_target_pairs={{0,16},{1,17},{2,18},{3,19},{4,20},{5,21},{6,22},{7,23},{8,24},{9,... | collective-permute-start | bytes 1572872 | tf_op jit(solution)/shard_map/ppermute | solution.py:317
  30.7 1.0 %project.5 = (f32[256,512]{1,0:T(8,128)S(1)}, f32[256,512]{1,0:T(8,128)S(1)}) custom-call(bf16[256,4096]{1,0:T(8,128)(2,1)S(1)} %get-tuple-element.54.xa_ref, bf16[128,4096]{1,0:T(8,128)(2,1)S(1)} %collective-permute-done.2.refs_0_, bf16[128,4096]{1,0:T(8,128)(2,1)S(1)} %collective-permute-done.3.refs_1_, bf16[512,512]{1,0:T(8,128)(2,1)S(1)} %copy-done.2, ...), custom_call_target="tpu_custom_call" | custom-call | flops 805306368 | bytes 5767168 | tf_op jit(solution)/shard_map/project/pallas_call | solution.py:121
  31.7 6.7 %collective-permute-done.8.refs_2_ = bf16[512,512]{1,0:T(8,128)(2,1)S(1)} collective-permute-done((bf16[512,512]{1,0:T(8,128)(2,1)S(1)}, bf16[512,512]{1,0:T(8,128)(2,1)S(1)}, u32[]{:S(2)}, u32[]{:S(2)}) %collective-permute-start.8) | collective-permute-done | bytes 524320 | tf_op jit(solution)/shard_map/ppermute | solution.py:317
  38.4 1.7 %collective-permute-start.14 = (bf16[512,512]{1,0:T(8,128)(2,1)S(1)}, bf16[512,512]{1,0:T(8,128)(2,1)S(1)}, u32[]{:S(2)}, u32[]{:S(2)}) collective-permute-start(bf16[512,512]{1,0:T(8,128)(2,1)S(1)} %collective-permute-done.8.refs_2_), channel_id=1, source_target_pairs={{0,16},{1,17},{2,18},{3,19},{4,20},{5,21},{6,22},{7,23},{8,24},{9,... | collective-permute-start | bytes 1572872 | tf_op jit(solution)/shard_map/ppermute | solution.py:317
  40.0 1.6 %collective-permute-start.16 = (bf16[512,512]{1,0:T(8,128)(2,1)S(1)}, bf16[512,512]{1,0:T(8,128)(2,1)S(1)}, u32[]{:S(2)}, u32[]{:S(2)}) collective-permute-start(bf16[512,512]{1,0:T(8,128)(2,1)S(1)} %collective-permute-done.8.refs_2_), channel_id=1, source_target_pairs={{0,4},{1,5},{4,8},{5,9},{8,12},{9,13},{12,14},{13,15},{14,10},{15,... | collective-permute-start | bytes 1572872 | tf_op jit(solution)/shard_map/ppermute | solution.py:317
  41.6 0.7 tables.1
  42.3 0.8 %collective-permute-done.11.refs_4_ = bf16[512,512]{1,0:T(8,128)(2,1)S(1)} collective-permute-done((bf16[512,512]{1,0:T(8,128)(2,1)S(1)}, bf16[512,512]{1,0:T(8,128)(2,1)S(1)}, u32[]{:S(2)}, u32[]{:S(2)}) %collective-permute-start.11) | collective-permute-done | bytes 524320 | tf_op jit(solution)/shard_map/ppermute | solution.py:317
  43.1 1.0 %project.6 = (f32[256,512]{1,0:T(8,128)S(1)}, f32[256,512]{1,0:T(8,128)S(1)}) custom-call(bf16[256,4096]{1,0:T(8,128)(2,1)S(1)} %get-tuple-element.54.xa_ref, bf16[128,4096]{1,0:T(8,128)(2,1)S(1)} %collective-permute-done.2.refs_0_, bf16[128,4096]{1,0:T(8,128)(2,1)S(1)} %collective-permute-done.3.refs_1_, ...), custom_call_target="tpu_custom_call" | custom-call | flops 805306368 | bytes 5767168 | tf_op jit(solution)/shard_map/project/pallas_call | solution.py:121
  44.1 7.5 %collective-permute-done.6.refs_6_ = bf16[512,512]{1,0:T(8,128)(2,1)S(1)} collective-permute-done((bf16[512,512]{1,0:T(8,128)(2,1)S(1)}, bf16[512,512]{1,0:T(8,128)(2,1)S(1)}, u32[]{:S(2)}, u32[]{:S(2)}) %collective-permute-start.6) | collective-permute-done | bytes 524320 | tf_op jit(solution)/shard_map/ppermute | solution.py:317
  52.0 1.6 %collective-permute-start.13 = (bf16[512,512]{1,0:T(8,128)(2,1)S(1)}, bf16[512,512]{1,0:T(8,128)(2,1)S(1)}, u32[]{:S(2)}, u32[]{:S(2)}) collective-permute-start(bf16[512,512]{1,0:T(8,128)(2,1)S(1)} %collective-permute-done.9.refs_5_), channel_id=1, source_target_pairs={{0,4},{1,5},{4,8},{5,9},{8,12},{9,13},{12,14},{13,15},{14,10},{15,... | collective-permute-start | bytes 1572872 | tf_op jit(solution)/shard_map/ppermute | solution.py:317
  54.0 0.7 project.7
  55.3 1.5 %project.8 = (f32[256,512]{1,0:T(8,128)S(1)}, f32[256,512]{1,0:T(8,128)S(1)}) custom-call(bf16[256,4096]{1,0:T(8,128)(2,1)S(1)} %get-tuple-element.54.xa_ref, bf16[128,4096]{1,0:T(8,128)(2,1)S(1)} %collective-permute-done.2.refs_0_, bf16[128,4096]{1,0:T(8,128)(2,1)S(1)} %collective-permute-done.3.refs_1_, bf16[512,512]{1,0:T(8,128)(2,1)S(1)} %copy-done.3, ...), custom_call_target="tpu_custom_call" | custom-call | flops 1342177280 | bytes 6815744 | tf_op jit(solution)/shard_map/project/pallas_call | solution.py:121
  57.1 2.0 %collective-permute-start.19 = (bf16[128,512]{1,0:T(8,128)(2,1)S(1)}, bf16[128,512]{1,0:T(8,128)(2,1)S(1)}, u32[]{:S(2)}, u32[]{:S(2)}) collective-permute-start(bf16[128,512]{1,0:T(8,128)(2,1)S(1)} %get-tuple-element.88), channel_id=1, source_target_pairs={{0,1},{1,2},{2,3},{3,4},{4,5},{5,6},{6,7},{7,8},{8,9},{9,10},{10,1... | collective-permute-start | bytes 393224 | tf_op jit(solution)/shard_map/ppermute | solution.py:32
  59.1 1.7 %scores.2.p_ref = bf16[4,1024,256]{2,1,0:T(8,128)(2,1)S(1)} custom-call(bf16[256,4096]{1,0:T(8,128)(2,1)S(1)} %copy-done, bf16[256,512]{1,0:T(8,128)(2,1)S(1)} %get-tuple-element.86.ka_ref.kb_ref, bf16[256,512]{1,0:T(8,128)(2,1)S(1)} %get-tuple-element.86.ka_ref.kb_ref, f32[2,128,256]{2,1,0:T(8,128)S(1)} %get-tuple-element.87.bias_ref), custom_call_target="tpu_custom_call" | custom-call | flops 268435456 | bytes 3145728 | tf_op jit(solution)/shard_map/scores/pallas_call | solution.py:238
  60.8 3.5 %collective-permute-done.19.ka_ref = bf16[128,512]{1,0:T(8,128)(2,1)S(1)} collective-permute-done((bf16[128,512]{1,0:T(8,128)(2,1)S(1)}, bf16[128,512]{1,0:T(8,128)(2,1)S(1)}, u32[]{:S(2)}, u32[]{:S(2)}) %collective-permute-start.19) | collective-permute-done | bytes 131104 | tf_op jit(solution)/shard_map/ppermute | solution.py:32
  64.3 1.0 %project.9 = (f32[256,512]{1,0:T(8,128)S(1)}, f32[256,512]{1,0:T(8,128)S(1)}) custom-call(bf16[256,4096]{1,0:T(8,128)(2,1)S(1)} %get-tuple-element.54.xa_ref, bf16[128,4096]{1,0:T(8,128)(2,1)S(1)} %collective-permute-done.2.refs_0_, bf16[128,4096]{1,0:T(8,128)(2,1)S(1)} %collective-permute-done.3.refs_1_, ...), custom_call_target="tpu_custom_call" | custom-call | flops 805306368 | bytes 5767168 | tf_op jit(solution)/shard_map/project/pallas_call | solution.py:121
  65.3 1.7 %scores.3.p_ref = bf16[4,1024,256]{2,1,0:T(8,128)(2,1)S(1)} custom-call(bf16[256,4096]{1,0:T(8,128)(2,1)S(1)} %copy-done, bf16[128,512]{1,0:T(8,128)(2,1)S(1)} %collective-permute-done.19.ka_ref, bf16[128,512]{1,0:T(8,128)(2,1)S(1)} %get-tuple-element.93.kb_ref, f32[2,128,256]{2,1,0:T(8,128)S(1)} %get-tuple-element.87.bias_ref), custom_call_target="tpu_custom_call" | custom-call | flops 268435456 | bytes 3145728 | tf_op jit(solution)/shard_map/scores/pallas_call | solution.py:238
  67.3 2.2 %collective-permute-start.21 = (bf16[128,512]{1,0:T(8,128)(2,1)S(1)}, bf16[128,512]{1,0:T(8,128)(2,1)S(1)}, u32[]{:S(2)}, u32[]{:S(2)}) collective-permute-start(bf16[128,512]{1,0:T(8,128)(2,1)S(1)} %get-tuple-element.97), channel_id=1, source_target_pairs={{0,1},{1,2},{2,3},{3,4},{4,5},{5,6},{6,7},{7,8},{8,9},{9,10},{10,1... | collective-permute-start | bytes 393224 | tf_op jit(solution)/shard_map/ppermute | solution.py:32
  69.5 1.6 %context.2.refs_0_ = bf16[256,4096]{1,0:T(8,128)(2,1)} custom-call(bf16[4,1024,256]{2,1,0:T(8,128)(2,1)S(1)} %scores.2.p_ref, bf16[256,512]{1,0:T(8,128)(2,1)S(1)} %get-tuple-element.100.va_ref.vb_ref, bf16[256,512]{1,0:T(8,128)(2,1)S(1)} %get-tuple-element.100.va_ref.vb_ref), custom_call_target="tpu_custom_call" | custom-call | flops 268435456 | bytes 3145728 | tf_op jit(solution)/shard_map/context/pallas_call | solution.py:276
  71.2 3.3 %collective-permute-done.21.va_ref = bf16[128,512]{1,0:T(8,128)(2,1)S(1)} collective-permute-done((bf16[128,512]{1,0:T(8,128)(2,1)S(1)}, bf16[128,512]{1,0:T(8,128)(2,1)S(1)}, u32[]{:S(2)}, u32[]{:S(2)}) %collective-permute-start.21) | collective-permute-done | bytes 131104 | tf_op jit(solution)/shard_map/ppermute | solution.py:32
  74.5 1.6 %context.3 = bf16[256,4096]{1,0:T(8,128)(2,1)} custom-call(bf16[4,1024,256]{2,1,0:T(8,128)(2,1)S(1)} %scores.3.p_ref, bf16[128,512]{1,0:T(8,128)(2,1)S(1)} %collective-permute-done.21.va_ref, bf16[128,512]{1,0:T(8,128)(2,1)S(1)} %get-tuple-element.98.vb_ref, bf16[256,4096]{1,0:T(8,128)(2,1)} %context.2.refs_0_), custom_call_target="tpu_custom_call", output_to_operand_aliasing={{}: (3, {})} | custom-call | flops 268435456 | bytes 3145728 | tf_op jit(solution)/shard_map/context/pallas_call | solution.py:276
  (38 shorter events, 3.9 us)
Async XLA Ops:
  0.0 14.1 %collective-permute-start = (bf16[512,512]{1,0:T(8,128)(2,1)}, bf16[512,512]{1,0:T(8,128)(2,1)S(1)}, u32[]{:S(2)}, u32[]{:S(2)}) collective-permute-start(bf16[512,512]{1,0:T(8,128)(2,1)} %refs_2_.2), channel_id=1, source_target_pairs={{0,4},{1,5},{4,8},{5,9},{8,12},{9,13},{12,14},{13,15},{14,10},{15,... | collective-permute-start | bytes 1572872 | tf_op jit(solution)/shard_map/ppermute | solution.py:317
  1.6 14.1 %collective-permute-start.4 = (bf16[512,512]{1,0:T(8,128)(2,1)}, bf16[512,512]{1,0:T(8,128)(2,1)S(1)}, u32[]{:S(2)}, u32[]{:S(2)}) collective-permute-start(bf16[512,512]{1,0:T(8,128)(2,1)} %refs_2_.3), channel_id=1, source_target_pairs={{0,2},{1,3},{4,0},{5,1},{8,4},{9,5},{12,8},{13,9},{14,12},{15,13},... | collective-permute-start | bytes 1572872 | tf_op jit(solution)/shard_map/ppermute | solution.py:317
  2.8 2.2 %copy-start.1 = (bf16[256,8192]{1,0:T(8,128)(2,1)S(1)}, bf16[256,8192]{1,0:T(8,128)(2,1)}, u32[]{:S(2)}) copy-start(bf16[256,8192]{1,0:T(8,128)(2,1)} %h_ref.1) | copy-start | bytes 12582916
  5.0 3.3 %copy-start.4 = (s32[256]{0:T(256)S(1)}, s32[256]{0:T(256)}, u32[]{:S(2)}) copy-start(s32[256]{0:T(256)} %param.12) | copy-start | bytes 3076
  5.0 23.3 %copy-start.2 = (bf16[512,512]{1,0:T(8,128)(2,1)S(1)}, bf16[512,512]{1,0:T(8,128)(2,1)}, u32[]{:S(2)}) copy-start(bf16[512,512]{1,0:T(8,128)(2,1)} %refs_2_.2) | copy-start | bytes 1572868
  7.6 21.1 %collective-permute-start.2 = (bf16[128,4096]{1,0:T(8,128)(2,1)S(1)}, bf16[128,4096]{1,0:T(8,128)(2,1)S(1)}, u32[]{:S(2)}, u32[]{:S(2)}) collective-permute-start(bf16[128,4096]{1,0:T(8,128)(2,1)S(1)} %get-tuple-element.55), channel_id=1, source_target_pairs={{0,1},{1,0},{2,3},{3,2},{4,5},{5,4},{6,7},{7,6},{8,9},{9,8},{10,11... | collective-permute-start | bytes 3145736 | tf_op jit(solution)/shard_map/ppermute | solution.py:320
  7.7 22.5 %collective-permute-start.3 = (bf16[128,4096]{1,0:T(8,128)(2,1)S(1)}, bf16[128,4096]{1,0:T(8,128)(2,1)S(1)}, u32[]{:S(2)}, u32[]{:S(2)}) collective-permute-start(bf16[128,4096]{1,0:T(8,128)(2,1)S(1)} %get-tuple-element.56), channel_id=1, source_target_pairs={{0,1},{1,0},{2,3},{3,2},{4,5},{5,4},{6,7},{7,6},{8,9},{9,8},{10,11... | collective-permute-start | bytes 3145736 | tf_op jit(solution)/shard_map/ppermute | solution.py:320
  8.2 5.8 %collective-permute-start.1 = (s32[256]{0:T(256)S(1)}, s32[256]{0:T(256)S(1)}, u32[]{:S(2)}, u32[]{:S(2)}) collective-permute-start(s32[256]{0:T(256)S(1)} %copy-done.4), channel_id=1, source_target_pairs={{0,1},{1,2},{2,3},{3,4},{4,5},{5,6},{6,7},{7,8},{8,9},{9,10},{10,1... | collective-permute-start | bytes 3080 | tf_op jit(solution)/shard_map/ppermute | solution.py:32
  14.1 27.6 %copy-start.5 = (f32[1,128]{1,0:T(1,128)S(1)}, f32[1,128]{1,0:T(1,128)}, u32[]{:S(2)}) copy-start(f32[1,128]{1,0:T(1,128)} %constant.2.clone.freq_ref) | copy-start | bytes 1540
  14.1 12.6 %collective-permute-start.7 = (bf16[512,512]{1,0:T(8,128)(2,1)S(1)}, bf16[512,512]{1,0:T(8,128)(2,1)S(1)}, u32[]{:S(2)}, u32[]{:S(2)}) collective-permute-start(bf16[512,512]{1,0:T(8,128)(2,1)S(1)} %collective-permute-done.refs_3_), channel_id=1, source_target_pairs={{0,4},{1,5},{4,8},{5,9},{8,12},{9,13},{12,14},{13,15},{14,10},{15,... | collective-permute-start | bytes 1572872 | tf_op jit(solution)/shard_map/ppermute | solution.py:317
  15.6 12.6 %collective-permute-start.5 = (bf16[512,512]{1,0:T(8,128)(2,1)S(1)}, bf16[512,512]{1,0:T(8,128)(2,1)S(1)}, u32[]{:S(2)}, u32[]{:S(2)}) collective-permute-start(bf16[512,512]{1,0:T(8,128)(2,1)S(1)} %collective-permute-done.4.refs_3_), channel_id=1, source_target_pairs={{0,2},{1,3},{4,0},{5,1},{8,4},{9,5},{12,8},{13,9},{14,12},{15,13},... | collective-permute-start | bytes 1572872 | tf_op jit(solution)/shard_map/ppermute | solution.py:317
  16.1 15.6 %collective-permute-start.9 = (bf16[512,512]{1,0:T(8,128)(2,1)S(1)}, bf16[512,512]{1,0:T(8,128)(2,1)S(1)}, u32[]{:S(2)}, u32[]{:S(2)}) collective-permute-start(bf16[512,512]{1,0:T(8,128)(2,1)S(1)} %collective-permute-done.4.refs_3_), channel_id=1, source_target_pairs={{0,16},{1,17},{2,18},{3,19},{4,20},{5,21},{6,22},{7,23},{8,24},{9,... | collective-permute-start | bytes 1572872 | tf_op jit(solution)/shard_map/ppermute | solution.py:317
  26.7 11.7 %collective-permute-start.8 = (bf16[512,512]{1,0:T(8,128)(2,1)S(1)}, bf16[512,512]{1,0:T(8,128)(2,1)S(1)}, u32[]{:S(2)}, u32[]{:S(2)}) collective-permute-start(bf16[512,512]{1,0:T(8,128)(2,1)S(1)} %collective-permute-done.7.refs_4_), channel_id=1, source_target_pairs={{0,4},{1,5},{4,8},{5,9},{8,12},{9,13},{12,14},{13,15},{14,10},{15,... | collective-permute-start | bytes 1572872 | tf_op jit(solution)/shard_map/ppermute | solution.py:317
  28.3 14.9 %collective-permute-start.11 = (bf16[512,512]{1,0:T(8,128)(2,1)S(1)}, bf16[512,512]{1,0:T(8,128)(2,1)S(1)}, u32[]{:S(2)}, u32[]{:S(2)}) collective-permute-start(bf16[512,512]{1,0:T(8,128)(2,1)S(1)} %copy-done.2), channel_id=1, source_target_pairs={{0,2},{1,3},{4,0},{5,1},{8,4},{9,5},{12,8},{13,9},{14,12},{15,13},... | collective-permute-start | bytes 1572872 | tf_op jit(solution)/shard_map/ppermute | solution.py:317
  28.7 14.4 %collective-permute-start.10 = (bf16[512,512]{1,0:T(8,128)(2,1)S(1)}, bf16[512,512]{1,0:T(8,128)(2,1)S(1)}, u32[]{:S(2)}, u32[]{:S(2)}) collective-permute-start(bf16[512,512]{1,0:T(8,128)(2,1)S(1)} %collective-permute-done.7.refs_4_), channel_id=1, source_target_pairs={{0,16},{1,17},{2,18},{3,19},{4,20},{5,21},{6,22},{7,23},{8,24},{9,... | collective-permute-start | bytes 1572872 | tf_op jit(solution)/shard_map/ppermute | solution.py:317
  30.2 21.3 %collective-permute-start.6 = (bf16[512,512]{1,0:T(8,128)(2,1)S(1)}, bf16[512,512]{1,0:T(8,128)(2,1)S(1)}, u32[]{:S(2)}, u32[]{:S(2)}) collective-permute-start(bf16[512,512]{1,0:T(8,128)(2,1)S(1)} %collective-permute-done.5.refs_4_), channel_id=1, source_target_pairs={{0,2},{1,3},{4,0},{5,1},{8,4},{9,5},{12,8},{13,9},{14,12},{15,13},... | collective-permute-start | bytes 1572872 | tf_op jit(solution)/shard_map/ppermute | solution.py:317
  38.4 15.3 %collective-permute-start.14 = (bf16[512,512]{1,0:T(8,128)(2,1)S(1)}, bf16[512,512]{1,0:T(8,128)(2,1)S(1)}, u32[]{:S(2)}, u32[]{:S(2)}) collective-permute-start(bf16[512,512]{1,0:T(8,128)(2,1)S(1)} %collective-permute-done.8.refs_2_), channel_id=1, source_target_pairs={{0,16},{1,17},{2,18},{3,19},{4,20},{5,21},{6,22},{7,23},{8,24},{9,... | collective-permute-start | bytes 1572872 | tf_op jit(solution)/shard_map/ppermute | solution.py:317
  40.0 14.0 %collective-permute-start.16 = (bf16[512,512]{1,0:T(8,128)(2,1)S(1)}, bf16[512,512]{1,0:T(8,128)(2,1)S(1)}, u32[]{:S(2)}, u32[]{:S(2)}) collective-permute-start(bf16[512,512]{1,0:T(8,128)(2,1)S(1)} %collective-permute-done.8.refs_2_), channel_id=1, source_target_pairs={{0,4},{1,5},{4,8},{5,9},{8,12},{9,13},{12,14},{13,15},{14,10},{15,... | collective-permute-start | bytes 1572872 | tf_op jit(solution)/shard_map/ppermute | solution.py:317
  51.6 3.7 %copy-start.3 = (bf16[512,512]{1,0:T(8,128)(2,1)S(1)}, bf16[512,512]{1,0:T(8,128)(2,1)}, u32[]{:S(2)}) copy-start(bf16[512,512]{1,0:T(8,128)(2,1)} %refs_2_.3) | copy-start | bytes 1572868
  51.6 12.7 %collective-permute-start.12 = (bf16[512,512]{1,0:T(8,128)(2,1)S(1)}, bf16[512,512]{1,0:T(8,128)(2,1)S(1)}, u32[]{:S(2)}, u32[]{:S(2)}) collective-permute-start(bf16[512,512]{1,0:T(8,128)(2,1)S(1)} %collective-permute-done.6.refs_6_), channel_id=1, source_target_pairs={{0,2},{1,3},{4,0},{5,1},{8,4},{9,5},{12,8},{13,9},{14,12},{15,13},... | collective-permute-start | bytes 1572872 | tf_op jit(solution)/shard_map/ppermute | solution.py:317
  52.0 12.3 %collective-permute-start.13 = (bf16[512,512]{1,0:T(8,128)(2,1)S(1)}, bf16[512,512]{1,0:T(8,128)(2,1)S(1)}, u32[]{:S(2)}, u32[]{:S(2)}) collective-permute-start(bf16[512,512]{1,0:T(8,128)(2,1)S(1)} %collective-permute-done.9.refs_5_), channel_id=1, source_target_pairs={{0,4},{1,5},{4,8},{5,9},{8,12},{9,13},{12,14},{13,15},{14,10},{15,... | collective-permute-start | bytes 1572872 | tf_op jit(solution)/shard_map/ppermute | solution.py:317
  53.6 10.7 %collective-permute-start.15 = (bf16[512,512]{1,0:T(8,128)(2,1)S(1)}, bf16[512,512]{1,0:T(8,128)(2,1)S(1)}, u32[]{:S(2)}, u32[]{:S(2)}) collective-permute-start(bf16[512,512]{1,0:T(8,128)(2,1)S(1)} %collective-permute-done.6.refs_6_), channel_id=1, source_target_pairs={{0,16},{1,17},{2,18},{3,19},{4,20},{5,21},{6,22},{7,23},{8,24},{9,... | collective-permute-start | bytes 1572872 | tf_op jit(solution)/shard_map/ppermute | solution.py:317
  54.7 2.1 %collective-permute-start.17 = (f32[128,512]{1,0:T(8,128)S(1)}, f32[128,512]{1,0:T(8,128)S(1)}, u32[]{:S(2)}, u32[]{:S(2)}) collective-permute-start(f32[128,512]{1,0:T(8,128)S(1)} %get-tuple-element.75), channel_id=1, source_target_pairs={{0,1},{1,0},{2,3},{3,2},{4,5},{5,4},{6,7},{7,6},{8,9},{9,8},{10,11... | collective-permute-start | bytes 786440 | tf_op jit(solution)/shard_map/ppermute | solution.py:320
  54.8 2.0 %collective-permute-start.18 = (f32[128,512]{1,0:T(8,128)S(1)}, f32[128,512]{1,0:T(8,128)S(1)}, u32[]{:S(2)}, u32[]{:S(2)}) collective-permute-start(f32[128,512]{1,0:T(8,128)S(1)} %get-tuple-element.76), channel_id=1, source_target_pairs={{0,1},{1,0},{2,3},{3,2},{4,5},{5,4},{6,7},{7,6},{8,9},{9,8},{10,11... | collective-permute-start | bytes 786440 | tf_op jit(solution)/shard_map/ppermute | solution.py:320
  55.3 3.8 %copy-start = (bf16[256,4096]{1,0:T(8,128)(2,1)S(1)}, bf16[256,4096]{1,0:T(8,128)(2,1)}, u32[]{:S(2)}) copy-start(bf16[256,4096]{1,0:T(8,128)(2,1)} %q_ref.3) | copy-start | bytes 6291460
  57.1 7.2 %collective-permute-start.19 = (bf16[128,512]{1,0:T(8,128)(2,1)S(1)}, bf16[128,512]{1,0:T(8,128)(2,1)S(1)}, u32[]{:S(2)}, u32[]{:S(2)}) collective-permute-start(bf16[128,512]{1,0:T(8,128)(2,1)S(1)} %get-tuple-element.88), channel_id=1, source_target_pairs={{0,1},{1,2},{2,3},{3,4},{4,5},{5,6},{6,7},{7,8},{8,9},{9,10},{10,1... | collective-permute-start | bytes 393224 | tf_op jit(solution)/shard_map/ppermute | solution.py:32
  65.3 2.0 %collective-permute-start.20 = (f32[256,512]{1,0:T(8,128)S(1)}, f32[256,512]{1,0:T(8,128)S(1)}, u32[]{:S(2)}, u32[]{:S(2)}) collective-permute-start(f32[256,512]{1,0:T(8,128)S(1)} %get-tuple-element.91), channel_id=1, source_target_pairs={{0,1},{1,0},{2,3},{3,2},{4,5},{5,4},{6,7},{7,6},{8,9},{9,8},{10,11... | collective-permute-start | bytes 1572872 | tf_op jit(solution)/shard_map/ppermute | solution.py:320
  67.3 7.2 %collective-permute-start.21 = (bf16[128,512]{1,0:T(8,128)(2,1)S(1)}, bf16[128,512]{1,0:T(8,128)(2,1)S(1)}, u32[]{:S(2)}, u32[]{:S(2)}) collective-permute-start(bf16[128,512]{1,0:T(8,128)(2,1)S(1)} %get-tuple-element.97), channel_id=1, source_target_pairs={{0,1},{1,2},{2,3},{3,4},{4,5},{5,6},{6,7},{7,8},{8,9},{9,10},{10,1... | collective-permute-start | bytes 393224 | tf_op jit(solution)/shard_map/ppermute | solution.py:32

commit v10 on v9

--- a/solution.py
+++ b/solution.py
@@ -256,13 +256,17 @@
     for h in range(p_ref.shape[0]):
         at = slice(h * HD, (h + 1) * HD)
         values = jnp.concatenate([va_ref[:rows, at], vb_ref[-rows:, at]], axis=0)
-        c = jnp.dot(p_ref[h], values, preferred_element_type=F32).astype(BF16)
-        for j in range(GROUP):
-            held[:, h * width + j * HD : h * width + (j + 1) * HD] = c[j * rows : (j + 1) * rows]
-        here = (pl.ds(0, rows), pl.ds(h * width, width))
-        there = (pl.ds(block * rows, rows), pl.ds(h * width, width))
-        copies.append(pltpu.make_async_copy(held.at[here], out_ref.at[there], sems.at[h]))
-        copies[-1].start()
+        for part in range(2):
+            some = GROUP // 2
+            p = p_ref[h, part * some * rows : (part + 1) * some * rows, :]
+            c = jnp.dot(p, values, preferred_element_type=F32).astype(BF16)
+            start = h * width + part * some * HD
+            for j in range(some):
+                held[:, start + j * HD : start + (j + 1) * HD] = c[j * rows : (j + 1) * rows]
+            here = (pl.ds(0, rows), pl.ds(start, some * HD))
+            there = (pl.ds(block * rows, rows), pl.ds(start, some * HD))
+            copies.append(pltpu.make_async_copy(held.at[here], out_ref.at[there], sems.at[2 * h + part]))
+            copies[-1].start()
     for copy in copies:
         copy.wait()
 
@@ -280,7 +284,7 @@
         out_shape=jax.ShapeDtypeStruct((2 * rows, GROUP * feats), BF16),
         scratch_shapes=[
             pltpu.VMEM((rows, GROUP * feats), BF16),
-            pltpu.SemaphoreType.DMA((heads,)),
+            pltpu.SemaphoreType.DMA((2 * heads,)),
         ],
         input_output_aliases={3: 0} if more else {},
         compiler_params=params(),

time: 76.5 us -> 76.4 us (level)
  no operation moved by 1% of the time
where the time goes in v10:
time: 76.4 us; the launch traced here: 76 us
  waiting for transfers between devices  35 us (46%)
  starting transfers between devices  22.7 us (30%)
  Pallas kernels  15.3 us (20%)
  local copies, waits for them, and re-layouts  2.94 us (4%)
    ppermute x14, waiting for transfers between devices, send(): return lax.ppermute(value, both, way)  24.1 us
    ppermute x14, starting transfers between devices, send(): return lax.ppermute(value, both, way)  15.3 us
    ppermute x3, waiting for transfers between devices, from_behind(): lax.ppermute(value, axis, [(source, source + steps) for source in range(i...  10.7 us
    ppermute x3, starting transfers between devices, from_behind(): lax.ppermute(value, axis, [(source, source + steps) for source in range(i...  6.2 us
    pallas_call x5, Pallas kernels, project(): pl.pallas_call(functools.partial(project_kernel, steps, len(others), len(...  5.16 us
    pallas_call x2, Pallas kernels, softmax_weights(): pl.pallas_call(functools.partial(scores_kernel, block), in_specs=[whole]...  3.42 us
    pallas_call x2, Pallas kernels, contexts(): pl.pallas_call(functools.partial(context_kernel, block), in_specs=[whole]...  3.11 us
    pallas_call x1, Pallas kernels, normalise(): pl.pallas_call(norm_kernel, grid=(rows // step,), in_specs=[pl.BlockSpec(...  2.66 us
  transfers between devices with their start and end apart: 22, of which 8 were waited for; matrix products, arithmetic and copies ran while one was open for 1% of the time, Pallas kernels for 17%

profile of v10, /device:TPU:8, one launch (start us, length us, event | category | flops | bytes accessed | tf_op | source)
XLA Modules:
  0.0 76.0 jit_solution(17261119586665438144)
XLA Ops:
  0.0 1.6 %collective-permute-start = (bf16[512,512]{1,0:T(8,128)(2,1)}, bf16[512,512]{1,0:T(8,128)(2,1)S(1)}, u32[]{:S(2)}, u32[]{:S(2)}) collective-permute-start(bf16[512,512]{1,0:T(8,128)(2,1)} %refs_2_.2), channel_id=1, source_target_pairs={{0,4},{1,5},{4,8},{5,9},{8,12},{9,13},{12,14},{13,15},{14,10},{15,... | collective-permute-start | bytes 1572872 | tf_op jit(solution)/shard_map/ppermute | solution.py:321
  2.0 0.7 reshape.9.g_ref
  2.8 2.2 %copy-done.1 = bf16[256,8192]{1,0:T(8,128)(2,1)S(1)} copy-done((bf16[256,8192]{1,0:T(8,128)(2,1)S(1)}, bf16[256,8192]{1,0:T(8,128)(2,1)}, u32[]{:S(2)}) %copy-start.1) | copy-done | bytes 4194328
  5.0 2.7 %norm.1 = (bf16[256,4096]{1,0:T(8,128)(2,1)S(1)}, bf16[128,4096]{1,0:T(8,128)(2,1)S(1)}, bf16[128,4096]{1,0:T(8,128)(2,1)S(1)}) custom-call(bf16[256,8192]{1,0:T(8,128)(2,1)S(1)} %copy-done.1, bf16[1,8192]{1,0:T(2,128)(2,1)S(1)} %reshape.9.g_ref), custom_call_target="tpu_custom_call" | custom-call | flops 16777216 | bytes 8388608 | tf_op jit(solution)/shard_map/norm/pallas_call | solution.py:64
  7.7 0.5 collective-permute-start.3
  8.2 2.0 %collective-permute-start.1 = (s32[256]{0:T(256)S(1)}, s32[256]{0:T(256)S(1)}, u32[]{:S(2)}, u32[]{:S(2)}) collective-permute-start(s32[256]{0:T(256)S(1)} %copy-done.4), channel_id=1, source_target_pairs={{0,1},{1,2},{2,3},{3,4},{4,5},{5,6},{6,7},{7,8},{8,9},{9,10},{10,1... | collective-permute-start | bytes 3080 | tf_op jit(solution)/shard_map/ppermute | solution.py:32
  10.2 3.9 %collective-permute-done.1 = s32[256]{0:T(256)S(1)} collective-permute-done((s32[256]{0:T(256)S(1)}, s32[256]{0:T(256)S(1)}, u32[]{:S(2)}, u32[]{:S(2)}) %collective-permute-start.1) | collective-permute-done | bytes 1056 | tf_op jit(solution)/shard_map/ppermute | solution.py:32
  14.1 1.6 %collective-permute-start.7 = (bf16[512,512]{1,0:T(8,128)(2,1)S(1)}, bf16[512,512]{1,0:T(8,128)(2,1)S(1)}, u32[]{:S(2)}, u32[]{:S(2)}) collective-permute-start(bf16[512,512]{1,0:T(8,128)(2,1)S(1)} %collective-permute-done.refs_3_), channel_id=1, source_target_pairs={{0,4},{1,5},{4,8},{5,9},{8,12},{9,13},{12,14},{13,15},{14,10},{15,... | collective-permute-start | bytes 1572872 | tf_op jit(solution)/shard_map/ppermute | solution.py:321
  16.1 1.5 %collective-permute-start.9 = (bf16[512,512]{1,0:T(8,128)(2,1)S(1)}, bf16[512,512]{1,0:T(8,128)(2,1)S(1)}, u32[]{:S(2)}, u32[]{:S(2)}) collective-permute-start(bf16[512,512]{1,0:T(8,128)(2,1)S(1)} %collective-permute-done.4.refs_3_), channel_id=1, source_target_pairs={{0,16},{1,17},{2,18},{3,19},{4,20},{5,21},{6,22},{7,23},{8,24},{9,... | collective-permute-start | bytes 1572872 | tf_op jit(solution)/shard_map/ppermute | solution.py:321
  17.6 9.1 %collective-permute-done.7.refs_4_ = bf16[512,512]{1,0:T(8,128)(2,1)S(1)} collective-permute-done((bf16[512,512]{1,0:T(8,128)(2,1)S(1)}, bf16[512,512]{1,0:T(8,128)(2,1)S(1)}, u32[]{:S(2)}, u32[]{:S(2)}) %collective-permute-start.7) | collective-permute-done | bytes 524320 | tf_op jit(solution)/shard_map/ppermute | solution.py:321
  26.7 1.6 %collective-permute-start.8 = (bf16[512,512]{1,0:T(8,128)(2,1)S(1)}, bf16[512,512]{1,0:T(8,128)(2,1)S(1)}, u32[]{:S(2)}, u32[]{:S(2)}) collective-permute-start(bf16[512,512]{1,0:T(8,128)(2,1)S(1)} %collective-permute-done.7.refs_4_), channel_id=1, source_target_pairs={{0,4},{1,5},{4,8},{5,9},{8,12},{9,13},{12,14},{13,15},{14,10},{15,... | collective-permute-start | bytes 1572872 | tf_op jit(solution)/shard_map/ppermute | solution.py:321
  28.7 1.5 %collective-permute-start.10 = (bf16[512,512]{1,0:T(8,128)(2,1)S(1)}, bf16[512,512]{1,0:T(8,128)(2,1)S(1)}, u32[]{:S(2)}, u32[]{:S(2)}) collective-permute-start(bf16[512,512]{1,0:T(8,128)(2,1)S(1)} %collective-permute-done.7.refs_4_), channel_id=1, source_target_pairs={{0,16},{1,17},{2,18},{3,19},{4,20},{5,21},{6,22},{7,23},{8,24},{9,... | collective-permute-start | bytes 1572872 | tf_op jit(solution)/shard_map/ppermute | solution.py:321
  30.7 1.0 %project.5 = (f32[256,512]{1,0:T(8,128)S(1)}, f32[256,512]{1,0:T(8,128)S(1)}) custom-call(bf16[256,4096]{1,0:T(8,128)(2,1)S(1)} %get-tuple-element.54.xa_ref, bf16[128,4096]{1,0:T(8,128)(2,1)S(1)} %collective-permute-done.2.refs_0_, bf16[128,4096]{1,0:T(8,128)(2,1)S(1)} %collective-permute-done.3.refs_1_, bf16[512,512]{1,0:T(8,128)(2,1)S(1)} %copy-done.2, ...), custom_call_target="tpu_custom_call" | custom-call | flops 805306368 | bytes 5767168 | tf_op jit(solution)/shard_map/project/pallas_call | solution.py:121
  31.7 6.7 %collective-permute-done.8.refs_2_ = bf16[512,512]{1,0:T(8,128)(2,1)S(1)} collective-permute-done((bf16[512,512]{1,0:T(8,128)(2,1)S(1)}, bf16[512,512]{1,0:T(8,128)(2,1)S(1)}, u32[]{:S(2)}, u32[]{:S(2)}) %collective-permute-start.8) | collective-permute-done | bytes 524320 | tf_op jit(solution)/shard_map/ppermute | solution.py:321
  38.4 1.7 %collective-permute-start.14 = (bf16[512,512]{1,0:T(8,128)(2,1)S(1)}, bf16[512,512]{1,0:T(8,128)(2,1)S(1)}, u32[]{:S(2)}, u32[]{:S(2)}) collective-permute-start(bf16[512,512]{1,0:T(8,128)(2,1)S(1)} %collective-permute-done.8.refs_2_), channel_id=1, source_target_pairs={{0,16},{1,17},{2,18},{3,19},{4,20},{5,21},{6,22},{7,23},{8,24},{9,... | collective-permute-start | bytes 1572872 | tf_op jit(solution)/shard_map/ppermute | solution.py:321
  40.0 1.6 %collective-permute-start.16 = (bf16[512,512]{1,0:T(8,128)(2,1)S(1)}, bf16[512,512]{1,0:T(8,128)(2,1)S(1)}, u32[]{:S(2)}, u32[]{:S(2)}) collective-permute-start(bf16[512,512]{1,0:T(8,128)(2,1)S(1)} %collective-permute-done.8.refs_2_), channel_id=1, source_target_pairs={{0,4},{1,5},{4,8},{5,9},{8,12},{9,13},{12,14},{13,15},{14,10},{15,... | collective-permute-start | bytes 1572872 | tf_op jit(solution)/shard_map/ppermute | solution.py:321
  41.6 0.7 tables.1
  42.3 0.8 %collective-permute-done.11.refs_4_ = bf16[512,512]{1,0:T(8,128)(2,1)S(1)} collective-permute-done((bf16[512,512]{1,0:T(8,128)(2,1)S(1)}, bf16[512,512]{1,0:T(8,128)(2,1)S(1)}, u32[]{:S(2)}, u32[]{:S(2)}) %collective-permute-start.11) | collective-permute-done | bytes 524320 | tf_op jit(solution)/shard_map/ppermute | solution.py:321
  43.1 1.0 %project.6 = (f32[256,512]{1,0:T(8,128)S(1)}, f32[256,512]{1,0:T(8,128)S(1)}) custom-call(bf16[256,4096]{1,0:T(8,128)(2,1)S(1)} %get-tuple-element.54.xa_ref, bf16[128,4096]{1,0:T(8,128)(2,1)S(1)} %collective-permute-done.2.refs_0_, bf16[128,4096]{1,0:T(8,128)(2,1)S(1)} %collective-permute-done.3.refs_1_, ...), custom_call_target="tpu_custom_call" | custom-call | flops 805306368 | bytes 5767168 | tf_op jit(solution)/shard_map/project/pallas_call | solution.py:121
  44.1 7.5 %collective-permute-done.6.refs_6_ = bf16[512,512]{1,0:T(8,128)(2,1)S(1)} collective-permute-done((bf16[512,512]{1,0:T(8,128)(2,1)S(1)}, bf16[512,512]{1,0:T(8,128)(2,1)S(1)}, u32[]{:S(2)}, u32[]{:S(2)}) %collective-permute-start.6) | collective-permute-done | bytes 524320 | tf_op jit(solution)/shard_map/ppermute | solution.py:321
  52.0 1.6 %collective-permute-start.13 = (bf16[512,512]{1,0:T(8,128)(2,1)S(1)}, bf16[512,512]{1,0:T(8,128)(2,1)S(1)}, u32[]{:S(2)}, u32[]{:S(2)}) collective-permute-start(bf16[512,512]{1,0:T(8,128)(2,1)S(1)} %collective-permute-done.9.refs_5_), channel_id=1, source_target_pairs={{0,4},{1,5},{4,8},{5,9},{8,12},{9,13},{12,14},{13,15},{14,10},{15,... | collective-permute-start | bytes 1572872 | tf_op jit(solution)/shard_map/ppermute | solution.py:321
  54.0 0.7 project.7
  55.3 1.5 %project.8 = (f32[256,512]{1,0:T(8,128)S(1)}, f32[256,512]{1,0:T(8,128)S(1)}) custom-call(bf16[256,4096]{1,0:T(8,128)(2,1)S(1)} %get-tuple-element.54.xa_ref, bf16[128,4096]{1,0:T(8,128)(2,1)S(1)} %collective-permute-done.2.refs_0_, bf16[128,4096]{1,0:T(8,128)(2,1)S(1)} %collective-permute-done.3.refs_1_, bf16[512,512]{1,0:T(8,128)(2,1)S(1)} %copy-done.3, ...), custom_call_target="tpu_custom_call" | custom-call | flops 1342177280 | bytes 6815744 | tf_op jit(solution)/shard_map/project/pallas_call | solution.py:121
  57.1 2.0 %collective-permute-start.19 = (bf16[128,512]{1,0:T(8,128)(2,1)S(1)}, bf16[128,512]{1,0:T(8,128)(2,1)S(1)}, u32[]{:S(2)}, u32[]{:S(2)}) collective-permute-start(bf16[128,512]{1,0:T(8,128)(2,1)S(1)} %get-tuple-element.88), channel_id=1, source_target_pairs={{0,1},{1,2},{2,3},{3,4},{4,5},{5,6},{6,7},{7,8},{8,9},{9,10},{10,1... | collective-permute-start | bytes 393224 | tf_op jit(solution)/shard_map/ppermute | solution.py:32
  59.1 1.7 %scores.2.p_ref = bf16[4,1024,256]{2,1,0:T(8,128)(2,1)S(1)} custom-call(bf16[256,4096]{1,0:T(8,128)(2,1)S(1)} %copy-done, bf16[256,512]{1,0:T(8,128)(2,1)S(1)} %get-tuple-element.86.ka_ref.kb_ref, bf16[256,512]{1,0:T(8,128)(2,1)S(1)} %get-tuple-element.86.ka_ref.kb_ref, f32[2,128,256]{2,1,0:T(8,128)S(1)} %get-tuple-element.87.bias_ref), custom_call_target="tpu_custom_call" | custom-call | flops 268435456 | bytes 3145728 | tf_op jit(solution)/shard_map/scores/pallas_call | solution.py:238
  60.8 3.5 %collective-permute-done.19.ka_ref = bf16[128,512]{1,0:T(8,128)(2,1)S(1)} collective-permute-done((bf16[128,512]{1,0:T(8,128)(2,1)S(1)}, bf16[128,512]{1,0:T(8,128)(2,1)S(1)}, u32[]{:S(2)}, u32[]{:S(2)}) %collective-permute-start.19) | collective-permute-done | bytes 131104 | tf_op jit(solution)/shard_map/ppermute | solution.py:32
  64.3 1.0 %project.9 = (f32[256,512]{1,0:T(8,128)S(1)}, f32[256,512]{1,0:T(8,128)S(1)}) custom-call(bf16[256,4096]{1,0:T(8,128)(2,1)S(1)} %get-tuple-element.54.xa_ref, bf16[128,4096]{1,0:T(8,128)(2,1)S(1)} %collective-permute-done.2.refs_0_, bf16[128,4096]{1,0:T(8,128)(2,1)S(1)} %collective-permute-done.3.refs_1_, ...), custom_call_target="tpu_custom_call" | custom-call | flops 805306368 | bytes 5767168 | tf_op jit(solution)/shard_map/project/pallas_call | solution.py:121
  65.3 1.7 %scores.3.p_ref = bf16[4,1024,256]{2,1,0:T(8,128)(2,1)S(1)} custom-call(bf16[256,4096]{1,0:T(8,128)(2,1)S(1)} %copy-done, bf16[128,512]{1,0:T(8,128)(2,1)S(1)} %collective-permute-done.19.ka_ref, bf16[128,512]{1,0:T(8,128)(2,1)S(1)} %get-tuple-element.93.kb_ref, f32[2,128,256]{2,1,0:T(8,128)S(1)} %get-tuple-element.87.bias_ref), custom_call_target="tpu_custom_call" | custom-call | flops 268435456 | bytes 3145728 | tf_op jit(solution)/shard_map/scores/pallas_call | solution.py:238
  67.3 2.2 %collective-permute-start.21 = (bf16[128,512]{1,0:T(8,128)(2,1)S(1)}, bf16[128,512]{1,0:T(8,128)(2,1)S(1)}, u32[]{:S(2)}, u32[]{:S(2)}) collective-permute-start(bf16[128,512]{1,0:T(8,128)(2,1)S(1)} %get-tuple-element.97), channel_id=1, source_target_pairs={{0,1},{1,2},{2,3},{3,4},{4,5},{5,6},{6,7},{7,8},{8,9},{9,10},{10,1... | collective-permute-start | bytes 393224 | tf_op jit(solution)/shard_map/ppermute | solution.py:32
  69.5 1.6 %context.2.refs_0_ = bf16[256,4096]{1,0:T(8,128)(2,1)} custom-call(bf16[4,1024,256]{2,1,0:T(8,128)(2,1)S(1)} %scores.2.p_ref, bf16[256,512]{1,0:T(8,128)(2,1)S(1)} %get-tuple-element.100.va_ref.vb_ref, bf16[256,512]{1,0:T(8,128)(2,1)S(1)} %get-tuple-element.100.va_ref.vb_ref), custom_call_target="tpu_custom_call" | custom-call | flops 268435456 | bytes 3145728 | tf_op jit(solution)/shard_map/context/pallas_call | solution.py:280
  71.1 3.4 %collective-permute-done.21.va_ref = bf16[128,512]{1,0:T(8,128)(2,1)S(1)} collective-permute-done((bf16[128,512]{1,0:T(8,128)(2,1)S(1)}, bf16[128,512]{1,0:T(8,128)(2,1)S(1)}, u32[]{:S(2)}, u32[]{:S(2)}) %collective-permute-start.21) | collective-permute-done | bytes 131104 | tf_op jit(solution)/shard_map/ppermute | solution.py:32
  74.5 1.6 %context.3 = bf16[256,4096]{1,0:T(8,128)(2,1)} custom-call(bf16[4,1024,256]{2,1,0:T(8,128)(2,1)S(1)} %scores.3.p_ref, bf16[128,512]{1,0:T(8,128)(2,1)S(1)} %collective-permute-done.21.va_ref, bf16[128,512]{1,0:T(8,128)(2,1)S(1)} %get-tuple-element.98.vb_ref, bf16[256,4096]{1,0:T(8,128)(2,1)} %context.2.refs_0_), custom_call_target="tpu_custom_call", output_to_operand_aliasing={{}: (3, {})} | custom-call | flops 268435456 | bytes 3145728 | tf_op jit(solution)/shard_map/context/pallas_call | solution.py:280
  (38 shorter events, 3.9 us)
Async XLA Ops:
  0.0 14.1 %collective-permute-start = (bf16[512,512]{1,0:T(8,128)(2,1)}, bf16[512,512]{1,0:T(8,128)(2,1)S(1)}, u32[]{:S(2)}, u32[]{:S(2)}) collective-permute-start(bf16[512,512]{1,0:T(8,128)(2,1)} %refs_2_.2), channel_id=1, source_target_pairs={{0,4},{1,5},{4,8},{5,9},{8,12},{9,13},{12,14},{13,15},{14,10},{15,... | collective-permute-start | bytes 1572872 | tf_op jit(solution)/shard_map/ppermute | solution.py:321
  1.6 14.1 %collective-permute-start.4 = (bf16[512,512]{1,0:T(8,128)(2,1)}, bf16[512,512]{1,0:T(8,128)(2,1)S(1)}, u32[]{:S(2)}, u32[]{:S(2)}) collective-permute-start(bf16[512,512]{1,0:T(8,128)(2,1)} %refs_2_.3), channel_id=1, source_target_pairs={{0,2},{1,3},{4,0},{5,1},{8,4},{9,5},{12,8},{13,9},{14,12},{15,13},... | collective-permute-start | bytes 1572872 | tf_op jit(solution)/shard_map/ppermute | solution.py:321
  2.8 2.2 %copy-start.1 = (bf16[256,8192]{1,0:T(8,128)(2,1)S(1)}, bf16[256,8192]{1,0:T(8,128)(2,1)}, u32[]{:S(2)}) copy-start(bf16[256,8192]{1,0:T(8,128)(2,1)} %h_ref.1) | copy-start | bytes 12582916
  5.0 3.3 %copy-start.4 = (s32[256]{0:T(256)S(1)}, s32[256]{0:T(256)}, u32[]{:S(2)}) copy-start(s32[256]{0:T(256)} %param.12) | copy-start | bytes 3076
  5.0 23.3 %copy-start.2 = (bf16[512,512]{1,0:T(8,128)(2,1)S(1)}, bf16[512,512]{1,0:T(8,128)(2,1)}, u32[]{:S(2)}) copy-start(bf16[512,512]{1,0:T(8,128)(2,1)} %refs_2_.2) | copy-start | bytes 1572868
  7.6 21.1 %collective-permute-start.2 = (bf16[128,4096]{1,0:T(8,128)(2,1)S(1)}, bf16[128,4096]{1,0:T(8,128)(2,1)S(1)}, u32[]{:S(2)}, u32[]{:S(2)}) collective-permute-start(bf16[128,4096]{1,0:T(8,128)(2,1)S(1)} %get-tuple-element.55), channel_id=1, source_target_pairs={{0,1},{1,0},{2,3},{3,2},{4,5},{5,4},{6,7},{7,6},{8,9},{9,8},{10,11... | collective-permute-start | bytes 3145736 | tf_op jit(solution)/shard_map/ppermute | solution.py:324
  7.7 22.5 %collective-permute-start.3 = (bf16[128,4096]{1,0:T(8,128)(2,1)S(1)}, bf16[128,4096]{1,0:T(8,128)(2,1)S(1)}, u32[]{:S(2)}, u32[]{:S(2)}) collective-permute-start(bf16[128,4096]{1,0:T(8,128)(2,1)S(1)} %get-tuple-element.56), channel_id=1, source_target_pairs={{0,1},{1,0},{2,3},{3,2},{4,5},{5,4},{6,7},{7,6},{8,9},{9,8},{10,11... | collective-permute-start | bytes 3145736 | tf_op jit(solution)/shard_map/ppermute | solution.py:324
  8.2 5.8 %collective-permute-start.1 = (s32[256]{0:T(256)S(1)}, s32[256]{0:T(256)S(1)}, u32[]{:S(2)}, u32[]{:S(2)}) collective-permute-start(s32[256]{0:T(256)S(1)} %copy-done.4), channel_id=1, source_target_pairs={{0,1},{1,2},{2,3},{3,4},{4,5},{5,6},{6,7},{7,8},{8,9},{9,10},{10,1... | collective-permute-start | bytes 3080 | tf_op jit(solution)/shard_map/ppermute | solution.py:32
  14.1 27.6 %copy-start.5 = (f32[1,128]{1,0:T(1,128)S(1)}, f32[1,128]{1,0:T(1,128)}, u32[]{:S(2)}) copy-start(f32[1,128]{1,0:T(1,128)} %constant.2.clone.freq_ref) | copy-start | bytes 1540
  14.1 12.6 %collective-permute-start.7 = (bf16[512,512]{1,0:T(8,128)(2,1)S(1)}, bf16[512,512]{1,0:T(8,128)(2,1)S(1)}, u32[]{:S(2)}, u32[]{:S(2)}) collective-permute-start(bf16[512,512]{1,0:T(8,128)(2,1)S(1)} %collective-permute-done.refs_3_), channel_id=1, source_target_pairs={{0,4},{1,5},{4,8},{5,9},{8,12},{9,13},{12,14},{13,15},{14,10},{15,... | collective-permute-start | bytes 1572872 | tf_op jit(solution)/shard_map/ppermute | solution.py:321
  15.6 12.6 %collective-permute-start.5 = (bf16[512,512]{1,0:T(8,128)(2,1)S(1)}, bf16[512,512]{1,0:T(8,128)(2,1)S(1)}, u32[]{:S(2)}, u32[]{:S(2)}) collective-permute-start(bf16[512,512]{1,0:T(8,128)(2,1)S(1)} %collective-permute-done.4.refs_3_), channel_id=1, source_target_pairs={{0,2},{1,3},{4,0},{5,1},{8,4},{9,5},{12,8},{13,9},{14,12},{15,13},... | collective-permute-start | bytes 1572872 | tf_op jit(solution)/shard_map/ppermute | solution.py:321
  16.1 15.6 %collective-permute-start.9 = (bf16[512,512]{1,0:T(8,128)(2,1)S(1)}, bf16[512,512]{1,0:T(8,128)(2,1)S(1)}, u32[]{:S(2)}, u32[]{:S(2)}) collective-permute-start(bf16[512,512]{1,0:T(8,128)(2,1)S(1)} %collective-permute-done.4.refs_3_), channel_id=1, source_target_pairs={{0,16},{1,17},{2,18},{3,19},{4,20},{5,21},{6,22},{7,23},{8,24},{9,... | collective-permute-start | bytes 1572872 | tf_op jit(solution)/shard_map/ppermute | solution.py:321
  26.7 11.7 %collective-permute-start.8 = (bf16[512,512]{1,0:T(8,128)(2,1)S(1)}, bf16[512,512]{1,0:T(8,128)(2,1)S(1)}, u32[]{:S(2)}, u32[]{:S(2)}) collective-permute-start(bf16[512,512]{1,0:T(8,128)(2,1)S(1)} %collective-permute-done.7.refs_4_), channel_id=1, source_target_pairs={{0,4},{1,5},{4,8},{5,9},{8,12},{9,13},{12,14},{13,15},{14,10},{15,... | collective-permute-start | bytes 1572872 | tf_op jit(solution)/shard_map/ppermute | solution.py:321
  28.3 14.9 %collective-permute-start.11 = (bf16[512,512]{1,0:T(8,128)(2,1)S(1)}, bf16[512,512]{1,0:T(8,128)(2,1)S(1)}, u32[]{:S(2)}, u32[]{:S(2)}) collective-permute-start(bf16[512,512]{1,0:T(8,128)(2,1)S(1)} %copy-done.2), channel_id=1, source_target_pairs={{0,2},{1,3},{4,0},{5,1},{8,4},{9,5},{12,8},{13,9},{14,12},{15,13},... | collective-permute-start | bytes 1572872 | tf_op jit(solution)/shard_map/ppermute | solution.py:321
  28.7 14.4 %collective-permute-start.10 = (bf16[512,512]{1,0:T(8,128)(2,1)S(1)}, bf16[512,512]{1,0:T(8,128)(2,1)S(1)}, u32[]{:S(2)}, u32[]{:S(2)}) collective-permute-start(bf16[512,512]{1,0:T(8,128)(2,1)S(1)} %collective-permute-done.7.refs_4_), channel_id=1, source_target_pairs={{0,16},{1,17},{2,18},{3,19},{4,20},{5,21},{6,22},{7,23},{8,24},{9,... | collective-permute-start | bytes 1572872 | tf_op jit(solution)/shard_map/ppermute | solution.py:321
  30.2 21.3 %collective-permute-start.6 = (bf16[512,512]{1,0:T(8,128)(2,1)S(1)}, bf16[512,512]{1,0:T(8,128)(2,1)S(1)}, u32[]{:S(2)}, u32[]{:S(2)}) collective-permute-start(bf16[512,512]{1,0:T(8,128)(2,1)S(1)} %collective-permute-done.5.refs_4_), channel_id=1, source_target_pairs={{0,2},{1,3},{4,0},{5,1},{8,4},{9,5},{12,8},{13,9},{14,12},{15,13},... | collective-permute-start | bytes 1572872 | tf_op jit(solution)/shard_map/ppermute | solution.py:321
  38.4 15.3 %collective-permute-start.14 = (bf16[512,512]{1,0:T(8,128)(2,1)S(1)}, bf16[512,512]{1,0:T(8,128)(2,1)S(1)}, u32[]{:S(2)}, u32[]{:S(2)}) collective-permute-start(bf16[512,512]{1,0:T(8,128)(2,1)S(1)} %collective-permute-done.8.refs_2_), channel_id=1, source_target_pairs={{0,16},{1,17},{2,18},{3,19},{4,20},{5,21},{6,22},{7,23},{8,24},{9,... | collective-permute-start | bytes 1572872 | tf_op jit(solution)/shard_map/ppermute | solution.py:321
  40.0 14.0 %collective-permute-start.16 = (bf16[512,512]{1,0:T(8,128)(2,1)S(1)}, bf16[512,512]{1,0:T(8,128)(2,1)S(1)}, u32[]{:S(2)}, u32[]{:S(2)}) collective-permute-start(bf16[512,512]{1,0:T(8,128)(2,1)S(1)} %collective-permute-done.8.refs_2_), channel_id=1, source_target_pairs={{0,4},{1,5},{4,8},{5,9},{8,12},{9,13},{12,14},{13,15},{14,10},{15,... | collective-permute-start | bytes 1572872 | tf_op jit(solution)/shard_map/ppermute | solution.py:321
  51.6 3.7 %copy-start.3 = (bf16[512,512]{1,0:T(8,128)(2,1)S(1)}, bf16[512,512]{1,0:T(8,128)(2,1)}, u32[]{:S(2)}) copy-start(bf16[512,512]{1,0:T(8,128)(2,1)} %refs_2_.3) | copy-start | bytes 1572868
  51.6 12.7 %collective-permute-start.12 = (bf16[512,512]{1,0:T(8,128)(2,1)S(1)}, bf16[512,512]{1,0:T(8,128)(2,1)S(1)}, u32[]{:S(2)}, u32[]{:S(2)}) collective-permute-start(bf16[512,512]{1,0:T(8,128)(2,1)S(1)} %collective-permute-done.6.refs_6_), channel_id=1, source_target_pairs={{0,2},{1,3},{4,0},{5,1},{8,4},{9,5},{12,8},{13,9},{14,12},{15,13},... | collective-permute-start | bytes 1572872 | tf_op jit(solution)/shard_map/ppermute | solution.py:321
  52.0 12.3 %collective-permute-start.13 = (bf16[512,512]{1,0:T(8,128)(2,1)S(1)}, bf16[512,512]{1,0:T(8,128)(2,1)S(1)}, u32[]{:S(2)}, u32[]{:S(2)}) collective-permute-start(bf16[512,512]{1,0:T(8,128)(2,1)S(1)} %collective-permute-done.9.refs_5_), channel_id=1, source_target_pairs={{0,4},{1,5},{4,8},{5,9},{8,12},{9,13},{12,14},{13,15},{14,10},{15,... | collective-permute-start | bytes 1572872 | tf_op jit(solution)/shard_map/ppermute | solution.py:321
  53.6 10.7 %collective-permute-start.15 = (bf16[512,512]{1,0:T(8,128)(2,1)S(1)}, bf16[512,512]{1,0:T(8,128)(2,1)S(1)}, u32[]{:S(2)}, u32[]{:S(2)}) collective-permute-start(bf16[512,512]{1,0:T(8,128)(2,1)S(1)} %collective-permute-done.6.refs_6_), channel_id=1, source_target_pairs={{0,16},{1,17},{2,18},{3,19},{4,20},{5,21},{6,22},{7,23},{8,24},{9,... | collective-permute-start | bytes 1572872 | tf_op jit(solution)/shard_map/ppermute | solution.py:321
  54.7 2.1 %collective-permute-start.17 = (f32[128,512]{1,0:T(8,128)S(1)}, f32[128,512]{1,0:T(8,128)S(1)}, u32[]{:S(2)}, u32[]{:S(2)}) collective-permute-start(f32[128,512]{1,0:T(8,128)S(1)} %get-tuple-element.75), channel_id=1, source_target_pairs={{0,1},{1,0},{2,3},{3,2},{4,5},{5,4},{6,7},{7,6},{8,9},{9,8},{10,11... | collective-permute-start | bytes 786440 | tf_op jit(solution)/shard_map/ppermute | solution.py:324
  54.8 2.0 %collective-permute-start.18 = (f32[128,512]{1,0:T(8,128)S(1)}, f32[128,512]{1,0:T(8,128)S(1)}, u32[]{:S(2)}, u32[]{:S(2)}) collective-permute-start(f32[128,512]{1,0:T(8,128)S(1)} %get-tuple-element.76), channel_id=1, source_target_pairs={{0,1},{1,0},{2,3},{3,2},{4,5},{5,4},{6,7},{7,6},{8,9},{9,8},{10,11... | collective-permute-start | bytes 786440 | tf_op jit(solution)/shard_map/ppermute | solution.py:324
  55.3 3.8 %copy-start = (bf16[256,4096]{1,0:T(8,128)(2,1)S(1)}, bf16[256,4096]{1,0:T(8,128)(2,1)}, u32[]{:S(2)}) copy-start(bf16[256,4096]{1,0:T(8,128)(2,1)} %q_ref.3) | copy-start | bytes 6291460
  57.1 7.2 %collective-permute-start.19 = (bf16[128,512]{1,0:T(8,128)(2,1)S(1)}, bf16[128,512]{1,0:T(8,128)(2,1)S(1)}, u32[]{:S(2)}, u32[]{:S(2)}) collective-permute-start(bf16[128,512]{1,0:T(8,128)(2,1)S(1)} %get-tuple-element.88), channel_id=1, source_target_pairs={{0,1},{1,2},{2,3},{3,4},{4,5},{5,6},{6,7},{7,8},{8,9},{9,10},{10,1... | collective-permute-start | bytes 393224 | tf_op jit(solution)/shard_map/ppermute | solution.py:32
  65.3 2.0 %collective-permute-start.20 = (f32[256,512]{1,0:T(8,128)S(1)}, f32[256,512]{1,0:T(8,128)S(1)}, u32[]{:S(2)}, u32[]{:S(2)}) collective-permute-start(f32[256,512]{1,0:T(8,128)S(1)} %get-tuple-element.91), channel_id=1, source_target_pairs={{0,1},{1,0},{2,3},{3,2},{4,5},{5,4},{6,7},{7,6},{8,9},{9,8},{10,11... | collective-permute-start | bytes 1572872 | tf_op jit(solution)/shard_map/ppermute | solution.py:324
  67.3 7.2 %collective-permute-start.21 = (bf16[128,512]{1,0:T(8,128)(2,1)S(1)}, bf16[128,512]{1,0:T(8,128)(2,1)S(1)}, u32[]{:S(2)}, u32[]{:S(2)}) collective-permute-start(bf16[128,512]{1,0:T(8,128)(2,1)S(1)} %get-tuple-element.97), channel_id=1, source_target_pairs={{0,1},{1,2},{2,3},{3,4},{4,5},{5,6},{6,7},{7,8},{8,9},{9,10},{10,1... | collective-permute-start | bytes 393224 | tf_op jit(solution)/shard_map/ppermute | solution.py:32

commit v11 on v9

--- a/solution.py
+++ b/solution.py
@@ -102,13 +102,14 @@
     columns = [pl.ds(pl.multiple_of(block_at(step) * depth, depth), depth) for step in steps]
     x = [jnp.concatenate([ref[:, c] for c in columns], axis=1) for ref in (xa_ref, *others)]
     w = jnp.concatenate([ref[...] for ref in weights], axis=0)
-    total = jnp.dot(jnp.concatenate(x, axis=0), w, preferred_element_type=F32)
-    held = jnp.concatenate([ref[...] for ref in before], axis=0) if carried else None
-    total = held + total if carried else total
-    at = 0
-    for ref in outs:
-        ref[...] = total[at : at + ref.shape[0]]
-        at += ref.shape[0]
+    blocks = [x[0], jnp.concatenate(x[1:], axis=0)]
+    for i, block in enumerate(blocks):
+        total = jnp.dot(block, w, preferred_element_type=F32)
+        total = before[i][...] + total if carried else total
+        at = 0
+        for ref in outs[:1] if i == 0 else outs[1:]:
+            ref[...] = total[at : at + ref.shape[0]]
+            at += ref.shape[0]
 
 
 def project(steps, xa, others, weights, before=(), split=1):

time: 76.5 us -> 76.5 us (level)
  no operation moved by 1% of the time
where the time goes in v11:
time: 76.5 us; the launch traced here: 76.1 us
  waiting for transfers between devices  34.9 us (46%)
  starting transfers between devices  22.7 us (30%)
  Pallas kernels  15.4 us (20%)
  local copies, waits for them, and re-layouts  2.94 us (4%)
    ppermute x14, waiting for transfers between devices, send(): return lax.ppermute(value, both, way)  24 us
    ppermute x14, starting transfers between devices, send(): return lax.ppermute(value, both, way)  15.3 us
    ppermute x3, waiting for transfers between devices, from_behind(): lax.ppermute(value, axis, [(source, source + steps) for source in range(i...  10.7 us
    ppermute x3, starting transfers between devices, from_behind(): lax.ppermute(value, axis, [(source, source + steps) for source in range(i...  6.2 us
    pallas_call x5, Pallas kernels, project(): pl.pallas_call(functools.partial(project_kernel, steps, len(others), len(...  5.22 us
    pallas_call x2, Pallas kernels, softmax_weights(): pl.pallas_call(functools.partial(scores_kernel, block), in_specs=[whole]...  3.42 us
    pallas_call x2, Pallas kernels, contexts(): pl.pallas_call(functools.partial(context_kernel, block), in_specs=[whole]...  3.2 us
    pallas_call x1, Pallas kernels, normalise(): pl.pallas_call(norm_kernel, grid=(rows // step,), in_specs=[pl.BlockSpec(...  2.66 us
  transfers between devices with their start and end apart: 22, of which 8 were waited for; matrix products, arithmetic and copies ran while one was open for 1% of the time, Pallas kernels for 17%

profile of v11, /device:TPU:8, one launch (start us, length us, event | category | flops | bytes accessed | tf_op | source)
XLA Modules:
  0.0 76.1 jit_solution(8849069410343827677)
XLA Ops:
  0.0 1.6 %collective-permute-start = (bf16[512,512]{1,0:T(8,128)(2,1)}, bf16[512,512]{1,0:T(8,128)(2,1)S(1)}, u32[]{:S(2)}, u32[]{:S(2)}) collective-permute-start(bf16[512,512]{1,0:T(8,128)(2,1)} %refs_2_.2), channel_id=1, source_target_pairs={{0,4},{1,5},{4,8},{5,9},{8,12},{9,13},{12,14},{13,15},{14,10},{15,... | collective-permute-start | bytes 1572872 | tf_op jit(solution)/shard_map/ppermute | solution.py:318
  2.0 0.7 reshape.9.g_ref
  2.8 2.2 %copy-done.1 = bf16[256,8192]{1,0:T(8,128)(2,1)S(1)} copy-done((bf16[256,8192]{1,0:T(8,128)(2,1)S(1)}, bf16[256,8192]{1,0:T(8,128)(2,1)}, u32[]{:S(2)}) %copy-start.1) | copy-done | bytes 4194328
  5.0 2.7 %norm.1 = (bf16[256,4096]{1,0:T(8,128)(2,1)S(1)}, bf16[128,4096]{1,0:T(8,128)(2,1)S(1)}, bf16[128,4096]{1,0:T(8,128)(2,1)S(1)}) custom-call(bf16[256,8192]{1,0:T(8,128)(2,1)S(1)} %copy-done.1, bf16[1,8192]{1,0:T(2,128)(2,1)S(1)} %reshape.9.g_ref), custom_call_target="tpu_custom_call" | custom-call | flops 16777216 | bytes 8388608 | tf_op jit(solution)/shard_map/norm/pallas_call | solution.py:64
  7.7 0.5 collective-permute-start.3
  8.2 2.0 %collective-permute-start.1 = (s32[256]{0:T(256)S(1)}, s32[256]{0:T(256)S(1)}, u32[]{:S(2)}, u32[]{:S(2)}) collective-permute-start(s32[256]{0:T(256)S(1)} %copy-done.4), channel_id=1, source_target_pairs={{0,1},{1,2},{2,3},{3,4},{4,5},{5,6},{6,7},{7,8},{8,9},{9,10},{10,1... | collective-permute-start | bytes 3080 | tf_op jit(solution)/shard_map/ppermute | solution.py:32
  10.2 3.9 %collective-permute-done.1 = s32[256]{0:T(256)S(1)} collective-permute-done((s32[256]{0:T(256)S(1)}, s32[256]{0:T(256)S(1)}, u32[]{:S(2)}, u32[]{:S(2)}) %collective-permute-start.1) | collective-permute-done | bytes 1056 | tf_op jit(solution)/shard_map/ppermute | solution.py:32
  14.1 1.6 %collective-permute-start.7 = (bf16[512,512]{1,0:T(8,128)(2,1)S(1)}, bf16[512,512]{1,0:T(8,128)(2,1)S(1)}, u32[]{:S(2)}, u32[]{:S(2)}) collective-permute-start(bf16[512,512]{1,0:T(8,128)(2,1)S(1)} %collective-permute-done.refs_3_), channel_id=1, source_target_pairs={{0,4},{1,5},{4,8},{5,9},{8,12},{9,13},{12,14},{13,15},{14,10},{15,... | collective-permute-start | bytes 1572872 | tf_op jit(solution)/shard_map/ppermute | solution.py:318
  16.1 1.5 %collective-permute-start.9 = (bf16[512,512]{1,0:T(8,128)(2,1)S(1)}, bf16[512,512]{1,0:T(8,128)(2,1)S(1)}, u32[]{:S(2)}, u32[]{:S(2)}) collective-permute-start(bf16[512,512]{1,0:T(8,128)(2,1)S(1)} %collective-permute-done.4.refs_3_), channel_id=1, source_target_pairs={{0,16},{1,17},{2,18},{3,19},{4,20},{5,21},{6,22},{7,23},{8,24},{9,... | collective-permute-start | bytes 1572872 | tf_op jit(solution)/shard_map/ppermute | solution.py:318
  17.6 9.1 %collective-permute-done.7.refs_4_ = bf16[512,512]{1,0:T(8,128)(2,1)S(1)} collective-permute-done((bf16[512,512]{1,0:T(8,128)(2,1)S(1)}, bf16[512,512]{1,0:T(8,128)(2,1)S(1)}, u32[]{:S(2)}, u32[]{:S(2)}) %collective-permute-start.7) | collective-permute-done | bytes 524320 | tf_op jit(solution)/shard_map/ppermute | solution.py:318
  26.7 1.6 %collective-permute-start.8 = (bf16[512,512]{1,0:T(8,128)(2,1)S(1)}, bf16[512,512]{1,0:T(8,128)(2,1)S(1)}, u32[]{:S(2)}, u32[]{:S(2)}) collective-permute-start(bf16[512,512]{1,0:T(8,128)(2,1)S(1)} %collective-permute-done.7.refs_4_), channel_id=1, source_target_pairs={{0,4},{1,5},{4,8},{5,9},{8,12},{9,13},{12,14},{13,15},{14,10},{15,... | collective-permute-start | bytes 1572872 | tf_op jit(solution)/shard_map/ppermute | solution.py:318
  28.7 1.5 %collective-permute-start.10 = (bf16[512,512]{1,0:T(8,128)(2,1)S(1)}, bf16[512,512]{1,0:T(8,128)(2,1)S(1)}, u32[]{:S(2)}, u32[]{:S(2)}) collective-permute-start(bf16[512,512]{1,0:T(8,128)(2,1)S(1)} %collective-permute-done.7.refs_4_), channel_id=1, source_target_pairs={{0,16},{1,17},{2,18},{3,19},{4,20},{5,21},{6,22},{7,23},{8,24},{9,... | collective-permute-start | bytes 1572872 | tf_op jit(solution)/shard_map/ppermute | solution.py:318
  30.7 1.0 %project.5 = (f32[256,512]{1,0:T(8,128)S(1)}, f32[256,512]{1,0:T(8,128)S(1)}) custom-call(bf16[256,4096]{1,0:T(8,128)(2,1)S(1)} %get-tuple-element.54.xa_ref, bf16[128,4096]{1,0:T(8,128)(2,1)S(1)} %collective-permute-done.2.refs_0_, bf16[128,4096]{1,0:T(8,128)(2,1)S(1)} %collective-permute-done.3.refs_1_, bf16[512,512]{1,0:T(8,128)(2,1)S(1)} %copy-done.2, ...), custom_call_target="tpu_custom_call" | custom-call | flops 805306368 | bytes 5767168 | tf_op jit(solution)/shard_map/project/pallas_call | solution.py:122
  31.7 6.7 %collective-permute-done.8.refs_2_ = bf16[512,512]{1,0:T(8,128)(2,1)S(1)} collective-permute-done((bf16[512,512]{1,0:T(8,128)(2,1)S(1)}, bf16[512,512]{1,0:T(8,128)(2,1)S(1)}, u32[]{:S(2)}, u32[]{:S(2)}) %collective-permute-start.8) | collective-permute-done | bytes 524320 | tf_op jit(solution)/shard_map/ppermute | solution.py:318
  38.4 1.7 %collective-permute-start.14 = (bf16[512,512]{1,0:T(8,128)(2,1)S(1)}, bf16[512,512]{1,0:T(8,128)(2,1)S(1)}, u32[]{:S(2)}, u32[]{:S(2)}) collective-permute-start(bf16[512,512]{1,0:T(8,128)(2,1)S(1)} %collective-permute-done.8.refs_2_), channel_id=1, source_target_pairs={{0,16},{1,17},{2,18},{3,19},{4,20},{5,21},{6,22},{7,23},{8,24},{9,... | collective-permute-start | bytes 1572872 | tf_op jit(solution)/shard_map/ppermute | solution.py:318
  40.0 1.6 %collective-permute-start.16 = (bf16[512,512]{1,0:T(8,128)(2,1)S(1)}, bf16[512,512]{1,0:T(8,128)(2,1)S(1)}, u32[]{:S(2)}, u32[]{:S(2)}) collective-permute-start(bf16[512,512]{1,0:T(8,128)(2,1)S(1)} %collective-permute-done.8.refs_2_), channel_id=1, source_target_pairs={{0,4},{1,5},{4,8},{5,9},{8,12},{9,13},{12,14},{13,15},{14,10},{15,... | collective-permute-start | bytes 1572872 | tf_op jit(solution)/shard_map/ppermute | solution.py:318
  41.6 0.7 tables.1
  42.3 0.8 %collective-permute-done.11.refs_4_ = bf16[512,512]{1,0:T(8,128)(2,1)S(1)} collective-permute-done((bf16[512,512]{1,0:T(8,128)(2,1)S(1)}, bf16[512,512]{1,0:T(8,128)(2,1)S(1)}, u32[]{:S(2)}, u32[]{:S(2)}) %collective-permute-start.11) | collective-permute-done | bytes 524320 | tf_op jit(solution)/shard_map/ppermute | solution.py:318
  43.1 1.0 %project.6 = (f32[256,512]{1,0:T(8,128)S(1)}, f32[256,512]{1,0:T(8,128)S(1)}) custom-call(bf16[256,4096]{1,0:T(8,128)(2,1)S(1)} %get-tuple-element.54.xa_ref, bf16[128,4096]{1,0:T(8,128)(2,1)S(1)} %collective-permute-done.2.refs_0_, bf16[128,4096]{1,0:T(8,128)(2,1)S(1)} %collective-permute-done.3.refs_1_, ...), custom_call_target="tpu_custom_call" | custom-call | flops 805306368 | bytes 5767168 | tf_op jit(solution)/shard_map/project/pallas_call | solution.py:122
  44.1 7.5 %collective-permute-done.6.refs_6_ = bf16[512,512]{1,0:T(8,128)(2,1)S(1)} collective-permute-done((bf16[512,512]{1,0:T(8,128)(2,1)S(1)}, bf16[512,512]{1,0:T(8,128)(2,1)S(1)}, u32[]{:S(2)}, u32[]{:S(2)}) %collective-permute-start.6) | collective-permute-done | bytes 524320 | tf_op jit(solution)/shard_map/ppermute | solution.py:318
  52.0 1.6 %collective-permute-start.13 = (bf16[512,512]{1,0:T(8,128)(2,1)S(1)}, bf16[512,512]{1,0:T(8,128)(2,1)S(1)}, u32[]{:S(2)}, u32[]{:S(2)}) collective-permute-start(bf16[512,512]{1,0:T(8,128)(2,1)S(1)} %collective-permute-done.9.refs_5_), channel_id=1, source_target_pairs={{0,4},{1,5},{4,8},{5,9},{8,12},{9,13},{12,14},{13,15},{14,10},{15,... | collective-permute-start | bytes 1572872 | tf_op jit(solution)/shard_map/ppermute | solution.py:318
  54.0 0.7 project.7
  55.3 1.5 %project.8 = (f32[256,512]{1,0:T(8,128)S(1)}, f32[256,512]{1,0:T(8,128)S(1)}) custom-call(bf16[256,4096]{1,0:T(8,128)(2,1)S(1)} %get-tuple-element.54.xa_ref, bf16[128,4096]{1,0:T(8,128)(2,1)S(1)} %collective-permute-done.2.refs_0_, bf16[128,4096]{1,0:T(8,128)(2,1)S(1)} %collective-permute-done.3.refs_1_, bf16[512,512]{1,0:T(8,128)(2,1)S(1)} %copy-done.3, ...), custom_call_target="tpu_custom_call" | custom-call | flops 1342177280 | bytes 6815744 | tf_op jit(solution)/shard_map/project/pallas_call | solution.py:122
  57.1 2.0 %collective-permute-start.19 = (bf16[128,512]{1,0:T(8,128)(2,1)S(1)}, bf16[128,512]{1,0:T(8,128)(2,1)S(1)}, u32[]{:S(2)}, u32[]{:S(2)}) collective-permute-start(bf16[128,512]{1,0:T(8,128)(2,1)S(1)} %get-tuple-element.88), channel_id=1, source_target_pairs={{0,1},{1,2},{2,3},{3,4},{4,5},{5,6},{6,7},{7,8},{8,9},{9,10},{10,1... | collective-permute-start | bytes 393224 | tf_op jit(solution)/shard_map/ppermute | solution.py:32
  59.1 1.7 %scores.2.p_ref = bf16[4,1024,256]{2,1,0:T(8,128)(2,1)S(1)} custom-call(bf16[256,4096]{1,0:T(8,128)(2,1)S(1)} %copy-done, bf16[256,512]{1,0:T(8,128)(2,1)S(1)} %get-tuple-element.86.ka_ref.kb_ref, bf16[256,512]{1,0:T(8,128)(2,1)S(1)} %get-tuple-element.86.ka_ref.kb_ref, f32[2,128,256]{2,1,0:T(8,128)S(1)} %get-tuple-element.87.bias_ref), custom_call_target="tpu_custom_call" | custom-call | flops 268435456 | bytes 3145728 | tf_op jit(solution)/shard_map/scores/pallas_call | solution.py:239
  60.8 3.5 %collective-permute-done.19.ka_ref = bf16[128,512]{1,0:T(8,128)(2,1)S(1)} collective-permute-done((bf16[128,512]{1,0:T(8,128)(2,1)S(1)}, bf16[128,512]{1,0:T(8,128)(2,1)S(1)}, u32[]{:S(2)}, u32[]{:S(2)}) %collective-permute-start.19) | collective-permute-done | bytes 131104 | tf_op jit(solution)/shard_map/ppermute | solution.py:32
  64.3 1.0 %project.9 = (f32[256,512]{1,0:T(8,128)S(1)}, f32[256,512]{1,0:T(8,128)S(1)}) custom-call(bf16[256,4096]{1,0:T(8,128)(2,1)S(1)} %get-tuple-element.54.xa_ref, bf16[128,4096]{1,0:T(8,128)(2,1)S(1)} %collective-permute-done.2.refs_0_, bf16[128,4096]{1,0:T(8,128)(2,1)S(1)} %collective-permute-done.3.refs_1_, ...), custom_call_target="tpu_custom_call" | custom-call | flops 805306368 | bytes 5767168 | tf_op jit(solution)/shard_map/project/pallas_call | solution.py:122
  65.4 1.7 %scores.3.p_ref = bf16[4,1024,256]{2,1,0:T(8,128)(2,1)S(1)} custom-call(bf16[256,4096]{1,0:T(8,128)(2,1)S(1)} %copy-done, bf16[128,512]{1,0:T(8,128)(2,1)S(1)} %collective-permute-done.19.ka_ref, bf16[128,512]{1,0:T(8,128)(2,1)S(1)} %get-tuple-element.93.kb_ref, f32[2,128,256]{2,1,0:T(8,128)S(1)} %get-tuple-element.87.bias_ref), custom_call_target="tpu_custom_call" | custom-call | flops 268435456 | bytes 3145728 | tf_op jit(solution)/shard_map/scores/pallas_call | solution.py:239
  67.3 2.2 %collective-permute-start.21 = (bf16[128,512]{1,0:T(8,128)(2,1)S(1)}, bf16[128,512]{1,0:T(8,128)(2,1)S(1)}, u32[]{:S(2)}, u32[]{:S(2)}) collective-permute-start(bf16[128,512]{1,0:T(8,128)(2,1)S(1)} %get-tuple-element.97), channel_id=1, source_target_pairs={{0,1},{1,2},{2,3},{3,4},{4,5},{5,6},{6,7},{7,8},{8,9},{9,10},{10,1... | collective-permute-start | bytes 393224 | tf_op jit(solution)/shard_map/ppermute | solution.py:32
  69.6 1.6 %context.2.refs_0_ = bf16[256,4096]{1,0:T(8,128)(2,1)} custom-call(bf16[4,1024,256]{2,1,0:T(8,128)(2,1)S(1)} %scores.2.p_ref, bf16[256,512]{1,0:T(8,128)(2,1)S(1)} %get-tuple-element.100.va_ref.vb_ref, bf16[256,512]{1,0:T(8,128)(2,1)S(1)} %get-tuple-element.100.va_ref.vb_ref), custom_call_target="tpu_custom_call" | custom-call | flops 268435456 | bytes 3145728 | tf_op jit(solution)/shard_map/context/pallas_call | solution.py:277
  71.2 3.3 %collective-permute-done.21.va_ref = bf16[128,512]{1,0:T(8,128)(2,1)S(1)} collective-permute-done((bf16[128,512]{1,0:T(8,128)(2,1)S(1)}, bf16[128,512]{1,0:T(8,128)(2,1)S(1)}, u32[]{:S(2)}, u32[]{:S(2)}) %collective-permute-start.21) | collective-permute-done | bytes 131104 | tf_op jit(solution)/shard_map/ppermute | solution.py:32
  74.5 1.6 %context.3 = bf16[256,4096]{1,0:T(8,128)(2,1)} custom-call(bf16[4,1024,256]{2,1,0:T(8,128)(2,1)S(1)} %scores.3.p_ref, bf16[128,512]{1,0:T(8,128)(2,1)S(1)} %collective-permute-done.21.va_ref, bf16[128,512]{1,0:T(8,128)(2,1)S(1)} %get-tuple-element.98.vb_ref, bf16[256,4096]{1,0:T(8,128)(2,1)} %context.2.refs_0_), custom_call_target="tpu_custom_call", output_to_operand_aliasing={{}: (3, {})} | custom-call | flops 268435456 | bytes 3145728 | tf_op jit(solution)/shard_map/context/pallas_call | solution.py:277
  (38 shorter events, 3.9 us)
Async XLA Ops:
  0.0 14.1 %collective-permute-start = (bf16[512,512]{1,0:T(8,128)(2,1)}, bf16[512,512]{1,0:T(8,128)(2,1)S(1)}, u32[]{:S(2)}, u32[]{:S(2)}) collective-permute-start(bf16[512,512]{1,0:T(8,128)(2,1)} %refs_2_.2), channel_id=1, source_target_pairs={{0,4},{1,5},{4,8},{5,9},{8,12},{9,13},{12,14},{13,15},{14,10},{15,... | collective-permute-start | bytes 1572872 | tf_op jit(solution)/shard_map/ppermute | solution.py:318
  1.6 14.1 %collective-permute-start.4 = (bf16[512,512]{1,0:T(8,128)(2,1)}, bf16[512,512]{1,0:T(8,128)(2,1)S(1)}, u32[]{:S(2)}, u32[]{:S(2)}) collective-permute-start(bf16[512,512]{1,0:T(8,128)(2,1)} %refs_2_.3), channel_id=1, source_target_pairs={{0,2},{1,3},{4,0},{5,1},{8,4},{9,5},{12,8},{13,9},{14,12},{15,13},... | collective-permute-start | bytes 1572872 | tf_op jit(solution)/shard_map/ppermute | solution.py:318
  2.8 2.2 %copy-start.1 = (bf16[256,8192]{1,0:T(8,128)(2,1)S(1)}, bf16[256,8192]{1,0:T(8,128)(2,1)}, u32[]{:S(2)}) copy-start(bf16[256,8192]{1,0:T(8,128)(2,1)} %h_ref.1) | copy-start | bytes 12582916
  5.0 3.3 %copy-start.4 = (s32[256]{0:T(256)S(1)}, s32[256]{0:T(256)}, u32[]{:S(2)}) copy-start(s32[256]{0:T(256)} %param.12) | copy-start | bytes 3076
  5.0 23.3 %copy-start.2 = (bf16[512,512]{1,0:T(8,128)(2,1)S(1)}, bf16[512,512]{1,0:T(8,128)(2,1)}, u32[]{:S(2)}) copy-start(bf16[512,512]{1,0:T(8,128)(2,1)} %refs_2_.2) | copy-start | bytes 1572868
  7.6 21.1 %collective-permute-start.2 = (bf16[128,4096]{1,0:T(8,128)(2,1)S(1)}, bf16[128,4096]{1,0:T(8,128)(2,1)S(1)}, u32[]{:S(2)}, u32[]{:S(2)}) collective-permute-start(bf16[128,4096]{1,0:T(8,128)(2,1)S(1)} %get-tuple-element.55), channel_id=1, source_target_pairs={{0,1},{1,0},{2,3},{3,2},{4,5},{5,4},{6,7},{7,6},{8,9},{9,8},{10,11... | collective-permute-start | bytes 3145736 | tf_op jit(solution)/shard_map/ppermute | solution.py:321
  7.7 22.5 %collective-permute-start.3 = (bf16[128,4096]{1,0:T(8,128)(2,1)S(1)}, bf16[128,4096]{1,0:T(8,128)(2,1)S(1)}, u32[]{:S(2)}, u32[]{:S(2)}) collective-permute-start(bf16[128,4096]{1,0:T(8,128)(2,1)S(1)} %get-tuple-element.56), channel_id=1, source_target_pairs={{0,1},{1,0},{2,3},{3,2},{4,5},{5,4},{6,7},{7,6},{8,9},{9,8},{10,11... | collective-permute-start | bytes 3145736 | tf_op jit(solution)/shard_map/ppermute | solution.py:321
  8.2 5.8 %collective-permute-start.1 = (s32[256]{0:T(256)S(1)}, s32[256]{0:T(256)S(1)}, u32[]{:S(2)}, u32[]{:S(2)}) collective-permute-start(s32[256]{0:T(256)S(1)} %copy-done.4), channel_id=1, source_target_pairs={{0,1},{1,2},{2,3},{3,4},{4,5},{5,6},{6,7},{7,8},{8,9},{9,10},{10,1... | collective-permute-start | bytes 3080 | tf_op jit(solution)/shard_map/ppermute | solution.py:32
  14.1 27.6 %copy-start.5 = (f32[1,128]{1,0:T(1,128)S(1)}, f32[1,128]{1,0:T(1,128)}, u32[]{:S(2)}) copy-start(f32[1,128]{1,0:T(1,128)} %constant.2.clone.freq_ref) | copy-start | bytes 1540
  14.1 12.6 %collective-permute-start.7 = (bf16[512,512]{1,0:T(8,128)(2,1)S(1)}, bf16[512,512]{1,0:T(8,128)(2,1)S(1)}, u32[]{:S(2)}, u32[]{:S(2)}) collective-permute-start(bf16[512,512]{1,0:T(8,128)(2,1)S(1)} %collective-permute-done.refs_3_), channel_id=1, source_target_pairs={{0,4},{1,5},{4,8},{5,9},{8,12},{9,13},{12,14},{13,15},{14,10},{15,... | collective-permute-start | bytes 1572872 | tf_op jit(solution)/shard_map/ppermute | solution.py:318
  15.6 12.6 %collective-permute-start.5 = (bf16[512,512]{1,0:T(8,128)(2,1)S(1)}, bf16[512,512]{1,0:T(8,128)(2,1)S(1)}, u32[]{:S(2)}, u32[]{:S(2)}) collective-permute-start(bf16[512,512]{1,0:T(8,128)(2,1)S(1)} %collective-permute-done.4.refs_3_), channel_id=1, source_target_pairs={{0,2},{1,3},{4,0},{5,1},{8,4},{9,5},{12,8},{13,9},{14,12},{15,13},... | collective-permute-start | bytes 1572872 | tf_op jit(solution)/shard_map/ppermute | solution.py:318
  16.1 15.6 %collective-permute-start.9 = (bf16[512,512]{1,0:T(8,128)(2,1)S(1)}, bf16[512,512]{1,0:T(8,128)(2,1)S(1)}, u32[]{:S(2)}, u32[]{:S(2)}) collective-permute-start(bf16[512,512]{1,0:T(8,128)(2,1)S(1)} %collective-permute-done.4.refs_3_), channel_id=1, source_target_pairs={{0,16},{1,17},{2,18},{3,19},{4,20},{5,21},{6,22},{7,23},{8,24},{9,... | collective-permute-start | bytes 1572872 | tf_op jit(solution)/shard_map/ppermute | solution.py:318
  26.7 11.7 %collective-permute-start.8 = (bf16[512,512]{1,0:T(8,128)(2,1)S(1)}, bf16[512,512]{1,0:T(8,128)(2,1)S(1)}, u32[]{:S(2)}, u32[]{:S(2)}) collective-permute-start(bf16[512,512]{1,0:T(8,128)(2,1)S(1)} %collective-permute-done.7.refs_4_), channel_id=1, source_target_pairs={{0,4},{1,5},{4,8},{5,9},{8,12},{9,13},{12,14},{13,15},{14,10},{15,... | collective-permute-start | bytes 1572872 | tf_op jit(solution)/shard_map/ppermute | solution.py:318
  28.3 14.9 %collective-permute-start.11 = (bf16[512,512]{1,0:T(8,128)(2,1)S(1)}, bf16[512,512]{1,0:T(8,128)(2,1)S(1)}, u32[]{:S(2)}, u32[]{:S(2)}) collective-permute-start(bf16[512,512]{1,0:T(8,128)(2,1)S(1)} %copy-done.2), channel_id=1, source_target_pairs={{0,2},{1,3},{4,0},{5,1},{8,4},{9,5},{12,8},{13,9},{14,12},{15,13},... | collective-permute-start | bytes 1572872 | tf_op jit(solution)/shard_map/ppermute | solution.py:318
  28.7 14.4 %collective-permute-start.10 = (bf16[512,512]{1,0:T(8,128)(2,1)S(1)}, bf16[512,512]{1,0:T(8,128)(2,1)S(1)}, u32[]{:S(2)}, u32[]{:S(2)}) collective-permute-start(bf16[512,512]{1,0:T(8,128)(2,1)S(1)} %collective-permute-done.7.refs_4_), channel_id=1, source_target_pairs={{0,16},{1,17},{2,18},{3,19},{4,20},{5,21},{6,22},{7,23},{8,24},{9,... | collective-permute-start | bytes 1572872 | tf_op jit(solution)/shard_map/ppermute | solution.py:318
  30.2 21.3 %collective-permute-start.6 = (bf16[512,512]{1,0:T(8,128)(2,1)S(1)}, bf16[512,512]{1,0:T(8,128)(2,1)S(1)}, u32[]{:S(2)}, u32[]{:S(2)}) collective-permute-start(bf16[512,512]{1,0:T(8,128)(2,1)S(1)} %collective-permute-done.5.refs_4_), channel_id=1, source_target_pairs={{0,2},{1,3},{4,0},{5,1},{8,4},{9,5},{12,8},{13,9},{14,12},{15,13},... | collective-permute-start | bytes 1572872 | tf_op jit(solution)/shard_map/ppermute | solution.py:318
  38.4 15.3 %collective-permute-start.14 = (bf16[512,512]{1,0:T(8,128)(2,1)S(1)}, bf16[512,512]{1,0:T(8,128)(2,1)S(1)}, u32[]{:S(2)}, u32[]{:S(2)}) collective-permute-start(bf16[512,512]{1,0:T(8,128)(2,1)S(1)} %collective-permute-done.8.refs_2_), channel_id=1, source_target_pairs={{0,16},{1,17},{2,18},{3,19},{4,20},{5,21},{6,22},{7,23},{8,24},{9,... | collective-permute-start | bytes 1572872 | tf_op jit(solution)/shard_map/ppermute | solution.py:318
  40.0 14.0 %collective-permute-start.16 = (bf16[512,512]{1,0:T(8,128)(2,1)S(1)}, bf16[512,512]{1,0:T(8,128)(2,1)S(1)}, u32[]{:S(2)}, u32[]{:S(2)}) collective-permute-start(bf16[512,512]{1,0:T(8,128)(2,1)S(1)} %collective-permute-done.8.refs_2_), channel_id=1, source_target_pairs={{0,4},{1,5},{4,8},{5,9},{8,12},{9,13},{12,14},{13,15},{14,10},{15,... | collective-permute-start | bytes 1572872 | tf_op jit(solution)/shard_map/ppermute | solution.py:318
  51.6 3.7 %copy-start.3 = (bf16[512,512]{1,0:T(8,128)(2,1)S(1)}, bf16[512,512]{1,0:T(8,128)(2,1)}, u32[]{:S(2)}) copy-start(bf16[512,512]{1,0:T(8,128)(2,1)} %refs_2_.3) | copy-start | bytes 1572868
  51.6 12.7 %collective-permute-start.12 = (bf16[512,512]{1,0:T(8,128)(2,1)S(1)}, bf16[512,512]{1,0:T(8,128)(2,1)S(1)}, u32[]{:S(2)}, u32[]{:S(2)}) collective-permute-start(bf16[512,512]{1,0:T(8,128)(2,1)S(1)} %collective-permute-done.6.refs_6_), channel_id=1, source_target_pairs={{0,2},{1,3},{4,0},{5,1},{8,4},{9,5},{12,8},{13,9},{14,12},{15,13},... | collective-permute-start | bytes 1572872 | tf_op jit(solution)/shard_map/ppermute | solution.py:318
  52.0 12.3 %collective-permute-start.13 = (bf16[512,512]{1,0:T(8,128)(2,1)S(1)}, bf16[512,512]{1,0:T(8,128)(2,1)S(1)}, u32[]{:S(2)}, u32[]{:S(2)}) collective-permute-start(bf16[512,512]{1,0:T(8,128)(2,1)S(1)} %collective-permute-done.9.refs_5_), channel_id=1, source_target_pairs={{0,4},{1,5},{4,8},{5,9},{8,12},{9,13},{12,14},{13,15},{14,10},{15,... | collective-permute-start | bytes 1572872 | tf_op jit(solution)/shard_map/ppermute | solution.py:318
  53.6 10.7 %collective-permute-start.15 = (bf16[512,512]{1,0:T(8,128)(2,1)S(1)}, bf16[512,512]{1,0:T(8,128)(2,1)S(1)}, u32[]{:S(2)}, u32[]{:S(2)}) collective-permute-start(bf16[512,512]{1,0:T(8,128)(2,1)S(1)} %collective-permute-done.6.refs_6_), channel_id=1, source_target_pairs={{0,16},{1,17},{2,18},{3,19},{4,20},{5,21},{6,22},{7,23},{8,24},{9,... | collective-permute-start | bytes 1572872 | tf_op jit(solution)/shard_map/ppermute | solution.py:318
  54.7 2.1 %collective-permute-start.17 = (f32[128,512]{1,0:T(8,128)S(1)}, f32[128,512]{1,0:T(8,128)S(1)}, u32[]{:S(2)}, u32[]{:S(2)}) collective-permute-start(f32[128,512]{1,0:T(8,128)S(1)} %get-tuple-element.75), channel_id=1, source_target_pairs={{0,1},{1,0},{2,3},{3,2},{4,5},{5,4},{6,7},{7,6},{8,9},{9,8},{10,11... | collective-permute-start | bytes 786440 | tf_op jit(solution)/shard_map/ppermute | solution.py:321
  54.8 2.1 %collective-permute-start.18 = (f32[128,512]{1,0:T(8,128)S(1)}, f32[128,512]{1,0:T(8,128)S(1)}, u32[]{:S(2)}, u32[]{:S(2)}) collective-permute-start(f32[128,512]{1,0:T(8,128)S(1)} %get-tuple-element.76), channel_id=1, source_target_pairs={{0,1},{1,0},{2,3},{3,2},{4,5},{5,4},{6,7},{7,6},{8,9},{9,8},{10,11... | collective-permute-start | bytes 786440 | tf_op jit(solution)/shard_map/ppermute | solution.py:321
  55.3 3.8 %copy-start = (bf16[256,4096]{1,0:T(8,128)(2,1)S(1)}, bf16[256,4096]{1,0:T(8,128)(2,1)}, u32[]{:S(2)}) copy-start(bf16[256,4096]{1,0:T(8,128)(2,1)} %q_ref.3) | copy-start | bytes 6291460
  57.1 7.2 %collective-permute-start.19 = (bf16[128,512]{1,0:T(8,128)(2,1)S(1)}, bf16[128,512]{1,0:T(8,128)(2,1)S(1)}, u32[]{:S(2)}, u32[]{:S(2)}) collective-permute-start(bf16[128,512]{1,0:T(8,128)(2,1)S(1)} %get-tuple-element.88), channel_id=1, source_target_pairs={{0,1},{1,2},{2,3},{3,4},{4,5},{5,6},{6,7},{7,8},{8,9},{9,10},{10,1... | collective-permute-start | bytes 393224 | tf_op jit(solution)/shard_map/ppermute | solution.py:32
  65.3 2.0 %collective-permute-start.20 = (f32[256,512]{1,0:T(8,128)S(1)}, f32[256,512]{1,0:T(8,128)S(1)}, u32[]{:S(2)}, u32[]{:S(2)}) collective-permute-start(f32[256,512]{1,0:T(8,128)S(1)} %get-tuple-element.91), channel_id=1, source_target_pairs={{0,1},{1,0},{2,3},{3,2},{4,5},{5,4},{6,7},{7,6},{8,9},{9,8},{10,11... | collective-permute-start | bytes 1572872 | tf_op jit(solution)/shard_map/ppermute | solution.py:321
  67.3 7.2 %collective-permute-start.21 = (bf16[128,512]{1,0:T(8,128)(2,1)S(1)}, bf16[128,512]{1,0:T(8,128)(2,1)S(1)}, u32[]{:S(2)}, u32[]{:S(2)}) collective-permute-start(bf16[128,512]{1,0:T(8,128)(2,1)S(1)} %get-tuple-element.97), channel_id=1, source_target_pairs={{0,1},{1,2},{2,3},{3,4},{4,5},{5,6},{6,7},{7,8},{8,9},{9,10},{10,1... | collective-permute-start | bytes 393224 | tf_op jit(solution)/shard_map/ppermute | solution.py:32
